TPU v7x, 32 devices: a whole 2x2x4 slice. The times are simulated.
32 devices in a mesh: grp: 2 (over x), pool: 8 (over z, y), tp: 2 (over core).
Axes of the slice: x: 2, y: 2, z: 4, core: 2. Of those that a mesh axis runs over, the one named last changes fastest.
Arguments:
- hidden_states: bfloat16 [6144, 5120], P(('grp', 'pool'), 'tp'), parts along dimension 0, may hold values from -6 to 6
- kv_weight: bfloat16 [5120, 4, 256], P('tp'), may hold values from -0.078125 to 0.078125
- shrink_factors: bfloat16 [16, 5120, 64], P(('grp', 'pool'), 'tp'), parts along dimension 0, may hold values from -0.078125 to 0.078125
- expand_factors: bfloat16 [16, 64, 4, 256], P(('grp', 'pool')), parts along dimension 0, may hold values from -0.75 to 0.75
- adapter_ids: int32 [128], P(('grp', 'pool')), parts along dimension 0, may hold values from 0 to 7, as said below
- cache_lengths: int32 [128], P(('grp', 'pool')), parts along dimension 0, may hold values from 2 to 128, as said below
- tree_parents: int32 [128, 48], P(('grp', 'pool')), parts along dimension 0, may hold values from 0 to 46, as said below
- queries: bfloat16 [6144, 32, 128], P(('grp', 'pool'), 'tp'), parts along dimension 0, may hold values from -120 to 120
- cache_keys: bfloat16 [128, 128, 4, 128], P(('grp', 'pool'), None, 'tp'), parts along dimension 0, may hold values from -6 to 6
- cache_values: bfloat16 [128, 128, 4, 128], P(('grp', 'pool'), None, 'tp'), parts along dimension 0, may hold values from -6 to 6
- key_gain: float32 [128], replicated, may hold values from 0.1 to 1.9
Outputs:
- attention: bfloat16 [6144, 32, 128], P(('grp', 'pool'), 'tp'), parts along dimension 0
- tree_cache: bfloat16 [6144, 4, 256], P(('grp', 'pool'), 'tp'), parts along dimension 0
There are 2 independent parts, one for each index of `grp`. A program takes and returns all parts, laid end to end along the dimension named above; an argument that names none is the same for every part. Nothing has to cross between parts.
Inputs may be any that keep to these rules, and one draw needn't show every extreme that they name: `adapter_ids`: the 8 requests on one index of pool name adapters of 8 different owners, the owner of adapter a being a; some owner's adapters are named by exactly one request of every index of pool. `cache_lengths`: some request holds exactly 128 positions. tree_parents[r, 0] = 0 and tree_parents[r, i] < i for i >= 1.
All inputs are finite; a program needn't handle non-finite values.
Results may differ from a plain program's by a relative error of at most 0.0054.
Values may be sent and summed in bfloat16 or wider, within the bound.
No kernel may reach another device: no remote copies, remote signals or barrier semaphores. Data moves between devices by JAX's collectives and lax.ppermute only.
A program may use at most 128 MiB of HBM per device.

v0:
```python
import math

import jax
import jax.numpy as jnp
from jax import lax
from jax.sharding import PartitionSpec as P


def ancestry(tree_parents):
    node_count = tree_parents.shape[-1]
    node_ids = jnp.arange(node_count, dtype=jnp.int32)
    parent_hot = (tree_parents[..., :, None] == node_ids).astype(jnp.float32)
    identity_mat = (node_ids[:, None] == node_ids[None, :]).astype(jnp.float32)
    reach = jnp.minimum(parent_hot + identity_mat, 1.0)
    span_now = 1
    while span_now < node_count:
        reach = jnp.minimum(
            jnp.einsum("...ij,...jk->...ik", reach, reach, precision=lax.Precision.HIGHEST), 1.0
        )
        span_now = span_now * 2
    return reach


def rotary(vectors, positions):
    head_size = vectors.shape[-1]
    half_size = head_size // 2
    frequency = jnp.exp(
        jnp.arange(half_size, dtype=jnp.float32) * (-2.0 * math.log(1000000.0) / head_size)
    )
    angles = positions[..., None] * frequency
    cosine = jnp.cos(angles)
    sine_part = jnp.sin(angles)
    front_half = vectors[..., :half_size]
    back_half = vectors[..., half_size:]
    return jnp.concatenate(
        [front_half * cosine - back_half * sine_part, back_half * cosine + front_half * sine_part],
        -1,
    )


def prepare(projected, key_gain, positions, head_size):
    key_part = projected[..., :head_size]
    value_part = projected[..., head_size:]
    norm_scale = lax.rsqrt(jnp.mean(key_part * key_part, -1, keepdims=True) + 1e-06)
    key_part = rotary(key_part * norm_scale * key_gain, positions)
    return jnp.concatenate([key_part, value_part], -1).astype(jnp.bfloat16)


def attend_all(queries, cache_keys, cache_values, tree_cache, cache_lengths, reach):
    requests, tree_size = (reach.shape[0], reach.shape[1])
    context = cache_keys.shape[1]
    heads_here = cache_keys.shape[2]
    head_size = cache_keys.shape[3]
    per_group = queries.shape[1] // heads_here
    query_blocks = queries.reshape(requests, tree_size, heads_here, per_group, head_size)
    score_scale = 1.0 / math.sqrt(head_size)
    tree_keys = tree_cache[..., :head_size]
    tree_values = tree_cache[..., head_size:]
    cache_scores = (
        jnp.einsum(
            "rtsgd,rcsd->rsgtc", query_blocks, cache_keys, preferred_element_type=jnp.float32
        )
        * score_scale
    )
    tree_scores = (
        jnp.einsum("rtsgd,rjsd->rsgtj", query_blocks, tree_keys, preferred_element_type=jnp.float32)
        * score_scale
    )
    cache_valid = jnp.arange(context)[None, :] < cache_lengths[:, None]
    cache_scores = jnp.where(cache_valid[:, None, None, None, :], cache_scores, -1e30)
    tree_scores = jnp.where((reach > 0.5)[:, None, None, :, :], tree_scores, -1e30)
    scores = jnp.concatenate([cache_scores, tree_scores], -1)
    row_max = jnp.max(scores, -1, keepdims=True)
    exponent = jnp.exp(scores - row_max)
    weights = (exponent / jnp.sum(exponent, -1, keepdims=True)).astype(jnp.bfloat16)
    output = jnp.einsum(
        "rsgtc,rcsd->rtsgd",
        weights[..., :context],
        cache_values,
        preferred_element_type=jnp.float32,
    )
    output = output + jnp.einsum(
        "rsgtj,rjsd->rtsgd", weights[..., context:], tree_values, preferred_element_type=jnp.float32
    )
    return output.astype(jnp.bfloat16).reshape(
        requests * tree_size, heads_here * per_group, head_size
    )


def per_device(
    hidden_states,
    kv_weight,
    shrink_factors,
    expand_factors,
    adapter_ids,
    cache_lengths,
    tree_parents,
    queries,
    cache_keys,
    cache_values,
    key_gain,
):
    requests, tree_size = tree_parents.shape
    row_count, half_width = hidden_states.shape
    kv_heads, kv_width = (kv_weight.shape[1], kv_weight.shape[2])
    head_size = kv_width // 2
    per_owner, rank_size = (shrink_factors.shape[0], shrink_factors.shape[2])
    pool_count = lax.axis_size("pool")
    heads_here = kv_heads // lax.axis_size("tp")
    base_part = jnp.dot(
        hidden_states,
        kv_weight.reshape(half_width, kv_heads * kv_width),
        preferred_element_type=jnp.float32,
    )
    grouped = hidden_states.reshape(requests, tree_size, half_width)
    flat_expand = expand_factors.reshape(per_owner, rank_size, kv_heads * kv_width)
    owners = adapter_ids // per_owner
    local_index = adapter_ids % per_owner
    matches = owners[None, :] == jnp.arange(pool_count)[:, None]
    slots = jnp.einsum(
        "pr,rtd->ptd", matches.astype(jnp.bfloat16), grouped, preferred_element_type=jnp.float32
    ).astype(jnp.bfloat16)
    slot_adapter = jnp.sum(jnp.where(matches, local_index[None, :] + 1, 0), 1) - 1
    slot_tags = jnp.broadcast_to(slot_adapter[:, None], (pool_count, tree_size))
    arrived = lax.all_to_all(slots, "pool", split_axis=0, concat_axis=0, tiled=True)
    tags_here = lax.all_to_all(slot_tags, "pool", split_axis=0, concat_axis=0, tiled=True)
    chooser = (tags_here[:, 0][:, None] == jnp.arange(per_owner)[None, :]).astype(jnp.bfloat16)
    chosen_shrink = jnp.einsum(
        "pa,adk->pdk", chooser, shrink_factors, preferred_element_type=jnp.float32
    ).astype(jnp.bfloat16)
    chosen_expand = jnp.einsum(
        "pa,akn->pkn", chooser, flat_expand, preferred_element_type=jnp.float32
    )
    shrunk = jnp.einsum("ptd,pdk->ptk", arrived, chosen_shrink, preferred_element_type=jnp.float32)
    deltas = jnp.einsum("ptk,pkn->ptn", shrunk, chosen_expand, precision=lax.Precision.HIGHEST)
    returned = lax.all_to_all(deltas, "pool", split_axis=0, concat_axis=0, tiled=True)
    delta_rows = jnp.einsum(
        "pr,ptn->rtn", matches.astype(jnp.float32), returned, precision=lax.Precision.HIGHEST
    )
    partial_sum = base_part + delta_rows.reshape(row_count, kv_heads * kv_width)
    summed = lax.psum(partial_sum, "tp").reshape(row_count, kv_heads, kv_width)
    own_heads = lax.dynamic_slice_in_dim(summed, lax.axis_index("tp") * heads_here, heads_here, 1)
    reach = ancestry(tree_parents)
    positions = cache_lengths.astype(jnp.float32)[:, None] + jnp.sum(reach, -1) - 1.0
    tree_cache = prepare(
        own_heads.reshape(requests, tree_size, heads_here, kv_width),
        key_gain,
        positions[:, :, None],
        head_size,
    )
    attention = attend_all(queries, cache_keys, cache_values, tree_cache, cache_lengths, reach)
    return (attention, tree_cache.reshape(row_count, heads_here, kv_width))


def solution(mesh):
    placed = (
        P(("grp", "pool"), "tp"),
        P("tp", None, None),
        P(("grp", "pool"), "tp", None),
        P(("grp", "pool"), None, None, None),
        P(("grp", "pool")),
        P(("grp", "pool")),
        P(("grp", "pool"), None),
        P(("grp", "pool"), "tp", None),
        P(("grp", "pool"), None, "tp", None),
        P(("grp", "pool"), None, "tp", None),
        P(),
    )
    return jax.shard_map(
        per_device,
        mesh=mesh,
        in_specs=placed,
        out_specs=(P(("grp", "pool"), "tp", None), P(("grp", "pool"), "tp", None)),
        check_vma=False,
    )
```

profile of v0, /device:TPU:0, one launch (start us, length us, event | category | flops | bytes accessed | tf_op | source)
XLA Modules:
  0.0 161.9 jit_solution(10986686416049024755)
XLA Ops:
  7.2 0.9 select_reduce_fusion
  8.1 0.7 broadcast_in_dim.39
  8.7 7.3 %all-to-all-start.1 = ((s32[8,1,48]{2,1,0:T(1,128)}), s32[8,1,48]{2,1,0:T(1,128)S(1)}, u32[]{:S(2)}, u32[]{:S(2)}) async-start(s32[8,1,48]{2,1,0:T(1,128)} %broadcast_in_dim.39), calls=%async_computation.1 | async-start | bytes 8192 | tf_op jit(solution)/shard_map/all_to_all | solution.py:126
  16.0 2.1 %convolution_convert_fusion = bf16[8,48,2560]{2,0,1:T(8,128)(2,1)S(1)} fusion(bf16[8,48,2560]{2,1,0:T(8,128)(2,1)S(1)} %bitcast.66, s32[8]{0:T(128)} %param.15), kind=kOutput, calls=%fused_computation.5 | convolution fusion | flops 16711744 | bytes 3932192 | tf_op jit(solution)/shard_map/pr,rtd->ptd/dot_general | solution.py:120
  18.2 1.8 %copy.87 = bf16[8,48,2560]{2,1,0:T(8,128)(2,1)} copy(bf16[8,48,2560]{2,0,1:T(8,128)(2,1)S(1)} %convolution_convert_fusion) | data formatting | bytes 3932160 | tf_op jit(solution)/shard_map/convert_element_type | solution.py:122
  20.0 2.4 %all-to-all-done.1 = s32[8,1,48]{2,1,0:T(1,128)S(1)} async-done(((s32[8,1,48]{2,1,0:T(1,128)}), s32[8,1,48]{2,1,0:T(1,128)S(1)}, u32[]{:S(2)}, u32[]{:S(2)}) %all-to-all-start.1) | async-done | bytes 1568 | tf_op jit(solution)/shard_map/all_to_all | solution.py:126
  22.4 4.3 %all-to-all-start = ((bf16[8,48,2560]{2,1,0:T(8,128)(2,1)}), bf16[8,48,2560]{2,1,0:T(8,128)(2,1)}, u32[]{:S(2)}, u32[]{:S(2)}) async-start(bf16[8,48,2560]{2,1,0:T(8,128)(2,1)} %copy.87), calls=%async_computation | async-start | bytes 3932160 | tf_op jit(solution)/shard_map/all_to_all | solution.py:125
  26.9 44.1 %all-to-all-done = bf16[8,48,2560]{2,1,0:T(8,128)(2,1)} async-done(((bf16[8,48,2560]{2,1,0:T(8,128)(2,1)}), bf16[8,48,2560]{2,1,0:T(8,128)(2,1)}, u32[]{:S(2)}, u32[]{:S(2)}) %all-to-all-start) | async-done | bytes 1966112 | tf_op jit(solution)/shard_map/all_to_all | solution.py:125
  71.1 2.5 %fusion.3 = f32[8,48,64]{2,1,0:T(8,128)S(1)} fusion(bf16[8,48,2560]{2,1,0:T(8,128)(2,1)} %all-to-all-done, f32[2560,64]{0,1:T(8,128)S(1)} %bitcast_convert_fusion, f32[8]{0:T(128)S(1)} %convert_reduce_fusion), kind=kOutput, calls=%fused_computation.10 | convolution fusion | flops 128450560 | bytes 2719776 | tf_op jit(solution)/shard_map/ptd,pdk->ptk/dot_general | solution.py:134
  73.6 2.7 %fusion.6 = f32[8,48,1024]{2,1,0:T(8,128)} fusion(f32[8,48,64]{2,1,0:T(8,128)S(1)} %fusion.3, f32[64,1024]{1,0:T(8,128)S(1)} %bitcast.76, f32[8]{0:T(128)S(1)} %convert_reduce_fusion), kind=kOutput, calls=%fused_computation.13 | convolution fusion | flops 302514176 | bytes 1933344 | tf_op jit(solution)/shard_map/ptk,pkn->ptn/dot_general | solution.py:135
  76.3 3.6 %all-to-all-start.2 = ((f32[8,48,1024]{2,1,0:T(8,128)}), f32[8,48,1024]{2,1,0:T(8,128)S(1)}, u32[]{:S(2)}, u32[]{:S(2)}) async-start(f32[8,48,1024]{2,1,0:T(8,128)} %fusion.6), calls=%async_computation.2 | async-start | bytes 3145728 | tf_op jit(solution)/shard_map/all_to_all | solution.py:136
  80.2 6.5 %copy.121 = bf16[320,8,4,256]{3,1,2,0:T(8,128)(2,1)} copy(bf16[320,8,4,256]{3,2,1,0:T(4,128)(2,1)} %bitcast.72) | data formatting | bytes 10485760
  86.7 0.4 convolution_minimum_fusion.5
  87.8 1.0 convolution_minimum_fusion.2
  88.8 28.3 %all-to-all-done.2 = f32[8,48,1024]{2,1,0:T(8,128)S(1)} async-done(((f32[8,48,1024]{2,1,0:T(8,128)}), f32[8,48,1024]{2,1,0:T(8,128)S(1)}, u32[]{:S(2)}, u32[]{:S(2)}) %all-to-all-start.2) | async-done | bytes 1572896 | tf_op jit(solution)/shard_map/all_to_all | solution.py:136
  117.1 1.7 %fusion.12 = f32[8,48,1024]{2,0,1:T(8,128)S(1)} fusion(f32[8,48,1024]{2,1,0:T(8,128)S(1)} %all-to-all-done.2, s32[8]{0:T(128)S(1)} %copy-done.7), kind=kOutput, calls=%fused_computation.21 | convolution fusion | flops 37748800 | bytes 3145760 | tf_op jit(solution)/shard_map/pr,ptn->rtn/dot_general | solution.py:137
  118.8 0.9 copy.89
  119.8 2.2 %bitcast_add_fusion.1 = f32[384,1024]{1,0:T(8,128)S(1)} fusion(f32[8,48,1024]{2,1,0:T(8,128)S(1)} %copy.89, bf16[384,2560]{1,0:T(8,128)(2,1)S(1)} %copy-done, bf16[2560,1024]{1,0:T(8,128)(2,1)S(1)} %bitcast.73), kind=kOutput, calls=%fused_computation.20 | convolution fusion | flops 2013659136 | bytes 10354688 | tf_op jit(solution)/shard_map/dot_general | solution.py:110
  122.0 1.3 copy.150
  123.6 0.3 broadcast_compare_fusion
  124.3 0.8 multiply_cosine_fusion
  125.1 4.0 %fusion.37 = (f32[8,2,8,48]{3,2,1,0:T(8,128)S(1)}, f32[8,2,8,48,128]{4,3,2,1,0:T(8,128)}) fusion(bf16[8,48,2,8,128]{4,3,2,1,0:T(8,128)(2,1)} %bitcast.83, bf16[8,128,2,128,1]{3,2,1,0,4:T(2,128)(2,1)S(1)} %bitcast.85, pred[8,128]{1,0:T(8,128)(4,1)S(1)} %iota_compare_fusion.4), kind=kOutput, calls=%fused_computation.73 | convolution fusion | flops 203679744 | bytes 5268480 | tf_op jit(solution)/shard_map/rtsgd,rcsd->rsgtc/dot_general | solution.py:60
  129.1 13.9 %all-reduce.2.cloned.1.call-done = f32[384,4,256]{2,0,1:T(8,128)} async-done(((f32[384,4,256]{2,0,1:T(8,128)}), f32[384,4,256]{2,0,1:T(8,128)}) %all-reduce.2.cloned.1.call-update) | async-done | bytes 1572880 | tf_op jit(solution)/shard_map/psum | solution.py:141
  143.0 1.3 constant_dynamic-slice_fusion
  145.0 1.2 fusion.38
  146.3 0.6 copy-done.1
  146.9 1.9 %fusion.1 = f32[8,2,8,48]{3,2,1,0:T(8,128)S(1)} fusion(f32[8,2,8,48,48]{4,3,2,1,0:T(8,128)S(1)} %get-tuple-element.19, f32[8,2,8,48,128]{4,3,2,1,0:T(8,128)S(1)} %copy-done.1, f32[8,2,8,48]{3,2,1,0:T(8,128)S(1)} %reduce_max.22), kind=kLoop, calls=%fused_computation.4 | loop fusion | flops 3237888 | bytes 4374528 | tf_op jit(solution)/shard_map/reduce_sum | solution.py:75
  148.8 2.2 %divide_convert_fusion = bf16[8,2,8,48,176]{4,3,2,1,0:T(8,128)(2,1)S(1)} fusion(f32[8,2,8,48,48]{4,3,2,1,0:T(8,128)S(1)} %get-tuple-element.19, f32[8,2,8,48,128]{4,3,2,1,0:T(8,128)S(1)} %copy-done.1, f32[8,2,8,48]{3,2,1,0:T(8,128)S(1)} %fusion.1, f32[8,2,8,48]{3,2,1,0:T(8,128)S(1)} %reduce_max.22), kind=kLoop, calls=%fused_computation.2 | loop fusion | flops 4325376 | bytes 6537216 | tf_op jit(solution)/shard_map/convert_element_type | solution.py:75
  151.0 0.6 fusion.10
  151.6 0.6 fusion.2
  152.1 1.5 copy.95
  153.9 1.2 copy.101
  (51 shorter events, 2.6 us)
Async XLA Ops:
  7.2 8.9 %copy-start = (bf16[384,2560]{1,0:T(8,128)(2,1)S(1)}, bf16[384,2560]{1,0:T(8,128)(2,1)}, u32[]{:S(2)}) copy-start(bf16[384,2560]{1,0:T(8,128)(2,1)} %param.11) | copy-start | bytes 5898244
  8.7 13.7 %all-to-all-start.1 = ((s32[8,1,48]{2,1,0:T(1,128)}), s32[8,1,48]{2,1,0:T(1,128)S(1)}, u32[]{:S(2)}, u32[]{:S(2)}) async-start(s32[8,1,48]{2,1,0:T(1,128)} %broadcast_in_dim.39), calls=%async_computation.1 | async-start | bytes 8192 | tf_op jit(solution)/shard_map/all_to_all | solution.py:126
  20.0 6.7 %copy-start.6 = (bf16[1,64,4,256]{3,2,1,0:T(4,128)(2,1)S(1)}, bf16[1,64,4,256]{3,2,1,0:T(4,128)(2,1)}, u32[]{:S(2)}) copy-start(bf16[1,64,4,256]{3,2,1,0:T(4,128)(2,1)} %param.14) | copy-start | bytes 393220
  20.0 6.8 %copy-start.5 = (bf16[1,2560,64]{1,2,0:T(8,128)(2,1)S(1)}, bf16[1,2560,64]{1,2,0:T(8,128)(2,1)}, u32[]{:S(2)}) copy-start(bf16[1,2560,64]{1,2,0:T(8,128)(2,1)} %param.13) | copy-start | bytes 983044
  22.4 48.7 %all-to-all-start = ((bf16[8,48,2560]{2,1,0:T(8,128)(2,1)}), bf16[8,48,2560]{2,1,0:T(8,128)(2,1)}, u32[]{:S(2)}, u32[]{:S(2)}) async-start(bf16[8,48,2560]{2,1,0:T(8,128)(2,1)} %copy.87), calls=%async_computation | async-start | bytes 3932160 | tf_op jit(solution)/shard_map/all_to_all | solution.py:125
  76.3 40.8 %all-to-all-start.2 = ((f32[8,48,1024]{2,1,0:T(8,128)}), f32[8,48,1024]{2,1,0:T(8,128)S(1)}, u32[]{:S(2)}, u32[]{:S(2)}) async-start(f32[8,48,1024]{2,1,0:T(8,128)} %fusion.6), calls=%async_computation.2 | async-start | bytes 3145728 | tf_op jit(solution)/shard_map/all_to_all | solution.py:136
  80.0 63.0 %all-reduce.2.cloned.1.call-start = ((), (), s32[]{:S(2)}) async-start(), calls=%async_computation.3 | async-start | bytes 3145728 | tf_op jit(solution)/shard_map/psum | solution.py:141
  80.2 6.5 %copy-start.12 = (s32[8]{0:T(128)S(1)}, s32[8]{0:T(128)}, u32[]{:S(2)}) copy-start(s32[8]{0:T(128)} %param.16) | copy-start | bytes 100
  80.2 6.5 %copy-start.11 = (s32[8,48]{1,0:T(8,128)S(1)}, s32[8,48]{1,0:T(8,128)}, u32[]{:S(2)}) copy-start(s32[8,48]{1,0:T(8,128)} %param.17) | copy-start | bytes 4612
  80.2 36.9 %copy-start.7 = (s32[8]{0:T(128)S(1)}, s32[8]{0:T(128)}, u32[]{:S(2)}) copy-start(s32[8]{0:T(128)} %param.15) | copy-start | bytes 100
  117.1 2.6 %copy-start.2 = (bf16[320,8,4,256]{3,1,2,0:T(8,128)(2,1)S(1)}, bf16[320,8,4,256]{3,1,2,0:T(8,128)(2,1)}, u32[]{:S(2)}) copy-start(bf16[320,8,4,256]{3,1,2,0:T(8,128)(2,1)} %copy.121) | copy-start | bytes 15728644
  122.0 1.3 copy-start.3
  122.0 3.1 %copy-start.10 = (bf16[8,128,2,128]{3,2,1,0:T(2,128)(2,1)S(1)}, bf16[8,128,2,128]{3,2,1,0:T(2,128)(2,1)}, u32[]{:S(2)}) copy-start(bf16[8,128,2,128]{3,2,1,0:T(2,128)(2,1)} %param.19) | copy-start | bytes 1572868
  125.0 19.5 %copy-start.8 = (f32[128]{0:T(128)S(1)}, f32[128]{0:T(128)}, u32[]{:S(2)}) copy-start(f32[128]{0:T(128)} %param.21) | copy-start | bytes 1540
  143.0 2.0 %copy-start.9 = (bf16[384,16,128]{2,1,0:T(8,128)(2,1)S(1)}, bf16[384,16,128]{2,1,0:T(8,128)(2,1)}, u32[]{:S(2)}) copy-start(bf16[384,16,128]{2,1,0:T(8,128)(2,1)} %param.18) | copy-start | bytes 4718596
  145.0 1.9 %copy-start.1 = (f32[8,2,8,48,128]{4,3,2,1,0:T(8,128)S(1)}, f32[8,2,8,48,128]{4,3,2,1,0:T(8,128)}, u32[]{:S(2)}) copy-start(f32[8,2,8,48,128]{4,3,2,1,0:T(8,128)} %get-tuple-element.17) | copy-start | bytes 9437188
  148.8 2.2 %copy-start.4 = (bf16[8,128,2,128]{3,2,1,0:T(2,128)(2,1)S(1)}, bf16[8,128,2,128]{3,2,1,0:T(2,128)(2,1)}, u32[]{:S(2)}) copy-start(bf16[8,128,2,128]{3,2,1,0:T(2,128)(2,1)} %param.20) | copy-start | bytes 1572868
Sparse Core Ops, SparseCore 0:
  123.4 19.4 all-reduce.1
where the time goes:
time: 162 us
  waiting for transfers between devices  88.8 us (55%)
  matrix products  20.3 us (13%)
  local copies, waits for them, and re-layouts  16 us (10%)
  starting transfers between devices  15.5 us (10%)
  between operations  14.4 us (9%)
  other arithmetic  7 us (4%)
    all_to_all x1, waiting for transfers between devices, per_device(): lax.all_to_all(slots, 'pool', split_axis=0, concat_axis=0, tiled=True)  44.1 us
    all_to_all x1, waiting for transfers between devices, per_device(): lax.all_to_all(deltas, 'pool', split_axis=0, concat_axis=0, tiled=True)  28.3 us
    psum x1, waiting for transfers between devices, per_device(): summed = lax.psum(partial_sum, 'tp').reshape(row_count, kv_heads, kv_width)  13.9 us
    unnamed x30, local copies, waits for them, and re-layouts  8.37 us
    all_to_all x1, starting transfers between devices, per_device(): lax.all_to_all(slot_tags, 'pool', split_axis=0, concat_axis=0, tiled=True)  7.28 us
    all_to_all x1, starting transfers between devices, per_device(): lax.all_to_all(slots, 'pool', split_axis=0, concat_axis=0, tiled=True)  4.32 us
    dot_general x1, matrix products, attend_all(): jnp.einsum('rtsgd,rcsd->rsgtc', query_blocks, cache_keys, preferred_eleme...  3.99 us
    all_to_all x1, starting transfers between devices, per_device(): lax.all_to_all(deltas, 'pool', split_axis=0, concat_axis=0, tiled=True)  3.64 us
  transfers between devices with their start and end apart: 4, of which 4 were waited for; matrix products, arithmetic and copies ran while one was open for 11% of the time, Pallas kernels for 0%

commit v1 on v0

v1 whole, which is shorter than its diff:
```python
import math

import jax
import jax.numpy as jnp
import numpy as np
from jax import lax
from jax.experimental import pallas as pl
from jax.experimental.pallas import tpu as pltpu
from jax.sharding import PartitionSpec as P

F32 = jnp.float32
BF16 = jnp.bfloat16


def ring_order(count):
    if count == 8:
        return list(range(0, count, 2)) + list(range(count - 1, 0, -2))
    return list(range(count))


def ancestry(tree_parents):
    node_count = tree_parents.shape[-1]
    node_ids = jnp.arange(node_count, dtype=jnp.int32)
    parent_hot = tree_parents[..., :, None] == node_ids
    identity_mat = node_ids[:, None] == node_ids[None, :]
    reach = (parent_hot | identity_mat).astype(BF16)
    span_now = 1
    while span_now < node_count:
        product = jnp.einsum("...ij,...jk->...ik", reach, reach, preferred_element_type=F32)
        reach = jnp.minimum(product, 1.0).astype(BF16)
        span_now = span_now * 2
    return reach.astype(F32)


def finish_kernel(
    request_ref,
    base_ref,
    shrunk_ref,
    expand_ref,
    cosine_ref,
    sine_ref,
    gain_ref,
    bias_ref,
    query_ref,
    key_ref,
    value_ref,
    *rest,
):
    attention_ref, cache_ref = rest[-2:]
    tree_size, heads, head_size = query_ref.shape
    kv_heads = key_ref.shape[1]
    context = key_ref.shape[2]
    per_group = heads // kv_heads
    score_scale = math.log2(math.e) / math.sqrt(head_size)
    expand = expand_ref[0]
    shrunk = shrunk_ref[0]
    high = shrunk.astype(BF16)
    left = shrunk - high.astype(F32)
    middle = left.astype(BF16)
    low = (left - middle.astype(F32)).astype(BF16)
    delta = (
        jnp.dot(low, expand, preferred_element_type=F32)
        + jnp.dot(middle, expand, preferred_element_type=F32)
        + jnp.dot(high, expand, preferred_element_type=F32)
    )
    projected = base_ref[...] + delta
    cosine = cosine_ref[...]
    sine = sine_ref[...]
    gain = gain_ref[...]
    queries = query_ref[...].astype(F32)
    bias = bias_ref[...]
    bias = jnp.broadcast_to(bias[:, None, :], (tree_size, per_group, bias.shape[1])).reshape(
        tree_size * per_group, bias.shape[1]
    )
    pad = jnp.zeros((bias.shape[1] - context - tree_size, head_size), BF16)
    outputs = []
    caches = []
    for g in range(kv_heads):
        at = 2 * head_size * g
        key = projected[:, at : at + head_size]
        value = projected[:, at + head_size : at + 2 * head_size]
        norm = lax.rsqrt(jnp.mean(key * key, -1, keepdims=True) + 1e-06)
        key = key * norm * gain
        key = key * cosine + pltpu.roll(key, head_size // 2, 1) * sine
        caches.append(jnp.concatenate([key, value], -1))
        keys = jnp.concatenate([key_ref[0, g], key.astype(BF16), pad], 0)
        values = jnp.concatenate([value_ref[0, g], value.astype(BF16), pad], 0)
        rows = queries[:, per_group * g : per_group * (g + 1), :].reshape(
            tree_size * per_group, head_size
        )
        scores = lax.dot_general(
            rows.astype(BF16), keys, (((1,), (1,)), ((), ())), preferred_element_type=F32
        )
        scores = scores + bias
        row_max = jnp.max(scores, -1, keepdims=True)
        exponent = jnp.exp2((scores - row_max) * score_scale)
        total = jnp.sum(exponent, -1, keepdims=True)
        weights = (exponent * (1.0 / total)).astype(BF16)
        output = jnp.dot(weights, values, preferred_element_type=F32)
        outputs.append(output.reshape(tree_size, per_group, head_size))
    attention_ref[...] = jnp.concatenate(outputs, 1).astype(BF16)
    cache_ref[...] = jnp.stack(caches, 1).astype(BF16)


def finish(batch, shared, previous):
    request_ids, shrunk, expand = batch
    base, cosine, sine, gain, bias, queries, keys, values = shared
    count, tree_size, rank_size = shrunk.shape
    rows, heads, head_size = queries.shape
    columns = base.shape[1]
    kv_heads, context = keys.shape[1], keys.shape[2]
    row_block = lambda width: pl.BlockSpec((tree_size, width), lambda i, ids: (ids[i], 0))
    in_specs = [
        row_block(columns),
        pl.BlockSpec((1, tree_size, rank_size), lambda i, ids: (i, 0, 0)),
        pl.BlockSpec((1, rank_size, columns), lambda i, ids: (i, 0, 0)),
        row_block(head_size),
        row_block(head_size),
        pl.BlockSpec((1, head_size), lambda i, ids: (0, 0)),
        row_block(bias.shape[1]),
        pl.BlockSpec((tree_size, heads, head_size), lambda i, ids: (ids[i], 0, 0)),
        pl.BlockSpec((1, kv_heads, context, head_size), lambda i, ids: (ids[i], 0, 0, 0)),
        pl.BlockSpec((1, kv_heads, context, head_size), lambda i, ids: (ids[i], 0, 0, 0)),
    ]
    operands = [request_ids, base, shrunk, expand, cosine, sine, gain, bias, queries, keys, values]
    aliases = {}
    if previous is not None:
        aliases = {len(operands): 0, len(operands) + 1: 1}
        operands += list(previous)
        in_specs += [pl.BlockSpec(memory_space=pl.ANY)] * 2
    return pl.pallas_call(
        finish_kernel,
        grid_spec=pltpu.PrefetchScalarGridSpec(
            num_scalar_prefetch=1,
            grid=(count,),
            in_specs=in_specs,
            out_specs=[
                pl.BlockSpec((tree_size, heads, head_size), lambda i, ids: (ids[i], 0, 0)),
                pl.BlockSpec((tree_size, kv_heads, 2 * head_size), lambda i, ids: (ids[i], 0, 0)),
            ],
        ),
        out_shape=[
            jax.ShapeDtypeStruct((rows, heads, head_size), BF16),
            jax.ShapeDtypeStruct((rows, kv_heads, 2 * head_size), BF16),
        ],
        input_output_aliases=aliases,
        compiler_params=pltpu.CompilerParams(vmem_limit_bytes=32 * 1024 * 1024),
        cost_estimate=pl.CostEstimate(
            flops=count * 80_000_000, bytes_accessed=count * 900_000, transcendentals=count * 200_000
        ),
    )(*operands)


def per_device(
    hidden_states,
    kv_weight,
    shrink_factors,
    expand_factors,
    adapter_ids,
    cache_lengths,
    tree_parents,
    queries,
    cache_keys,
    cache_values,
    key_gain,
):
    requests, tree_size = tree_parents.shape
    row_count, half_width = hidden_states.shape
    kv_heads, kv_width = (kv_weight.shape[1], kv_weight.shape[2])
    head_size = kv_width // 2
    rank_size = shrink_factors.shape[2]
    context = cache_keys.shape[1]
    pool_count = lax.axis_size("pool")
    heads_here = kv_heads // lax.axis_size("tp")
    columns = heads_here * kv_width
    me = lax.axis_index("pool")
    core = lax.axis_index("tp")
    swap = [(0, 1), (1, 0)]

    shrink = shrink_factors[0].T
    expand = lax.dynamic_slice_in_dim(expand_factors[0], core * heads_here, heads_here, 1)
    cut = (half_width + columns) // 2 - columns
    first = jnp.concatenate([expand.reshape(rank_size, columns), shrink[:, :cut]], 1)
    second = shrink[:, cut:]

    order = ring_order(pool_count)
    onward = [(order[i], order[(i + 1) % pool_count]) for i in range(pool_count)]
    backward = [(b, a) for a, b in onward]
    order_array = jnp.asarray(np.array(order, np.int32))
    place_array = jnp.asarray(np.argsort(np.array(order)).astype(np.int32))
    place = place_array[me]

    def owner_at(offset):
        return order_array[(place + offset + pool_count) % pool_count]

    arrivals = [[(owner_at(0), first, second)]]
    front = rear = (first, second)
    for step in range(1, pool_count // 2):
        front = tuple(lax.ppermute(piece, "pool", onward) for piece in front)
        rear = tuple(lax.ppermute(piece, "pool", backward) for piece in rear)
        arrivals.append([(owner_at(-step), *front), (owner_at(step), *rear)])
    arrivals.append(
        [
            (
                owner_at(pool_count // 2),
                lax.ppermute(front[0], "pool", onward),
                lax.ppermute(rear[1], "pool", backward),
            )
        ]
    )

    base_part = jnp.dot(
        hidden_states,
        kv_weight.reshape(half_width, kv_heads * kv_width),
        preferred_element_type=F32,
    )
    base_away = lax.dynamic_slice_in_dim(base_part, (1 - core) * columns, columns, 1)
    base_here = lax.dynamic_slice_in_dim(base_part, core * columns, columns, 1)
    base = base_here + lax.ppermute(base_away, "tp", swap)

    reach = ancestry(tree_parents)
    positions = cache_lengths.astype(F32)[:, None] + jnp.sum(reach, -1) - 1.0
    half_size = head_size // 2
    frequency = jnp.exp(
        jnp.arange(half_size, dtype=F32) * (-2.0 * math.log(1000000.0) / head_size)
    )
    angles = positions.reshape(row_count, 1) * frequency
    cosine = jnp.cos(angles)
    sine = jnp.sin(angles)
    cosine = jnp.concatenate([cosine, cosine], 1)
    sine = jnp.concatenate([-sine, sine], 1)
    cache_valid = jnp.arange(context)[None, :] < cache_lengths[:, None]
    cache_valid = jnp.broadcast_to(cache_valid[:, None, :], (requests, tree_size, context))
    span = -(-(context + tree_size) // 128) * 128
    spare = jnp.zeros((requests, tree_size, span - context - tree_size), bool)
    allowed = jnp.concatenate([cache_valid, reach > 0.5, spare], -1)
    bias = jnp.where(allowed, 0.0, -1e30).astype(F32).reshape(row_count, span)
    keys = cache_keys.transpose(0, 2, 1, 3)
    values = cache_values.transpose(0, 2, 1, 3)
    shared = (base, cosine, sine, key_gain.reshape(1, head_size), bias, queries, keys, values)

    def shrunk_of(owner, one, two):
        hot = adapter_ids == owner
        request = jnp.argmax(hot).astype(jnp.int32)
        rows = lax.dynamic_slice_in_dim(hidden_states, request * tree_size, tree_size, 0)
        partial = lax.dot_general(
            rows[:, :cut], one[:, columns:], (((1,), (1,)), ((), ())), preferred_element_type=F32
        ) + lax.dot_general(
            rows[:, cut:], two, (((1,), (1,)), ((), ())), preferred_element_type=F32
        )
        return request, partial, one[:, :columns]

    if pool_count == requests:
        groups = [sum(arrivals, [])]
    else:
        groups = None
    if groups is not None:
        outputs = None
        for group in groups:
            found = [shrunk_of(*arrival) for arrival in group]
            request_ids = jnp.stack([item[0] for item in found])
            partial = jnp.stack([item[1] for item in found])
            shrunk = partial + lax.ppermute(partial, "tp", swap)
            batch = (request_ids, shrunk, jnp.stack([item[2] for item in found]))
            outputs = finish(batch, shared, outputs)
    else:
        flat = sum(arrivals, [])
        owners = jnp.stack([arrival[0] for arrival in flat])
        found = [shrunk_of(*arrival) for arrival in flat]
        slot = jnp.argmax(adapter_ids[:, None] == owners[None, :], 1)
        partial = jnp.stack([item[1] for item in found])[slot]
        shrunk = partial + lax.ppermute(partial, "tp", swap)
        batch = (
            jnp.arange(requests, dtype=jnp.int32),
            shrunk,
            jnp.stack([item[2] for item in found])[slot],
        )
        outputs = finish(batch, shared, None)
    return tuple(outputs)


def solution(mesh):
    placed = (
        P(("grp", "pool"), "tp"),
        P("tp", None, None),
        P(("grp", "pool"), "tp", None),
        P(("grp", "pool"), None, None, None),
        P(("grp", "pool")),
        P(("grp", "pool")),
        P(("grp", "pool"), None),
        P(("grp", "pool"), "tp", None),
        P(("grp", "pool"), None, "tp", None),
        P(("grp", "pool"), None, "tp", None),
        P(),
    )
    return jax.shard_map(
        per_device,
        mesh=mesh,
        in_specs=placed,
        out_specs=(P(("grp", "pool"), "tp", None), P(("grp", "pool"), "tp", None)),
        check_vma=False,
    )
```

time: 162 us -> 117 us (0.72)
  waiting for transfers between devices: 88.8 us -> 7.74 us
  local copies, waits for them, and re-layouts: 16 us -> 29.4 us
  Pallas kernels: 0 us -> 12.1 us
  other arithmetic: 7 us -> 18.1 us
  between operations: 14.4 us -> 11.1 us
    all_to_all x3 -> x0, waiting for transfers between devices: 74.9 us -> none  [the longest x1 44.1 us: per_device(): lax.all_to_all(slots, 'pool', split_axis=0, concat_axis=0, tiled=True)]
    ppermute x0 -> x16, starting transfers between devices: none -> 15.7 us  [the longest x6 12.3 us: per_device(): front = tuple((lax.ppermute(piece, 'pool', onward) for piece in front))]
    all_to_all x3 -> x0, starting transfers between devices: 15.2 us -> none  [the longest x1 7.28 us: per_device(): lax.all_to_all(slot_tags, 'pool', split_axis=0, concat_axis=0, tiled=True)]
    psum x1 -> x0, waiting for transfers between devices: 13.9 us -> none  [per_device(): summed = lax.psum(partial_sum, 'tp').reshape(row_count, kv_heads, kv_width)]
    pallas_call x0 -> x1, Pallas kernels: none -> 12.1 us  [finish(): pl.pallas_call(finish_kernel, grid_spec=pltpu.PrefetchScalarGridSpec(num_...]
    another operation x3 -> x8, other arithmetic: 0.38 us -> 10.7 us  [shrunk_of(): request = jnp.argmax(hot).astype(jnp.int32)]
    ppermute x0 -> x16, waiting for transfers between devices: none -> 7.74 us  [the longest x6 6.92 us: per_device(): rear = tuple((lax.ppermute(piece, 'pool', backward) for piece in rear))]
    another operation x0 -> x3, local copies, waits for them, and re-layouts: none -> 6.64 us  [the longest x1 5.13 us: per_device(): request_ids = jnp.stack([item[0] for item in found])]
  transfers between devices with their start and end apart: 4 -> 16, of which waited for: 4 -> 4; matrix products, arithmetic and copies ran while one was open for 11% -> 58% of each run, Pallas kernels for 0% -> 0%
where the time goes in v1:
time: 117 us; the launch traced here: 116 us
  local copies, waits for them, and re-layouts  29.4 us (25%)
  matrix products  21.3 us (18%)
  other arithmetic  18.1 us (15%)
  starting transfers between devices  15.7 us (13%)
  Pallas kernels  12.1 us (10%)
  between operations  11.1 us (9%)
  waiting for transfers between devices  7.74 us (7%)
    unnamed x39, local copies, waits for them, and re-layouts  13.6 us
    ppermute x6, starting transfers between devices, per_device(): front = tuple((lax.ppermute(piece, 'pool', onward) for piece in front))  12.3 us
    pallas_call x1, Pallas kernels, finish(): pl.pallas_call(finish_kernel, grid_spec=pltpu.PrefetchScalarGridSpec(num_...  12.1 us
    another operation x8, other arithmetic, shrunk_of(): request = jnp.argmax(hot).astype(jnp.int32)  10.7 us
    dot_general x4, matrix products, ancestry(): jnp.einsum('...ij,...jk->...ik', reach, reach, preferred_element_type=F32)  7.79 us
    ppermute x6, waiting for transfers between devices, per_device(): rear = tuple((lax.ppermute(piece, 'pool', backward) for piece in rear))  6.92 us
    another operation x1, local copies, waits for them, and re-layouts, per_device(): request_ids = jnp.stack([item[0] for item in found])  5.13 us
    dot_general x8, matrix products, shrunk_of(): lax.dot_general(rows[:, cut:], two, (((1,), (1,)), ((), ())), preferred_e...  4.77 us
  transfers between devices with their start and end apart: 16, of which 4 were waited for; matrix products, arithmetic and copies ran while one was open for 58% of the time, Pallas kernels for 0%

profile of v1, /device:TPU:0, one launch (start us, length us, event | category | flops | bytes accessed | tf_op | source)
XLA Modules:
  0.0 115.5 jit_solution(2594396711311982955)
XLA Ops:
  0.6 1.8 %slice.129 = bf16[64,1536]{1,0:T(8,128)(2,1)} slice(bf16[64,2560]{1,0:T(8,128)(2,1)} %bitcast.117), slice={[0:64], [1024:2560]} | slice | bytes 393216 | tf_op jit(solution)/shard_map/slice | solution.py:184
  2.4 3.0 %collective-permute-start.2 = (bf16[64,1536]{1,0:T(8,128)(2,1)}, bf16[64,1536]{1,0:T(8,128)(2,1)}, u32[]{:S(2)}, u32[]{:S(2)}) collective-permute-start(bf16[64,1536]{1,0:T(8,128)(2,1)} %slice.129), channel_id=1, source_target_pairs={{0,4},{4,8},{8,12},{12,14},{14,10},{10,6},{6,2},{2,0},{1,5},{5,9},... | collective-permute-start | bytes 589832 | tf_op jit(solution)/shard_map/ppermute | solution.py:199
  8.1 2.0 %collective-permute-start.1 = (bf16[64,1536]{1,0:T(8,128)(2,1)}, bf16[64,1536]{1,0:T(8,128)(2,1)}, u32[]{:S(2)}, u32[]{:S(2)}) collective-permute-start(bf16[64,1536]{1,0:T(8,128)(2,1)} %pad_maximum_fusion), channel_id=1, source_target_pairs={{0,4},{4,8},{8,12},{12,14},{14,10},{10,6},{6,2},{2,0},{1,5},{5,9},... | collective-permute-start | bytes 589832 | tf_op jit(solution)/shard_map/ppermute | solution.py:199
  10.1 6.5 %copy.24 = bf16[320,8,4,256]{3,1,2,0:T(8,128)(2,1)} copy(bf16[320,8,4,256]{3,2,1,0:T(4,128)(2,1)} %bitcast.115) | data formatting | bytes 10485760
  16.6 4.7 %fusion.82 = f32[384,1024]{1,0:T(8,128)S(1)} fusion(bf16[384,2560]{1,0:T(8,128)(2,1)S(1)} %copy-done, bf16[2560,1024]{1,0:T(8,128)(2,1)} %bitcast.116), kind=kOutput, calls=%fused_computation.128 | convolution fusion | flops 2013265920 | bytes 8781824 | tf_op jit(solution)/shard_map/dot_general | solution.py:212
  32.6 1.4 %compare_reduce_fusion.5 = (pred[]{:T(512)}, s32[]{:T(128)}) fusion(s32[8]{0:T(128)S(1)} %copy-done.12, s32[]{:T(128)} %bitcast.7), kind=kLoop, calls=%fused_computation.118 | loop fusion | flops 57 | bytes 41 | tf_op jit(solution)/shard_map/per_device.<locals>.shrunk_of/reduce | solution.py:244
  36.6 1.3 %compare_reduce_fusion.3 = (pred[]{:T(512)}, s32[]{:T(128)}) fusion(s32[8]{0:T(128)S(1)} %copy-done.12, s32[]{:T(128)} %bitcast.13), kind=kLoop, calls=%fused_computation.116 | loop fusion | flops 57 | bytes 41 | tf_op jit(solution)/shard_map/per_device.<locals>.shrunk_of/reduce | solution.py:244
  38.6 1.3 %compare_reduce_fusion.2 = (pred[]{:T(512)}, s32[]{:T(128)}) fusion(s32[8]{0:T(128)S(1)} %copy-done.12, s32[]{:T(128)} %bitcast.16), kind=kLoop, calls=%fused_computation.115 | loop fusion | flops 57 | bytes 41 | tf_op jit(solution)/shard_map/per_device.<locals>.shrunk_of/reduce | solution.py:244
  40.5 1.3 %compare_reduce_fusion.1 = (pred[]{:T(512)}, s32[]{:T(128)}) fusion(s32[8]{0:T(128)S(1)} %copy-done.12, s32[]{:T(128)} %bitcast.19), kind=kLoop, calls=%fused_computation.114 | loop fusion | flops 57 | bytes 41 | tf_op jit(solution)/shard_map/per_device.<locals>.shrunk_of/reduce | solution.py:244
  42.5 1.3 %compare_reduce_fusion = (pred[]{:T(512)}, s32[]{:T(128)}) fusion(s32[8]{0:T(128)S(1)} %copy-done.12, s32[]{:T(128)} %bitcast.22), kind=kLoop, calls=%fused_computation.113 | loop fusion | flops 57 | bytes 41 | tf_op jit(solution)/shard_map/per_device.<locals>.shrunk_of/reduce | solution.py:244
  44.6 1.5 %stack_reshape.3 = bf16[1,64,512]{2,1,0:T(8,128)(2,1)} reshape(bf16[1,64,2,256]{3,2,1,0:T(2,128)(2,1)} %copy-done.8) | data formatting | bytes 131072 | tf_op jit(solution)/shard_map/stack;reshape | solution.py:264
  47.4 1.5 %constant_dynamic-update-slice_fusion = bf16[8,64,512]{2,1,0:T(8,128)(2,1)} fusion(bf16[1,64,512]{2,1,0:T(8,128)(2,1)} %stack_reshape.3), kind=kLoop, calls=%fused_computation.99 | loop fusion | bytes 131072
  48.9 1.7 %fusion.6 = bf16[8,48,48]{1,2,0:T(8,128)(2,1)} fusion(s32[8,48]{1,0:T(8,128)} %param.19, pred[48,48]{1,0:T(8,128)(4,1)S(1)} %iota_compare_fusion.1), kind=kOutput, calls=%fused_computation.12 | convolution fusion | flops 1843200 | bytes 40704 | tf_op jit(solution)/shard_map/...ij,...jk->...ik/dot_general | solution.py:29
  50.6 2.1 %fusion.1 = bf16[8,48,48]{1,2,0:T(8,128)(2,1)} fusion(bf16[8,48,48]{1,2,0:T(8,128)(2,1)} %fusion.6), kind=kOutput, calls=%fused_computation.7 | convolution fusion | flops 3612672 | bytes 73728 | tf_op jit(solution)/shard_map/...ij,...jk->...ik/dot_general | solution.py:29
  52.7 2.1 %fusion.3 = bf16[8,48,48]{1,2,0:T(8,128)(2,1)} fusion(bf16[8,48,48]{1,2,0:T(8,128)(2,1)} %fusion.1), kind=kOutput, calls=%fused_computation.9 | convolution fusion | flops 3612672 | bytes 73728 | tf_op jit(solution)/shard_map/...ij,...jk->...ik/dot_general | solution.py:29
  54.8 1.8 %fusion.81 = (f32[8,48]{1,0:T(8,128)S(1)}, f32[8,48,48]{1,2,0:T(8,128)}) fusion(bf16[8,48,48]{1,2,0:T(8,128)(2,1)} %fusion.3), kind=kOutput, calls=%fused_computation.127 | convolution fusion | flops 1842816 | bytes 112128 | tf_op jit(solution)/shard_map/...ij,...jk->...ik/dot_general | solution.py:29
  56.8 1.6 %broadcast_compare_fusion = pred[8,48,48]{1,2,0:T(8,128)(4,1)} fusion(f32[8,48,48]{1,2,0:T(8,128)} %get-tuple-element.30), kind=kLoop, calls=%fused_computation.79 | loop fusion | flops 18432 | bytes 92160 | tf_op jit(solution)/shard_map/gt | solution.py:236
  58.4 1.5 %copy.20 = pred[8,48,48]{2,1,0:T(8,128)(4,1)} copy(pred[8,48,48]{1,2,0:T(8,128)(4,1)} %broadcast_compare_fusion) | data formatting | bytes 36864 | tf_op jit(solution)/shard_map/gt | solution.py:236
  60.0 1.7 %fusion.39 = f32[48,64]{1,0:T(8,128)} fusion(bf16[384,2560]{1,0:T(8,128)(2,1)S(1)} %copy-done, s32[]{:T(128)S(6)} %select_n.137, s32[]{:T(128)S(6)} %add.261, bf16[64,2560]{1,0:T(8,128)(2,1)} %bitcast.119), kind=kOutput, calls=%fused_computation.62 | convolution fusion | flops 9437184 | bytes 356360 | tf_op jit(solution)/shard_map/dot_general | solution.py:248
  61.7 1.4 %fusion.67 = (f32[384,64]{1,0:T(8,128)S(1)}, f32[384,64]{1,0:T(8,128)S(1)}, f32[384,64]{1,0:T(8,128)S(1)}) fusion(f32[64]{0:T(128)} %multiply_exponential_fusion, f32[384]{0:T(512)S(1)} %sub.11), kind=kLoop, calls=%fused_computation.98 | loop fusion | flops 49152 | bytes 296704 | tf_op jit(solution)/shard_map/neg | solution.py:231
  63.2 1.5 %copy_bitcast_fusion = (bf16[8,2,128,128]{3,2,1,0:T(8,128)(2,1)S(1)}, bf16[8,2,128,128]{3,2,1,0:T(8,128)(2,1)S(1)}) fusion(bf16[8,128,2,128]{3,2,1,0:T(2,128)(2,1)} %param.22, bf16[8,128,2,128]{3,2,1,0:T(2,128)(2,1)} %param.21), kind=kLoop, calls=%fused_computation.38 | loop fusion | bytes 2097152 | tf_op jit(solution)/shard_map/transpose | solution.py:239
  65.7 5.1 %stack.86.request_ref = s32[8]{0:T(128)S(1)} concatenate(s32[1]{0:T(128)} %bitcast.2, s32[1]{0:T(128)} %bitcast.5, s32[1]{0:T(128)} %bitcast.8, s32[1]{0:T(128)} %bitcast.11, s32[1]{0:T(128)} %bitcast.14, s32[1]{0:T(128)} %bitcast.17, s32[1]{0:T(128)} %bitcast.20, s32[1]{0:T(128)} %bitcast.23), dimensions={0} | concatenate | bytes 64 | tf_op jit(solution)/shard_map/stack | solution.py:261
  71.9 2.1 %collective-permute-start.6 = (bf16[64,1536]{1,0:T(8,128)(2,1)}, bf16[64,1536]{1,0:T(8,128)(2,1)S(1)}, u32[]{:S(2)}, u32[]{:S(2)}) collective-permute-start(bf16[64,1536]{1,0:T(8,128)(2,1)} %collective-permute-done.2), channel_id=1, source_target_pairs={{0,4},{4,8},{8,12},{12,14},{14,10},{10,6},{6,2},{2,0},{1,5},{5,9},... | collective-permute-start | bytes 589832 | tf_op jit(solution)/shard_map/ppermute | solution.py:199
  74.0 1.6 %collective-permute-start.5 = (bf16[64,1536]{1,0:T(8,128)(2,1)}, bf16[64,1536]{1,0:T(8,128)(2,1)S(1)}, u32[]{:S(2)}, u32[]{:S(2)}) collective-permute-start(bf16[64,1536]{1,0:T(8,128)(2,1)} %collective-permute-done.1), channel_id=1, source_target_pairs={{0,4},{4,8},{8,12},{12,14},{14,10},{10,6},{6,2},{2,0},{1,5},{5,9},... | collective-permute-start | bytes 589832 | tf_op jit(solution)/shard_map/ppermute | solution.py:199
  78.4 1.5 %fusion.66 = bf16[8,64,512]{2,1,0:T(8,128)(2,1)} fusion(bf16[8,64,512]{2,1,0:T(8,128)(2,1)} %constant_dynamic-update-slice_fusion, bf16[64,1536]{1,0:T(8,128)(2,1)} %collective-permute-done.1), kind=kLoop, calls=%fused_computation.97 | loop fusion | bytes 131072
  82.1 1.6 %fusion.65 = bf16[8,64,512]{2,1,0:T(8,128)(2,1)} fusion(bf16[8,64,512]{2,1,0:T(8,128)(2,1)} %fusion.66, bf16[64,1536]{1,0:T(8,128)(2,1)} %collective-permute-done.3), kind=kLoop, calls=%fused_computation.95 | loop fusion | bytes 131072
  83.6 2.0 %collective-permute-start.10 = (bf16[64,1536]{1,0:T(8,128)(2,1)S(1)}, bf16[64,1536]{1,0:T(8,128)(2,1)S(1)}, u32[]{:S(2)}, u32[]{:S(2)}) collective-permute-start(bf16[64,1536]{1,0:T(8,128)(2,1)S(1)} %collective-permute-done.6), channel_id=1, source_target_pairs={{0,4},{4,8},{8,12},{12,14},{14,10},{10,6},{6,2},{2,0},{1,5},{5,9},... | collective-permute-start | bytes 589832 | tf_op jit(solution)/shard_map/ppermute | solution.py:199
  85.7 1.6 %collective-permute-start.9 = (bf16[64,1536]{1,0:T(8,128)(2,1)S(1)}, bf16[64,1536]{1,0:T(8,128)(2,1)S(1)}, u32[]{:S(2)}, u32[]{:S(2)}) collective-permute-start(bf16[64,1536]{1,0:T(8,128)(2,1)S(1)} %collective-permute-done.5), channel_id=1, source_target_pairs={{0,4},{4,8},{8,12},{12,14},{14,10},{10,6},{6,2},{2,0},{1,5},{5,9},... | collective-permute-start | bytes 589832 | tf_op jit(solution)/shard_map/ppermute | solution.py:199
  90.0 5.3 %collective-permute-done.12 = bf16[64,1536]{1,0:T(8,128)(2,1)S(1)} collective-permute-done((bf16[64,1536]{1,0:T(8,128)(2,1)S(1)}, bf16[64,1536]{1,0:T(8,128)(2,1)S(1)}, u32[]{:S(2)}, u32[]{:S(2)}) %collective-permute-start.12) | collective-permute-done | bytes 196640 | tf_op jit(solution)/shard_map/ppermute | solution.py:200
  95.8 1.6 %collective-permute-start.13 = (bf16[64,1536]{1,0:T(8,128)(2,1)S(1)}, bf16[64,1536]{1,0:T(8,128)(2,1)S(1)}, u32[]{:S(2)}, u32[]{:S(2)}) collective-permute-start(bf16[64,1536]{1,0:T(8,128)(2,1)S(1)} %collective-permute-done.9), channel_id=1, source_target_pairs={{0,4},{4,8},{8,12},{12,14},{14,10},{10,6},{6,2},{2,0},{1,5},{5,9},... | collective-permute-start | bytes 589832 | tf_op jit(solution)/shard_map/ppermute | solution.py:206
  97.9 1.5 %collective-permute-done.11 = bf16[64,1536]{1,0:T(8,128)(2,1)S(1)} collective-permute-done((bf16[64,1536]{1,0:T(8,128)(2,1)S(1)}, bf16[64,1536]{1,0:T(8,128)(2,1)S(1)}, u32[]{:S(2)}, u32[]{:S(2)}) %collective-permute-start.11) | collective-permute-done | bytes 196640 | tf_op jit(solution)/shard_map/ppermute | solution.py:200
  103.5 12.1 %shard_map.140 = (bf16[384,16,128]{2,1,0:T(8,128)(2,1)}, bf16[384,2,256]{2,1,0:T(2,128)(2,1)}) custom-call(s32[8]{0:T(128)S(1)} %stack.86.request_ref, f32[384,512]{1,0:T(8,128)S(1)} %dynamic-slice_add_fusion.base_ref, f32[8,48,64]{2,1,0:T(8,128)S(1)} %add.256.shrunk_ref, bf16[8,64,512]{2,1,0:T(8,128)(2,1)S(1)} %fusion.60.expand_ref, ...), custom_call_target="tpu_custom_call" | custom-call | flops 640000000 | bytes 7200000 | tf_op jit(solution)/shard_map/pallas_call | solution.py:131
  (96 shorter events, 25.2 us)
Async XLA Ops:
  0.6 16.0 %copy-start = (bf16[384,2560]{1,0:T(8,128)(2,1)S(1)}, bf16[384,2560]{1,0:T(8,128)(2,1)}, u32[]{:S(2)}) copy-start(bf16[384,2560]{1,0:T(8,128)(2,1)} %param.13) | copy-start | bytes 5898244
  2.4 69.5 %collective-permute-start.2 = (bf16[64,1536]{1,0:T(8,128)(2,1)}, bf16[64,1536]{1,0:T(8,128)(2,1)}, u32[]{:S(2)}, u32[]{:S(2)}) collective-permute-start(bf16[64,1536]{1,0:T(8,128)(2,1)} %slice.129), channel_id=1, source_target_pairs={{0,4},{4,8},{8,12},{12,14},{14,10},{10,6},{6,2},{2,0},{1,5},{5,9},... | collective-permute-start | bytes 589832 | tf_op jit(solution)/shard_map/ppermute | solution.py:199
  5.4 71.3 %collective-permute-start.4 = (bf16[64,1536]{1,0:T(8,128)(2,1)}, bf16[64,1536]{1,0:T(8,128)(2,1)}, u32[]{:S(2)}, u32[]{:S(2)}) collective-permute-start(bf16[64,1536]{1,0:T(8,128)(2,1)} %slice.129), channel_id=1, source_target_pairs={{4,0},{8,4},{12,8},{14,12},{10,14},{6,10},{2,6},{0,2},{5,1},{9,5},... | collective-permute-start | bytes 589832 | tf_op jit(solution)/shard_map/ppermute | solution.py:200
  7.3 9.3 %copy-start.8 = (bf16[1,64,2,256]{3,2,1,0:T(2,128)(2,1)}, bf16[1,64,2,256]{3,2,1,0:T(2,128)(2,1)S(1)}, u32[]{:S(2)}) copy-start(bf16[1,64,2,256]{3,2,1,0:T(2,128)(2,1)S(1)} %constant_dynamic-slice_fusion) | copy-start | bytes 196612
  8.1 65.9 %collective-permute-start.1 = (bf16[64,1536]{1,0:T(8,128)(2,1)}, bf16[64,1536]{1,0:T(8,128)(2,1)}, u32[]{:S(2)}, u32[]{:S(2)}) collective-permute-start(bf16[64,1536]{1,0:T(8,128)(2,1)} %pad_maximum_fusion), channel_id=1, source_target_pairs={{0,4},{4,8},{8,12},{12,14},{14,10},{10,6},{6,2},{2,0},{1,5},{5,9},... | collective-permute-start | bytes 589832 | tf_op jit(solution)/shard_map/ppermute | solution.py:199
  10.1 68.3 %collective-permute-start.3 = (bf16[64,1536]{1,0:T(8,128)(2,1)}, bf16[64,1536]{1,0:T(8,128)(2,1)}, u32[]{:S(2)}, u32[]{:S(2)}) collective-permute-start(bf16[64,1536]{1,0:T(8,128)(2,1)} %pad_maximum_fusion), channel_id=1, source_target_pairs={{4,0},{8,4},{12,8},{14,12},{10,14},{6,10},{2,6},{0,2},{5,1},{9,5},... | collective-permute-start | bytes 589832 | tf_op jit(solution)/shard_map/ppermute | solution.py:200
  16.6 5.8 %copy-start.14 = (s32[8]{0:T(128)S(1)}, s32[8]{0:T(128)}, u32[]{:S(2)}) copy-start(s32[8]{0:T(128)} %constant.130.clone) | copy-start | bytes 100
  16.6 11.4 %copy-start.11 = (s32[8]{0:T(128)S(1)}, s32[8]{0:T(128)}, u32[]{:S(2)}) copy-start(s32[8]{0:T(128)} %constant.129.clone) | copy-start | bytes 100
  16.6 12.1 %copy-start.12 = (s32[8]{0:T(128)S(1)}, s32[8]{0:T(128)}, u32[]{:S(2)}) copy-start(s32[8]{0:T(128)} %param.17) | copy-start | bytes 100
  21.3 40.4 %copy-start.6 = (f32[384,1024]{1,0:T(8,128)}, f32[384,1024]{1,0:T(8,128)S(1)}, u32[]{:S(2)}) copy-start(f32[384,1024]{1,0:T(8,128)S(1)} %fusion.82) | copy-start | bytes 4718596
  21.3 25.3 %copy-start.13 = (s32[8]{0:T(128)S(1)}, s32[8]{0:T(128)}, u32[]{:S(2)}) copy-start(s32[8]{0:T(128)} %param.18) | copy-start | bytes 100
  22.4 79.6 %collective-permute-start = (f32[384,512]{1,0:T(8,128)}, f32[384,512]{1,0:T(8,128)}, u32[]{:S(2)}, u32[]{:S(2)}) collective-permute-start(f32[384,512]{1,0:T(8,128)} %constant_dynamic-slice_fusion.1), channel_id=1, source_target_pairs={{0,1},{1,0},{2,3},{3,2},{4,5},{5,4},{6,7},{7,6},{8,9},{9,8},{10,11... | collective-permute-start | bytes 2359304 | tf_op jit(solution)/shard_map/ppermute | solution.py:219
  61.7 3.9 %copy-start.9 = (pred[8,48,48]{2,1,0:T(8,128)(4,1)S(1)}, pred[8,48,48]{2,1,0:T(8,128)(4,1)}, u32[]{:S(2)}) copy-start(pred[8,48,48]{2,1,0:T(8,128)(4,1)} %copy.20) | copy-start | bytes 55300
  63.2 7.6 %copy-start.10 = (f32[48,64]{1,0:T(8,128)S(1)}, f32[48,64]{1,0:T(8,128)}, u32[]{:S(2)}) copy-start(f32[48,64]{1,0:T(8,128)} %fusion.39) | copy-start | bytes 36868
  71.9 11.7 %collective-permute-start.6 = (bf16[64,1536]{1,0:T(8,128)(2,1)}, bf16[64,1536]{1,0:T(8,128)(2,1)S(1)}, u32[]{:S(2)}, u32[]{:S(2)}) collective-permute-start(bf16[64,1536]{1,0:T(8,128)(2,1)} %collective-permute-done.2), channel_id=1, source_target_pairs={{0,4},{4,8},{8,12},{12,14},{14,10},{10,6},{6,2},{2,0},{1,5},{5,9},... | collective-permute-start | bytes 589832 | tf_op jit(solution)/shard_map/ppermute | solution.py:199
  74.0 11.7 %collective-permute-start.5 = (bf16[64,1536]{1,0:T(8,128)(2,1)}, bf16[64,1536]{1,0:T(8,128)(2,1)S(1)}, u32[]{:S(2)}, u32[]{:S(2)}) collective-permute-start(bf16[64,1536]{1,0:T(8,128)(2,1)} %collective-permute-done.1), channel_id=1, source_target_pairs={{0,4},{4,8},{8,12},{12,14},{14,10},{10,6},{6,2},{2,0},{1,5},{5,9},... | collective-permute-start | bytes 589832 | tf_op jit(solution)/shard_map/ppermute | solution.py:199
  76.7 10.7 %collective-permute-start.8 = (bf16[64,1536]{1,0:T(8,128)(2,1)}, bf16[64,1536]{1,0:T(8,128)(2,1)S(1)}, u32[]{:S(2)}, u32[]{:S(2)}) collective-permute-start(bf16[64,1536]{1,0:T(8,128)(2,1)} %collective-permute-done.4), channel_id=1, source_target_pairs={{4,0},{8,4},{12,8},{14,12},{10,14},{6,10},{2,6},{0,2},{5,1},{9,5},... | collective-permute-start | bytes 589832 | tf_op jit(solution)/shard_map/ppermute | solution.py:200
  78.4 9.7 %collective-permute-start.7 = (bf16[64,1536]{1,0:T(8,128)(2,1)}, bf16[64,1536]{1,0:T(8,128)(2,1)S(1)}, u32[]{:S(2)}, u32[]{:S(2)}) collective-permute-start(bf16[64,1536]{1,0:T(8,128)(2,1)} %collective-permute-done.3), channel_id=1, source_target_pairs={{4,0},{8,4},{12,8},{14,12},{10,14},{6,10},{2,6},{0,2},{5,1},{9,5},... | collective-permute-start | bytes 589832 | tf_op jit(solution)/shard_map/ppermute | solution.py:200
  82.1 19.9 %copy-start.7 = (f32[384,1024]{1,0:T(8,128)S(1)}, f32[384,1024]{1,0:T(8,128)}, u32[]{:S(2)}) copy-start(f32[384,1024]{1,0:T(8,128)} %copy-done.6) | copy-start | bytes 4718596
  83.6 13.9 %collective-permute-start.10 = (bf16[64,1536]{1,0:T(8,128)(2,1)S(1)}, bf16[64,1536]{1,0:T(8,128)(2,1)S(1)}, u32[]{:S(2)}, u32[]{:S(2)}) collective-permute-start(bf16[64,1536]{1,0:T(8,128)(2,1)S(1)} %collective-permute-done.6), channel_id=1, source_target_pairs={{0,4},{4,8},{8,12},{12,14},{14,10},{10,6},{6,2},{2,0},{1,5},{5,9},... | collective-permute-start | bytes 589832 | tf_op jit(solution)/shard_map/ppermute | solution.py:199
  85.7 10.1 %collective-permute-start.9 = (bf16[64,1536]{1,0:T(8,128)(2,1)S(1)}, bf16[64,1536]{1,0:T(8,128)(2,1)S(1)}, u32[]{:S(2)}, u32[]{:S(2)}) collective-permute-start(bf16[64,1536]{1,0:T(8,128)(2,1)S(1)} %collective-permute-done.5), channel_id=1, source_target_pairs={{0,4},{4,8},{8,12},{12,14},{14,10},{10,6},{6,2},{2,0},{1,5},{5,9},... | collective-permute-start | bytes 589832 | tf_op jit(solution)/shard_map/ppermute | solution.py:199
  87.4 7.9 %collective-permute-start.12 = (bf16[64,1536]{1,0:T(8,128)(2,1)S(1)}, bf16[64,1536]{1,0:T(8,128)(2,1)S(1)}, u32[]{:S(2)}, u32[]{:S(2)}) collective-permute-start(bf16[64,1536]{1,0:T(8,128)(2,1)S(1)} %collective-permute-done.8), channel_id=1, source_target_pairs={{4,0},{8,4},{12,8},{14,12},{10,14},{6,10},{2,6},{0,2},{5,1},{9,5},... | collective-permute-start | bytes 589832 | tf_op jit(solution)/shard_map/ppermute | solution.py:200
  88.1 11.3 %collective-permute-start.11 = (bf16[64,1536]{1,0:T(8,128)(2,1)S(1)}, bf16[64,1536]{1,0:T(8,128)(2,1)S(1)}, u32[]{:S(2)}, u32[]{:S(2)}) collective-permute-start(bf16[64,1536]{1,0:T(8,128)(2,1)S(1)} %collective-permute-done.7), channel_id=1, source_target_pairs={{4,0},{8,4},{12,8},{14,12},{10,14},{6,10},{2,6},{0,2},{5,1},{9,5},... | collective-permute-start | bytes 589832 | tf_op jit(solution)/shard_map/ppermute | solution.py:200
  95.3 6.2 %collective-permute-start.14 = (bf16[64,1536]{1,0:T(8,128)(2,1)S(1)}, bf16[64,1536]{1,0:T(8,128)(2,1)S(1)}, u32[]{:S(2)}, u32[]{:S(2)}) collective-permute-start(bf16[64,1536]{1,0:T(8,128)(2,1)S(1)} %collective-permute-done.12), channel_id=1, source_target_pairs={{4,0},{8,4},{12,8},{14,12},{10,14},{6,10},{2,6},{0,2},{5,1},{9,5},... | collective-permute-start | bytes 589832 | tf_op jit(solution)/shard_map/ppermute | solution.py:207
  95.8 5.9 %collective-permute-start.13 = (bf16[64,1536]{1,0:T(8,128)(2,1)S(1)}, bf16[64,1536]{1,0:T(8,128)(2,1)S(1)}, u32[]{:S(2)}, u32[]{:S(2)}) collective-permute-start(bf16[64,1536]{1,0:T(8,128)(2,1)S(1)} %collective-permute-done.9), channel_id=1, source_target_pairs={{0,4},{4,8},{8,12},{12,14},{14,10},{10,6},{6,2},{2,0},{1,5},{5,9},... | collective-permute-start | bytes 589832 | tf_op jit(solution)/shard_map/ppermute | solution.py:206
  100.2 3.2 %copy-start.1 = (bf16[384,16,128]{2,1,0:T(8,128)(2,1)S(1)}, bf16[384,16,128]{2,1,0:T(8,128)(2,1)}, u32[]{:S(2)}) copy-start(bf16[384,16,128]{2,1,0:T(8,128)(2,1)} %query_ref.1) | copy-start | bytes 4718596
  100.2 3.2 %copy-start.2 = (f32[384,128]{1,0:T(8,128)S(1)}, f32[384,128]{1,0:T(8,128)}, u32[]{:S(2)}) copy-start(f32[384,128]{1,0:T(8,128)} %get-tuple-element.31.cosine_ref) | copy-start | bytes 589828
  100.2 3.2 %copy-start.3 = (f32[384,128]{1,0:T(8,128)S(1)}, f32[384,128]{1,0:T(8,128)}, u32[]{:S(2)}) copy-start(f32[384,128]{1,0:T(8,128)} %get-tuple-element.32.sine_ref) | copy-start | bytes 589828
  100.2 3.2 %copy-start.5 = (f32[128]{0:T(128)S(1)}, f32[128]{0:T(128)}, u32[]{:S(2)}) copy-start(f32[128]{0:T(128)} %param.23) | copy-start | bytes 1540
  100.9 2.4 %copy-start.4 = (bf16[8,64,512]{2,1,0:T(8,128)(2,1)S(1)}, bf16[8,64,512]{2,1,0:T(8,128)(2,1)}, u32[]{:S(2)}) copy-start(bf16[8,64,512]{2,1,0:T(8,128)(2,1)} %fusion.61) | copy-start | bytes 1572868
  101.9 1.5 %collective-permute-start.15 = (f32[8,48,64]{2,1,0:T(8,128)S(1)}, f32[8,48,64]{2,1,0:T(8,128)S(1)}, u32[]{:S(2)}, u32[]{:S(2)}) collective-permute-start(f32[8,48,64]{2,1,0:T(8,128)S(1)} %fusion.8), channel_id=1, source_target_pairs={{0,1},{1,0},{2,3},{3,2},{4,5},{5,4},{6,7},{7,6},{8,9},{9,8},{10,11... | collective-permute-start | bytes 294920 | tf_op jit(solution)/shard_map/ppermute | solution.py:263

commit v2 on v1

v2 whole, which is shorter than its diff:
```python
import functools
import math

import jax
import jax.numpy as jnp
import numpy as np
from jax import lax
from jax.experimental import pallas as pl
from jax.experimental.pallas import tpu as pltpu
from jax.sharding import PartitionSpec as P

F32 = jnp.float32
BF16 = jnp.bfloat16


def ring_order(count):
    if count == 8:
        return list(range(0, count, 2)) + list(range(count - 1, 0, -2))
    return list(range(count))


def sorting_matrix(rows, columns, inner, source_inner):
    row = lax.broadcasted_iota(jnp.int32, (rows, columns), 0)
    column = lax.broadcasted_iota(jnp.int32, (rows, columns), 1)
    return (column == (row % inner) * source_inner + row // inner).astype(F32).astype(BF16)


def pack_kernel(core_ref, shrink_ref, expand_ref, first_ref, second_ref, *, cut, heads_here):
    rank_size = shrink_ref.shape[0]
    groups = expand_ref.shape[0] // rank_size
    heads = groups // 2
    ranks = 256 // groups
    row = lax.broadcasted_iota(jnp.int32, (2 * heads_here * ranks, 256), 0)
    column = lax.broadcasted_iota(jnp.int32, (2 * heads_here * ranks, 256), 1)
    group = row // ranks
    head = core_ref[0] * heads_here + group // 2
    pick = (column == (row % ranks) * groups + (group % 2) * heads + head).astype(F32).astype(BF16)
    columns = 2 * heads_here * 128
    for block in range(rank_size // ranks):
        sorted_rows = jnp.dot(
            pick, expand_ref[256 * block : 256 * (block + 1), :], preferred_element_type=F32
        ).astype(BF16)
        for g in range(2 * heads_here):
            first_ref[ranks * block : ranks * (block + 1), 128 * g : 128 * (g + 1)] = sorted_rows[
                ranks * g : ranks * (g + 1), :
            ]
    first_ref[:, columns:] = shrink_ref[:, :cut]
    second_ref[...] = shrink_ref[:, cut:]


def pack(core, shrink, expand_rows, cut, heads_here):
    rank_size, half_width = shrink.shape
    columns = 2 * heads_here * 128
    return pl.pallas_call(
        functools.partial(pack_kernel, cut=cut, heads_here=heads_here),
        grid_spec=pltpu.PrefetchScalarGridSpec(
            num_scalar_prefetch=1,
            grid=(1,),
            in_specs=[
                pl.BlockSpec(shrink.shape, lambda i, c: (0, 0)),
                pl.BlockSpec(expand_rows.shape, lambda i, c: (0, 0)),
            ],
            out_specs=[
                pl.BlockSpec((rank_size, columns + cut), lambda i, c: (0, 0)),
                pl.BlockSpec((rank_size, half_width - cut), lambda i, c: (0, 0)),
            ],
        ),
        out_shape=[
            jax.ShapeDtypeStruct((rank_size, columns + cut), BF16),
            jax.ShapeDtypeStruct((rank_size, half_width - cut), BF16),
        ],
        name="pack",
    )(core, shrink, expand_rows)


def base_kernel(core_ref, hidden_ref, weight_ref, here_ref, away_ref, total_ref, sorted_ref):
    step = pl.program_id(0)
    depth, width = sorted_ref.shape
    groups = weight_ref.shape[0] // depth
    heads = groups // 2
    span = 256 // groups
    order = sorting_matrix(256, 256, span, groups)
    for block in range(depth // (2 * span)):
        at = 512 * block
        pair = jnp.concatenate(
            [weight_ref[at : at + 256, :], weight_ref[at + 256 : at + 512, :]], 1
        )
        rows = jnp.dot(order, pair, preferred_element_type=F32).astype(BF16)
        for group in range(groups):
            tile, head = group // heads, group % heads
            lanes = slice(256 * head + 128 * tile, 256 * head + 128 * (tile + 1))
            for half in range(2):
                top = 2 * span * block + span * half
                sorted_ref[top : top + span, lanes] = rows[
                    span * group : span * (group + 1), 128 * half : 128 * (half + 1)
                ]
    product = jnp.dot(hidden_ref[...], sorted_ref[...], preferred_element_type=F32)

    @pl.when(step == 0)
    def _():
        total_ref[...] = product

    @pl.when(step > 0)
    def _():
        total_ref[...] += product

    @pl.when(step == pl.num_programs(0) - 1)
    def _():
        columns = here_ref.shape[1]

        @pl.when(core_ref[0] == 0)
        def _():
            here_ref[...] = total_ref[:, :columns]
            away_ref[...] = total_ref[:, columns:]

        @pl.when(core_ref[0] == 1)
        def _():
            here_ref[...] = total_ref[:, columns:]
            away_ref[...] = total_ref[:, :columns]


def base_product(core, hidden_states, weight_rows, width):
    rows, half_width = hidden_states.shape
    groups = weight_rows.shape[0] // half_width
    depth = 512
    return pl.pallas_call(
        base_kernel,
        grid_spec=pltpu.PrefetchScalarGridSpec(
            num_scalar_prefetch=1,
            grid=(half_width // depth,),
            in_specs=[
                pl.BlockSpec((rows, depth), lambda i, c: (0, i)),
                pl.BlockSpec((depth * groups, 128), lambda i, c: (i, 0)),
            ],
            out_specs=[
                pl.BlockSpec((rows, width // 2), lambda i, c: (0, 0)),
                pl.BlockSpec((rows, width // 2), lambda i, c: (0, 0)),
            ],
            scratch_shapes=[pltpu.VMEM((rows, width), F32), pltpu.VMEM((depth, width), BF16)],
        ),
        out_shape=[jax.ShapeDtypeStruct((rows, width // 2), F32)] * 2,
        compiler_params=pltpu.CompilerParams(vmem_limit_bytes=24 * 1024 * 1024),
        cost_estimate=pl.CostEstimate(
            flops=4_000_000_000, bytes_accessed=9_000_000, transcendentals=0
        ),
        name="base",
    )(core, hidden_states, weight_rows)


def tree_kernel(length_ref, parent_ref, frequency_ref, *rest, context):
    cosine_ref, sine_ref, bias_ref = rest[-3:]
    requests, nodes = parent_ref.shape
    span = bias_ref.shape[1]
    node = lax.broadcasted_iota(jnp.int32, (nodes, nodes), 0)
    same = node == lax.broadcasted_iota(jnp.int32, (nodes, nodes), 1)
    parents = parent_ref[...]
    below = [
        (same | (parents[r : r + 1, :] == node)).astype(F32).astype(BF16) for r in range(requests)
    ]
    reached = 1
    while 2 * reached < nodes:
        below = [
            jnp.minimum(jnp.dot(b, b, preferred_element_type=F32), 1.0).astype(BF16) for b in below
        ]
        reached = 2 * reached
    lane = lax.broadcasted_iota(jnp.int32, (nodes, 128), 1)
    sign = jnp.where(lane < 64, -1.0, 1.0)
    cache_lane = lax.broadcasted_iota(jnp.int32, (nodes, context), 1)
    spare = jnp.full((nodes, span - context - nodes), -1e30, F32)
    for r in range(requests):
        b = below[r]
        product = lax.dot_general(b, b, (((0,), (1,)), ((), ())), preferred_element_type=F32)
        reach = jnp.minimum(product, 1.0)
        length = length_ref[r]
        positions = length.astype(F32) + jnp.sum(reach, -1, keepdims=True) - 1.0
        angles = positions * frequency_ref[...]
        rows = slice(nodes * r, nodes * (r + 1))
        cosine_ref[rows, :] = jnp.cos(angles)
        sine_ref[rows, :] = jnp.sin(angles) * sign
        bias_ref[rows, :] = jnp.concatenate(
            [
                jnp.where(cache_lane < length, 0.0, -1e30),
                jnp.where(reach > 0.5, 0.0, -1e30),
                spare,
            ],
            1,
        )


def tree_tables(cache_lengths, tree_parents, head_size, context, after):
    requests, nodes = tree_parents.shape
    span = -(-(context + nodes) // 128) * 128
    half_size = head_size // 2
    frequency = jnp.exp(
        jnp.arange(half_size, dtype=F32) * (-2.0 * math.log(1000000.0) / head_size)
    )
    frequency = jnp.concatenate([frequency, frequency]).reshape(1, head_size)
    whole = lambda shape: pl.BlockSpec(shape, lambda i, n: (0,) * len(shape))
    rows = requests * nodes
    return pl.pallas_call(
        functools.partial(tree_kernel, context=context),
        grid_spec=pltpu.PrefetchScalarGridSpec(
            num_scalar_prefetch=1,
            grid=(1,),
            in_specs=[whole(tree_parents.shape), whole((1, head_size))]
            + [pl.BlockSpec(memory_space=pl.ANY)] * len(after),
            out_specs=[whole((rows, head_size)), whole((rows, head_size)), whole((rows, span))],
        ),
        out_shape=[
            jax.ShapeDtypeStruct((rows, head_size), F32),
            jax.ShapeDtypeStruct((rows, head_size), F32),
            jax.ShapeDtypeStruct((rows, span), F32),
        ],
        cost_estimate=pl.CostEstimate(
            flops=50_000_000, bytes_accessed=8_000_000, transcendentals=100_000
        ),
        name="tree",
    )(cache_lengths, tree_parents, frequency, *after)


def shrink_kernel(request_ref, *refs, columns, cut):
    output_ref = refs[-1]
    contract = (((1,), (1,)), ((), ()))
    for b in range(output_ref.shape[0]):
        hidden_ref, one_ref, two_ref = refs[3 * b : 3 * b + 3]
        output_ref[b] = lax.dot_general(
            hidden_ref[:, :cut], one_ref[:, columns:], contract, preferred_element_type=F32
        ) + lax.dot_general(hidden_ref[:, cut:], two_ref[...], contract, preferred_element_type=F32)


def shrink_rows(request_ids, hidden_states, pieces, tree_size, columns, cut):
    rank_size = pieces[0][0].shape[0]
    in_specs, operands = [], []
    for b, (one, two) in enumerate(pieces):
        in_specs += [
            pl.BlockSpec((tree_size, hidden_states.shape[1]), lambda i, ids, b=b: (ids[b], 0)),
            pl.BlockSpec(one.shape, lambda i, ids: (0, 0)),
            pl.BlockSpec(two.shape, lambda i, ids: (0, 0)),
        ]
        operands += [hidden_states, one, two]
    count = len(pieces)
    return pl.pallas_call(
        functools.partial(shrink_kernel, columns=columns, cut=cut),
        grid_spec=pltpu.PrefetchScalarGridSpec(
            num_scalar_prefetch=1,
            grid=(1,),
            in_specs=in_specs,
            out_specs=pl.BlockSpec((count, tree_size, rank_size), lambda i, ids: (0, 0, 0)),
        ),
        out_shape=jax.ShapeDtypeStruct((count, tree_size, rank_size), F32),
        compiler_params=pltpu.CompilerParams(vmem_limit_bytes=24 * 1024 * 1024),
        cost_estimate=pl.CostEstimate(
            flops=count * 100_000_000, bytes_accessed=count * 1_500_000, transcendentals=0
        ),
        name="shrink",
    )(request_ids, *operands)


def finish_kernel(
    request_ref,
    here_ref,
    there_ref,
    shrunk_here_ref,
    shrunk_there_ref,
    cosine_ref,
    sine_ref,
    gain_ref,
    bias_ref,
    query_ref,
    key_ref,
    value_ref,
    *rest,
    count,
):
    expand_refs = rest[:count]
    attention_ref, cache_ref, expand_ref = rest[-3:]
    tree_size, heads, head_size = query_ref.shape
    kv_heads = cache_ref.shape[0] // (2 * tree_size)
    context = key_ref.shape[0] // kv_heads
    per_group = heads // kv_heads
    score_scale = math.log2(math.e) / math.sqrt(head_size)
    if count == 1:
        expand = expand_refs[0][...]
    else:
        for b in range(count):

            @pl.when(pl.program_id(0) == b)
            def _():
                expand_ref[...] = expand_refs[b][...]

        expand = expand_ref[...]
    shrunk = shrunk_here_ref[0] + shrunk_there_ref[0]
    high = shrunk.astype(BF16)
    left = shrunk - high.astype(F32)
    middle = left.astype(BF16)
    low = (left - middle.astype(F32)).astype(BF16)
    delta = (
        jnp.dot(low, expand, preferred_element_type=F32)
        + jnp.dot(middle, expand, preferred_element_type=F32)
        + jnp.dot(high, expand, preferred_element_type=F32)
    )
    projected = (here_ref[...] + there_ref[...]) + delta
    cosine = cosine_ref[...]
    sine = sine_ref[...]
    gain = gain_ref[...]
    cached = jnp.dot(
        sorting_matrix(kv_heads * context, kv_heads * context, context, kv_heads),
        jnp.concatenate([key_ref[...], value_ref[...]], 1),
        preferred_element_type=F32,
    ).astype(BF16)
    queries = query_ref[...].astype(F32)
    bias = bias_ref[...]
    bias = jnp.broadcast_to(bias[:, None, :], (tree_size, per_group, bias.shape[1])).reshape(
        tree_size * per_group, bias.shape[1]
    )
    pad = jnp.zeros((bias.shape[1] - context - tree_size, head_size), BF16)
    outputs, new_keys, new_values = [], [], []
    for g in range(kv_heads):
        at = 2 * head_size * g
        key = projected[:, at : at + head_size]
        value = projected[:, at + head_size : at + 2 * head_size].astype(BF16)
        norm = lax.rsqrt(jnp.mean(key * key, -1, keepdims=True) + 1e-06)
        key = key * norm * gain
        key = (key * cosine + pltpu.roll(key, head_size // 2, 1) * sine).astype(BF16)
        new_keys.append(key)
        new_values.append(value)
        keys = jnp.concatenate([cached[context * g : context * (g + 1), :head_size], key, pad], 0)
        values = jnp.concatenate(
            [cached[context * g : context * (g + 1), head_size:], value, pad], 0
        )
        rows = queries[:, per_group * g : per_group * (g + 1), :].reshape(
            tree_size * per_group, head_size
        )
        scores = lax.dot_general(
            rows.astype(BF16), keys, (((1,), (1,)), ((), ())), preferred_element_type=F32
        )
        scores = scores + bias
        row_max = jnp.max(scores, -1, keepdims=True)
        exponent = jnp.exp2((scores - row_max) * score_scale)
        total = jnp.sum(exponent, -1, keepdims=True)
        weights = (exponent * (1.0 / total)).astype(BF16)
        output = jnp.dot(weights, values, preferred_element_type=F32)
        outputs.append(output.reshape(tree_size, per_group, head_size))
    attention_ref[...] = jnp.concatenate(outputs, 1).astype(BF16)
    stacked = jnp.concatenate(new_keys + new_values, 0)
    size = stacked.shape[0]
    cache_ref[...] = jnp.dot(
        sorting_matrix(size, size, size // tree_size, tree_size),
        stacked,
        preferred_element_type=F32,
    ).astype(BF16)


def finish(batch, shared, previous):
    request_ids, shrunk_here, shrunk_there, pieces = batch
    here, there, cosine, sine, gain, bias, queries, key_rows, value_rows, context = shared
    count, tree_size, rank_size = shrunk_here.shape
    rows, heads, head_size = queries.shape
    columns = here.shape[1]
    kv_heads = columns // (2 * head_size)
    row_block = lambda width: pl.BlockSpec((tree_size, width), lambda i, ids: (ids[i], 0))
    shrunk_block = pl.BlockSpec((1, tree_size, rank_size), lambda i, ids: (i, 0, 0))
    cached_block = pl.BlockSpec((kv_heads * context, head_size), lambda i, ids: (ids[i], 0))
    in_specs = [
        row_block(columns),
        row_block(columns),
        shrunk_block,
        shrunk_block,
        row_block(head_size),
        row_block(head_size),
        pl.BlockSpec((1, head_size), lambda i, ids: (0, 0)),
        row_block(bias.shape[1]),
        pl.BlockSpec((tree_size, heads, head_size), lambda i, ids: (ids[i], 0, 0)),
        cached_block,
        cached_block,
    ] + [pl.BlockSpec((rank_size, columns), lambda i, ids: (0, 0))] * count
    operands = [
        request_ids,
        here,
        there,
        shrunk_here,
        shrunk_there,
        cosine,
        sine,
        gain,
        bias,
        queries,
        key_rows,
        value_rows,
        *pieces,
    ]
    aliases = {}
    if previous is not None:
        aliases = {len(operands): 0, len(operands) + 1: 1}
        operands += list(previous)
        in_specs += [pl.BlockSpec(memory_space=pl.ANY)] * 2
    cache_rows = 2 * kv_heads * tree_size
    return pl.pallas_call(
        functools.partial(finish_kernel, count=count),
        grid_spec=pltpu.PrefetchScalarGridSpec(
            num_scalar_prefetch=1,
            grid=(count,),
            in_specs=in_specs,
            out_specs=[
                pl.BlockSpec((tree_size, heads, head_size), lambda i, ids: (ids[i], 0, 0)),
                pl.BlockSpec((cache_rows, head_size), lambda i, ids: (ids[i], 0)),
            ],
            scratch_shapes=[pltpu.VMEM((rank_size, columns), BF16)],
        ),
        out_shape=[
            jax.ShapeDtypeStruct((rows, heads, head_size), BF16),
            jax.ShapeDtypeStruct((rows * 2 * kv_heads, head_size), BF16),
        ],
        input_output_aliases=aliases,
        compiler_params=pltpu.CompilerParams(vmem_limit_bytes=24 * 1024 * 1024),
        cost_estimate=pl.CostEstimate(
            flops=count * 500_000_000, bytes_accessed=count * 3_000_000, transcendentals=count * 200_000
        ),
        name="finish",
    )(*operands)


def per_device(
    hidden_states,
    kv_weight,
    shrink_factors,
    expand_factors,
    adapter_ids,
    cache_lengths,
    tree_parents,
    queries,
    cache_keys,
    cache_values,
    key_gain,
):
    requests, tree_size = tree_parents.shape
    row_count, half_width = hidden_states.shape
    kv_heads, kv_width = (kv_weight.shape[1], kv_weight.shape[2])
    head_size = kv_width // 2
    rank_size = shrink_factors.shape[2]
    context = cache_keys.shape[1]
    pool_count = lax.axis_size("pool")
    heads_here = kv_heads // lax.axis_size("tp")
    columns = heads_here * kv_width
    me = lax.axis_index("pool")
    core = lax.axis_index("tp").astype(jnp.int32).reshape(1)
    swap = [(0, 1), (1, 0)]

    def tile_rows(array):
        lead, heads = array.shape[0], array.shape[1]
        return array.reshape(lead, heads, 2, 128).transpose(0, 2, 1, 3).reshape(-1, 128)

    cut = (half_width + columns) // 2 - columns
    first, second = pack(
        core, shrink_factors[0].T, tile_rows(expand_factors[0]), cut, heads_here
    )

    order = ring_order(pool_count)
    onward = [(order[i], order[(i + 1) % pool_count]) for i in range(pool_count)]
    backward = [(b, a) for a, b in onward]
    half = pool_count // 2
    offsets = [[0]] + [[-step, step] for step in range(1, half)] + [[half]]
    flat_offsets = sum(offsets, [])
    owners = np.zeros((pool_count, pool_count), np.int32)
    for spot, index in enumerate(order):
        owners[index] = [order[(spot + offset) % pool_count] for offset in flat_offsets]
    owners_here = lax.dynamic_index_in_dim(jnp.asarray(owners), me, 0, keepdims=False)

    arrivals = [[(first, second)]]
    front = rear = (first, second)
    for step in range(1, half):
        front = tuple(lax.ppermute(piece, "pool", onward) for piece in front)
        rear = tuple(lax.ppermute(piece, "pool", backward) for piece in rear)
        arrivals.append([front, rear])
    arrivals.append(
        [(lax.ppermute(front[0], "pool", onward), lax.ppermute(rear[1], "pool", backward))]
    )

    here, away = base_product(core, hidden_states, tile_rows(kv_weight), kv_heads * kv_width)
    there = lax.ppermute(away, "tp", swap)
    after = [arrivals[1][1][1]]
    cosine, sine, bias = tree_tables(cache_lengths, tree_parents, head_size, context, after)
    shared = (
        here,
        there,
        cosine,
        sine,
        key_gain.reshape(1, head_size),
        bias,
        queries,
        cache_keys.reshape(-1, head_size),
        cache_values.reshape(-1, head_size),
        context,
    )

    hot = (adapter_ids[None, :] == owners_here[:, None]).astype(jnp.int32)
    asked = jnp.sum(hot * jnp.arange(requests, dtype=jnp.int32)[None, :], 1)
    outputs = None
    if pool_count == requests:
        groups = [arrivals[0] + arrivals[1] + arrivals[2]] + arrivals[3:]
        at = 0
        for group in groups:
            ids = asked[at : at + len(group)]
            at += len(group)
            partial = shrink_rows(ids, hidden_states, group, tree_size, columns, cut)
            batch = (ids, partial, lax.ppermute(partial, "tp", swap), [piece[0] for piece in group])
            outputs = finish(batch, shared, outputs)
    else:
        parts = []
        for slot, piece in enumerate(sum(arrivals, [])):
            parts.append(
                shrink_rows(asked[slot : slot + 1], hidden_states, [piece], tree_size, columns, cut)
            )
        slots = jnp.sum(hot * jnp.arange(pool_count, dtype=jnp.int32)[:, None], 0)
        partial = jnp.concatenate(parts, 0)[slots]
        expands = jnp.stack([piece[0][:, :columns] for piece in sum(arrivals, [])])[slots]
        ids = jnp.arange(requests, dtype=jnp.int32)
        pieces = [expands[r] for r in range(requests)]
        outputs = finish((ids, partial, lax.ppermute(partial, "tp", swap), pieces), shared, None)
    attention, cache_rows = outputs
    tree_cache = (
        cache_rows.reshape(row_count, 2, heads_here, head_size)
        .transpose(0, 2, 1, 3)
        .reshape(row_count, heads_here, kv_width)
    )
    return attention, tree_cache


def solution(mesh):
    placed = (
        P(("grp", "pool"), "tp"),
        P("tp", None, None),
        P(("grp", "pool"), "tp", None),
        P(("grp", "pool"), None, None, None),
        P(("grp", "pool")),
        P(("grp", "pool")),
        P(("grp", "pool"), None),
        P(("grp", "pool"), "tp", None),
        P(("grp", "pool"), None, "tp", None),
        P(("grp", "pool"), None, "tp", None),
        P(),
    )
    return jax.shard_map(
        per_device,
        mesh=mesh,
        in_specs=placed,
        out_specs=(P(("grp", "pool"), "tp", None), P(("grp", "pool"), "tp", None)),
        check_vma=False,
    )
```

time: 117 us -> 72.9 us (0.62)
  Pallas kernels: 12.1 us -> 35.1 us
  local copies, waits for them, and re-layouts: 29.4 us -> 8.05 us
  matrix products: 21.3 us -> 0 us
  other arithmetic: 18.1 us -> 0.78 us
  between operations: 11.1 us -> 0.8 us
  waiting for transfers between devices: 7.74 us -> 11.5 us
    pallas_call x1 -> x9, Pallas kernels: 12.1 us -> 35.1 us  [the longest x3 15.5 us: finish(): pl.pallas_call(functools.partial(finish_kernel, count=count), grid_spec=p...]
    dot_general x21 -> x0, matrix products: 21.3 us -> none  [the longest x4 7.79 us: ancestry(): jnp.einsum('...ij,...jk->...ik', reach, reach, preferred_element_type=F32)]
    ppermute x6, waiting for transfers between devices: 0.03 us -> 11.5 us  [per_device(): front = tuple((lax.ppermute(piece, 'pool', onward) for piece in front))]
    another operation x8 -> x0, other arithmetic: 10.7 us -> none  [shrunk_of(): request = jnp.argmax(hot).astype(jnp.int32)]
    ppermute x6, starting transfers between devices: 12.3 us -> 2.93 us  [per_device(): front = tuple((lax.ppermute(piece, 'pool', onward) for piece in front))]
    ppermute x6, starting transfers between devices: 1.36 us -> 10.4 us  [per_device(): rear = tuple((lax.ppermute(piece, 'pool', backward) for piece in rear))]
    unnamed x39 -> x32, local copies, waits for them, and re-layouts: 13.6 us -> 6.63 us
    ppermute x6, waiting for transfers between devices: 6.92 us -> 0.02 us  [per_device(): rear = tuple((lax.ppermute(piece, 'pool', backward) for piece in rear))]
  transfers between devices with their start and end apart: 16 -> 18, of which waited for: 4 -> 3; matrix products, arithmetic and copies ran while one was open for 58% -> 3% of each run, Pallas kernels for 0% -> 42%
where the time goes in v2:
time: 72.9 us; the launch traced here: 72.3 us
  Pallas kernels  35.1 us (48%)
  starting transfers between devices  16 us (22%)
  waiting for transfers between devices  11.5 us (16%)
  local copies, waits for them, and re-layouts  8.05 us (11%)
  between operations  0.8 us (1%)
  other arithmetic  0.78 us (1%)
    pallas_call x3, Pallas kernels, finish(): pl.pallas_call(functools.partial(finish_kernel, count=count), grid_spec=p...  15.5 us
    ppermute x6, waiting for transfers between devices, per_device(): front = tuple((lax.ppermute(piece, 'pool', onward) for piece in front))  11.5 us
    ppermute x6, starting transfers between devices, per_device(): rear = tuple((lax.ppermute(piece, 'pool', backward) for piece in rear))  10.4 us
    pallas_call x3, Pallas kernels, shrink_rows(): pl.pallas_call(functools.partial(shrink_kernel, columns=columns, cut=cut)...  7.22 us
    pallas_call x1, Pallas kernels, base_product(): pl.pallas_call(base_kernel, grid_spec=pltpu.PrefetchScalarGridSpec(num_sc...  6.71 us
    unnamed x32, local copies, waits for them, and re-layouts  6.63 us
    pallas_call x1, Pallas kernels, tree_tables(): pl.pallas_call(functools.partial(tree_kernel, context=context), grid_spec...  3.88 us
    ppermute x6, starting transfers between devices, per_device(): front = tuple((lax.ppermute(piece, 'pool', onward) for piece in front))  2.93 us
  transfers between devices with their start and end apart: 18, of which 3 were waited for; matrix products, arithmetic and copies ran while one was open for 3% of the time, Pallas kernels for 42%

profile of v2, /device:TPU:0, one launch (start us, length us, event | category | flops | bytes accessed | tf_op | source)
XLA Modules:
  0.0 72.3 jit_solution(12740159684893489450)
XLA Ops:
  0.6 1.9 %pack.1 = (bf16[64,1536]{1,0:T(8,128)(2,1)}, bf16[64,1536]{1,0:T(8,128)(2,1)}) custom-call(s32[1]{0:T(128)} %bitcast.1.core_ref, bf16[64,2560]{1,0:T(8,128)(2,1)} %bitcast.40, bf16[512,128]{1,0:T(8,128)(2,1)} %bitcast.41), custom_call_target="tpu_custom_call" | custom-call | tf_op jit(solution)/shard_map/pack/pallas_call | solution.py:54
  2.5 3.0 %collective-permute-start.13 = (bf16[64,1536]{1,0:T(8,128)(2,1)}, bf16[64,1536]{1,0:T(8,128)(2,1)}, u32[]{:S(2)}, u32[]{:S(2)}) collective-permute-start(bf16[64,1536]{1,0:T(8,128)(2,1)} %get-tuple-element.17.refs_1_.rest_0_), channel_id=1, source_target_pairs={{4,0},{8,4},{12,8},{14,12},{10,14},{6,10},{2,6},{0,2},{5,1},{9,5},... | collective-permute-start | bytes 589832 | tf_op jit(solution)/shard_map/ppermute | solution.py:473
  5.5 2.0 %collective-permute-start.5 = (bf16[64,1536]{1,0:T(8,128)(2,1)}, bf16[64,1536]{1,0:T(8,128)(2,1)}, u32[]{:S(2)}, u32[]{:S(2)}) collective-permute-start(bf16[64,1536]{1,0:T(8,128)(2,1)} %get-tuple-element.18.refs_2_), channel_id=1, source_target_pairs={{4,0},{8,4},{12,8},{14,12},{10,14},{6,10},{2,6},{0,2},{5,1},{9,5},... | collective-permute-start | bytes 589832 | tf_op jit(solution)/shard_map/ppermute | solution.py:473
  7.5 1.5 %copy-done = bf16[384,2560]{1,0:T(8,128)(2,1)S(1)} copy-done((bf16[384,2560]{1,0:T(8,128)(2,1)S(1)}, bf16[384,2560]{1,0:T(8,128)(2,1)}, u32[]{:S(2)}) %copy-start) | copy-done | bytes 1966104
  9.0 2.5 %copy-done.14 = bf16[2560,4,256]{2,1,0:T(4,128)(2,1)S(1)} copy-done((bf16[2560,4,256]{2,1,0:T(4,128)(2,1)S(1)}, bf16[2560,4,256]{2,1,0:T(4,128)(2,1)}, u32[]{:S(2)}) %copy-start.14) | copy-done | bytes 5242904
  11.5 6.7 %base.1 = (f32[384,512]{1,0:T(8,128)S(1)}, f32[384,512]{1,0:T(8,128)}) custom-call(s32[1]{0:T(128)} %bitcast.1.core_ref, bf16[384,2560]{1,0:T(8,128)(2,1)S(1)} %copy-done, bf16[20480,128]{1,0:T(8,128)(2,1)S(1)} %bitcast.38), custom_call_target="tpu_custom_call" | custom-call | flops 4000000000 | bytes 9000000 | tf_op jit(solution)/shard_map/base/pallas_call | solution.py:126
  18.3 2.0 %collective-permute-start.2 = (bf16[64,1536]{1,0:T(8,128)(2,1)}, bf16[64,1536]{1,0:T(8,128)(2,1)}, u32[]{:S(2)}, u32[]{:S(2)}) collective-permute-start(bf16[64,1536]{1,0:T(8,128)(2,1)} %collective-permute-done.1.refs_4_.rest_1_), channel_id=1, source_target_pairs={{0,4},{4,8},{8,12},{12,14},{14,10},{10,6},{6,2},{2,0},{1,5},{5,9},... | collective-permute-start | bytes 589832 | tf_op jit(solution)/shard_map/ppermute | solution.py:472
  20.3 2.0 %collective-permute-start.14 = (bf16[64,1536]{1,0:T(8,128)(2,1)}, bf16[64,1536]{1,0:T(8,128)(2,1)}, u32[]{:S(2)}, u32[]{:S(2)}) collective-permute-start(bf16[64,1536]{1,0:T(8,128)(2,1)} %collective-permute-done.13.refs_7_.rest_2_), channel_id=1, source_target_pairs={{4,0},{8,4},{12,8},{14,12},{10,14},{6,10},{2,6},{0,2},{5,1},{9,5},... | collective-permute-start | bytes 589832 | tf_op jit(solution)/shard_map/ppermute | solution.py:473
  22.3 3.9 %collective-permute-done.10.refs_5_ = bf16[64,1536]{1,0:T(8,128)(2,1)} collective-permute-done((bf16[64,1536]{1,0:T(8,128)(2,1)}, bf16[64,1536]{1,0:T(8,128)(2,1)}, u32[]{:S(2)}, u32[]{:S(2)}) %collective-permute-start.10) | collective-permute-done | bytes 196640 | tf_op jit(solution)/shard_map/ppermute | solution.py:472
  26.2 0.1 collective-permute-start.11
  26.4 4.1 %collective-permute-done.2.refs_10_.rest_3_ = bf16[64,1536]{1,0:T(8,128)(2,1)} collective-permute-done((bf16[64,1536]{1,0:T(8,128)(2,1)}, bf16[64,1536]{1,0:T(8,128)(2,1)}, u32[]{:S(2)}, u32[]{:S(2)}) %collective-permute-start.2) | collective-permute-done | bytes 196640 | tf_op jit(solution)/shard_map/ppermute | solution.py:472
  30.6 1.9 %collective-permute-start.7 = (bf16[64,1536]{1,0:T(8,128)(2,1)}, bf16[64,1536]{1,0:T(8,128)(2,1)}, u32[]{:S(2)}, u32[]{:S(2)}) collective-permute-start(bf16[64,1536]{1,0:T(8,128)(2,1)} %collective-permute-done.6.refs_14_), channel_id=1, source_target_pairs={{4,0},{8,4},{12,8},{14,12},{10,14},{6,10},{2,6},{0,2},{5,1},{9,5},... | collective-permute-start | bytes 589832 | tf_op jit(solution)/shard_map/ppermute | solution.py:473
  32.5 0.7 dynamic-slice_bitcast_fusion
  33.2 1.6 %collective-permute-start.15 = (bf16[64,1536]{1,0:T(8,128)(2,1)}, bf16[64,1536]{1,0:T(8,128)(2,1)S(1)}, u32[]{:S(2)}, u32[]{:S(2)}) collective-permute-start(bf16[64,1536]{1,0:T(8,128)(2,1)} %collective-permute-done.14.refs_13_.rest_4_), channel_id=1, source_target_pairs={{4,0},{8,4},{12,8},{14,12},{10,14},{6,10},{2,6},{0,2},{5,1},{9,5},... | collective-permute-start | bytes 589832 | tf_op jit(solution)/shard_map/ppermute | solution.py:473
  34.8 0.2 select_reduce_fusion
  35.0 0.5 collective-permute-start.12
  35.5 3.4 %collective-permute-done.3.refs_1_.rest_0_ = bf16[64,1536]{1,0:T(8,128)(2,1)} collective-permute-done((bf16[64,1536]{1,0:T(8,128)(2,1)}, bf16[64,1536]{1,0:T(8,128)(2,1)}, u32[]{:S(2)}, u32[]{:S(2)}) %collective-permute-start.3) | collective-permute-done | bytes 196640 | tf_op jit(solution)/shard_map/ppermute | solution.py:472
  39.0 1.9 %collective-permute-start.8 = (bf16[64,1536]{1,0:T(8,128)(2,1)}, bf16[64,1536]{1,0:T(8,128)(2,1)}, u32[]{:S(2)}, u32[]{:S(2)}) collective-permute-start(bf16[64,1536]{1,0:T(8,128)(2,1)} %collective-permute-done.7.refs_5_), channel_id=1, source_target_pairs={{4,0},{8,4},{12,8},{14,12},{10,14},{6,10},{2,6},{0,2},{5,1},{9,5},... | collective-permute-start | bytes 589832 | tf_op jit(solution)/shard_map/ppermute | solution.py:476
  40.9 0.9 %copy-done.11 = bf16[64,1536]{1,0:T(8,128)(2,1)S(1)} copy-done((bf16[64,1536]{1,0:T(8,128)(2,1)S(1)}, bf16[64,1536]{1,0:T(8,128)(2,1)}, u32[]{:S(2)}) %copy-start.11) | copy-done | bytes 196632
  41.9 3.3 %shrink.5.shrunk_here_ref = f32[5,48,64]{2,1,0:T(8,128)} custom-call(s32[5]{0:T(128)S(1)} %bitcast.36, bf16[384,2560]{1,0:T(8,128)(2,1)S(1)} %copy-done.1, bf16[64,1536]{1,0:T(8,128)(2,1)S(1)} %copy-done.11, bf16[64,1536]{1,0:T(8,128)(2,1)} %get-tuple-element.18.refs_2_, bf16[384,2560]{1,0:T(8,128)(2,1)S(1)} %copy-done.1, ...), custom_call_target="tpu_custom_call" | custom-call | flops 500000000 | bytes 7500000 | tf_op jit(solution)/shard_map/shrink/pallas_call | solution.py:242
  45.1 0.7 copy-done.6
  45.8 0.6 maximum_bitcast_fusion.frequency_ref
  46.5 0.7 slice.9.request_ref
  47.1 3.9 %tree.1 = (f32[384,128]{1,0:T(8,128)}, f32[384,128]{1,0:T(8,128)}, f32[384,256]{1,0:T(8,128)}) custom-call(s32[8]{0:T(128)} %length_ref.1, s32[8,48]{1,0:T(8,128)} %parent_ref.1, f32[1,128]{1,0:T(1,128)} %maximum_bitcast_fusion.frequency_ref, bf16[64,1536]{1,0:T(8,128)(2,1)} %collective-permute-done.5.rest_0_.refs_8_), custom_call_target="tpu_custom_call" | custom-call | flops 50000000 | bytes 8000000 | tf_op jit(solution)/shard_map/tree/pallas_call | solution.py:200
  51.0 0.9 %copy-done.7 = bf16[64,1536]{1,0:T(8,128)(2,1)S(1)} copy-done((bf16[64,1536]{1,0:T(8,128)(2,1)S(1)}, bf16[64,1536]{1,0:T(8,128)(2,1)}, u32[]{:S(2)}) %copy-start.7) | copy-done | bytes 196632
  52.0 2.0 %shrink.4.shrunk_here_ref = f32[2,48,64]{2,1,0:T(8,128)S(1)} custom-call(s32[2]{0:T(128)S(1)} %slice.10.request_ref, bf16[384,2560]{1,0:T(8,128)(2,1)S(1)} %copy-done.1, bf16[64,1536]{1,0:T(8,128)(2,1)} %collective-permute-done.3.refs_1_.rest_0_, bf16[64,1536]{1,0:T(8,128)(2,1)} %collective-permute-done.12.refs_2_, bf16[384,2560]{1,0:T(8,128)(2,1)S(1)} %copy-done.1, ...), custom_call_target="tpu_custom_call" | custom-call | flops 200000000 | bytes 3000000 | tf_op jit(solution)/shard_map/shrink/pallas_call | solution.py:242
  54.0 0.6 collective-permute-start.16
  54.6 2.0 %shrink.3.shrunk_here_ref = f32[1,48,64]{2,1,0:T(8,128)S(1)} custom-call(s32[1]{0:T(128)} %slice.9.request_ref, bf16[384,2560]{1,0:T(8,128)(2,1)S(1)} %copy-done.1, bf16[64,1536]{1,0:T(8,128)(2,1)} %collective-permute-done.4.refs_1_.rest_0_, bf16[64,1536]{1,0:T(8,128)(2,1)} %collective-permute-done.8.refs_2_), custom_call_target="tpu_custom_call" | custom-call | flops 100000000 | bytes 1500000 | tf_op jit(solution)/shard_map/shrink/pallas_call | solution.py:242
  56.6 0.1 collective-permute-start.9
  56.8 7.9 %finish.3 = (bf16[384,16,128]{2,1,0:T(8,128)(2,1)}, bf16[1536,128]{1,0:T(8,128)(2,1)}) custom-call(s32[5]{0:T(128)S(1)} %bitcast.37, f32[384,512]{1,0:T(8,128)S(1)} %get-tuple-element.15.here_ref, f32[384,512]{1,0:T(8,128)S(1)} %collective-permute-done.there_ref, f32[5,48,64]{2,1,0:T(8,128)} %shrink.5.shrunk_here_ref, ...), custom_call_target="tpu_custom_call" | custom-call | flops 2500000000 | bytes 15000000 | tf_op jit(solution)/shard_map/finish/pallas_call | solution.py:398
  64.7 4.3 %finish.4 = (bf16[384,16,128]{2,1,0:T(8,128)(2,1)}, bf16[1536,128]{1,0:T(8,128)(2,1)}) custom-call(s32[2]{0:T(128)S(1)} %slice.10.request_ref, f32[384,512]{1,0:T(8,128)S(1)} %get-tuple-element.15.here_ref, f32[384,512]{1,0:T(8,128)S(1)} %collective-permute-done.there_ref, ...), custom_call_target="tpu_custom_call", output_to_operand_aliasing={{0}: (14, {}), {1}: (15, {})} | custom-call | flops 1000000000 | bytes 6000000 | tf_op jit(solution)/shard_map/finish/pallas_call | solution.py:398
  69.0 3.3 %finish.5 = (bf16[384,16,128]{2,1,0:T(8,128)(2,1)}, bf16[1536,128]{1,0:T(8,128)(2,1)}) custom-call(s32[1]{0:T(128)} %slice.9.request_ref, f32[384,512]{1,0:T(8,128)S(1)} %get-tuple-element.15.here_ref, f32[384,512]{1,0:T(8,128)S(1)} %collective-permute-done.there_ref, ...), custom_call_target="tpu_custom_call", output_to_operand_aliasing={{0}: (13, {}), {1}: (14, {})} | custom-call | flops 500000000 | bytes 3000000 | tf_op jit(solution)/shard_map/finish/pallas_call | solution.py:398
  (51 shorter events, 0.6 us)
Async XLA Ops:
  2.5 17.8 %collective-permute-start.13 = (bf16[64,1536]{1,0:T(8,128)(2,1)}, bf16[64,1536]{1,0:T(8,128)(2,1)}, u32[]{:S(2)}, u32[]{:S(2)}) collective-permute-start(bf16[64,1536]{1,0:T(8,128)(2,1)} %get-tuple-element.17.refs_1_.rest_0_), channel_id=1, source_target_pairs={{4,0},{8,4},{12,8},{14,12},{10,14},{6,10},{2,6},{0,2},{5,1},{9,5},... | collective-permute-start | bytes 589832 | tf_op jit(solution)/shard_map/ppermute | solution.py:473
  5.5 12.8 %collective-permute-start.1 = (bf16[64,1536]{1,0:T(8,128)(2,1)}, bf16[64,1536]{1,0:T(8,128)(2,1)}, u32[]{:S(2)}, u32[]{:S(2)}) collective-permute-start(bf16[64,1536]{1,0:T(8,128)(2,1)} %get-tuple-element.17.refs_1_.rest_0_), channel_id=1, source_target_pairs={{0,4},{4,8},{8,12},{12,14},{14,10},{10,6},{6,2},{2,0},{1,5},{5,9},... | collective-permute-start | bytes 589832 | tf_op jit(solution)/shard_map/ppermute | solution.py:472
  5.5 14.8 %collective-permute-start.5 = (bf16[64,1536]{1,0:T(8,128)(2,1)}, bf16[64,1536]{1,0:T(8,128)(2,1)}, u32[]{:S(2)}, u32[]{:S(2)}) collective-permute-start(bf16[64,1536]{1,0:T(8,128)(2,1)} %get-tuple-element.18.refs_2_), channel_id=1, source_target_pairs={{4,0},{8,4},{12,8},{14,12},{10,14},{6,10},{2,6},{0,2},{5,1},{9,5},... | collective-permute-start | bytes 589832 | tf_op jit(solution)/shard_map/ppermute | solution.py:473
  7.5 1.5 %copy-start = (bf16[384,2560]{1,0:T(8,128)(2,1)S(1)}, bf16[384,2560]{1,0:T(8,128)(2,1)}, u32[]{:S(2)}) copy-start(bf16[384,2560]{1,0:T(8,128)(2,1)} %refs_12_.1) | copy-start | bytes 5898244
  9.0 2.5 %copy-start.14 = (bf16[2560,4,256]{2,1,0:T(4,128)(2,1)S(1)}, bf16[2560,4,256]{2,1,0:T(4,128)(2,1)}, u32[]{:S(2)}) copy-start(bf16[2560,4,256]{2,1,0:T(4,128)(2,1)} %param.13) | copy-start | bytes 15728644
  11.5 23.2 %copy-start.15 = (s32[8]{0:T(128)S(1)}, s32[8]{0:T(128)}, u32[]{:S(2)}) copy-start(s32[8]{0:T(128)} %param.16) | copy-start | bytes 100
  11.5 29.4 %copy-start.1 = (bf16[384,2560]{1,0:T(8,128)(2,1)S(1)}, bf16[384,2560]{1,0:T(8,128)(2,1)}, u32[]{:S(2)}) copy-start(bf16[384,2560]{1,0:T(8,128)(2,1)} %refs_12_.1) | copy-start | bytes 5898244
  18.2 38.5 %collective-permute-start = (f32[384,512]{1,0:T(8,128)}, f32[384,512]{1,0:T(8,128)S(1)}, u32[]{:S(2)}, u32[]{:S(2)}) collective-permute-start(f32[384,512]{1,0:T(8,128)} %get-tuple-element.16), channel_id=1, source_target_pairs={{0,1},{1,0},{2,3},{3,2},{4,5},{5,4},{6,7},{7,6},{8,9},{9,8},{10,11... | collective-permute-start | bytes 2359304 | tf_op jit(solution)/shard_map/ppermute | solution.py:480
  18.2 8.0 %collective-permute-start.10 = (bf16[64,1536]{1,0:T(8,128)(2,1)}, bf16[64,1536]{1,0:T(8,128)(2,1)}, u32[]{:S(2)}, u32[]{:S(2)}) collective-permute-start(bf16[64,1536]{1,0:T(8,128)(2,1)} %get-tuple-element.18.refs_2_), channel_id=1, source_target_pairs={{0,4},{4,8},{8,12},{12,14},{14,10},{10,6},{6,2},{2,0},{1,5},{5,9},... | collective-permute-start | bytes 589832 | tf_op jit(solution)/shard_map/ppermute | solution.py:472
  18.3 12.2 %collective-permute-start.2 = (bf16[64,1536]{1,0:T(8,128)(2,1)}, bf16[64,1536]{1,0:T(8,128)(2,1)}, u32[]{:S(2)}, u32[]{:S(2)}) collective-permute-start(bf16[64,1536]{1,0:T(8,128)(2,1)} %collective-permute-done.1.refs_4_.rest_1_), channel_id=1, source_target_pairs={{0,4},{4,8},{8,12},{12,14},{14,10},{10,6},{6,2},{2,0},{1,5},{5,9},... | collective-permute-start | bytes 589832 | tf_op jit(solution)/shard_map/ppermute | solution.py:472
  20.3 10.3 %collective-permute-start.6 = (bf16[64,1536]{1,0:T(8,128)(2,1)}, bf16[64,1536]{1,0:T(8,128)(2,1)}, u32[]{:S(2)}, u32[]{:S(2)}) collective-permute-start(bf16[64,1536]{1,0:T(8,128)(2,1)} %collective-permute-done.5.rest_0_.refs_8_), channel_id=1, source_target_pairs={{4,0},{8,4},{12,8},{14,12},{10,14},{6,10},{2,6},{0,2},{5,1},{9,5},... | collective-permute-start | bytes 589832 | tf_op jit(solution)/shard_map/ppermute | solution.py:473
  20.3 12.9 %collective-permute-start.14 = (bf16[64,1536]{1,0:T(8,128)(2,1)}, bf16[64,1536]{1,0:T(8,128)(2,1)}, u32[]{:S(2)}, u32[]{:S(2)}) collective-permute-start(bf16[64,1536]{1,0:T(8,128)(2,1)} %collective-permute-done.13.refs_7_.rest_2_), channel_id=1, source_target_pairs={{4,0},{8,4},{12,8},{14,12},{10,14},{6,10},{2,6},{0,2},{5,1},{9,5},... | collective-permute-start | bytes 589832 | tf_op jit(solution)/shard_map/ppermute | solution.py:473
  26.2 8.7 %collective-permute-start.11 = (bf16[64,1536]{1,0:T(8,128)(2,1)}, bf16[64,1536]{1,0:T(8,128)(2,1)}, u32[]{:S(2)}, u32[]{:S(2)}) collective-permute-start(bf16[64,1536]{1,0:T(8,128)(2,1)} %collective-permute-done.10.refs_5_), channel_id=1, source_target_pairs={{0,4},{4,8},{8,12},{12,14},{14,10},{10,6},{6,2},{2,0},{1,5},{5,9},... | collective-permute-start | bytes 589832 | tf_op jit(solution)/shard_map/ppermute | solution.py:472
  30.5 8.4 %collective-permute-start.3 = (bf16[64,1536]{1,0:T(8,128)(2,1)}, bf16[64,1536]{1,0:T(8,128)(2,1)}, u32[]{:S(2)}, u32[]{:S(2)}) collective-permute-start(bf16[64,1536]{1,0:T(8,128)(2,1)} %collective-permute-done.2.refs_10_.rest_3_), channel_id=1, source_target_pairs={{0,4},{4,8},{8,12},{12,14},{14,10},{10,6},{6,2},{2,0},{1,5},{5,9},... | collective-permute-start | bytes 589832 | tf_op jit(solution)/shard_map/ppermute | solution.py:472
  30.6 8.4 %collective-permute-start.7 = (bf16[64,1536]{1,0:T(8,128)(2,1)}, bf16[64,1536]{1,0:T(8,128)(2,1)}, u32[]{:S(2)}, u32[]{:S(2)}) collective-permute-start(bf16[64,1536]{1,0:T(8,128)(2,1)} %collective-permute-done.6.refs_14_), channel_id=1, source_target_pairs={{4,0},{8,4},{12,8},{14,12},{10,14},{6,10},{2,6},{0,2},{5,1},{9,5},... | collective-permute-start | bytes 589832 | tf_op jit(solution)/shard_map/ppermute | solution.py:473
  33.2 11.9 %collective-permute-start.15 = (bf16[64,1536]{1,0:T(8,128)(2,1)}, bf16[64,1536]{1,0:T(8,128)(2,1)S(1)}, u32[]{:S(2)}, u32[]{:S(2)}) collective-permute-start(bf16[64,1536]{1,0:T(8,128)(2,1)} %collective-permute-done.14.refs_13_.rest_4_), channel_id=1, source_target_pairs={{4,0},{8,4},{12,8},{14,12},{10,14},{6,10},{2,6},{0,2},{5,1},{9,5},... | collective-permute-start | bytes 589832 | tf_op jit(solution)/shard_map/ppermute | solution.py:473
  35.0 16.1 %collective-permute-start.12 = (bf16[64,1536]{1,0:T(8,128)(2,1)}, bf16[64,1536]{1,0:T(8,128)(2,1)}, u32[]{:S(2)}, u32[]{:S(2)}) collective-permute-start(bf16[64,1536]{1,0:T(8,128)(2,1)} %collective-permute-done.11.refs_11_), channel_id=1, source_target_pairs={{0,4},{4,8},{8,12},{12,14},{14,10},{10,6},{6,2},{2,0},{1,5},{5,9},... | collective-permute-start | bytes 589832 | tf_op jit(solution)/shard_map/ppermute | solution.py:472
  38.9 15.7 %collective-permute-start.4 = (bf16[64,1536]{1,0:T(8,128)(2,1)}, bf16[64,1536]{1,0:T(8,128)(2,1)}, u32[]{:S(2)}, u32[]{:S(2)}) collective-permute-start(bf16[64,1536]{1,0:T(8,128)(2,1)} %collective-permute-done.3.refs_1_.rest_0_), channel_id=1, source_target_pairs={{0,4},{4,8},{8,12},{12,14},{14,10},{10,6},{6,2},{2,0},{1,5},{5,9},... | collective-permute-start | bytes 589832 | tf_op jit(solution)/shard_map/ppermute | solution.py:476
  39.0 15.5 %collective-permute-start.8 = (bf16[64,1536]{1,0:T(8,128)(2,1)}, bf16[64,1536]{1,0:T(8,128)(2,1)}, u32[]{:S(2)}, u32[]{:S(2)}) collective-permute-start(bf16[64,1536]{1,0:T(8,128)(2,1)} %collective-permute-done.7.refs_5_), channel_id=1, source_target_pairs={{4,0},{8,4},{12,8},{14,12},{10,14},{6,10},{2,6},{0,2},{5,1},{9,5},... | collective-permute-start | bytes 589832 | tf_op jit(solution)/shard_map/ppermute | solution.py:476
  40.9 0.9 %copy-start.11 = (bf16[64,1536]{1,0:T(8,128)(2,1)S(1)}, bf16[64,1536]{1,0:T(8,128)(2,1)}, u32[]{:S(2)}) copy-start(bf16[64,1536]{1,0:T(8,128)(2,1)} %get-tuple-element.17.refs_1_.rest_0_) | copy-start | bytes 589828
  45.8 10.9 %collective-permute-start.17 = (f32[5,48,64]{2,1,0:T(8,128)}, f32[5,48,64]{2,1,0:T(8,128)}, u32[]{:S(2)}, u32[]{:S(2)}) collective-permute-start(f32[5,48,64]{2,1,0:T(8,128)} %shrink.5.shrunk_here_ref), channel_id=1, source_target_pairs={{0,1},{1,0},{2,3},{3,2},{4,5},{5,4},{6,7},{7,6},{8,9},{9,8},{10,11... | collective-permute-start | bytes 184328 | tf_op jit(solution)/shard_map/ppermute | solution.py:506
  52.0 4.8 %copy-start.4 = (bf16[8,128,2,128]{3,2,1,0:T(2,128)(2,1)S(1)}, bf16[8,128,2,128]{3,2,1,0:T(2,128)(2,1)}, u32[]{:S(2)}) copy-start(bf16[8,128,2,128]{3,2,1,0:T(2,128)(2,1)} %param.21) | copy-start | bytes 1572868
  52.0 4.8 %copy-start.5 = (f32[384,256]{1,0:T(8,128)S(1)}, f32[384,256]{1,0:T(8,128)}, u32[]{:S(2)}) copy-start(f32[384,256]{1,0:T(8,128)} %get-tuple-element.21.bias_ref) | copy-start | bytes 1179652
  52.0 4.8 %copy-start.10 = (f32[384,128]{1,0:T(8,128)S(1)}, f32[384,128]{1,0:T(8,128)}, u32[]{:S(2)}) copy-start(f32[384,128]{1,0:T(8,128)} %get-tuple-element.20.sine_ref) | copy-start | bytes 589828
  52.0 4.8 %copy-start.12 = (bf16[64,1536]{1,0:T(8,128)(2,1)S(1)}, bf16[64,1536]{1,0:T(8,128)(2,1)}, u32[]{:S(2)}) copy-start(bf16[64,1536]{1,0:T(8,128)(2,1)} %get-tuple-element.17.refs_1_.rest_0_) | copy-start | bytes 589828
  53.9 2.8 %copy-start.2 = (bf16[384,16,128]{2,1,0:T(8,128)(2,1)S(1)}, bf16[384,16,128]{2,1,0:T(8,128)(2,1)}, u32[]{:S(2)}) copy-start(bf16[384,16,128]{2,1,0:T(8,128)(2,1)} %query_ref.5) | copy-start | bytes 4718596
  53.9 2.8 %copy-start.3 = (bf16[8,128,2,128]{3,2,1,0:T(2,128)(2,1)S(1)}, bf16[8,128,2,128]{3,2,1,0:T(2,128)(2,1)}, u32[]{:S(2)}) copy-start(bf16[8,128,2,128]{3,2,1,0:T(2,128)(2,1)} %param.20) | copy-start | bytes 1572868
  53.9 2.8 %copy-start.9 = (f32[384,128]{1,0:T(8,128)S(1)}, f32[384,128]{1,0:T(8,128)}, u32[]{:S(2)}) copy-start(f32[384,128]{1,0:T(8,128)} %get-tuple-element.19.cosine_ref) | copy-start | bytes 589828
  54.0 2.8 %copy-start.13 = (f32[128]{0:T(128)S(1)}, f32[128]{0:T(128)}, u32[]{:S(2)}) copy-start(f32[128]{0:T(128)} %param.22) | copy-start | bytes 1540
  54.0 10.8 %collective-permute-start.16 = (f32[2,48,64]{2,1,0:T(8,128)S(1)}, f32[2,48,64]{2,1,0:T(8,128)S(1)}, u32[]{:S(2)}, u32[]{:S(2)}) collective-permute-start(f32[2,48,64]{2,1,0:T(8,128)S(1)} %shrink.4.shrunk_here_ref), channel_id=1, source_target_pairs={{0,1},{1,0},{2,3},{3,2},{4,5},{5,4},{6,7},{7,6},{8,9},{9,8},{10,11... | collective-permute-start | bytes 73736 | tf_op jit(solution)/shard_map/ppermute | solution.py:506
  56.6 12.5 %collective-permute-start.9 = (f32[1,48,64]{2,1,0:T(8,128)S(1)}, f32[1,48,64]{2,1,0:T(8,128)S(1)}, u32[]{:S(2)}, u32[]{:S(2)}) collective-permute-start(f32[1,48,64]{2,1,0:T(8,128)S(1)} %shrink.3.shrunk_here_ref), channel_id=1, source_target_pairs={{0,1},{1,0},{2,3},{3,2},{4,5},{5,4},{6,7},{7,6},{8,9},{9,8},{10,11... | collective-permute-start | bytes 36872 | tf_op jit(solution)/shard_map/ppermute | solution.py:506
  56.8 7.9 %copy-start.8 = (bf16[64,1536]{1,0:T(8,128)(2,1)S(1)}, bf16[64,1536]{1,0:T(8,128)(2,1)}, u32[]{:S(2)}) copy-start(bf16[64,1536]{1,0:T(8,128)(2,1)} %copy-done.6) | copy-start | bytes 589828
  (2 other events, 1.6 us)

commit v3 on v2

v3 whole, which is shorter than its diff:
```python
import functools
import math

import jax
import jax.numpy as jnp
import numpy as np
from jax import lax
from jax.experimental import pallas as pl
from jax.experimental.pallas import tpu as pltpu
from jax.sharding import PartitionSpec as P

F32 = jnp.float32
BF16 = jnp.bfloat16


ANYWHERE = pl.BlockSpec(memory_space=pl.ANY)


def shapes_of(arrays):
    return [jax.ShapeDtypeStruct(array.shape, array.dtype) for array in arrays]


def ring_order(count):
    if count == 8:
        return list(range(0, count, 2)) + list(range(count - 1, 0, -2))
    return list(range(count))


def sorting_matrix(rows, columns, inner, source_inner):
    row = lax.broadcasted_iota(jnp.int32, (rows, columns), 0)
    column = lax.broadcasted_iota(jnp.int32, (rows, columns), 1)
    return (column == (row % inner) * source_inner + row // inner).astype(F32).astype(BF16)


def picking_matrix(wanted, inner, groups, first_head):
    row = lax.broadcasted_iota(jnp.int32, (wanted * inner, 256), 0)
    column = lax.broadcasted_iota(jnp.int32, (wanted * inner, 256), 1)
    group = row // inner
    source = (group % 2) * (groups // 2) + first_head + group // 2
    return (column == (row % inner) * groups + source).astype(F32).astype(BF16)


def request_at(where, slot):
    me_ref, owner_ref, adapter_ref = where
    owner = owner_ref[me_ref[0], slot]
    request = jnp.int32(0)
    for r in range(1, adapter_ref.shape[0]):
        request = jnp.where(adapter_ref[r] == owner, jnp.int32(r), request)
    return request


def slot_of(where, request):
    me_ref, owner_ref, adapter_ref = where
    adapter = adapter_ref[request]
    slot = jnp.int32(0)
    for k in range(1, owner_ref.shape[1]):
        slot = jnp.where(owner_ref[me_ref[0], k] == adapter, jnp.int32(k), slot)
    return slot


def pack_kernel(core_ref, shrink_ref, expand_ref, first_ref, second_ref, *, cut, heads_here):
    rank_size = shrink_ref.shape[0]
    groups = expand_ref.shape[0] // rank_size
    ranks = 256 // groups
    pick = picking_matrix(2 * heads_here, ranks, groups, core_ref[0] * heads_here)
    columns = 2 * heads_here * 128
    for block in range(rank_size // ranks):
        sorted_rows = jnp.dot(
            pick, expand_ref[256 * block : 256 * (block + 1), :], preferred_element_type=F32
        ).astype(BF16)
        for g in range(2 * heads_here):
            first_ref[ranks * block : ranks * (block + 1), 128 * g : 128 * (g + 1)] = sorted_rows[
                ranks * g : ranks * (g + 1), :
            ]
    first_ref[:, columns:] = shrink_ref[:, :cut]
    second_ref[...] = shrink_ref[:, cut:]


def pack(core, shrink, expand_rows, cut, heads_here):
    rank_size, half_width = shrink.shape
    columns = 2 * heads_here * 128
    return pl.pallas_call(
        functools.partial(pack_kernel, cut=cut, heads_here=heads_here),
        grid_spec=pltpu.PrefetchScalarGridSpec(
            num_scalar_prefetch=1,
            grid=(1,),
            in_specs=[
                pl.BlockSpec(shrink.shape, lambda i, c: (0, 0)),
                pl.BlockSpec(expand_rows.shape, lambda i, c: (0, 0)),
            ],
            out_specs=[
                pl.BlockSpec((rank_size, columns + cut), lambda i, c: (0, 0)),
                pl.BlockSpec((rank_size, half_width - cut), lambda i, c: (0, 0)),
            ],
        ),
        out_shape=[
            jax.ShapeDtypeStruct((rank_size, columns + cut), BF16),
            jax.ShapeDtypeStruct((rank_size, half_width - cut), BF16),
        ],
        name="pack",
    )(core, shrink, expand_rows)


def base_kernel(core_ref, hidden_ref, weight_ref, *rest, held_count):
    total_ref, wide_ref = rest[-2:]
    here_ref, away_ref = rest[-2 - held_count - 2 : -2 - held_count]
    step = pl.program_id(0)
    depth = hidden_ref.shape[1]
    groups = weight_ref.shape[0] // depth
    heads = groups // 2
    wide_ref[...] = weight_ref[...].astype(F32)
    parts = []
    for head in range(heads):
        tiles = [
            wide_ref[pl.ds(tile * heads + head, depth, stride=groups), :].astype(BF16)
            for tile in range(2)
        ]
        parts.append(
            jnp.dot(hidden_ref[...], jnp.concatenate(tiles, 1), preferred_element_type=F32)
        )
    product = jnp.concatenate(parts, 1)

    @pl.when(step == 0)
    def _():
        total_ref[...] = product

    @pl.when(step > 0)
    def _():
        total_ref[...] += product

    @pl.when(step == pl.num_programs(0) - 1)
    def _():
        columns = here_ref.shape[1]

        @pl.when(core_ref[0] == 0)
        def _():
            here_ref[...] = total_ref[:, :columns]
            away_ref[...] = total_ref[:, columns:]

        @pl.when(core_ref[0] == 1)
        def _():
            here_ref[...] = total_ref[:, columns:]
            away_ref[...] = total_ref[:, :columns]


def base_product(core, hidden_states, weight_rows, width, held):
    rows, half_width = hidden_states.shape
    groups = weight_rows.shape[0] // half_width
    depth = half_width // 2
    return pl.pallas_call(
        functools.partial(base_kernel, held_count=len(held)),
        grid_spec=pltpu.PrefetchScalarGridSpec(
            num_scalar_prefetch=1,
            grid=(half_width // depth,),
            in_specs=[
                pl.BlockSpec((rows, depth), lambda i, c: (0, i)),
                pl.BlockSpec((depth * groups, 128), lambda i, c: (i, 0)),
            ]
            + [ANYWHERE] * len(held),
            out_specs=[pl.BlockSpec((rows, width // 2), lambda i, c: (0, 0))] * 2
            + [ANYWHERE] * len(held),
            scratch_shapes=[
                pltpu.VMEM((rows, width), F32),
                pltpu.VMEM((depth * groups, 128), F32),
            ],
        ),
        out_shape=[jax.ShapeDtypeStruct((rows, width // 2), F32)] * 2 + shapes_of(held),
        input_output_aliases={3 + k: 2 + k for k in range(len(held))},
        compiler_params=pltpu.CompilerParams(vmem_limit_bytes=56 * 1024 * 1024),
        cost_estimate=pl.CostEstimate(
            flops=4_000_000_000, bytes_accessed=9_000_000, transcendentals=0
        ),
        name="base",
    )(core, hidden_states, weight_rows, *held)


def tree_kernel(length_ref, parent_ref, frequency_ref, *rest, per_group):
    table_ref, bias_ref = rest[-2:]
    requests, nodes = parent_ref.shape
    head_size = frequency_ref.shape[1]
    node = lax.broadcasted_iota(jnp.int32, (nodes, nodes), 0)
    same = node == lax.broadcasted_iota(jnp.int32, (nodes, nodes), 1)
    spread = lax.broadcasted_iota(jnp.int32, (nodes, nodes * per_group), 1) // per_group
    spread = spread == lax.broadcasted_iota(jnp.int32, (nodes, nodes * per_group), 0)
    spread = spread.astype(F32).astype(BF16)
    parents = parent_ref[...]
    below = [
        (same | (parents[r : r + 1, :] == node)).astype(F32).astype(BF16) for r in range(requests)
    ]
    reached = 1
    while reached < nodes:
        below = [
            jnp.minimum(jnp.dot(b, b, preferred_element_type=F32), 1.0).astype(BF16) for b in below
        ]
        reached = 2 * reached
    lane = lax.broadcasted_iota(jnp.int32, (nodes, head_size), 1)
    sign = jnp.where(lane < head_size // 2, -1.0, 1.0)
    ones = jnp.ones((nodes, head_size), BF16)
    for r in range(requests):
        b = below[r]
        depth = lax.dot_general(b, ones, (((0,), (0,)), ((), ())), preferred_element_type=F32)
        positions = length_ref[r].astype(F32) + depth - 1.0
        angles = positions * frequency_ref[...]
        rows = slice(nodes * r, nodes * (r + 1))
        table_ref[rows, :] = jnp.concatenate([jnp.cos(angles), jnp.sin(angles) * sign], 1)
        wide = jnp.dot(b, spread, preferred_element_type=F32)
        bias_ref[rows, :] = jnp.where(wide > 0.5, 0.0, -1e30)


def tree_tables(cache_lengths, tree_parents, head_size, per_group, after):
    requests, nodes = tree_parents.shape
    half_size = head_size // 2
    frequency = np.exp(np.arange(half_size) * (-2.0 * math.log(1000000.0) / head_size))
    frequency = np.concatenate([frequency, frequency]).reshape(1, head_size).astype(np.float32)
    whole = lambda shape: pl.BlockSpec(shape, lambda i, n: (0,) * len(shape))
    rows = requests * nodes
    shapes = [(rows, 2 * head_size), (rows, nodes * per_group)]
    return pl.pallas_call(
        functools.partial(tree_kernel, per_group=per_group),
        grid_spec=pltpu.PrefetchScalarGridSpec(
            num_scalar_prefetch=1,
            grid=(1,),
            in_specs=[whole(tree_parents.shape), whole((1, head_size))] + [ANYWHERE] * len(after),
            out_specs=[whole(shape) for shape in shapes],
        ),
        out_shape=[jax.ShapeDtypeStruct(shape, F32) for shape in shapes],
        cost_estimate=pl.CostEstimate(
            flops=1_000_000_000, bytes_accessed=8_000_000, transcendentals=0
        ),
        name="tree",
    )(cache_lengths, tree_parents, frequency, *after)


def cache_kernel(length_ref, query_ref, key_ref, value_ref, *rest, first_request, held_count, kv_heads):
    output_ref, stat_ref = rest[-2 - held_count : len(rest) - held_count]
    tree_size, heads, head_size = query_ref.shape
    context = key_ref.shape[0] // kv_heads
    per_group = heads // kv_heads
    rows = tree_size * per_group
    score_scale = math.log2(math.e) / math.sqrt(head_size)
    length = length_ref[first_request + pl.program_id(0)]
    cached = jnp.dot(
        sorting_matrix(kv_heads * context, kv_heads * context, context, kv_heads),
        jnp.concatenate([key_ref[...], value_ref[...]], 1),
        preferred_element_type=F32,
    ).astype(BF16)
    queries = query_ref[...].astype(F32)
    allowed = lax.broadcasted_iota(jnp.int32, (context, rows), 0) < length
    stats = []
    for g in range(kv_heads):
        mine = slice(context * g, context * (g + 1))
        query = queries[:, per_group * g : per_group * (g + 1), :].reshape(rows, head_size)
        scores = lax.dot_general(
            cached[mine, :head_size],
            query.astype(BF16),
            (((1,), (1,)), ((), ())),
            preferred_element_type=F32,
        )
        scores = jnp.where(allowed, scores, -1e30)
        top = jnp.max(scores, 0, keepdims=True)
        exponent = jnp.exp2((scores - top) * score_scale)
        stats += [top, jnp.sum(exponent, 0, keepdims=True)]
        output_ref[rows * g : rows * (g + 1), :] = lax.dot_general(
            exponent.astype(BF16),
            cached[mine, head_size:],
            (((0,), (0,)), ((), ())),
            preferred_element_type=F32,
        )
    stats.append(jnp.zeros((stat_ref.shape[0] - len(stats), rows), F32))
    stat_ref[...] = jnp.concatenate(stats, 0)


def cache_attention(lengths, queries, key_rows, value_rows, kv_heads, first_request, count, held, after):
    rows, heads, head_size = queries.shape
    requests = lengths.shape[0]
    tree_size = rows // requests
    cached = key_rows.shape[0] // requests
    pair_rows = tree_size * heads
    return pl.pallas_call(
        functools.partial(
            cache_kernel, first_request=first_request, held_count=len(held), kv_heads=kv_heads
        ),
        grid_spec=pltpu.PrefetchScalarGridSpec(
            num_scalar_prefetch=1,
            grid=(count,),
            in_specs=[
                pl.BlockSpec((tree_size, heads, head_size), lambda i, n: (first_request + i, 0, 0)),
                pl.BlockSpec((cached, head_size), lambda i, n: (first_request + i, 0)),
                pl.BlockSpec((cached, head_size), lambda i, n: (first_request + i, 0)),
            ]
            + [ANYWHERE] * (len(held) + len(after)),
            out_specs=[
                pl.BlockSpec((pair_rows, head_size), lambda i, n: (i, 0)),
                pl.BlockSpec((8, pair_rows // kv_heads), lambda i, n: (i, 0)),
            ]
            + [ANYWHERE] * len(held),
        ),
        out_shape=[
            jax.ShapeDtypeStruct((count * pair_rows, head_size), F32),
            jax.ShapeDtypeStruct((count * 8, pair_rows // kv_heads), F32),
        ]
        + shapes_of(held),
        input_output_aliases={4 + k: 2 + k for k in range(len(held))},
        compiler_params=pltpu.CompilerParams(vmem_limit_bytes=24 * 1024 * 1024),
        cost_estimate=pl.CostEstimate(
            flops=count * 700_000_000, bytes_accessed=count * 2_000_000, transcendentals=0
        ),
        name="cached",
    )(lengths, queries, key_rows, value_rows, *held, *after)


def shrink_kernel(me_ref, owner_ref, adapter_ref, *refs, columns, cut):
    output_ref = refs[-1]
    contract = (((1,), (1,)), ((), ()))
    for b in range(output_ref.shape[0]):
        hidden_ref, one_ref, two_ref = refs[3 * b : 3 * b + 3]
        output_ref[b] = lax.dot_general(
            hidden_ref[:, :cut], one_ref[:, columns:], contract, preferred_element_type=F32
        ) + lax.dot_general(hidden_ref[:, cut:], two_ref[...], contract, preferred_element_type=F32)


def shrink_rows(where, slot, hidden_states, pieces, tree_size, columns, cut, after):
    rank_size = pieces[0][0].shape[0]
    in_specs, operands = [], []
    for b, (one, two) in enumerate(pieces):
        in_specs += [
            pl.BlockSpec(
                (tree_size, hidden_states.shape[1]),
                lambda i, *refs, b=b: (request_at(refs, slot + b), 0),
            ),
            pl.BlockSpec(one.shape, lambda i, *refs: (0, 0)),
            pl.BlockSpec(two.shape, lambda i, *refs: (0, 0)),
        ]
        operands += [hidden_states, one, two]
    count = len(pieces)
    return pl.pallas_call(
        functools.partial(shrink_kernel, columns=columns, cut=cut),
        grid_spec=pltpu.PrefetchScalarGridSpec(
            num_scalar_prefetch=3,
            grid=(1,),
            in_specs=in_specs + [pl.BlockSpec(memory_space=pl.ANY)] * len(after),
            out_specs=pl.BlockSpec((count, tree_size, rank_size), lambda i, *refs: (0, 0, 0)),
        ),
        out_shape=jax.ShapeDtypeStruct((count, tree_size, rank_size), F32),
        compiler_params=pltpu.CompilerParams(vmem_limit_bytes=24 * 1024 * 1024),
        cost_estimate=pl.CostEstimate(
            flops=count * 300_000_000, bytes_accessed=count * 2_000_000, transcendentals=0
        ),
        name="shrink",
    )(*where, *operands, *after)


def finish_kernel(
    me_ref,
    owner_ref,
    adapter_ref,
    here_ref,
    there_ref,
    table_ref,
    bias_ref,
    query_ref,
    gain_ref,
    *rest,
    group,
    parts,
    split,
    kv_heads,
):
    cached_refs = rest[: 2 * split]
    shrunk_refs = rest[2 * split : 2 * split + 2 * parts]
    expand_refs = rest[2 * split + 2 * parts : -4]
    attention_ref, cache_ref, expand_ref, shrunk_ref = rest[-4:]
    where = (me_ref, owner_ref, adapter_ref)
    step = pl.program_id(0)
    head_size = query_ref.shape[2]
    tree_size = query_ref.shape[0] // group
    per_group = query_ref.shape[1] // kv_heads
    cache_rows = 2 * kv_heads * tree_size
    pairs = tree_size * per_group
    score_scale = math.log2(math.e) / math.sqrt(head_size)

    @pl.when(step == 0)
    def _():
        for slot, ref in enumerate(expand_refs):
            expand_ref[slot] = ref[...]
        slot = 0
        for k in range(parts):
            count = shrunk_refs[2 * k].shape[0]
            shrunk_ref[slot : slot + count] = shrunk_refs[2 * k][...] + shrunk_refs[2 * k + 1][...]
            slot += count

    gain = gain_ref[...]
    sort_new = sorting_matrix(cache_rows, cache_rows, cache_rows // tree_size, tree_size)
    for b in range(group):
        slot = slot_of(where, step * group + b)
        shrunk = shrunk_ref[slot]
        high = shrunk.astype(BF16)
        left = shrunk - high.astype(F32)
        middle = left.astype(BF16)
        low = (left - middle.astype(F32)).astype(BF16)
        terms = jnp.dot(
            jnp.concatenate([low, middle, high], 0), expand_ref[slot], preferred_element_type=F32
        )
        delta = terms[:tree_size] + terms[tree_size : 2 * tree_size] + terms[2 * tree_size :]
        rows = slice(tree_size * b, tree_size * (b + 1))
        projected = (here_ref[rows, :] + there_ref[rows, :]) + delta
        cosine = table_ref[rows, :head_size]
        sine = table_ref[rows, head_size:]
        keys, values, outputs = [], [], []
        for g in range(kv_heads):
            at = 2 * head_size * g
            key = projected[:, at : at + head_size]
            values.append(projected[:, at + head_size : at + 2 * head_size].astype(BF16))
            norm = lax.rsqrt(jnp.mean(key * key, -1, keepdims=True) + 1e-06)
            key = key * norm * gain
            keys.append((key * cosine + pltpu.roll(key, head_size // 2, 1) * sine).astype(BF16))
        queries = query_ref[rows, :, :].astype(F32)
        for g in range(kv_heads):
            query = queries[:, per_group * g : per_group * (g + 1), :].reshape(pairs, head_size)
            scores = lax.dot_general(
                keys[g], query.astype(BF16), (((1,), (1,)), ((), ())), preferred_element_type=F32
            )
            scores = scores + bias_ref[rows, :]
            top_cached = pick_half(cached_refs[1::2], step, group, b, 8, 2 * g, 1)
            sum_cached = pick_half(cached_refs[1::2], step, group, b, 8, 2 * g + 1, 1)
            top = jnp.maximum(jnp.max(scores, 0, keepdims=True), top_cached)
            exponent = jnp.exp2((scores - top) * score_scale)
            shift = jnp.exp2((top_cached - top) * score_scale)
            inverse = 1.0 / (jnp.sum(exponent, 0, keepdims=True) + shift * sum_cached)
            weights = (exponent * inverse).astype(BF16)
            output = lax.dot_general(
                weights, values[g], (((0,), (0,)), ((), ())), preferred_element_type=F32
            )
            factor = jnp.broadcast_to(shift * inverse, (8, pairs)).T[:, :1]
            old = pick_half(cached_refs[0::2], step, group, b, kv_heads * pairs, pairs * g, pairs)
            outputs.append((output + old * factor).reshape(tree_size, per_group, head_size))
        attention_ref[rows, :, :] = jnp.concatenate(outputs, 1).astype(BF16)
        cache_ref[cache_rows * b : cache_rows * (b + 1), :] = jnp.dot(
            sort_new, jnp.concatenate(keys + values, 0), preferred_element_type=F32
        ).astype(BF16)


def pick_half(refs, step, group, b, stride, start, size):
    at = stride * b + start
    rows = refs[0][at : at + size, :]
    if len(refs) == 2:
        rows = jnp.where(2 * step >= pl.num_programs(0), refs[1][at : at + size, :], rows)
    return rows


def finish(where, shared, cached, shrunk, pieces):
    gain, here, there, table, bias, queries = shared
    rows, heads, head_size = queries.shape
    requests = where[2].shape[0]
    tree_size = rows // requests
    columns = here.shape[1]
    kv_heads = columns // (2 * head_size)
    rank_size = pieces[0].shape[0]
    group = 2
    steps = requests // group
    split = len(cached)
    part = steps // split
    row_block = lambda width: pl.BlockSpec((group * tree_size, width), lambda i, *refs: (i, 0))
    whole = lambda shape: pl.BlockSpec(shape, lambda i, *refs: (0,) * len(shape))
    query_block = pl.BlockSpec((group * tree_size, heads, head_size), lambda i, *refs: (i, 0, 0))
    in_specs = [
        row_block(columns),
        row_block(columns),
        row_block(table.shape[1]),
        row_block(bias.shape[1]),
        query_block,
        whole(gain.shape),
    ]
    operands = [*where, here, there, table, bias, queries, gain]
    for k, pair in enumerate(cached):
        for array in pair:
            block = (group * (array.shape[0] * split // requests), array.shape[1])
            in_specs.append(
                pl.BlockSpec(
                    block, lambda i, *refs, k=k: (jnp.clip(i - k * part, 0, part - 1), 0)
                )
            )
            operands.append(array)
    for pair in shrunk:
        for array in pair:
            in_specs.append(whole(array.shape))
            operands.append(array)
    in_specs += [whole((rank_size, columns))] * len(pieces)
    operands += pieces
    cache_rows = 2 * kv_heads * tree_size
    return pl.pallas_call(
        functools.partial(
            finish_kernel, group=group, parts=len(shrunk), split=split, kv_heads=kv_heads
        ),
        grid_spec=pltpu.PrefetchScalarGridSpec(
            num_scalar_prefetch=3,
            grid=(steps,),
            in_specs=in_specs,
            out_specs=[
                query_block,
                pl.BlockSpec((group * cache_rows, head_size), lambda i, *refs: (i, 0)),
            ],
            scratch_shapes=[
                pltpu.VMEM((len(pieces), rank_size, columns), BF16),
                pltpu.VMEM((len(pieces), tree_size, rank_size), F32),
            ],
        ),
        out_shape=[
            jax.ShapeDtypeStruct((rows, heads, head_size), BF16),
            jax.ShapeDtypeStruct((rows * 2 * kv_heads, head_size), BF16),
        ],
        compiler_params=pltpu.CompilerParams(vmem_limit_bytes=32 * 1024 * 1024),
        cost_estimate=pl.CostEstimate(
            flops=4_000_000_000, bytes_accessed=12_000_000, transcendentals=0
        ),
        name="finish",
    )(*operands)


def per_device(
    hidden_states,
    kv_weight,
    shrink_factors,
    expand_factors,
    adapter_ids,
    cache_lengths,
    tree_parents,
    queries,
    cache_keys,
    cache_values,
    key_gain,
):
    requests, tree_size = tree_parents.shape
    row_count, half_width = hidden_states.shape
    kv_heads, kv_width = (kv_weight.shape[1], kv_weight.shape[2])
    head_size = kv_width // 2
    rank_size = shrink_factors.shape[2]
    context = cache_keys.shape[1]
    pool_count = lax.axis_size("pool")
    heads_here = kv_heads // lax.axis_size("tp")
    columns = heads_here * kv_width
    me = lax.axis_index("pool")
    core = lax.axis_index("tp").astype(jnp.int32).reshape(1)
    swap = [(0, 1), (1, 0)]

    def tile_rows(array):
        lead, heads = array.shape[0], array.shape[1]
        return array.reshape(lead, heads, 2, 128).transpose(0, 2, 1, 3).reshape(-1, 128)

    cut = (half_width + columns) // 2 - columns
    first, second = pack(
        core, shrink_factors[0].T, tile_rows(expand_factors[0]), cut, heads_here
    )

    order = ring_order(pool_count)
    onward = [(order[i], order[(i + 1) % pool_count]) for i in range(pool_count)]
    backward = [(b, a) for a, b in onward]
    half = pool_count // 2
    offsets = [[0]] + [[-step, step] for step in range(1, half)] + [[half]]
    flat_offsets = sum(offsets, [])
    owners = np.zeros((pool_count, pool_count), np.int32)
    for spot, index in enumerate(order):
        owners[index] = [order[(spot + offset) % pool_count] for offset in flat_offsets]
    where = (me.astype(jnp.int32).reshape(1), jnp.asarray(owners), adapter_ids)

    weight_rows = tile_rows(kv_weight)
    key_rows = cache_keys.reshape(-1, head_size)
    value_rows = cache_values.reshape(-1, head_size)
    halves = requests // 2

    arrivals = [(first, second)]
    front = rear = (first, second)
    cached = [None, None]
    table, bias = tree_tables(
        cache_lengths, tree_parents, head_size, queries.shape[1] // heads_here, [first]
    )
    for step in range(1, half):
        front = tuple(lax.ppermute(piece, "pool", onward) for piece in front)
        rear = tuple(lax.ppermute(piece, "pool", backward) for piece in rear)
        held = [front[1], rear[1]]
        if step == 1:
            here, away, *held = base_product(
                core, hidden_states, weight_rows, kv_heads * kv_width, held
            )
        if step == 2:
            *cached[0], front_piece, rear_piece = cache_attention(
                cache_lengths, queries, key_rows, value_rows, heads_here, 0, halves, held, []
            )
            held = [front_piece, rear_piece]
        front, rear = (front[0], held[0]), (rear[0], held[1])
        arrivals += [front, rear]
    arrivals.append(
        (lax.ppermute(front[0], "pool", onward), lax.ppermute(rear[1], "pool", backward))
    )
    there = lax.ppermute(away, "tp", swap)
    cached[1] = cache_attention(
        cache_lengths,
        queries,
        key_rows,
        value_rows,
        heads_here,
        halves,
        requests - halves,
        [],
        [arrivals[5][0]],
    )

    shrunk = []
    slot = 0
    for group in (arrivals[:-3], arrivals[-3:]):
        partial = shrink_rows(where, slot, hidden_states, group, tree_size, columns, cut, [])
        shrunk.append((partial, lax.ppermute(partial, "tp", swap)))
        slot += len(group)
    shared = (key_gain.reshape(1, head_size), here, there, table, bias, queries)
    attention, cache_rows = finish(where, shared, cached, shrunk, [piece[0] for piece in arrivals])
    tree_cache = (
        cache_rows.reshape(row_count, 2, heads_here, head_size)
        .transpose(0, 2, 1, 3)
        .reshape(row_count, heads_here, kv_width)
    )
    return attention, tree_cache


def solution(mesh):
    placed = (
        P(("grp", "pool"), "tp"),
        P("tp", None, None),
        P(("grp", "pool"), "tp", None),
        P(("grp", "pool"), None, None, None),
        P(("grp", "pool")),
        P(("grp", "pool")),
        P(("grp", "pool"), None),
        P(("grp", "pool"), "tp", None),
        P(("grp", "pool"), None, "tp", None),
        P(("grp", "pool"), None, "tp", None),
        P(),
    )
    return jax.shard_map(
        per_device,
        mesh=mesh,
        in_specs=placed,
        out_specs=(P(("grp", "pool"), "tp", None), P(("grp", "pool"), "tp", None)),
        check_vma=False,
    )
```

time: 72.9 us -> 70.9 us (0.973)
  local copies, waits for them, and re-layouts: 8.05 us -> 4.39 us
  waiting for transfers between devices: 11.5 us -> 14.4 us
  Pallas kernels: 35.1 us -> 33.8 us
  starting transfers between devices: 16 us -> 17.1 us
  other arithmetic: 0.78 us -> 0 us
    ppermute x6, starting transfers between devices: 2.93 us -> 11.5 us  [per_device(): front = tuple((lax.ppermute(piece, 'pool', onward) for piece in front))]
    ppermute x6, starting transfers between devices: 10.4 us -> 1.99 us  [per_device(): rear = tuple((lax.ppermute(piece, 'pool', backward) for piece in rear))]
    ppermute x6, waiting for transfers between devices: 0.02 us -> 6.41 us  [per_device(): rear = tuple((lax.ppermute(piece, 'pool', backward) for piece in rear))]
    ppermute x6, waiting for transfers between devices: 11.5 us -> 7.94 us  [per_device(): front = tuple((lax.ppermute(piece, 'pool', onward) for piece in front))]
    pallas_call x3 -> x2, Pallas kernels: 7.22 us -> 4.4 us  [shrink_rows(): pl.pallas_call(functools.partial(shrink_kernel, columns=columns, cut=cut)...]
    unnamed x32 -> x50, local copies, waits for them, and re-layouts: 6.63 us -> 4.39 us
    ppermute x1, starting transfers between devices: 0.14 us -> 2.01 us  [per_device(): lax.ppermute(front[0], 'pool', onward)]
    pallas_call x5, Pallas kernels: 26.1 us -> 27.5 us  [the longest x1 10.7 us: finish(): pl.pallas_call(functools.partial(finish_kernel, group=group, parts=len(sh...]
  transfers between devices with their start and end apart: 18 -> 17, of which waited for: 3 -> 5; matrix products, arithmetic and copies ran while one was open for 3% -> 0% of each run, Pallas kernels for 42% -> 30%
where the time goes in v3:
time: 70.9 us; the launch traced here: 70.6 us
  Pallas kernels  33.8 us (48%)
  starting transfers between devices  17.1 us (24%)
  waiting for transfers between devices  14.4 us (20%)
  local copies, waits for them, and re-layouts  4.39 us (6%)
  between operations  0.95 us (1%)
    ppermute x6, starting transfers between devices, per_device(): front = tuple((lax.ppermute(piece, 'pool', onward) for piece in front))  11.5 us
    pallas_call x1, Pallas kernels, finish(): pl.pallas_call(functools.partial(finish_kernel, group=group, parts=len(sh...  10.7 us
    ppermute x6, waiting for transfers between devices, per_device(): front = tuple((lax.ppermute(piece, 'pool', onward) for piece in front))  7.94 us
    pallas_call x1, Pallas kernels, base_product(): pl.pallas_call(functools.partial(base_kernel, held_count=len(held)), grid...  6.83 us
    ppermute x6, waiting for transfers between devices, per_device(): rear = tuple((lax.ppermute(piece, 'pool', backward) for piece in rear))  6.41 us
    pallas_call x2, Pallas kernels, cache_attention(): pl.pallas_call(functools.partial(cache_kernel, first_request=first_reques...  5.92 us
    pallas_call x2, Pallas kernels, shrink_rows(): pl.pallas_call(functools.partial(shrink_kernel, columns=columns, cut=cut)...  4.4 us
    unnamed x50, local copies, waits for them, and re-layouts  4.39 us
  transfers between devices with their start and end apart: 17, of which 5 were waited for; matrix products, arithmetic and copies ran while one was open for 0% of the time, Pallas kernels for 30%

profile of v3, /device:TPU:0, one launch (start us, length us, event | category | flops | bytes accessed | tf_op | source)
XLA Modules:
  0.0 70.6 jit_solution(4396996847013480721)
XLA Ops:
  0.6 1.9 %pack.1 = (bf16[64,1536]{1,0:T(8,128)(2,1)}, bf16[64,1536]{1,0:T(8,128)(2,1)}) custom-call(s32[1]{0:T(128)} %bitcast.1.core_ref, bf16[64,2560]{1,0:T(8,128)(2,1)} %bitcast.28, bf16[512,128]{1,0:T(8,128)(2,1)} %bitcast.29), custom_call_target="tpu_custom_call" | custom-call | tf_op jit(solution)/shard_map/pack/pallas_call | solution.py:82
  2.5 3.0 %collective-permute-start.5 = (bf16[64,1536]{1,0:T(8,128)(2,1)}, bf16[64,1536]{1,0:T(8,128)(2,1)S(1)}, u32[]{:S(2)}, u32[]{:S(2)}) collective-permute-start(bf16[64,1536]{1,0:T(8,128)(2,1)} %get-tuple-element.21.rest_0_.refs_1_.rest_8_), channel_id=1, source_target_pairs={{0,4},{4,8},{8,12},{12,14},{14,10},{10,6},{6,2},{2,0},{1,5},{5,9},... | collective-permute-start | bytes 589832 | tf_op jit(solution)/shard_map/ppermute | solution.py:578
  5.5 2.0 %collective-permute-start = (bf16[64,1536]{1,0:T(8,128)(2,1)}, bf16[64,1536]{1,0:T(8,128)(2,1)S(1)}, u32[]{:S(2)}, u32[]{:S(2)}) collective-permute-start(bf16[64,1536]{1,0:T(8,128)(2,1)} %get-tuple-element.18.refs_2_), channel_id=1, source_target_pairs={{0,4},{4,8},{8,12},{12,14},{14,10},{10,6},{6,2},{2,0},{1,5},{5,9},... | collective-permute-start | bytes 589832 | tf_op jit(solution)/shard_map/ppermute | solution.py:578
  7.5 3.9 %collective-permute-done.5.refs_4_.rest_9_ = bf16[64,1536]{1,0:T(8,128)(2,1)S(1)} collective-permute-done((bf16[64,1536]{1,0:T(8,128)(2,1)}, bf16[64,1536]{1,0:T(8,128)(2,1)S(1)}, u32[]{:S(2)}, u32[]{:S(2)}) %collective-permute-start.5) | collective-permute-done | bytes 196640 | tf_op jit(solution)/shard_map/ppermute | solution.py:578
  11.4 2.1 %collective-permute-start.6 = (bf16[64,1536]{1,0:T(8,128)(2,1)S(1)}, bf16[64,1536]{1,0:T(8,128)(2,1)S(1)}, u32[]{:S(2)}, u32[]{:S(2)}) collective-permute-start(bf16[64,1536]{1,0:T(8,128)(2,1)S(1)} %collective-permute-done.5.refs_4_.rest_9_), channel_id=1, source_target_pairs={{0,4},{4,8},{8,12},{12,14},{14,10},{10,6},{6,2},{2,0},{1,5},{5,9},... | collective-permute-start | bytes 589832 | tf_op jit(solution)/shard_map/ppermute | solution.py:578
  13.5 0.0 collective-permute-done.1.rest_1_
  13.6 2.1 %collective-permute-done.rest_0_ = bf16[64,1536]{1,0:T(8,128)(2,1)S(1)} collective-permute-done((bf16[64,1536]{1,0:T(8,128)(2,1)}, bf16[64,1536]{1,0:T(8,128)(2,1)S(1)}, u32[]{:S(2)}, u32[]{:S(2)}) %collective-permute-start) | collective-permute-done | bytes 196640 | tf_op jit(solution)/shard_map/ppermute | solution.py:578
  15.6 0.7 copy-done.5
  16.3 6.8 %base.1 = (f32[384,512]{1,0:T(8,128)}, f32[384,512]{1,0:T(8,128)}, bf16[64,1536]{1,0:T(8,128)(2,1)}, bf16[64,1536]{1,0:T(8,128)(2,1)}) custom-call(s32[1]{0:T(128)} %bitcast.1.core_ref, bf16[384,2560]{1,0:T(8,128)(2,1)} %refs_6_.3, bf16[20480,128]{1,0:T(8,128)(2,1)} %bitcast.30, ...), custom_call_target="tpu_custom_call", output_to_operand_aliasing={{2}: (3, {}), {3}: (4, {})} | custom-call | flops 4000000000 | bytes 9000000 | tf_op jit(solution)/shard_map/base/pallas_call | solution.py:150
  23.1 2.1 %collective-permute-start.3 = (bf16[64,1536]{1,0:T(8,128)(2,1)}, bf16[64,1536]{1,0:T(8,128)(2,1)}, u32[]{:S(2)}, u32[]{:S(2)}) collective-permute-start(bf16[64,1536]{1,0:T(8,128)(2,1)} %get-tuple-element.24.refs_5_), channel_id=1, source_target_pairs={{0,4},{4,8},{8,12},{12,14},{14,10},{10,6},{6,2},{2,0},{1,5},{5,9},... | collective-permute-start | bytes 589832 | tf_op jit(solution)/shard_map/ppermute | solution.py:578
  25.3 2.0 %collective-permute-start.9 = (bf16[64,1536]{1,0:T(8,128)(2,1)S(1)}, bf16[64,1536]{1,0:T(8,128)(2,1)S(1)}, u32[]{:S(2)}, u32[]{:S(2)}) collective-permute-start(bf16[64,1536]{1,0:T(8,128)(2,1)S(1)} %collective-permute-done.8.refs_7_.rest_10_), channel_id=1, source_target_pairs={{4,0},{8,4},{12,8},{14,12},{10,14},{6,10},{2,6},{0,2},{5,1},{9,5},... | collective-permute-start | bytes 589832 | tf_op jit(solution)/shard_map/ppermute | solution.py:579
  27.2 0.1 collective-permute-start.7
  27.4 2.0 %collective-permute-done.3.rest_0_ = bf16[64,1536]{1,0:T(8,128)(2,1)} collective-permute-done((bf16[64,1536]{1,0:T(8,128)(2,1)}, bf16[64,1536]{1,0:T(8,128)(2,1)}, u32[]{:S(2)}, u32[]{:S(2)}) %collective-permute-start.3) | collective-permute-done | bytes 196640 | tf_op jit(solution)/shard_map/ppermute | solution.py:578
  29.4 3.6 %collective-permute-done.4.rest_1_ = bf16[64,1536]{1,0:T(8,128)(2,1)} collective-permute-done((bf16[64,1536]{1,0:T(8,128)(2,1)}, bf16[64,1536]{1,0:T(8,128)(2,1)}, u32[]{:S(2)}, u32[]{:S(2)}) %collective-permute-start.4) | collective-permute-done | bytes 196640 | tf_op jit(solution)/shard_map/ppermute | solution.py:579
  33.0 3.0 %cached.2 = (f32[3072,128]{1,0:T(8,128)S(1)}, f32[32,384]{1,0:T(8,128)S(1)}, bf16[64,1536]{1,0:T(8,128)(2,1)}, bf16[64,1536]{1,0:T(8,128)(2,1)}) custom-call(s32[8]{0:T(128)S(1)} %copy-done.15, bf16[384,16,128]{2,1,0:T(8,128)(2,1)S(1)} %copy-done.9, bf16[2048,128]{1,0:T(8,128)(2,1)S(1)} %bitcast.23, ...), custom_call_target="tpu_custom_call", output_to_operand_aliasing={{2}: (4, {}), {3}: (5, {})} | custom-call | flops 2800000000 | bytes 8000000 | tf_op jit(solution)/shard_map/cached/pallas_call | solution.py:279
  36.0 1.1 %copy-done.18 = f32[3072,128]{1,0:T(8,128)} copy-done((f32[3072,128]{1,0:T(8,128)}, f32[3072,128]{1,0:T(8,128)S(1)}, u32[]{:S(2)}) %copy-start.18) | copy-done | bytes 1572888
  37.1 0.6 copy-done.23
  37.8 2.1 %collective-permute-start.11 = (bf16[64,1536]{1,0:T(8,128)(2,1)}, bf16[64,1536]{1,0:T(8,128)(2,1)}, u32[]{:S(2)}, u32[]{:S(2)}) collective-permute-start(bf16[64,1536]{1,0:T(8,128)(2,1)} %get-tuple-element.30.refs_11_), channel_id=1, source_target_pairs={{0,4},{4,8},{8,12},{12,14},{14,10},{10,6},{6,2},{2,0},{1,5},{5,9},... | collective-permute-start | bytes 589832 | tf_op jit(solution)/shard_map/ppermute | solution.py:578
  39.8 0.0 collective-permute-start.12
  39.8 2.0 %collective-permute-start.14 = (bf16[64,1536]{1,0:T(8,128)(2,1)S(1)}, bf16[64,1536]{1,0:T(8,128)(2,1)}, u32[]{:S(2)}, u32[]{:S(2)}) collective-permute-start(bf16[64,1536]{1,0:T(8,128)(2,1)S(1)} %collective-permute-done.7.rest_0_.refs_1_.rest_13_), channel_id=1, source_target_pairs={{0,4},{4,8},{8,12},{12,14},{14,10},{10,6},{6,2},{2,0},{1,5},{5,9},... | collective-permute-start | bytes 589832 | tf_op jit(solution)/shard_map/ppermute | solution.py:593
  41.9 2.8 %collective-permute-done.13.refs_5_ = bf16[64,1536]{1,0:T(8,128)(2,1)} collective-permute-done((bf16[64,1536]{1,0:T(8,128)(2,1)}, bf16[64,1536]{1,0:T(8,128)(2,1)}, u32[]{:S(2)}, u32[]{:S(2)}) %collective-permute-start.13) | collective-permute-done | bytes 196640 | tf_op jit(solution)/shard_map/ppermute | solution.py:579
  44.6 1.0 %collective-permute-start.15 = (bf16[64,1536]{1,0:T(8,128)(2,1)}, bf16[64,1536]{1,0:T(8,128)(2,1)}, u32[]{:S(2)}, u32[]{:S(2)}) collective-permute-start(bf16[64,1536]{1,0:T(8,128)(2,1)} %collective-permute-done.13.refs_5_), channel_id=1, source_target_pairs={{4,0},{8,4},{12,8},{14,12},{10,14},{6,10},{2,6},{0,2},{5,1},{9,5},... | collective-permute-start | bytes 589832 | tf_op jit(solution)/shard_map/ppermute | solution.py:593
  45.7 4.1 %tree.1 = (f32[384,256]{1,0:T(8,128)}, f32[384,384]{1,0:T(8,128)}) custom-call(s32[8]{0:T(128)} %length_ref.5, s32[8,48]{1,0:T(8,128)} %parent_ref.1, f32[1,128]{1,0:T(1,128)} %constant.13.clone.frequency_ref, bf16[64,1536]{1,0:T(8,128)(2,1)} %get-tuple-element.21.rest_0_.refs_1_.rest_8_), custom_call_target="tpu_custom_call" | custom-call | flops 1000000000 | bytes 8000000 | tf_op jit(solution)/shard_map/tree/pallas_call | solution.py:218
  49.8 0.9 %copy-done.4 = bf16[64,1536]{1,0:T(8,128)(2,1)S(1)} copy-done((bf16[64,1536]{1,0:T(8,128)(2,1)S(1)}, bf16[64,1536]{1,0:T(8,128)(2,1)}, u32[]{:S(2)}) %copy-start.4) | copy-done | bytes 196632
  50.7 0.9 %copy-done.6 = bf16[64,1536]{1,0:T(8,128)(2,1)S(1)} copy-done((bf16[64,1536]{1,0:T(8,128)(2,1)S(1)}, bf16[64,1536]{1,0:T(8,128)(2,1)}, u32[]{:S(2)}) %copy-start.6) | copy-done | bytes 196632
  51.6 2.2 %shrink.2.rest_4_ = f32[5,48,64]{2,1,0:T(8,128)S(1)} custom-call(s32[1]{0:T(128)} %bitcast.me_ref, s32[8,8]{1,0:T(8,128)S(1)} %copy-done.7, s32[8]{0:T(128)S(1)} %copy-done.8, bf16[384,2560]{1,0:T(8,128)(2,1)S(1)} %copy-done, bf16[64,1536]{1,0:T(8,128)(2,1)S(1)} %copy-done.1, bf16[64,1536]{1,0:T(8,128)(2,1)S(1)} %copy-done.2, bf16[384,2560]{1,0:T(8,128)(2,1)S(1)} %copy-done, ...), custom_call_target="tpu_custom_call" | custom-call | flops 1500000000 | bytes 10000000 | tf_op jit(solution)/shard_map/shrink/pallas_call | solution.py:336
  53.8 0.0 copy-start.10
  53.8 0.1 collective-permute-start.10
  54.0 2.2 %shrink.3.rest_6_ = f32[3,48,64]{2,1,0:T(8,128)S(1)} custom-call(s32[1]{0:T(128)} %bitcast.me_ref, s32[8,8]{1,0:T(8,128)S(1)} %copy-done.7, s32[8]{0:T(128)S(1)} %copy-done.8, bf16[384,2560]{1,0:T(8,128)(2,1)S(1)} %copy-done, bf16[64,1536]{1,0:T(8,128)(2,1)S(1)} %collective-permute-done.7.rest_0_.refs_1_.rest_13_, ...), custom_call_target="tpu_custom_call" | custom-call | flops 900000000 | bytes 6000000 | tf_op jit(solution)/shard_map/shrink/pallas_call | solution.py:336
  56.3 0.5 collective-permute-start.16
  56.8 3.0 %cached.3 = (f32[3072,128]{1,0:T(8,128)S(1)}, f32[32,384]{1,0:T(8,128)S(1)}) custom-call(s32[8]{0:T(128)S(1)} %copy-done.16, bf16[384,16,128]{2,1,0:T(8,128)(2,1)S(1)} %copy-done.10, bf16[2048,128]{1,0:T(8,128)(2,1)S(1)} %bitcast.24, bf16[2048,128]{1,0:T(8,128)(2,1)S(1)} %bitcast.26, bf16[64,1536]{1,0:T(8,128)(2,1)S(1)} %collective-permute-done.7.rest_0_.refs_1_.rest_13_), custom_call_target="tpu_custom_call" | custom-call | flops 2800000000 | bytes 8000000 | tf_op jit(solution)/shard_map/cached/pallas_call | solution.py:279
  59.8 10.7 %finish.1 = (bf16[384,16,128]{2,1,0:T(8,128)(2,1)}, bf16[1536,128]{1,0:T(8,128)(2,1)}) custom-call(s32[1]{0:T(128)} %bitcast.me_ref, s32[8,8]{1,0:T(8,128)S(1)} %copy-done.7, s32[8]{0:T(128)S(1)} %copy-done.8, f32[384,512]{1,0:T(8,128)S(1)} %copy-done.22, f32[384,512]{1,0:T(8,128)} %collective-permute-done.2.there_ref, f32[384,256]{1,0:T(8,128)S(1)} %copy-done.21, ...), custom_call_target="tpu_custom_call" | custom-call | flops 4000000000 | bytes 12000000 | tf_op jit(solution)/shard_map/finish/pallas_call | solution.py:491
  (60 shorter events, 0.1 us)
Async XLA Ops:
  2.5 8.9 %collective-permute-start.5 = (bf16[64,1536]{1,0:T(8,128)(2,1)}, bf16[64,1536]{1,0:T(8,128)(2,1)S(1)}, u32[]{:S(2)}, u32[]{:S(2)}) collective-permute-start(bf16[64,1536]{1,0:T(8,128)(2,1)} %get-tuple-element.21.rest_0_.refs_1_.rest_8_), channel_id=1, source_target_pairs={{0,4},{4,8},{8,12},{12,14},{14,10},{10,6},{6,2},{2,0},{1,5},{5,9},... | collective-permute-start | bytes 589832 | tf_op jit(solution)/shard_map/ppermute | solution.py:578
  5.5 8.0 %collective-permute-start.1 = (bf16[64,1536]{1,0:T(8,128)(2,1)}, bf16[64,1536]{1,0:T(8,128)(2,1)S(1)}, u32[]{:S(2)}, u32[]{:S(2)}) collective-permute-start(bf16[64,1536]{1,0:T(8,128)(2,1)} %get-tuple-element.18.refs_2_), channel_id=1, source_target_pairs={{4,0},{8,4},{12,8},{14,12},{10,14},{6,10},{2,6},{0,2},{5,1},{9,5},... | collective-permute-start | bytes 589832 | tf_op jit(solution)/shard_map/ppermute | solution.py:579
  5.5 10.1 %collective-permute-start = (bf16[64,1536]{1,0:T(8,128)(2,1)}, bf16[64,1536]{1,0:T(8,128)(2,1)S(1)}, u32[]{:S(2)}, u32[]{:S(2)}) collective-permute-start(bf16[64,1536]{1,0:T(8,128)(2,1)} %get-tuple-element.18.refs_2_), channel_id=1, source_target_pairs={{0,4},{4,8},{8,12},{12,14},{14,10},{10,6},{6,2},{2,0},{1,5},{5,9},... | collective-permute-start | bytes 589832 | tf_op jit(solution)/shard_map/ppermute | solution.py:578
  7.5 17.7 %collective-permute-start.8 = (bf16[64,1536]{1,0:T(8,128)(2,1)}, bf16[64,1536]{1,0:T(8,128)(2,1)S(1)}, u32[]{:S(2)}, u32[]{:S(2)}) collective-permute-start(bf16[64,1536]{1,0:T(8,128)(2,1)} %get-tuple-element.21.rest_0_.refs_1_.rest_8_), channel_id=1, source_target_pairs={{4,0},{8,4},{12,8},{14,12},{10,14},{6,10},{2,6},{0,2},{5,1},{9,5},... | collective-permute-start | bytes 589832 | tf_op jit(solution)/shard_map/ppermute | solution.py:579
  11.4 15.8 %collective-permute-start.6 = (bf16[64,1536]{1,0:T(8,128)(2,1)S(1)}, bf16[64,1536]{1,0:T(8,128)(2,1)S(1)}, u32[]{:S(2)}, u32[]{:S(2)}) collective-permute-start(bf16[64,1536]{1,0:T(8,128)(2,1)S(1)} %collective-permute-done.5.refs_4_.rest_9_), channel_id=1, source_target_pairs={{0,4},{4,8},{8,12},{12,14},{14,10},{10,6},{6,2},{2,0},{1,5},{5,9},... | collective-permute-start | bytes 589832 | tf_op jit(solution)/shard_map/ppermute | solution.py:578
  16.3 16.7 %copy-start.9 = (bf16[384,16,128]{2,1,0:T(8,128)(2,1)S(1)}, bf16[384,16,128]{2,1,0:T(8,128)(2,1)}, u32[]{:S(2)}) copy-start(bf16[384,16,128]{2,1,0:T(8,128)(2,1)} %query_ref.5) | copy-start | bytes 4718596
  16.3 16.7 %copy-start.11 = (bf16[8,128,2,128]{3,2,1,0:T(2,128)(2,1)S(1)}, bf16[8,128,2,128]{3,2,1,0:T(2,128)(2,1)}, u32[]{:S(2)}) copy-start(bf16[8,128,2,128]{3,2,1,0:T(2,128)(2,1)} %param.21) | copy-start | bytes 1572868
  16.3 16.7 %copy-start.13 = (bf16[8,128,2,128]{3,2,1,0:T(2,128)(2,1)S(1)}, bf16[8,128,2,128]{3,2,1,0:T(2,128)(2,1)}, u32[]{:S(2)}) copy-start(bf16[8,128,2,128]{3,2,1,0:T(2,128)(2,1)} %param.22) | copy-start | bytes 1572868
  16.3 16.7 %copy-start.15 = (s32[8]{0:T(128)S(1)}, s32[8]{0:T(128)}, u32[]{:S(2)}) copy-start(s32[8]{0:T(128)} %length_ref.5) | copy-start | bytes 100
  23.1 6.2 %collective-permute-start.3 = (bf16[64,1536]{1,0:T(8,128)(2,1)}, bf16[64,1536]{1,0:T(8,128)(2,1)}, u32[]{:S(2)}, u32[]{:S(2)}) collective-permute-start(bf16[64,1536]{1,0:T(8,128)(2,1)} %get-tuple-element.24.refs_5_), channel_id=1, source_target_pairs={{0,4},{4,8},{8,12},{12,14},{14,10},{10,6},{6,2},{2,0},{1,5},{5,9},... | collective-permute-start | bytes 589832 | tf_op jit(solution)/shard_map/ppermute | solution.py:578
  25.3 7.7 %collective-permute-start.4 = (bf16[64,1536]{1,0:T(8,128)(2,1)}, bf16[64,1536]{1,0:T(8,128)(2,1)}, u32[]{:S(2)}, u32[]{:S(2)}) collective-permute-start(bf16[64,1536]{1,0:T(8,128)(2,1)} %get-tuple-element.25.refs_8_), channel_id=1, source_target_pairs={{4,0},{8,4},{12,8},{14,12},{10,14},{6,10},{2,6},{0,2},{5,1},{9,5},... | collective-permute-start | bytes 589832 | tf_op jit(solution)/shard_map/ppermute | solution.py:579
  25.3 34.5 %collective-permute-start.2 = (f32[384,512]{1,0:T(8,128)}, f32[384,512]{1,0:T(8,128)}, u32[]{:S(2)}, u32[]{:S(2)}) collective-permute-start(f32[384,512]{1,0:T(8,128)} %get-tuple-element.20), channel_id=1, source_target_pairs={{0,1},{1,0},{2,3},{3,2},{4,5},{5,4},{6,7},{7,6},{8,9},{9,8},{10,11... | collective-permute-start | bytes 2359304 | tf_op jit(solution)/shard_map/ppermute | solution.py:595
  25.3 14.6 %collective-permute-start.9 = (bf16[64,1536]{1,0:T(8,128)(2,1)S(1)}, bf16[64,1536]{1,0:T(8,128)(2,1)S(1)}, u32[]{:S(2)}, u32[]{:S(2)}) collective-permute-start(bf16[64,1536]{1,0:T(8,128)(2,1)S(1)} %collective-permute-done.8.refs_7_.rest_10_), channel_id=1, source_target_pairs={{4,0},{8,4},{12,8},{14,12},{10,14},{6,10},{2,6},{0,2},{5,1},{9,5},... | collective-permute-start | bytes 589832 | tf_op jit(solution)/shard_map/ppermute | solution.py:579
  27.2 12.6 %collective-permute-start.7 = (bf16[64,1536]{1,0:T(8,128)(2,1)S(1)}, bf16[64,1536]{1,0:T(8,128)(2,1)S(1)}, u32[]{:S(2)}, u32[]{:S(2)}) collective-permute-start(bf16[64,1536]{1,0:T(8,128)(2,1)S(1)} %collective-permute-done.6.refs_10_.rest_11_), channel_id=1, source_target_pairs={{0,4},{4,8},{8,12},{12,14},{14,10},{10,6},{6,2},{2,0},{1,5},{5,9},... | collective-permute-start | bytes 589832 | tf_op jit(solution)/shard_map/ppermute | solution.py:578
  37.7 6.9 %collective-permute-start.13 = (bf16[64,1536]{1,0:T(8,128)(2,1)}, bf16[64,1536]{1,0:T(8,128)(2,1)}, u32[]{:S(2)}, u32[]{:S(2)}) collective-permute-start(bf16[64,1536]{1,0:T(8,128)(2,1)} %get-tuple-element.31.refs_14_), channel_id=1, source_target_pairs={{4,0},{8,4},{12,8},{14,12},{10,14},{6,10},{2,6},{0,2},{5,1},{9,5},... | collective-permute-start | bytes 589832 | tf_op jit(solution)/shard_map/ppermute | solution.py:579
  37.7 12.0 %copy-start = (bf16[384,2560]{1,0:T(8,128)(2,1)S(1)}, bf16[384,2560]{1,0:T(8,128)(2,1)}, u32[]{:S(2)}) copy-start(bf16[384,2560]{1,0:T(8,128)(2,1)} %refs_6_.3) | copy-start | bytes 5898244
  37.7 12.0 %copy-start.1 = (bf16[64,1536]{1,0:T(8,128)(2,1)S(1)}, bf16[64,1536]{1,0:T(8,128)(2,1)}, u32[]{:S(2)}) copy-start(bf16[64,1536]{1,0:T(8,128)(2,1)} %get-tuple-element.21.rest_0_.refs_1_.rest_8_) | copy-start | bytes 589828
  37.7 12.0 %copy-start.2 = (bf16[64,1536]{1,0:T(8,128)(2,1)S(1)}, bf16[64,1536]{1,0:T(8,128)(2,1)}, u32[]{:S(2)}) copy-start(bf16[64,1536]{1,0:T(8,128)(2,1)} %get-tuple-element.18.refs_2_) | copy-start | bytes 589828
  37.7 12.0 %copy-start.7 = (s32[8,8]{1,0:T(8,128)S(1)}, s32[8,8]{1,0:T(8,128)}, u32[]{:S(2)}) copy-start(s32[8,8]{1,0:T(8,128)} %constant.12.clone.owner_ref) | copy-start | bytes 772
  37.7 12.0 %copy-start.8 = (s32[8]{0:T(128)S(1)}, s32[8]{0:T(128)}, u32[]{:S(2)}) copy-start(s32[8]{0:T(128)} %adapter_ref.5) | copy-start | bytes 100
  37.8 16.2 %collective-permute-start.11 = (bf16[64,1536]{1,0:T(8,128)(2,1)}, bf16[64,1536]{1,0:T(8,128)(2,1)}, u32[]{:S(2)}, u32[]{:S(2)}) collective-permute-start(bf16[64,1536]{1,0:T(8,128)(2,1)} %get-tuple-element.30.refs_11_), channel_id=1, source_target_pairs={{0,4},{4,8},{8,12},{12,14},{14,10},{10,6},{6,2},{2,0},{1,5},{5,9},... | collective-permute-start | bytes 589832 | tf_op jit(solution)/shard_map/ppermute | solution.py:578
  39.8 14.0 %collective-permute-start.12 = (bf16[64,1536]{1,0:T(8,128)(2,1)S(1)}, bf16[64,1536]{1,0:T(8,128)(2,1)S(1)}, u32[]{:S(2)}, u32[]{:S(2)}) collective-permute-start(bf16[64,1536]{1,0:T(8,128)(2,1)S(1)} %collective-permute-done.9.refs_13_.rest_12_), channel_id=1, source_target_pairs={{4,0},{8,4},{12,8},{14,12},{10,14},{6,10},{2,6},{0,2},{5,1},{9,5},... | collective-permute-start | bytes 589832 | tf_op jit(solution)/shard_map/ppermute | solution.py:579
  39.8 14.1 %collective-permute-start.14 = (bf16[64,1536]{1,0:T(8,128)(2,1)S(1)}, bf16[64,1536]{1,0:T(8,128)(2,1)}, u32[]{:S(2)}, u32[]{:S(2)}) collective-permute-start(bf16[64,1536]{1,0:T(8,128)(2,1)S(1)} %collective-permute-done.7.rest_0_.refs_1_.rest_13_), channel_id=1, source_target_pairs={{0,4},{4,8},{8,12},{12,14},{14,10},{10,6},{6,2},{2,0},{1,5},{5,9},... | collective-permute-start | bytes 589832 | tf_op jit(solution)/shard_map/ppermute | solution.py:593
  44.6 9.3 %collective-permute-start.15 = (bf16[64,1536]{1,0:T(8,128)(2,1)}, bf16[64,1536]{1,0:T(8,128)(2,1)}, u32[]{:S(2)}, u32[]{:S(2)}) collective-permute-start(bf16[64,1536]{1,0:T(8,128)(2,1)} %collective-permute-done.13.refs_5_), channel_id=1, source_target_pairs={{4,0},{8,4},{12,8},{14,12},{10,14},{6,10},{2,6},{0,2},{5,1},{9,5},... | collective-permute-start | bytes 589832 | tf_op jit(solution)/shard_map/ppermute | solution.py:593
  53.8 5.9 %collective-permute-start.10 = (f32[5,48,64]{2,1,0:T(8,128)S(1)}, f32[5,48,64]{2,1,0:T(8,128)S(1)}, u32[]{:S(2)}, u32[]{:S(2)}) collective-permute-start(f32[5,48,64]{2,1,0:T(8,128)S(1)} %shrink.2.rest_4_), channel_id=1, source_target_pairs={{0,1},{1,0},{2,3},{3,2},{4,5},{5,4},{6,7},{7,6},{8,9},{9,8},{10,11... | collective-permute-start | bytes 184328 | tf_op jit(solution)/shard_map/ppermute | solution.py:612
  56.2 3.6 %copy-start.17 = (f32[128]{0:T(128)S(1)}, f32[128]{0:T(128)}, u32[]{:S(2)}) copy-start(f32[128]{0:T(128)} %param.23) | copy-start | bytes 1540
  56.2 3.6 %copy-start.19 = (f32[3072,128]{1,0:T(8,128)S(1)}, f32[3072,128]{1,0:T(8,128)}, u32[]{:S(2)}) copy-start(f32[3072,128]{1,0:T(8,128)} %copy-done.18) | copy-start | bytes 4718596
  56.2 3.6 %copy-start.20 = (f32[384,384]{1,0:T(8,128)S(1)}, f32[384,384]{1,0:T(8,128)}, u32[]{:S(2)}) copy-start(f32[384,384]{1,0:T(8,128)} %get-tuple-element.23.bias_ref) | copy-start | bytes 1769476
  56.2 3.6 %copy-start.21 = (f32[384,256]{1,0:T(8,128)S(1)}, f32[384,256]{1,0:T(8,128)}, u32[]{:S(2)}) copy-start(f32[384,256]{1,0:T(8,128)} %get-tuple-element.22.table_ref) | copy-start | bytes 1179652
  56.2 3.6 %copy-start.22 = (f32[384,512]{1,0:T(8,128)S(1)}, f32[384,512]{1,0:T(8,128)}, u32[]{:S(2)}) copy-start(f32[384,512]{1,0:T(8,128)} %get-tuple-element.19.here_ref) | copy-start | bytes 2359300
  56.3 3.6 %copy-start.24 = (f32[32,384]{1,0:T(8,128)S(1)}, f32[32,384]{1,0:T(8,128)}, u32[]{:S(2)}) copy-start(f32[32,384]{1,0:T(8,128)} %copy-done.23) | copy-start | bytes 147460
  56.3 3.5 %collective-permute-start.16 = (f32[3,48,64]{2,1,0:T(8,128)S(1)}, f32[3,48,64]{2,1,0:T(8,128)S(1)}, u32[]{:S(2)}, u32[]{:S(2)}) collective-permute-start(f32[3,48,64]{2,1,0:T(8,128)S(1)} %shrink.3.rest_6_), channel_id=1, source_target_pairs={{0,1},{1,0},{2,3},{3,2},{4,5},{5,4},{6,7},{7,6},{8,9},{9,8},{10,11... | collective-permute-start | bytes 110600 | tf_op jit(solution)/shard_map/ppermute | solution.py:612
  (10 other events, 18.3 us)

commit v4 on v2

v4 whole, which is shorter than its diff:
```python
import functools
import math

import jax
import jax.numpy as jnp
import numpy as np
from jax import lax
from jax.experimental import pallas as pl
from jax.experimental.pallas import tpu as pltpu
from jax.sharding import PartitionSpec as P

F32 = jnp.float32
BF16 = jnp.bfloat16


ANYWHERE = pl.BlockSpec(memory_space=pl.ANY)


def shapes_of(arrays):
    return [jax.ShapeDtypeStruct(array.shape, array.dtype) for array in arrays]


def ring_order(count):
    if count == 8:
        return list(range(0, count, 2)) + list(range(count - 1, 0, -2))
    return list(range(count))


def sorting_matrix(rows, columns, inner, source_inner):
    row = lax.broadcasted_iota(jnp.int32, (rows, columns), 0)
    column = lax.broadcasted_iota(jnp.int32, (rows, columns), 1)
    return (column == (row % inner) * source_inner + row // inner).astype(F32).astype(BF16)


def picking_matrix(wanted, inner, groups, first_head):
    row = lax.broadcasted_iota(jnp.int32, (wanted * inner, 256), 0)
    column = lax.broadcasted_iota(jnp.int32, (wanted * inner, 256), 1)
    group = row // inner
    source = (group % 2) * (groups // 2) + first_head + group // 2
    return (column == (row % inner) * groups + source).astype(F32).astype(BF16)


def request_at(where, slot):
    me_ref, owner_ref, adapter_ref = where
    owner = owner_ref[me_ref[0], slot]
    request = jnp.int32(0)
    for r in range(1, adapter_ref.shape[0]):
        request = jnp.where(adapter_ref[r] == owner, jnp.int32(r), request)
    return request


def pack_kernel(core_ref, shrink_ref, expand_ref, first_ref, second_ref, *, cut, heads_here):
    rank_size = shrink_ref.shape[0]
    groups = expand_ref.shape[0] // rank_size
    ranks = 256 // groups
    pick = picking_matrix(2 * heads_here, ranks, groups, core_ref[0] * heads_here)
    columns = 2 * heads_here * 128
    for block in range(rank_size // ranks):
        sorted_rows = jnp.dot(
            pick, expand_ref[256 * block : 256 * (block + 1), :], preferred_element_type=F32
        ).astype(BF16)
        for g in range(2 * heads_here):
            first_ref[ranks * block : ranks * (block + 1), 128 * g : 128 * (g + 1)] = sorted_rows[
                ranks * g : ranks * (g + 1), :
            ]
    first_ref[:, columns:] = shrink_ref[:, :cut]
    second_ref[...] = shrink_ref[:, cut:]


def pack(core, shrink, expand_rows, cut, heads_here):
    rank_size, half_width = shrink.shape
    columns = 2 * heads_here * 128
    return pl.pallas_call(
        functools.partial(pack_kernel, cut=cut, heads_here=heads_here),
        grid_spec=pltpu.PrefetchScalarGridSpec(
            num_scalar_prefetch=1,
            grid=(1,),
            in_specs=[
                pl.BlockSpec(shrink.shape, lambda i, c: (0, 0)),
                pl.BlockSpec(expand_rows.shape, lambda i, c: (0, 0)),
            ],
            out_specs=[
                pl.BlockSpec((rank_size, columns + cut), lambda i, c: (0, 0)),
                pl.BlockSpec((rank_size, half_width - cut), lambda i, c: (0, 0)),
            ],
        ),
        out_shape=[
            jax.ShapeDtypeStruct((rank_size, columns + cut), BF16),
            jax.ShapeDtypeStruct((rank_size, half_width - cut), BF16),
        ],
        name="pack",
    )(core, shrink, expand_rows)


def base_kernel(core_ref, hidden_ref, weight_ref, *rest, held_count):
    total_ref, wide_ref = rest[-2:]
    here_ref, away_ref = rest[-2 - held_count - 2 : -2 - held_count]
    step = pl.program_id(0)
    depth = hidden_ref.shape[1]
    groups = weight_ref.shape[0] // depth
    heads = groups // 2
    wide_ref[...] = weight_ref[...].astype(F32)
    parts = []
    for head in range(heads):
        tiles = [
            wide_ref[pl.ds(tile * heads + head, depth, stride=groups), :].astype(BF16)
            for tile in range(2)
        ]
        parts.append(
            jnp.dot(hidden_ref[...], jnp.concatenate(tiles, 1), preferred_element_type=F32)
        )
    product = jnp.concatenate(parts, 1)

    @pl.when(step == 0)
    def _():
        total_ref[...] = product

    @pl.when(step > 0)
    def _():
        total_ref[...] += product

    @pl.when(step == pl.num_programs(0) - 1)
    def _():
        columns = here_ref.shape[1]

        @pl.when(core_ref[0] == 0)
        def _():
            here_ref[...] = total_ref[:, :columns]
            away_ref[...] = total_ref[:, columns:]

        @pl.when(core_ref[0] == 1)
        def _():
            here_ref[...] = total_ref[:, columns:]
            away_ref[...] = total_ref[:, :columns]


def base_product(core, hidden_states, weight_rows, width, held):
    rows, half_width = hidden_states.shape
    groups = weight_rows.shape[0] // half_width
    depth = half_width // 2
    return pl.pallas_call(
        functools.partial(base_kernel, held_count=len(held)),
        grid_spec=pltpu.PrefetchScalarGridSpec(
            num_scalar_prefetch=1,
            grid=(half_width // depth,),
            in_specs=[
                pl.BlockSpec((rows, depth), lambda i, c: (0, i)),
                pl.BlockSpec((depth * groups, 128), lambda i, c: (i, 0)),
            ]
            + [ANYWHERE] * len(held),
            out_specs=[pl.BlockSpec((rows, width // 2), lambda i, c: (0, 0))] * 2
            + [ANYWHERE] * len(held),
            scratch_shapes=[
                pltpu.VMEM((rows, width), F32),
                pltpu.VMEM((depth * groups, 128), F32),
            ],
        ),
        out_shape=[jax.ShapeDtypeStruct((rows, width // 2), F32)] * 2 + shapes_of(held),
        input_output_aliases={3 + k: 2 + k for k in range(len(held))},
        compiler_params=pltpu.CompilerParams(vmem_limit_bytes=56 * 1024 * 1024),
        cost_estimate=pl.CostEstimate(
            flops=4_000_000_000, bytes_accessed=9_000_000, transcendentals=0
        ),
        name="base",
    )(core, hidden_states, weight_rows, *held)


def tree_kernel(length_ref, parent_ref, frequency_ref, *rest, kv_heads, held_count):
    table_ref = rest[len(rest) - held_count - 1]
    requests, nodes = parent_ref.shape
    head_size = frequency_ref.shape[1]
    node = lax.broadcasted_iota(jnp.int32, (nodes, nodes), 0)
    same = node == lax.broadcasted_iota(jnp.int32, (nodes, nodes), 1)
    spare = table_ref.shape[1] - 2 * head_size
    spread_node = lax.broadcasted_iota(jnp.int32, (nodes, spare), 0)
    spread_lane = lax.broadcasted_iota(jnp.int32, (nodes, spare), 1)
    spread = spread_lane == spread_node
    for g in range(1, kv_heads):
        spread = spread | (spread_lane == spread_node + nodes * g)
    spread = spread.astype(F32).astype(BF16)
    parents = parent_ref[...]
    below = [
        (same | (parents[r : r + 1, :] == node)).astype(F32).astype(BF16) for r in range(requests)
    ]
    reached = 1
    while reached < nodes:
        below = [
            jnp.minimum(jnp.dot(b, b, preferred_element_type=F32), 1.0).astype(BF16) for b in below
        ]
        reached = 2 * reached
    lane = lax.broadcasted_iota(jnp.int32, (nodes, head_size), 1)
    sign = jnp.where(lane < head_size // 2, -1.0, 1.0)
    ones = jnp.ones((nodes, head_size), BF16)
    for r in range(requests):
        b = below[r]
        depth = lax.dot_general(b, ones, (((0,), (0,)), ((), ())), preferred_element_type=F32)
        positions = length_ref[r].astype(F32) + depth - 1.0
        angles = positions * frequency_ref[...]
        rows = slice(nodes * r, nodes * (r + 1))
        wide = lax.dot_general(b, spread, (((0,), (0,)), ((), ())), preferred_element_type=F32)
        table_ref[rows, :] = jnp.concatenate(
            [jnp.cos(angles), jnp.sin(angles) * sign, jnp.where(wide > 0.5, 0.0, -1e30)], 1
        )


def tree_tables(cache_lengths, tree_parents, head_size, kv_heads, held):
    requests, nodes = tree_parents.shape
    half_size = head_size // 2
    frequency = np.exp(np.arange(half_size) * (-2.0 * math.log(1000000.0) / head_size))
    frequency = np.concatenate([frequency, frequency]).reshape(1, head_size).astype(np.float32)
    whole = lambda shape: pl.BlockSpec(shape, lambda i, n: (0,) * len(shape))
    rows = requests * nodes
    width = 2 * head_size + -(-kv_heads * nodes // 128) * 128
    return pl.pallas_call(
        functools.partial(tree_kernel, kv_heads=kv_heads, held_count=len(held)),
        grid_spec=pltpu.PrefetchScalarGridSpec(
            num_scalar_prefetch=1,
            grid=(1,),
            in_specs=[whole(tree_parents.shape), whole((1, head_size))] + [ANYWHERE] * len(held),
            out_specs=[whole((rows, width))] + [ANYWHERE] * len(held),
        ),
        out_shape=[jax.ShapeDtypeStruct((rows, width), F32)] + shapes_of(held),
        input_output_aliases={3 + k: 1 + k for k in range(len(held))},
        cost_estimate=pl.CostEstimate(
            flops=1_000_000_000, bytes_accessed=8_000_000, transcendentals=0
        ),
        name="tree",
    )(cache_lengths, tree_parents, frequency, *held)


def shrink_kernel(me_ref, owner_ref, adapter_ref, *refs, columns, cut, held_count):
    output_ref = refs[len(refs) - held_count - 1]
    contract = (((1,), (1,)), ((), ()))
    for b in range(output_ref.shape[0]):
        hidden_ref, one_ref, two_ref = refs[3 * b : 3 * b + 3]
        output_ref[b] = lax.dot_general(
            hidden_ref[:, :cut], one_ref[:, columns:], contract, preferred_element_type=F32
        ) + lax.dot_general(hidden_ref[:, cut:], two_ref[...], contract, preferred_element_type=F32)


def shrink_rows(where, slot, hidden_states, pieces, tree_size, columns, cut, after, held):
    rank_size = pieces[0][0].shape[0]
    in_specs, operands = [], []
    for b, (one, two) in enumerate(pieces):
        in_specs += [
            pl.BlockSpec(
                (tree_size, hidden_states.shape[1]),
                lambda i, *refs, b=b: (request_at(refs, slot + b), 0),
            ),
            pl.BlockSpec(one.shape, lambda i, *refs: (0, 0)),
            pl.BlockSpec(two.shape, lambda i, *refs: (0, 0)),
        ]
        operands += [hidden_states, one, two]
    count = len(pieces)
    return pl.pallas_call(
        functools.partial(shrink_kernel, columns=columns, cut=cut, held_count=len(held)),
        grid_spec=pltpu.PrefetchScalarGridSpec(
            num_scalar_prefetch=3,
            grid=(1,),
            in_specs=in_specs + [ANYWHERE] * (len(after) + len(held)),
            out_specs=[pl.BlockSpec((count, tree_size, rank_size), lambda i, *refs: (0, 0, 0))]
            + [ANYWHERE] * len(held),
        ),
        out_shape=[jax.ShapeDtypeStruct((count, tree_size, rank_size), F32)] + shapes_of(held),
        input_output_aliases={3 + len(operands) + len(after) + k: 1 + k for k in range(len(held))},
        compiler_params=pltpu.CompilerParams(vmem_limit_bytes=24 * 1024 * 1024),
        cost_estimate=pl.CostEstimate(
            flops=count * 300_000_000, bytes_accessed=count * 2_000_000, transcendentals=0
        ),
        name="shrink",
    )(*where, *operands, *after, *held)


def finish_kernel(
    me_ref,
    owner_ref,
    adapter_ref,
    length_ref,
    here_ref,
    there_ref,
    shrunk_here_ref,
    shrunk_there_ref,
    table_ref,
    gain_ref,
    query_ref,
    key_ref,
    value_ref,
    *rest,
    count,
    slot,
    kv_heads,
):
    expand_refs = rest[:count]
    attention_ref, cache_ref, expand_ref = rest[-3:]
    tree_size, heads, head_size = query_ref.shape
    cached = key_ref.shape[0]
    per_group = heads // kv_heads
    rows = tree_size * heads
    columns = kv_heads * 2 * head_size
    spare = table_ref.shape[1] - 2 * head_size
    score_scale = math.log2(math.e) / math.sqrt(head_size)
    if count == 1:
        expand = expand_refs[0][...]
    else:
        for b in range(count):

            @pl.when(pl.program_id(0) == b)
            def _():
                expand_ref[...] = expand_refs[b][...]

        expand = expand_ref[...]
    length = length_ref[request_at((me_ref, owner_ref, adapter_ref), slot + pl.program_id(0))]
    shrunk = shrunk_here_ref[0] + shrunk_there_ref[0]
    high = shrunk.astype(BF16)
    left = shrunk - high.astype(F32)
    middle = left.astype(BF16)
    low = (left - middle.astype(F32)).astype(BF16)
    terms = jnp.dot(jnp.concatenate([low, middle, high], 0), expand, preferred_element_type=F32)
    delta = terms[:tree_size] + terms[tree_size : 2 * tree_size] + terms[2 * tree_size :]
    projected = (here_ref[...] + there_ref[...]) + delta
    cosine = table_ref[:, :head_size]
    sine = table_ref[:, head_size : 2 * head_size]
    gain = gain_ref[...]
    new_keys, new_values = [], []
    for g in range(kv_heads):
        at = 2 * head_size * g
        key = projected[:, at : at + head_size]
        new_values.append(projected[:, at + head_size : at + 2 * head_size].astype(BF16))
        norm = lax.rsqrt(jnp.mean(key * key, -1, keepdims=True) + 1e-06)
        key = key * norm * gain
        new_keys.append((key * cosine + pltpu.roll(key, head_size // 2, 1) * sine).astype(BF16))
    pad = jnp.zeros((spare - kv_heads * tree_size, head_size), BF16)
    keys = jnp.concatenate([key_ref[...]] + new_keys + [pad], 0)
    values = jnp.concatenate([value_ref[...]] + new_values + [pad], 0)
    scores = lax.dot_general(
        query_ref[...].reshape(rows, head_size),
        keys,
        (((1,), (1,)), ((), ())),
        preferred_element_type=F32,
    ).reshape(tree_size, heads, cached + spare)
    lane = lax.broadcasted_iota(jnp.int32, (heads, cached), 1)
    mine = lax.broadcasted_iota(jnp.int32, (heads, cached), 0) // per_group
    allowed = (lane % kv_heads == mine) & (lane // kv_heads < length)
    cached_bias = jnp.where(allowed, 0.0, -1e30)
    lane = lax.broadcasted_iota(jnp.int32, (heads, spare), 1)
    first = lax.broadcasted_iota(jnp.int32, (heads, spare), 0) // per_group * tree_size
    head_bias = jnp.where((lane >= first) & (lane < first + tree_size), 0.0, -1e30)
    node_bias = table_ref[:, 2 * head_size :]
    cached_scores = scores[:, :, :cached] + cached_bias[None]
    tree_scores = scores[:, :, cached:] + (node_bias[:, None, :] + head_bias[None])
    top = jnp.maximum(
        jnp.max(cached_scores, -1, keepdims=True), jnp.max(tree_scores, -1, keepdims=True)
    )
    cached_exponent = jnp.exp2((cached_scores - top) * score_scale)
    tree_exponent = jnp.exp2((tree_scores - top) * score_scale)
    total = jnp.sum(cached_exponent, -1, keepdims=True) + jnp.sum(tree_exponent, -1, keepdims=True)
    exponent = jnp.concatenate([cached_exponent, tree_exponent], -1)
    output = jnp.dot(
        exponent.astype(BF16).reshape(rows, cached + spare), values, preferred_element_type=F32
    ).reshape(tree_size, heads, head_size)
    attention_ref[...] = (output * (1.0 / total)).astype(BF16)
    stacked = jnp.concatenate(new_keys + new_values, 0)
    size = stacked.shape[0]
    cache_ref[...] = jnp.dot(
        sorting_matrix(size, size, size // tree_size, tree_size),
        stacked,
        preferred_element_type=F32,
    ).astype(BF16)


def finish(where, slot, batch, there, shared, previous):
    shrunk_here, shrunk_there, pieces = batch
    lengths, gain, here, table, queries, key_rows, value_rows = shared
    spot = lambda i, refs: request_at(refs[:3], slot + i)
    count, tree_size, rank_size = shrunk_here.shape
    requests = lengths.shape[0]
    rows, heads, head_size = queries.shape
    columns = here.shape[1]
    kv_heads = columns // (2 * head_size)
    row_block = lambda width: pl.BlockSpec((tree_size, width), lambda i, *refs: (spot(i, refs), 0))
    shrunk_block = pl.BlockSpec((1, tree_size, rank_size), lambda i, *refs: (i, 0, 0))
    cached_block = pl.BlockSpec(
        (key_rows.shape[0] // requests, head_size), lambda i, *refs: (spot(i, refs), 0)
    )
    query_block = pl.BlockSpec(
        (tree_size, heads, head_size), lambda i, *refs: (spot(i, refs), 0, 0)
    )
    in_specs = [
        row_block(columns),
        row_block(columns),
        shrunk_block,
        shrunk_block,
        row_block(table.shape[1]),
        pl.BlockSpec((1, head_size), lambda i, *refs: (0, 0)),
        query_block,
        cached_block,
        cached_block,
    ] + [pl.BlockSpec((rank_size, columns), lambda i, *refs: (0, 0))] * count
    operands = [*where, lengths, here, there, shrunk_here, shrunk_there, table, gain, queries]
    operands += [key_rows, value_rows, *pieces]
    aliases = {}
    if previous is not None:
        aliases = {len(operands): 0, len(operands) + 1: 1}
        operands += list(previous)
        in_specs += [ANYWHERE] * 2
    cache_rows = 2 * kv_heads * tree_size
    return pl.pallas_call(
        functools.partial(finish_kernel, count=count, slot=slot, kv_heads=kv_heads),
        grid_spec=pltpu.PrefetchScalarGridSpec(
            num_scalar_prefetch=4,
            grid=(count,),
            in_specs=in_specs,
            out_specs=[
                query_block,
                pl.BlockSpec((cache_rows, head_size), lambda i, *refs: (spot(i, refs), 0)),
            ],
            scratch_shapes=[pltpu.VMEM((rank_size, columns), BF16)],
        ),
        out_shape=[
            jax.ShapeDtypeStruct((rows, heads, head_size), BF16),
            jax.ShapeDtypeStruct((rows * 2 * kv_heads, head_size), BF16),
        ],
        input_output_aliases=aliases,
        compiler_params=pltpu.CompilerParams(vmem_limit_bytes=24 * 1024 * 1024),
        cost_estimate=pl.CostEstimate(
            flops=count * 900_000_000, bytes_accessed=count * 3_000_000, transcendentals=0
        ),
        name="finish",
    )(*operands)


def per_device(
    hidden_states,
    kv_weight,
    shrink_factors,
    expand_factors,
    adapter_ids,
    cache_lengths,
    tree_parents,
    queries,
    cache_keys,
    cache_values,
    key_gain,
):
    requests, tree_size = tree_parents.shape
    row_count, half_width = hidden_states.shape
    kv_heads, kv_width = (kv_weight.shape[1], kv_weight.shape[2])
    head_size = kv_width // 2
    rank_size = shrink_factors.shape[2]
    context = cache_keys.shape[1]
    pool_count = lax.axis_size("pool")
    heads_here = kv_heads // lax.axis_size("tp")
    columns = heads_here * kv_width
    me = lax.axis_index("pool")
    core = lax.axis_index("tp").astype(jnp.int32).reshape(1)
    swap = [(0, 1), (1, 0)]

    def tile_rows(array):
        lead, heads = array.shape[0], array.shape[1]
        return array.reshape(lead, heads, 2, 128).transpose(0, 2, 1, 3).reshape(-1, 128)

    cut = (half_width + columns) // 2 - columns
    first, second = pack(
        core, shrink_factors[0].T, tile_rows(expand_factors[0]), cut, heads_here
    )

    order = ring_order(pool_count)
    onward = [(order[i], order[(i + 1) % pool_count]) for i in range(pool_count)]
    backward = [(b, a) for a, b in onward]
    half = pool_count // 2
    offsets = [[0]] + [[-step, step] for step in range(1, half)] + [[half]]
    flat_offsets = sum(offsets, [])
    owners = np.zeros((pool_count, pool_count), np.int32)
    for spot, index in enumerate(order):
        owners[index] = [order[(spot + offset) % pool_count] for offset in flat_offsets]
    where = (me.astype(jnp.int32).reshape(1), jnp.asarray(owners), adapter_ids)

    weight_rows = tile_rows(kv_weight)
    key_rows = cache_keys.reshape(-1, head_size)
    value_rows = cache_values.reshape(-1, head_size)

    arrivals = [(first, second)]
    front = rear = (first, second)
    for step in range(1, half):
        front = tuple(lax.ppermute(piece, "pool", onward) for piece in front)
        rear = tuple(lax.ppermute(piece, "pool", backward) for piece in rear)
        held = [front[1], rear[1]]
        if step == 1:
            here, away, *held = base_product(
                core, hidden_states, weight_rows, kv_heads * kv_width, held
            )
        if step == 2:
            table, *held = tree_tables(cache_lengths, tree_parents, head_size, heads_here, held)
        front, rear = (front[0], held[0]), (rear[0], held[1])
        arrivals += [front, rear]
    arrivals.append(
        (lax.ppermute(front[0], "pool", onward), lax.ppermute(rear[1], "pool", backward))
    )
    shared = (
        cache_lengths,
        key_gain.reshape(1, head_size),
        here,
        table,
        queries,
        key_rows,
        value_rows,
    )
    outputs = None
    if pool_count == requests:
        slot = 0
        for group in (arrivals[:-3], arrivals[-3:]):
            after = [] if outputs is None else [outputs[0]]
            held = [away] if outputs is None else []
            partial, *held = shrink_rows(
                where, slot, hidden_states, group, tree_size, columns, cut, after, held
            )
            if held:
                there = lax.ppermute(held[0], "tp", swap)
            batch = (partial, lax.ppermute(partial, "tp", swap), [piece[0] for piece in group])
            outputs = finish(where, slot, batch, there, shared, outputs)
            slot += len(group)
    else:
        parts = [
            shrink_rows(where, slot, hidden_states, [piece], tree_size, columns, cut, [], [])[0]
            for slot, piece in enumerate(arrivals)
        ]
        owners_here = lax.dynamic_index_in_dim(jnp.asarray(owners), me, 0, keepdims=False)
        hot = (adapter_ids[None, :] == owners_here[:, None]).astype(jnp.int32)
        slots = jnp.sum(hot * jnp.arange(pool_count, dtype=jnp.int32)[:, None], 0)
        partial = jnp.concatenate(parts, 0)[slots]
        expands = jnp.stack([piece[0][:, :columns] for piece in arrivals])[slots]
        every = jnp.arange(requests, dtype=jnp.int32)
        batch = (
            partial,
            lax.ppermute(partial, "tp", swap),
            [expands[r] for r in range(requests)],
        )
        there = lax.ppermute(away, "tp", swap)
        outputs = finish((every[:1], every[None, :], every), 0, batch, there, shared, None)
    attention, cache_rows = outputs
    tree_cache = (
        cache_rows.reshape(row_count, 2, heads_here, head_size)
        .transpose(0, 2, 1, 3)
        .reshape(row_count, heads_here, kv_width)
    )
    return attention, tree_cache


def solution(mesh):
    placed = (
        P(("grp", "pool"), "tp"),
        P("tp", None, None),
        P(("grp", "pool"), "tp", None),
        P(("grp", "pool"), None, None, None),
        P(("grp", "pool")),
        P(("grp", "pool")),
        P(("grp", "pool"), None),
        P(("grp", "pool"), "tp", None),
        P(("grp", "pool"), None, "tp", None),
        P(("grp", "pool"), None, "tp", None),
        P(),
    )
    return jax.shard_map(
        per_device,
        mesh=mesh,
        in_specs=placed,
        out_specs=(P(("grp", "pool"), "tp", None), P(("grp", "pool"), "tp", None)),
        check_vma=False,
    )
```

time: 72.9 us -> 63.2 us (0.87)
  Pallas kernels: 35.1 us -> 27.9 us
  local copies, waits for them, and re-layouts: 8.05 us -> 4.91 us
  waiting for transfers between devices: 11.5 us -> 13 us
  other arithmetic: 0.78 us -> 0 us
    pallas_call x8 -> x6, Pallas kernels: 33.3 us -> 26.1 us  [the longest x2 11.9 us: finish(): pl.pallas_call(functools.partial(finish_kernel, count=count, slot=slot, k...]
    ppermute x6, waiting for transfers between devices: 0.02 us -> 3.95 us  [per_device(): rear = tuple((lax.ppermute(piece, 'pool', backward) for piece in rear))]
    ppermute x6, waiting for transfers between devices: 11.5 us -> 7.8 us  [per_device(): front = tuple((lax.ppermute(piece, 'pool', onward) for piece in front))]
    unnamed x32 -> x36, local copies, waits for them, and re-layouts: 6.63 us -> 4.91 us
    ppermute x1, starting transfers between devices: 1.89 us -> 0.44 us  [per_device(): lax.ppermute(rear[1], 'pool', backward)]
    ppermute x1, starting transfers between devices: 0.14 us -> 1.58 us  [per_device(): lax.ppermute(front[0], 'pool', onward)]
    ppermute x3 -> x2, waiting for transfers between devices: 0.01 us -> 1.28 us  [per_device(): lax.ppermute(partial, 'tp', swap)]
    ppermute x6, starting transfers between devices: 2.93 us -> 3.89 us  [per_device(): front = tuple((lax.ppermute(piece, 'pool', onward) for piece in front))]
  transfers between devices with their start and end apart: 18 -> 17, of which waited for: 3 -> 5; matrix products, arithmetic and copies ran while one was open for 3% -> 0% of each run, Pallas kernels for 42% -> 29%
where the time goes in v4:
time: 63.2 us; the launch traced here: 62.9 us
  Pallas kernels  27.9 us (44%)
  starting transfers between devices  16.1 us (25%)
  waiting for transfers between devices  13 us (21%)
  local copies, waits for them, and re-layouts  4.91 us (8%)
  between operations  0.84 us (1%)
    pallas_call x2, Pallas kernels, finish(): pl.pallas_call(functools.partial(finish_kernel, count=count, slot=slot, k...  11.9 us
    ppermute x6, starting transfers between devices, per_device(): rear = tuple((lax.ppermute(piece, 'pool', backward) for piece in rear))  10.2 us
    ppermute x6, waiting for transfers between devices, per_device(): front = tuple((lax.ppermute(piece, 'pool', onward) for piece in front))  7.8 us
    pallas_call x1, Pallas kernels, base_product(): pl.pallas_call(functools.partial(base_kernel, held_count=len(held)), grid...  6.64 us
    unnamed x36, local copies, waits for them, and re-layouts  4.91 us
    ppermute x6, waiting for transfers between devices, per_device(): rear = tuple((lax.ppermute(piece, 'pool', backward) for piece in rear))  3.95 us
    pallas_call x1, Pallas kernels, tree_tables(): pl.pallas_call(functools.partial(tree_kernel, kv_heads=kv_heads, held_cou...  3.92 us
    ppermute x6, starting transfers between devices, per_device(): front = tuple((lax.ppermute(piece, 'pool', onward) for piece in front))  3.89 us
  transfers between devices with their start and end apart: 17, of which 5 were waited for; matrix products, arithmetic and copies ran while one was open for 0% of the time, Pallas kernels for 29%

profile of v4, /device:TPU:0, one launch (start us, length us, event | category | flops | bytes accessed | tf_op | source)
XLA Modules:
  0.0 62.9 jit_solution(16151380438763190162)
XLA Ops:
  0.6 1.9 %pack.1 = (bf16[64,1536]{1,0:T(8,128)(2,1)}, bf16[64,1536]{1,0:T(8,128)(2,1)}) custom-call(s32[1]{0:T(128)} %bitcast.1.core_ref, bf16[64,2560]{1,0:T(8,128)(2,1)} %bitcast.29, bf16[512,128]{1,0:T(8,128)(2,1)} %bitcast.30), custom_call_target="tpu_custom_call" | custom-call | tf_op jit(solution)/shard_map/pack/pallas_call | solution.py:73
  2.5 3.0 %collective-permute-start.1 = (bf16[64,1536]{1,0:T(8,128)(2,1)}, bf16[64,1536]{1,0:T(8,128)(2,1)S(1)}, u32[]{:S(2)}, u32[]{:S(2)}) collective-permute-start(bf16[64,1536]{1,0:T(8,128)(2,1)} %get-tuple-element.17.refs_2_), channel_id=1, source_target_pairs={{4,0},{8,4},{12,8},{14,12},{10,14},{6,10},{2,6},{0,2},{5,1},{9,5},... | collective-permute-start | bytes 589832 | tf_op jit(solution)/shard_map/ppermute | solution.py:486
  5.5 0.1 collective-permute-start
  5.5 2.0 %collective-permute-start.3 = (bf16[64,1536]{1,0:T(8,128)(2,1)}, bf16[64,1536]{1,0:T(8,128)(2,1)S(1)}, u32[]{:S(2)}, u32[]{:S(2)}) collective-permute-start(bf16[64,1536]{1,0:T(8,128)(2,1)} %get-tuple-element.19.refs_1_.rest_0_), channel_id=1, source_target_pairs={{4,0},{8,4},{12,8},{14,12},{10,14},{6,10},{2,6},{0,2},{5,1},{9,5},... | collective-permute-start | bytes 589832 | tf_op jit(solution)/shard_map/ppermute | solution.py:486
  7.5 0.1 collective-permute-start.2
  7.5 3.9 %collective-permute-done.1.rest_1_ = bf16[64,1536]{1,0:T(8,128)(2,1)S(1)} collective-permute-done((bf16[64,1536]{1,0:T(8,128)(2,1)}, bf16[64,1536]{1,0:T(8,128)(2,1)S(1)}, u32[]{:S(2)}, u32[]{:S(2)}) %collective-permute-start.1) | collective-permute-done | bytes 196640 | tf_op jit(solution)/shard_map/ppermute | solution.py:486
  11.5 2.0 %collective-permute-done.rest_0_ = bf16[64,1536]{1,0:T(8,128)(2,1)S(1)} collective-permute-done((bf16[64,1536]{1,0:T(8,128)(2,1)}, bf16[64,1536]{1,0:T(8,128)(2,1)S(1)}, u32[]{:S(2)}, u32[]{:S(2)}) %collective-permute-start) | collective-permute-done | bytes 196640 | tf_op jit(solution)/shard_map/ppermute | solution.py:485
  13.5 0.7 %copy-done.7 = bf16[64,1536]{1,0:T(8,128)(2,1)} copy-done((bf16[64,1536]{1,0:T(8,128)(2,1)}, bf16[64,1536]{1,0:T(8,128)(2,1)S(1)}, u32[]{:S(2)}) %copy-start.7) | copy-done | bytes 196632
  14.2 6.6 %base.1 = (f32[384,512]{1,0:T(8,128)}, f32[384,512]{1,0:T(8,128)}, bf16[64,1536]{1,0:T(8,128)(2,1)}, bf16[64,1536]{1,0:T(8,128)(2,1)}) custom-call(s32[1]{0:T(128)} %bitcast.1.core_ref, bf16[384,2560]{1,0:T(8,128)(2,1)} %refs_6_.3, bf16[20480,128]{1,0:T(8,128)(2,1)} %bitcast.31, ...), custom_call_target="tpu_custom_call", output_to_operand_aliasing={{2}: (3, {}), {3}: (4, {})} | custom-call | flops 4000000000 | bytes 9000000 | tf_op jit(solution)/shard_map/base/pallas_call | solution.py:141
  20.8 0.1 collective-permute-start.5
  20.9 1.9 %collective-permute-start.6 = (bf16[64,1536]{1,0:T(8,128)(2,1)}, bf16[64,1536]{1,0:T(8,128)(2,1)}, u32[]{:S(2)}, u32[]{:S(2)}) collective-permute-start(bf16[64,1536]{1,0:T(8,128)(2,1)} %get-tuple-element.21.refs_8_), channel_id=1, source_target_pairs={{4,0},{8,4},{12,8},{14,12},{10,14},{6,10},{2,6},{0,2},{5,1},{9,5},... | collective-permute-start | bytes 589832 | tf_op jit(solution)/shard_map/ppermute | solution.py:486
  22.9 1.6 %collective-permute-start.7 = (bf16[64,1536]{1,0:T(8,128)(2,1)S(1)}, bf16[64,1536]{1,0:T(8,128)(2,1)S(1)}, u32[]{:S(2)}, u32[]{:S(2)}) collective-permute-start(bf16[64,1536]{1,0:T(8,128)(2,1)S(1)} %collective-permute-done.3.refs_7_.rest_2_), channel_id=1, source_target_pairs={{4,0},{8,4},{12,8},{14,12},{10,14},{6,10},{2,6},{0,2},{5,1},{9,5},... | collective-permute-start | bytes 589832 | tf_op jit(solution)/shard_map/ppermute | solution.py:486
  24.4 0.4 collective-permute-start.4
  24.9 2.8 %collective-permute-done.5.rest_0_ = bf16[64,1536]{1,0:T(8,128)(2,1)} collective-permute-done((bf16[64,1536]{1,0:T(8,128)(2,1)}, bf16[64,1536]{1,0:T(8,128)(2,1)}, u32[]{:S(2)}, u32[]{:S(2)}) %collective-permute-start.5) | collective-permute-done | bytes 196640 | tf_op jit(solution)/shard_map/ppermute | solution.py:485
  27.7 3.9 %tree.1 = (f32[384,384]{1,0:T(8,128)}, bf16[64,1536]{1,0:T(8,128)(2,1)}, bf16[64,1536]{1,0:T(8,128)(2,1)}) custom-call(s32[8]{0:T(128)} %length_ref.5, s32[8,48]{1,0:T(8,128)} %parent_ref.1, f32[1,128]{1,0:T(1,128)} %constant.13.clone.frequency_ref, bf16[64,1536]{1,0:T(8,128)(2,1)} %collective-permute-done.5.rest_0_, ...), custom_call_target="tpu_custom_call", output_to_operand_aliasing={{1}: (3, {}), {2}: (4, {})} | custom-call | flops 1000000000 | bytes 8000000 | tf_op jit(solution)/shard_map/tree/pallas_call | solution.py:214
  31.7 0.9 %copy-done.4 = bf16[64,1536]{1,0:T(8,128)(2,1)S(1)} copy-done((bf16[64,1536]{1,0:T(8,128)(2,1)S(1)}, bf16[64,1536]{1,0:T(8,128)(2,1)}, u32[]{:S(2)}) %copy-start.4) | copy-done | bytes 196632
  32.6 0.9 %copy-done.6 = bf16[64,1536]{1,0:T(8,128)(2,1)S(1)} copy-done((bf16[64,1536]{1,0:T(8,128)(2,1)S(1)}, bf16[64,1536]{1,0:T(8,128)(2,1)}, u32[]{:S(2)}) %copy-start.6) | copy-done | bytes 196632
  33.5 0.9 %copy-done.8 = bf16[64,1536]{1,0:T(8,128)(2,1)S(1)} copy-done((bf16[64,1536]{1,0:T(8,128)(2,1)S(1)}, bf16[64,1536]{1,0:T(8,128)(2,1)}, u32[]{:S(2)}) %copy-start.8) | copy-done | bytes 196632
  34.5 2.6 %shrink.2 = (f32[5,48,64]{2,1,0:T(8,128)S(1)}, f32[384,512]{1,0:T(8,128)S(1)}) custom-call(s32[1]{0:T(128)} %bitcast.me_ref, s32[8,8]{1,0:T(8,128)S(1)} %copy-done.9, s32[8]{0:T(128)S(1)} %copy-done.10, bf16[384,2560]{1,0:T(8,128)(2,1)S(1)} %copy-done, bf16[64,1536]{1,0:T(8,128)(2,1)S(1)} %copy-done.3, ...), custom_call_target="tpu_custom_call", output_to_operand_aliasing={{1}: (18, {})} | custom-call | flops 1500000000 | bytes 10000000 | tf_op jit(solution)/shard_map/shrink/pallas_call | solution.py:255
  37.1 1.6 %collective-permute-start.9 = (bf16[64,1536]{1,0:T(8,128)(2,1)}, bf16[64,1536]{1,0:T(8,128)(2,1)S(1)}, u32[]{:S(2)}, u32[]{:S(2)}) collective-permute-start(bf16[64,1536]{1,0:T(8,128)(2,1)} %collective-permute-done.4.refs_10_.rest_3_), channel_id=1, source_target_pairs={{0,4},{4,8},{8,12},{12,14},{14,10},{10,6},{6,2},{2,0},{1,5},{5,9},... | collective-permute-start | bytes 589832 | tf_op jit(solution)/shard_map/ppermute | solution.py:485
  38.8 0.4 collective-permute-start.12
  39.2 1.6 %collective-permute-start.10 = (bf16[64,1536]{1,0:T(8,128)(2,1)}, bf16[64,1536]{1,0:T(8,128)(2,1)S(1)}, u32[]{:S(2)}, u32[]{:S(2)}) collective-permute-start(bf16[64,1536]{1,0:T(8,128)(2,1)} %get-tuple-element.22.refs_11_), channel_id=1, source_target_pairs={{0,4},{4,8},{8,12},{12,14},{14,10},{10,6},{6,2},{2,0},{1,5},{5,9},... | collective-permute-start | bytes 589832 | tf_op jit(solution)/shard_map/ppermute | solution.py:485
  40.8 1.3 %collective-permute-start.11 = (bf16[64,1536]{1,0:T(8,128)(2,1)S(1)}, bf16[64,1536]{1,0:T(8,128)(2,1)S(1)}, u32[]{:S(2)}, u32[]{:S(2)}) collective-permute-start(bf16[64,1536]{1,0:T(8,128)(2,1)S(1)} %collective-permute-done.7.refs_13_.rest_4_), channel_id=1, source_target_pairs={{4,0},{8,4},{12,8},{14,12},{10,14},{6,10},{2,6},{0,2},{5,1},{9,5},... | collective-permute-start | bytes 589832 | tf_op jit(solution)/shard_map/ppermute | solution.py:486
  42.1 3.0 %collective-permute-done.9.refs_1_.rest_0_ = bf16[64,1536]{1,0:T(8,128)(2,1)S(1)} collective-permute-done((bf16[64,1536]{1,0:T(8,128)(2,1)}, bf16[64,1536]{1,0:T(8,128)(2,1)S(1)}, u32[]{:S(2)}, u32[]{:S(2)}) %collective-permute-start.9) | collective-permute-done | bytes 196640 | tf_op jit(solution)/shard_map/ppermute | solution.py:485
  45.1 1.6 %collective-permute-start.13 = (bf16[64,1536]{1,0:T(8,128)(2,1)S(1)}, bf16[64,1536]{1,0:T(8,128)(2,1)S(1)}, u32[]{:S(2)}, u32[]{:S(2)}) collective-permute-start(bf16[64,1536]{1,0:T(8,128)(2,1)S(1)} %collective-permute-done.9.refs_1_.rest_0_), channel_id=1, source_target_pairs={{0,4},{4,8},{8,12},{12,14},{14,10},{10,6},{6,2},{2,0},{1,5},{5,9},... | collective-permute-start | bytes 589832 | tf_op jit(solution)/shard_map/ppermute | solution.py:497
  46.7 0.0 collective-permute-done.12.refs_5_
  46.7 0.4 collective-permute-start.14
  47.2 7.5 %finish.2 = (bf16[384,16,128]{2,1,0:T(8,128)(2,1)}, bf16[1536,128]{1,0:T(8,128)(2,1)}) custom-call(s32[1]{0:T(128)} %bitcast.me_ref, s32[8,8]{1,0:T(8,128)S(1)} %copy-done.9, s32[8]{0:T(128)S(1)} %copy-done.10, s32[8]{0:T(128)S(1)} %copy-done.14, f32[384,512]{1,0:T(8,128)S(1)} %copy-done.16, f32[384,512]{1,0:T(8,128)S(1)} %collective-permute-done.8.there_ref, ...), custom_call_target="tpu_custom_call" | custom-call | flops 4499999744 | bytes 15000000 | tf_op jit(solution)/shard_map/finish/pallas_call | solution.py:407
  54.7 1.4 %copy-done.1 = bf16[384,16,128]{2,1,0:T(8,128)(2,1)S(1)} copy-done((bf16[384,16,128]{2,1,0:T(8,128)(2,1)S(1)}, bf16[384,16,128]{2,1,0:T(8,128)(2,1)}, u32[]{:S(2)}) %copy-start.1) | copy-done | bytes 1572888
  56.1 1.0 %shrink.3.shrunk_here_ref = f32[3,48,64]{2,1,0:T(8,128)S(1)} custom-call(s32[1]{0:T(128)} %bitcast.me_ref, s32[8,8]{1,0:T(8,128)S(1)} %copy-done.9, s32[8]{0:T(128)S(1)} %copy-done.10, bf16[384,2560]{1,0:T(8,128)(2,1)S(1)} %copy-done, bf16[64,1536]{1,0:T(8,128)(2,1)S(1)} %collective-permute-done.9.refs_1_.rest_0_, ...), custom_call_target="tpu_custom_call" | custom-call | flops 900000000 | bytes 6000000 | tf_op jit(solution)/shard_map/shrink/pallas_call | solution.py:255
  57.1 1.3 %collective-permute-done.16.shrunk_there_ref = f32[3,48,64]{2,1,0:T(8,128)S(1)} collective-permute-done((f32[3,48,64]{2,1,0:T(8,128)S(1)}, f32[3,48,64]{2,1,0:T(8,128)S(1)}, u32[]{:S(2)}, u32[]{:S(2)}) %collective-permute-start.16) | collective-permute-done | bytes 36896 | tf_op jit(solution)/shard_map/ppermute | solution.py:519
  58.4 4.5 %finish.3 = (bf16[384,16,128]{2,1,0:T(8,128)(2,1)}, bf16[1536,128]{1,0:T(8,128)(2,1)}) custom-call(s32[1]{0:T(128)} %bitcast.me_ref, s32[8,8]{1,0:T(8,128)S(1)} %copy-done.9, s32[8]{0:T(128)S(1)} %copy-done.10, s32[8]{0:T(128)S(1)} %copy-done.14, f32[384,512]{1,0:T(8,128)S(1)} %copy-done.16, ...), custom_call_target="tpu_custom_call", output_to_operand_aliasing={{0}: (16, {}), {1}: (17, {})} | custom-call | flops 2700000000 | bytes 9000000 | tf_op jit(solution)/shard_map/finish/pallas_call | solution.py:407
  (45 shorter events, 0.1 us)
Async XLA Ops:
  2.5 9.0 %collective-permute-start.1 = (bf16[64,1536]{1,0:T(8,128)(2,1)}, bf16[64,1536]{1,0:T(8,128)(2,1)S(1)}, u32[]{:S(2)}, u32[]{:S(2)}) collective-permute-start(bf16[64,1536]{1,0:T(8,128)(2,1)} %get-tuple-element.17.refs_2_), channel_id=1, source_target_pairs={{4,0},{8,4},{12,8},{14,12},{10,14},{6,10},{2,6},{0,2},{5,1},{9,5},... | collective-permute-start | bytes 589832 | tf_op jit(solution)/shard_map/ppermute | solution.py:486
  5.5 8.0 %collective-permute-start = (bf16[64,1536]{1,0:T(8,128)(2,1)}, bf16[64,1536]{1,0:T(8,128)(2,1)S(1)}, u32[]{:S(2)}, u32[]{:S(2)}) collective-permute-start(bf16[64,1536]{1,0:T(8,128)(2,1)} %get-tuple-element.17.refs_2_), channel_id=1, source_target_pairs={{0,4},{4,8},{8,12},{12,14},{14,10},{10,6},{6,2},{2,0},{1,5},{5,9},... | collective-permute-start | bytes 589832 | tf_op jit(solution)/shard_map/ppermute | solution.py:485
  5.5 17.3 %collective-permute-start.3 = (bf16[64,1536]{1,0:T(8,128)(2,1)}, bf16[64,1536]{1,0:T(8,128)(2,1)S(1)}, u32[]{:S(2)}, u32[]{:S(2)}) collective-permute-start(bf16[64,1536]{1,0:T(8,128)(2,1)} %get-tuple-element.19.refs_1_.rest_0_), channel_id=1, source_target_pairs={{4,0},{8,4},{12,8},{14,12},{10,14},{6,10},{2,6},{0,2},{5,1},{9,5},... | collective-permute-start | bytes 589832 | tf_op jit(solution)/shard_map/ppermute | solution.py:486
  7.5 17.0 %collective-permute-start.2 = (bf16[64,1536]{1,0:T(8,128)(2,1)}, bf16[64,1536]{1,0:T(8,128)(2,1)S(1)}, u32[]{:S(2)}, u32[]{:S(2)}) collective-permute-start(bf16[64,1536]{1,0:T(8,128)(2,1)} %get-tuple-element.19.refs_1_.rest_0_), channel_id=1, source_target_pairs={{0,4},{4,8},{8,12},{12,14},{14,10},{10,6},{6,2},{2,0},{1,5},{5,9},... | collective-permute-start | bytes 589832 | tf_op jit(solution)/shard_map/ppermute | solution.py:485
  11.5 2.0 %copy-start.5 = (bf16[64,1536]{1,0:T(8,128)(2,1)}, bf16[64,1536]{1,0:T(8,128)(2,1)S(1)}, u32[]{:S(2)}) copy-start(bf16[64,1536]{1,0:T(8,128)(2,1)S(1)} %collective-permute-done.1.rest_1_) | copy-start | bytes 589828
  20.8 6.9 %collective-permute-start.5 = (bf16[64,1536]{1,0:T(8,128)(2,1)}, bf16[64,1536]{1,0:T(8,128)(2,1)}, u32[]{:S(2)}, u32[]{:S(2)}) collective-permute-start(bf16[64,1536]{1,0:T(8,128)(2,1)} %get-tuple-element.20.refs_5_), channel_id=1, source_target_pairs={{0,4},{4,8},{8,12},{12,14},{14,10},{10,6},{6,2},{2,0},{1,5},{5,9},... | collective-permute-start | bytes 589832 | tf_op jit(solution)/shard_map/ppermute | solution.py:485
  20.9 6.8 %collective-permute-start.6 = (bf16[64,1536]{1,0:T(8,128)(2,1)}, bf16[64,1536]{1,0:T(8,128)(2,1)}, u32[]{:S(2)}, u32[]{:S(2)}) collective-permute-start(bf16[64,1536]{1,0:T(8,128)(2,1)} %get-tuple-element.21.refs_8_), channel_id=1, source_target_pairs={{4,0},{8,4},{12,8},{14,12},{10,14},{6,10},{2,6},{0,2},{5,1},{9,5},... | collective-permute-start | bytes 589832 | tf_op jit(solution)/shard_map/ppermute | solution.py:486
  22.9 8.8 %collective-permute-start.7 = (bf16[64,1536]{1,0:T(8,128)(2,1)S(1)}, bf16[64,1536]{1,0:T(8,128)(2,1)S(1)}, u32[]{:S(2)}, u32[]{:S(2)}) collective-permute-start(bf16[64,1536]{1,0:T(8,128)(2,1)S(1)} %collective-permute-done.3.refs_7_.rest_2_), channel_id=1, source_target_pairs={{4,0},{8,4},{12,8},{14,12},{10,14},{6,10},{2,6},{0,2},{5,1},{9,5},... | collective-permute-start | bytes 589832 | tf_op jit(solution)/shard_map/ppermute | solution.py:486
  24.4 7.2 %collective-permute-start.4 = (bf16[64,1536]{1,0:T(8,128)(2,1)S(1)}, bf16[64,1536]{1,0:T(8,128)(2,1)}, u32[]{:S(2)}, u32[]{:S(2)}) collective-permute-start(bf16[64,1536]{1,0:T(8,128)(2,1)S(1)} %collective-permute-done.2.refs_4_.rest_1_), channel_id=1, source_target_pairs={{0,4},{4,8},{8,12},{12,14},{14,10},{10,6},{6,2},{2,0},{1,5},{5,9},... | collective-permute-start | bytes 589832 | tf_op jit(solution)/shard_map/ppermute | solution.py:485
  24.9 6.7 %copy-start = (bf16[384,2560]{1,0:T(8,128)(2,1)S(1)}, bf16[384,2560]{1,0:T(8,128)(2,1)}, u32[]{:S(2)}) copy-start(bf16[384,2560]{1,0:T(8,128)(2,1)} %refs_6_.3) | copy-start | bytes 5898244
  24.9 6.7 %copy-start.2 = (f32[384,512]{1,0:T(8,128)S(1)}, f32[384,512]{1,0:T(8,128)}, u32[]{:S(2)}) copy-start(f32[384,512]{1,0:T(8,128)} %get-tuple-element.24.refs_15_) | copy-start | bytes 2359300
  24.9 6.8 %copy-start.3 = (bf16[64,1536]{1,0:T(8,128)(2,1)S(1)}, bf16[64,1536]{1,0:T(8,128)(2,1)}, u32[]{:S(2)}) copy-start(bf16[64,1536]{1,0:T(8,128)(2,1)} %get-tuple-element.19.refs_1_.rest_0_) | copy-start | bytes 589828
  24.9 6.8 %copy-start.9 = (s32[8,8]{1,0:T(8,128)S(1)}, s32[8,8]{1,0:T(8,128)}, u32[]{:S(2)}) copy-start(s32[8,8]{1,0:T(8,128)} %constant.12.clone.owner_ref) | copy-start | bytes 772
  24.9 6.8 %copy-start.10 = (s32[8]{0:T(128)S(1)}, s32[8]{0:T(128)}, u32[]{:S(2)}) copy-start(s32[8]{0:T(128)} %adapter_ref.7) | copy-start | bytes 100
  31.7 0.9 %copy-start.4 = (bf16[64,1536]{1,0:T(8,128)(2,1)S(1)}, bf16[64,1536]{1,0:T(8,128)(2,1)}, u32[]{:S(2)}) copy-start(bf16[64,1536]{1,0:T(8,128)(2,1)} %get-tuple-element.17.refs_2_) | copy-start | bytes 589828
  34.5 12.7 %copy-start.11 = (bf16[384,16,128]{2,1,0:T(8,128)(2,1)S(1)}, bf16[384,16,128]{2,1,0:T(8,128)(2,1)}, u32[]{:S(2)}) copy-start(bf16[384,16,128]{2,1,0:T(8,128)(2,1)} %query_ref.3) | copy-start | bytes 4718596
  34.5 12.7 %copy-start.12 = (bf16[8,128,2,128]{3,2,1,0:T(2,128)(2,1)S(1)}, bf16[8,128,2,128]{3,2,1,0:T(2,128)(2,1)}, u32[]{:S(2)}) copy-start(bf16[8,128,2,128]{3,2,1,0:T(2,128)(2,1)} %param.21) | copy-start | bytes 1572868
  34.5 12.7 %copy-start.13 = (bf16[8,128,2,128]{3,2,1,0:T(2,128)(2,1)S(1)}, bf16[8,128,2,128]{3,2,1,0:T(2,128)(2,1)}, u32[]{:S(2)}) copy-start(bf16[8,128,2,128]{3,2,1,0:T(2,128)(2,1)} %param.22) | copy-start | bytes 1572868
  34.5 12.7 %copy-start.14 = (s32[8]{0:T(128)S(1)}, s32[8]{0:T(128)}, u32[]{:S(2)}) copy-start(s32[8]{0:T(128)} %length_ref.5) | copy-start | bytes 100
  34.5 12.7 %copy-start.15 = (f32[128]{0:T(128)S(1)}, f32[128]{0:T(128)}, u32[]{:S(2)}) copy-start(f32[128]{0:T(128)} %param.23) | copy-start | bytes 1540
  34.5 12.7 %copy-start.16 = (f32[384,512]{1,0:T(8,128)S(1)}, f32[384,512]{1,0:T(8,128)}, u32[]{:S(2)}) copy-start(f32[384,512]{1,0:T(8,128)} %get-tuple-element.18.here_ref) | copy-start | bytes 2359300
  34.5 12.7 %copy-start.17 = (f32[384,384]{1,0:T(8,128)S(1)}, f32[384,384]{1,0:T(8,128)}, u32[]{:S(2)}) copy-start(f32[384,384]{1,0:T(8,128)} %get-tuple-element.27.table_ref) | copy-start | bytes 1769476
  37.1 10.1 %collective-permute-start.8 = (f32[384,512]{1,0:T(8,128)S(1)}, f32[384,512]{1,0:T(8,128)S(1)}, u32[]{:S(2)}, u32[]{:S(2)}) collective-permute-start(f32[384,512]{1,0:T(8,128)S(1)} %get-tuple-element.25), channel_id=1, source_target_pairs={{0,1},{1,0},{2,3},{3,2},{4,5},{5,4},{6,7},{7,6},{8,9},{9,8},{10,11... | collective-permute-start | bytes 2359304 | tf_op jit(solution)/shard_map/ppermute | solution.py:518
  37.1 8.0 %collective-permute-start.9 = (bf16[64,1536]{1,0:T(8,128)(2,1)}, bf16[64,1536]{1,0:T(8,128)(2,1)S(1)}, u32[]{:S(2)}, u32[]{:S(2)}) collective-permute-start(bf16[64,1536]{1,0:T(8,128)(2,1)} %collective-permute-done.4.refs_10_.rest_3_), channel_id=1, source_target_pairs={{0,4},{4,8},{8,12},{12,14},{14,10},{10,6},{6,2},{2,0},{1,5},{5,9},... | collective-permute-start | bytes 589832 | tf_op jit(solution)/shard_map/ppermute | solution.py:485
  38.8 8.0 %collective-permute-start.12 = (bf16[64,1536]{1,0:T(8,128)(2,1)}, bf16[64,1536]{1,0:T(8,128)(2,1)S(1)}, u32[]{:S(2)}, u32[]{:S(2)}) collective-permute-start(bf16[64,1536]{1,0:T(8,128)(2,1)} %get-tuple-element.23.refs_14_), channel_id=1, source_target_pairs={{4,0},{8,4},{12,8},{14,12},{10,14},{6,10},{2,6},{0,2},{5,1},{9,5},... | collective-permute-start | bytes 589832 | tf_op jit(solution)/shard_map/ppermute | solution.py:486
  39.2 1.6 %collective-permute-start.15 = (f32[5,48,64]{2,1,0:T(8,128)S(1)}, f32[5,48,64]{2,1,0:T(8,128)S(1)}, u32[]{:S(2)}, u32[]{:S(2)}) collective-permute-start(f32[5,48,64]{2,1,0:T(8,128)S(1)} %get-tuple-element.26.shrunk_here_ref), channel_id=1, source_target_pairs={{0,1},{1,0},{2,3},{3,2},{4,5},{5,4},{6,7},{7,6},{8,9},{9,8},{10,11... | collective-permute-start | bytes 184328 | tf_op jit(solution)/shard_map/ppermute | solution.py:519
  39.2 15.5 %collective-permute-start.10 = (bf16[64,1536]{1,0:T(8,128)(2,1)}, bf16[64,1536]{1,0:T(8,128)(2,1)S(1)}, u32[]{:S(2)}, u32[]{:S(2)}) collective-permute-start(bf16[64,1536]{1,0:T(8,128)(2,1)} %get-tuple-element.22.refs_11_), channel_id=1, source_target_pairs={{0,4},{4,8},{8,12},{12,14},{14,10},{10,6},{6,2},{2,0},{1,5},{5,9},... | collective-permute-start | bytes 589832 | tf_op jit(solution)/shard_map/ppermute | solution.py:485
  40.8 13.9 %collective-permute-start.11 = (bf16[64,1536]{1,0:T(8,128)(2,1)S(1)}, bf16[64,1536]{1,0:T(8,128)(2,1)S(1)}, u32[]{:S(2)}, u32[]{:S(2)}) collective-permute-start(bf16[64,1536]{1,0:T(8,128)(2,1)S(1)} %collective-permute-done.7.refs_13_.rest_4_), channel_id=1, source_target_pairs={{4,0},{8,4},{12,8},{14,12},{10,14},{6,10},{2,6},{0,2},{5,1},{9,5},... | collective-permute-start | bytes 589832 | tf_op jit(solution)/shard_map/ppermute | solution.py:486
  45.1 9.6 %collective-permute-start.13 = (bf16[64,1536]{1,0:T(8,128)(2,1)S(1)}, bf16[64,1536]{1,0:T(8,128)(2,1)S(1)}, u32[]{:S(2)}, u32[]{:S(2)}) collective-permute-start(bf16[64,1536]{1,0:T(8,128)(2,1)S(1)} %collective-permute-done.9.refs_1_.rest_0_), channel_id=1, source_target_pairs={{0,4},{4,8},{8,12},{12,14},{14,10},{10,6},{6,2},{2,0},{1,5},{5,9},... | collective-permute-start | bytes 589832 | tf_op jit(solution)/shard_map/ppermute | solution.py:497
  46.7 8.0 %collective-permute-start.14 = (bf16[64,1536]{1,0:T(8,128)(2,1)S(1)}, bf16[64,1536]{1,0:T(8,128)(2,1)S(1)}, u32[]{:S(2)}, u32[]{:S(2)}) collective-permute-start(bf16[64,1536]{1,0:T(8,128)(2,1)S(1)} %collective-permute-done.12.refs_5_), channel_id=1, source_target_pairs={{4,0},{8,4},{12,8},{14,12},{10,14},{6,10},{2,6},{0,2},{5,1},{9,5},... | collective-permute-start | bytes 589832 | tf_op jit(solution)/shard_map/ppermute | solution.py:497
  54.7 1.4 %copy-start.1 = (bf16[384,16,128]{2,1,0:T(8,128)(2,1)S(1)}, bf16[384,16,128]{2,1,0:T(8,128)(2,1)}, u32[]{:S(2)}) copy-start(bf16[384,16,128]{2,1,0:T(8,128)(2,1)} %get-tuple-element.28.refs_9_.rest_3_) | copy-start | bytes 4718596
  57.1 1.3 %collective-permute-start.16 = (f32[3,48,64]{2,1,0:T(8,128)S(1)}, f32[3,48,64]{2,1,0:T(8,128)S(1)}, u32[]{:S(2)}, u32[]{:S(2)}) collective-permute-start(f32[3,48,64]{2,1,0:T(8,128)S(1)} %shrink.3.shrunk_here_ref), channel_id=1, source_target_pairs={{0,1},{1,0},{2,3},{3,2},{4,5},{5,4},{6,7},{7,6},{8,9},{9,8},{10,11... | collective-permute-start | bytes 110600 | tf_op jit(solution)/shard_map/ppermute | solution.py:519
  (3 other events, 2.5 us)

commit v5 on v4

--- a/solution.py
+++ b/solution.py
@@ -88,6 +88,7 @@
             jax.ShapeDtypeStruct((rank_size, columns + cut), BF16),
             jax.ShapeDtypeStruct((rank_size, half_width - cut), BF16),
         ],
+        compiler_params=pltpu.CompilerParams(vmem_limit_bytes=8 * 1024 * 1024),
         name="pack",
     )(core, shrink, expand_rows)
 
@@ -134,7 +135,7 @@
             away_ref[...] = total_ref[:, :columns]
 
 
-def base_product(core, hidden_states, weight_rows, width, held):
+def base_product(core, hidden_states, weight_rows, width, after, held):
     rows, half_width = hidden_states.shape
     groups = weight_rows.shape[0] // half_width
     depth = half_width // 2
@@ -147,7 +148,7 @@
                 pl.BlockSpec((rows, depth), lambda i, c: (0, i)),
                 pl.BlockSpec((depth * groups, 128), lambda i, c: (i, 0)),
             ]
-            + [ANYWHERE] * len(held),
+            + [ANYWHERE] * (len(after) + len(held)),
             out_specs=[pl.BlockSpec((rows, width // 2), lambda i, c: (0, 0))] * 2
             + [ANYWHERE] * len(held),
             scratch_shapes=[
@@ -156,17 +157,19 @@
             ],
         ),
         out_shape=[jax.ShapeDtypeStruct((rows, width // 2), F32)] * 2 + shapes_of(held),
-        input_output_aliases={3 + k: 2 + k for k in range(len(held))},
-        compiler_params=pltpu.CompilerParams(vmem_limit_bytes=56 * 1024 * 1024),
+        input_output_aliases={3 + len(after) + k: 2 + k for k in range(len(held))},
         cost_estimate=pl.CostEstimate(
             flops=4_000_000_000, bytes_accessed=9_000_000, transcendentals=0
         ),
+        compiler_params=pltpu.CompilerParams(vmem_limit_bytes=24 * 1024 * 1024),
         name="base",
-    )(core, hidden_states, weight_rows, *held)
-
-
-def tree_kernel(length_ref, parent_ref, frequency_ref, *rest, kv_heads, held_count):
-    table_ref = rest[len(rest) - held_count - 1]
+    )(core, hidden_states, weight_rows, *after, *held)
+
+
+def tree_kernel(length_ref, parent_ref, frequency_ref, weight_ref, *rest, kv_heads):
+    table_ref, moved_ref, semaphore = rest[-3:]
+    move = pltpu.make_async_copy(weight_ref, moved_ref, semaphore)
+    move.start()
     requests, nodes = parent_ref.shape
     head_size = frequency_ref.shape[1]
     node = lax.broadcasted_iota(jnp.int32, (nodes, nodes), 0)
@@ -201,9 +204,10 @@
         table_ref[rows, :] = jnp.concatenate(
             [jnp.cos(angles), jnp.sin(angles) * sign, jnp.where(wide > 0.5, 0.0, -1e30)], 1
         )
-
-
-def tree_tables(cache_lengths, tree_parents, head_size, kv_heads, held):
+    move.wait()
+
+
+def tree_tables(cache_lengths, tree_parents, head_size, kv_heads, weight_rows, after):
     requests, nodes = tree_parents.shape
     half_size = head_size // 2
     frequency = np.exp(np.arange(half_size) * (-2.0 * math.log(1000000.0) / head_size))
@@ -212,20 +216,22 @@
     rows = requests * nodes
     width = 2 * head_size + -(-kv_heads * nodes // 128) * 128
     return pl.pallas_call(
-        functools.partial(tree_kernel, kv_heads=kv_heads, held_count=len(held)),
+        functools.partial(tree_kernel, kv_heads=kv_heads),
         grid_spec=pltpu.PrefetchScalarGridSpec(
             num_scalar_prefetch=1,
             grid=(1,),
-            in_specs=[whole(tree_parents.shape), whole((1, head_size))] + [ANYWHERE] * len(held),
-            out_specs=[whole((rows, width))] + [ANYWHERE] * len(held),
-        ),
-        out_shape=[jax.ShapeDtypeStruct((rows, width), F32)] + shapes_of(held),
-        input_output_aliases={3 + k: 1 + k for k in range(len(held))},
+            in_specs=[whole(tree_parents.shape), whole((1, head_size)), pl.BlockSpec(memory_space=pltpu.HBM)]
+            + [ANYWHERE] * len(after),
+            out_specs=[whole((rows, width)), ANYWHERE],
+            scratch_shapes=[pltpu.SemaphoreType.DMA],
+        ),
+        out_shape=[jax.ShapeDtypeStruct((rows, width), F32)] + shapes_of([weight_rows]),
         cost_estimate=pl.CostEstimate(
             flops=1_000_000_000, bytes_accessed=8_000_000, transcendentals=0
         ),
+        compiler_params=pltpu.CompilerParams(vmem_limit_bytes=8 * 1024 * 1024),
         name="tree",
-    )(cache_lengths, tree_parents, frequency, *held)
+    )(cache_lengths, tree_parents, frequency, weight_rows, *after)
 
 
 def shrink_kernel(me_ref, owner_ref, adapter_ref, *refs, columns, cut, held_count):
@@ -263,10 +269,10 @@
         ),
         out_shape=[jax.ShapeDtypeStruct((count, tree_size, rank_size), F32)] + shapes_of(held),
         input_output_aliases={3 + len(operands) + len(after) + k: 1 + k for k in range(len(held))},
-        compiler_params=pltpu.CompilerParams(vmem_limit_bytes=24 * 1024 * 1024),
         cost_estimate=pl.CostEstimate(
             flops=count * 300_000_000, bytes_accessed=count * 2_000_000, transcendentals=0
         ),
+        compiler_params=pltpu.CompilerParams(vmem_limit_bytes=14 * 1024 * 1024),
         name="shrink",
     )(*where, *operands, *after, *held)
 
@@ -291,7 +297,8 @@
     kv_heads,
 ):
     expand_refs = rest[:count]
-    attention_ref, cache_ref, expand_ref = rest[-3:]
+    attention_ref, cache_ref, token_ref, expand_ref = rest[-4:]
+    token_ref[...] = jnp.zeros_like(token_ref)
     tree_size, heads, head_size = query_ref.shape
     cached = key_ref.shape[0]
     per_group = heads // kv_heads
@@ -401,7 +408,7 @@
     aliases = {}
     if previous is not None:
         aliases = {len(operands): 0, len(operands) + 1: 1}
-        operands += list(previous)
+        operands += previous[:2]
         in_specs += [ANYWHERE] * 2
     cache_rows = 2 * kv_heads * tree_size
     return pl.pallas_call(
@@ -413,18 +420,20 @@
             out_specs=[
                 query_block,
                 pl.BlockSpec((cache_rows, head_size), lambda i, *refs: (spot(i, refs), 0)),
+                pl.BlockSpec((8, 128), lambda i, *refs: (0, 0)),
             ],
             scratch_shapes=[pltpu.VMEM((rank_size, columns), BF16)],
         ),
         out_shape=[
             jax.ShapeDtypeStruct((rows, heads, head_size), BF16),
             jax.ShapeDtypeStruct((rows * 2 * kv_heads, head_size), BF16),
+            jax.ShapeDtypeStruct((8, 128), F32),
         ],
         input_output_aliases=aliases,
-        compiler_params=pltpu.CompilerParams(vmem_limit_bytes=24 * 1024 * 1024),
         cost_estimate=pl.CostEstimate(
             flops=count * 900_000_000, bytes_accessed=count * 3_000_000, transcendentals=0
         ),
+        compiler_params=pltpu.CompilerParams(vmem_limit_bytes=16 * 1024 * 1024),
         name="finish",
     )(*operands)
 
@@ -481,16 +490,17 @@
 
     arrivals = [(first, second)]
     front = rear = (first, second)
+    table, weight_rows = tree_tables(
+        cache_lengths, tree_parents, head_size, heads_here, weight_rows, [first]
+    )
     for step in range(1, half):
         front = tuple(lax.ppermute(piece, "pool", onward) for piece in front)
         rear = tuple(lax.ppermute(piece, "pool", backward) for piece in rear)
         held = [front[1], rear[1]]
         if step == 1:
             here, away, *held = base_product(
-                core, hidden_states, weight_rows, kv_heads * kv_width, held
+                core, hidden_states, weight_rows, kv_heads * kv_width, [table], held
             )
-        if step == 2:
-            table, *held = tree_tables(cache_lengths, tree_parents, head_size, heads_here, held)
         front, rear = (front[0], held[0]), (rear[0], held[1])
         arrivals += [front, rear]
     arrivals.append(
@@ -509,7 +519,7 @@
     if pool_count == requests:
         slot = 0
         for group in (arrivals[:-3], arrivals[-3:]):
-            after = [] if outputs is None else [outputs[0]]
+            after = [] if outputs is None else [outputs[2]]
             held = [away] if outputs is None else []
             partial, *held = shrink_rows(
                 where, slot, hidden_states, group, tree_size, columns, cut, after, held
@@ -537,7 +547,7 @@
         )
         there = lax.ppermute(away, "tp", swap)
         outputs = finish((every[:1], every[None, :], every), 0, batch, there, shared, None)
-    attention, cache_rows = outputs
+    attention, cache_rows, _ = outputs
     tree_cache = (
         cache_rows.reshape(row_count, 2, heads_here, head_size)
         .transpose(0, 2, 1, 3)

time: 63.2 us -> 59.9 us (0.948)
  Pallas kernels: 27.9 us -> 22.2 us
  local copies, waits for them, and re-layouts: 4.91 us -> 8.21 us
  starting transfers between devices: 16.1 us -> 15.3 us
    ppermute x6, starting transfers between devices: 10.2 us -> 0.81 us  [per_device(): rear = tuple((lax.ppermute(piece, 'pool', backward) for piece in rear))]
    ppermute x6, starting transfers between devices: 3.89 us -> 12.5 us  [per_device(): front = tuple((lax.ppermute(piece, 'pool', onward) for piece in front))]
    unnamed x36 -> x40, local copies, waits for them, and re-layouts: 4.91 us -> 8.21 us
    ppermute x6, waiting for transfers between devices: 7.8 us -> 4.68 us  [per_device(): front = tuple((lax.ppermute(piece, 'pool', onward) for piece in front))]
    ppermute x6, waiting for transfers between devices: 3.95 us -> 6.95 us  [per_device(): rear = tuple((lax.ppermute(piece, 'pool', backward) for piece in rear))]
    pallas_call x1, Pallas kernels: 6.64 us -> 3.67 us  [base_product(): pl.pallas_call(functools.partial(base_kernel, held_count=len(held)), grid...]
    pallas_call x1, Pallas kernels: 1.86 us -> 0.17 us  [pack(): pl.pallas_call(functools.partial(pack_kernel, cut=cut, heads_here=heads_h...]
    pallas_call x1, Pallas kernels: 3.92 us -> 2.63 us  [tree_tables(): pl.pallas_call(functools.partial(tree_kernel, kv_heads=kv_heads), grid_sp...]
  transfers between devices with their start and end apart: 17 -> 17, of which waited for: 5 -> 6; matrix products, arithmetic and copies ran while one was open for 0% -> 0% of each run, Pallas kernels for 29% -> 23%
where the time goes in v5:
time: 59.9 us; the launch traced here: 59.6 us
  Pallas kernels  22.2 us (37%)
  starting transfers between devices  15.3 us (26%)
  waiting for transfers between devices  12.9 us (22%)
  local copies, waits for them, and re-layouts  8.21 us (14%)
  between operations  0.88 us (1%)
    ppermute x6, starting transfers between devices, per_device(): front = tuple((lax.ppermute(piece, 'pool', onward) for piece in front))  12.5 us
    pallas_call x2, Pallas kernels, finish(): pl.pallas_call(functools.partial(finish_kernel, count=count, slot=slot, k...  12 us
    unnamed x40, local copies, waits for them, and re-layouts  8.21 us
    ppermute x6, waiting for transfers between devices, per_device(): rear = tuple((lax.ppermute(piece, 'pool', backward) for piece in rear))  6.95 us
    ppermute x6, waiting for transfers between devices, per_device(): front = tuple((lax.ppermute(piece, 'pool', onward) for piece in front))  4.68 us
    pallas_call x2, Pallas kernels, shrink_rows(): pl.pallas_call(functools.partial(shrink_kernel, columns=columns, cut=cut,...  3.74 us
    pallas_call x1, Pallas kernels, base_product(): pl.pallas_call(functools.partial(base_kernel, held_count=len(held)), grid...  3.67 us
    pallas_call x1, Pallas kernels, tree_tables(): pl.pallas_call(functools.partial(tree_kernel, kv_heads=kv_heads), grid_sp...  2.63 us
  transfers between devices with their start and end apart: 17, of which 6 were waited for; matrix products, arithmetic and copies ran while one was open for 0% of the time, Pallas kernels for 23%

profile of v5, /device:TPU:0, one launch (start us, length us, event | category | flops | bytes accessed | tf_op | source)
XLA Modules:
  0.0 59.6 jit_solution(4593864717459627479)
XLA Ops:
  0.6 1.0 %copy-done.2 = bf16[1,2560,64]{1,2,0:T(8,128)(2,1)S(1)} copy-done((bf16[1,2560,64]{1,2,0:T(8,128)(2,1)S(1)}, bf16[1,2560,64]{1,2,0:T(8,128)(2,1)}, u32[]{:S(2)}) %copy-start.2) | copy-done | bytes 327704
  1.6 0.9 %copy-done.5 = bf16[1,64,4,256]{3,2,1,0:T(4,128)(2,1)S(1)} copy-done((bf16[1,64,4,256]{3,2,1,0:T(4,128)(2,1)S(1)}, bf16[1,64,4,256]{3,2,1,0:T(4,128)(2,1)}, u32[]{:S(2)}) %copy-start.5) | copy-done | bytes 131096
  2.5 0.2 pack.1
  2.7 3.1 %collective-permute-start = (bf16[64,1536]{1,0:T(8,128)(2,1)S(1)}, bf16[64,1536]{1,0:T(8,128)(2,1)}, u32[]{:S(2)}, u32[]{:S(2)}) collective-permute-start(bf16[64,1536]{1,0:T(8,128)(2,1)S(1)} %get-tuple-element.20.refs_2_), channel_id=1, source_target_pairs={{0,4},{4,8},{8,12},{12,14},{14,10},{10,6},{6,2},{2,0},{1,5},{5,9},... | collective-permute-start | bytes 589832 | tf_op jit(solution)/shard_map/ppermute | solution.py:497
  5.8 2.0 %collective-permute-start.2 = (bf16[64,1536]{1,0:T(8,128)(2,1)S(1)}, bf16[64,1536]{1,0:T(8,128)(2,1)S(1)}, u32[]{:S(2)}, u32[]{:S(2)}) collective-permute-start(bf16[64,1536]{1,0:T(8,128)(2,1)S(1)} %get-tuple-element.17.rest_0_.refs_1_), channel_id=1, source_target_pairs={{0,4},{4,8},{8,12},{12,14},{14,10},{10,6},{6,2},{2,0},{1,5},{5,9},... | collective-permute-start | bytes 589832 | tf_op jit(solution)/shard_map/ppermute | solution.py:497
  7.8 2.5 %copy-done.1 = bf16[2560,4,256]{2,1,0:T(4,128)(2,1)S(1)} copy-done((bf16[2560,4,256]{2,1,0:T(4,128)(2,1)S(1)}, bf16[2560,4,256]{2,1,0:T(4,128)(2,1)}, u32[]{:S(2)}) %copy-start.1) | copy-done | bytes 5242904
  10.3 0.7 %copy-done.7 = s32[8,48]{1,0:T(8,128)S(1)} copy-done((s32[8,48]{1,0:T(8,128)S(1)}, s32[8,48]{1,0:T(8,128)}, u32[]{:S(2)}) %copy-start.7) | copy-done | bytes 1560
  11.0 0.7 %copy-done.9 = s32[8]{0:T(128)S(1)} copy-done((s32[8]{0:T(128)S(1)}, s32[8]{0:T(128)}, u32[]{:S(2)}) %copy-start.9) | copy-done | bytes 56
  11.7 0.7 %copy-done.11 = f32[1,128]{1,0:T(1,128)S(1)} copy-done((f32[1,128]{1,0:T(1,128)S(1)}, f32[1,128]{1,0:T(1,128)}, u32[]{:S(2)}) %copy-start.11) | copy-done | bytes 536
  12.3 2.6 %tree.1 = (f32[384,384]{1,0:T(8,128)S(1)}, bf16[20480,128]{1,0:T(8,128)(2,1)S(1)}) custom-call(s32[8]{0:T(128)S(1)} %copy-done.9, s32[8,48]{1,0:T(8,128)S(1)} %copy-done.7, f32[1,128]{1,0:T(1,128)S(1)} %copy-done.11, bf16[20480,128]{1,0:T(8,128)(2,1)S(1)} %bitcast.23, bf16[64,1536]{1,0:T(8,128)(2,1)S(1)} %get-tuple-element.17.rest_0_.refs_1_), custom_call_target="tpu_custom_call" | custom-call | flops 1000000000 | bytes 8000000 | tf_op jit(solution)/shard_map/tree/pallas_call | solution.py:218
  15.0 3.7 %base.1 = (f32[384,512]{1,0:T(8,128)S(1)}, f32[384,512]{1,0:T(8,128)S(1)}, bf16[64,1536]{1,0:T(8,128)(2,1)}, bf16[64,1536]{1,0:T(8,128)(2,1)}) custom-call(s32[1]{0:T(128)} %bitcast.1.core_ref, bf16[384,2560]{1,0:T(8,128)(2,1)S(1)} %copy-done, bf16[20480,128]{1,0:T(8,128)(2,1)S(1)} %get-tuple-element.18.weight_ref, ...), custom_call_target="tpu_custom_call", output_to_operand_aliasing={{2}: (4, {}), {3}: (5, {})} | custom-call | flops 4000000000 | bytes 9000000 | tf_op jit(solution)/shard_map/base/pallas_call | solution.py:142
  18.7 0.9 %copy-done.18 = f32[384,512]{1,0:T(8,128)} copy-done((f32[384,512]{1,0:T(8,128)}, f32[384,512]{1,0:T(8,128)S(1)}, u32[]{:S(2)}) %copy-start.18) | copy-done | bytes 786456
  19.6 2.0 %collective-permute-start.5 = (bf16[64,1536]{1,0:T(8,128)(2,1)}, bf16[64,1536]{1,0:T(8,128)(2,1)S(1)}, u32[]{:S(2)}, u32[]{:S(2)}) collective-permute-start(bf16[64,1536]{1,0:T(8,128)(2,1)} %get-tuple-element.22.refs_5_), channel_id=1, source_target_pairs={{0,4},{4,8},{8,12},{12,14},{14,10},{10,6},{6,2},{2,0},{1,5},{5,9},... | collective-permute-start | bytes 589832 | tf_op jit(solution)/shard_map/ppermute | solution.py:497
  21.6 2.0 %collective-permute-start.4 = (bf16[64,1536]{1,0:T(8,128)(2,1)S(1)}, bf16[64,1536]{1,0:T(8,128)(2,1)}, u32[]{:S(2)}, u32[]{:S(2)}) collective-permute-start(bf16[64,1536]{1,0:T(8,128)(2,1)S(1)} %collective-permute-done.2.refs_4_.rest_1_), channel_id=1, source_target_pairs={{0,4},{4,8},{8,12},{12,14},{14,10},{10,6},{6,2},{2,0},{1,5},{5,9},... | collective-permute-start | bytes 589832 | tf_op jit(solution)/shard_map/ppermute | solution.py:497
  23.7 4.0 %collective-permute-done.5.refs_11_ = bf16[64,1536]{1,0:T(8,128)(2,1)S(1)} collective-permute-done((bf16[64,1536]{1,0:T(8,128)(2,1)}, bf16[64,1536]{1,0:T(8,128)(2,1)S(1)}, u32[]{:S(2)}, u32[]{:S(2)}) %collective-permute-start.5) | collective-permute-done | bytes 196640 | tf_op jit(solution)/shard_map/ppermute | solution.py:497
  27.6 1.6 %collective-permute-done.7.refs_14_ = bf16[64,1536]{1,0:T(8,128)(2,1)} collective-permute-done((bf16[64,1536]{1,0:T(8,128)(2,1)}, bf16[64,1536]{1,0:T(8,128)(2,1)}, u32[]{:S(2)}, u32[]{:S(2)}) %collective-permute-start.7) | collective-permute-done | bytes 196640 | tf_op jit(solution)/shard_map/ppermute | solution.py:498
  29.3 0.6 %collective-permute-done.4.refs_10_.rest_3_ = bf16[64,1536]{1,0:T(8,128)(2,1)} collective-permute-done((bf16[64,1536]{1,0:T(8,128)(2,1)S(1)}, bf16[64,1536]{1,0:T(8,128)(2,1)}, u32[]{:S(2)}, u32[]{:S(2)}) %collective-permute-start.4) | collective-permute-done | bytes 196640 | tf_op jit(solution)/shard_map/ppermute | solution.py:497
  29.9 1.5 %collective-permute-done.6.refs_13_.rest_4_ = bf16[64,1536]{1,0:T(8,128)(2,1)} collective-permute-done((bf16[64,1536]{1,0:T(8,128)(2,1)S(1)}, bf16[64,1536]{1,0:T(8,128)(2,1)}, u32[]{:S(2)}, u32[]{:S(2)}) %collective-permute-start.6) | collective-permute-done | bytes 196640 | tf_op jit(solution)/shard_map/ppermute | solution.py:498
  31.4 0.9 %copy-done.4 = bf16[64,1536]{1,0:T(8,128)(2,1)S(1)} copy-done((bf16[64,1536]{1,0:T(8,128)(2,1)S(1)}, bf16[64,1536]{1,0:T(8,128)(2,1)}, u32[]{:S(2)}) %copy-start.4) | copy-done | bytes 196632
  32.4 2.8 %shrink.2 = (f32[5,48,64]{2,1,0:T(8,128)S(1)}, f32[384,512]{1,0:T(8,128)S(1)}) custom-call(s32[1]{0:T(128)} %bitcast.me_ref, s32[8,8]{1,0:T(8,128)S(1)} %copy-done.6, s32[8]{0:T(128)S(1)} %copy-done.8, bf16[384,2560]{1,0:T(8,128)(2,1)S(1)} %copy-done, bf16[64,1536]{1,0:T(8,128)(2,1)S(1)} %get-tuple-element.17.rest_0_.refs_1_, ...), custom_call_target="tpu_custom_call", output_to_operand_aliasing={{1}: (18, {})} | custom-call | flops 1500000000 | bytes 10000000 | tf_op jit(solution)/shard_map/shrink/pallas_call | solution.py:261
  35.2 0.3 collective-permute-start.12
  35.5 1.7 %collective-permute-start.9 = (bf16[64,1536]{1,0:T(8,128)(2,1)}, bf16[64,1536]{1,0:T(8,128)(2,1)S(1)}, u32[]{:S(2)}, u32[]{:S(2)}) collective-permute-start(bf16[64,1536]{1,0:T(8,128)(2,1)} %collective-permute-done.4.refs_10_.rest_3_), channel_id=1, source_target_pairs={{0,4},{4,8},{8,12},{12,14},{14,10},{10,6},{6,2},{2,0},{1,5},{5,9},... | collective-permute-start | bytes 589832 | tf_op jit(solution)/shard_map/ppermute | solution.py:497
  37.2 1.6 %collective-permute-start.10 = (bf16[64,1536]{1,0:T(8,128)(2,1)S(1)}, bf16[64,1536]{1,0:T(8,128)(2,1)S(1)}, u32[]{:S(2)}, u32[]{:S(2)}) collective-permute-start(bf16[64,1536]{1,0:T(8,128)(2,1)S(1)} %collective-permute-done.5.refs_11_), channel_id=1, source_target_pairs={{0,4},{4,8},{8,12},{12,14},{14,10},{10,6},{6,2},{2,0},{1,5},{5,9},... | collective-permute-start | bytes 589832 | tf_op jit(solution)/shard_map/ppermute | solution.py:497
  38.8 0.4 collective-permute-start.11
  39.3 3.9 %collective-permute-done.12.refs_5_ = bf16[64,1536]{1,0:T(8,128)(2,1)S(1)} collective-permute-done((bf16[64,1536]{1,0:T(8,128)(2,1)}, bf16[64,1536]{1,0:T(8,128)(2,1)S(1)}, u32[]{:S(2)}, u32[]{:S(2)}) %collective-permute-start.12) | collective-permute-done | bytes 196640 | tf_op jit(solution)/shard_map/ppermute | solution.py:498
  43.1 0.3 collective-permute-start.14
  43.4 0.0 collective-permute-done.9.refs_1_.rest_0_
  43.5 1.7 %collective-permute-start.13 = (bf16[64,1536]{1,0:T(8,128)(2,1)S(1)}, bf16[64,1536]{1,0:T(8,128)(2,1)S(1)}, u32[]{:S(2)}, u32[]{:S(2)}) collective-permute-start(bf16[64,1536]{1,0:T(8,128)(2,1)S(1)} %collective-permute-done.9.refs_1_.rest_0_), channel_id=1, source_target_pairs={{0,4},{4,8},{8,12},{12,14},{14,10},{10,6},{6,2},{2,0},{1,5},{5,9},... | collective-permute-start | bytes 589832 | tf_op jit(solution)/shard_map/ppermute | solution.py:507
  45.3 7.5 %finish.2 = (bf16[384,16,128]{2,1,0:T(8,128)(2,1)}, bf16[1536,128]{1,0:T(8,128)(2,1)}, f32[8,128]{1,0:T(8,128)S(1)}) custom-call(s32[1]{0:T(128)} %bitcast.me_ref, s32[8,8]{1,0:T(8,128)S(1)} %copy-done.6, s32[8]{0:T(128)S(1)} %copy-done.8, s32[8]{0:T(128)S(1)} %copy-done.10, f32[384,512]{1,0:T(8,128)S(1)} %copy-done.19, ...), custom_call_target="tpu_custom_call" | custom-call | flops 4499999744 | bytes 15000000 | tf_op jit(solution)/shard_map/finish/pallas_call | solution.py:414
  52.8 1.0 %shrink.3.shrunk_here_ref = f32[3,48,64]{2,1,0:T(8,128)S(1)} custom-call(s32[1]{0:T(128)} %bitcast.me_ref, s32[8,8]{1,0:T(8,128)S(1)} %copy-done.6, s32[8]{0:T(128)S(1)} %copy-done.8, bf16[384,2560]{1,0:T(8,128)(2,1)S(1)} %copy-done, bf16[64,1536]{1,0:T(8,128)(2,1)S(1)} %collective-permute-done.9.refs_1_.rest_0_, ...), custom_call_target="tpu_custom_call" | custom-call | flops 900000000 | bytes 6000000 | tf_op jit(solution)/shard_map/shrink/pallas_call | solution.py:261
  53.8 1.3 %collective-permute-done.16.shrunk_there_ref = f32[3,48,64]{2,1,0:T(8,128)S(1)} collective-permute-done((f32[3,48,64]{2,1,0:T(8,128)S(1)}, f32[3,48,64]{2,1,0:T(8,128)S(1)}, u32[]{:S(2)}, u32[]{:S(2)}) %collective-permute-start.16) | collective-permute-done | bytes 36896 | tf_op jit(solution)/shard_map/ppermute | solution.py:529
  55.1 4.5 %finish.3 = (bf16[384,16,128]{2,1,0:T(8,128)(2,1)}, bf16[1536,128]{1,0:T(8,128)(2,1)}, f32[8,128]{1,0:T(8,128)}) custom-call(s32[1]{0:T(128)} %bitcast.me_ref, s32[8,8]{1,0:T(8,128)S(1)} %copy-done.6, s32[8]{0:T(128)S(1)} %copy-done.8, s32[8]{0:T(128)S(1)} %copy-done.10, f32[384,512]{1,0:T(8,128)S(1)} %copy-done.19, ...), custom_call_target="tpu_custom_call", output_to_operand_aliasing={{0}: (16, {}), {1}: (17, {})} | custom-call | flops 2700000000 | bytes 9000000 | tf_op jit(solution)/shard_map/finish/pallas_call | solution.py:414
  (49 shorter events, 0.2 us)
Async XLA Ops:
  0.6 1.0 %copy-start.2 = (bf16[1,2560,64]{1,2,0:T(8,128)(2,1)S(1)}, bf16[1,2560,64]{1,2,0:T(8,128)(2,1)}, u32[]{:S(2)}) copy-start(bf16[1,2560,64]{1,2,0:T(8,128)(2,1)} %param.15) | copy-start | bytes 983044
  2.7 12.3 %copy-start.3 = (bf16[64,1536]{1,0:T(8,128)(2,1)}, bf16[64,1536]{1,0:T(8,128)(2,1)S(1)}, u32[]{:S(2)}) copy-start(bf16[64,1536]{1,0:T(8,128)(2,1)S(1)} %get-tuple-element.20.refs_2_) | copy-start | bytes 589828
  2.7 12.3 %collective-permute-start = (bf16[64,1536]{1,0:T(8,128)(2,1)S(1)}, bf16[64,1536]{1,0:T(8,128)(2,1)}, u32[]{:S(2)}, u32[]{:S(2)}) collective-permute-start(bf16[64,1536]{1,0:T(8,128)(2,1)S(1)} %get-tuple-element.20.refs_2_), channel_id=1, source_target_pairs={{0,4},{4,8},{8,12},{12,14},{14,10},{10,6},{6,2},{2,0},{1,5},{5,9},... | collective-permute-start | bytes 589832 | tf_op jit(solution)/shard_map/ppermute | solution.py:497
  5.8 9.2 %collective-permute-start.1 = (bf16[64,1536]{1,0:T(8,128)(2,1)S(1)}, bf16[64,1536]{1,0:T(8,128)(2,1)}, u32[]{:S(2)}, u32[]{:S(2)}) collective-permute-start(bf16[64,1536]{1,0:T(8,128)(2,1)S(1)} %get-tuple-element.20.refs_2_), channel_id=1, source_target_pairs={{4,0},{8,4},{12,8},{14,12},{10,14},{6,10},{2,6},{0,2},{5,1},{9,5},... | collective-permute-start | bytes 589832 | tf_op jit(solution)/shard_map/ppermute | solution.py:498
  5.8 15.8 %collective-permute-start.2 = (bf16[64,1536]{1,0:T(8,128)(2,1)S(1)}, bf16[64,1536]{1,0:T(8,128)(2,1)S(1)}, u32[]{:S(2)}, u32[]{:S(2)}) collective-permute-start(bf16[64,1536]{1,0:T(8,128)(2,1)S(1)} %get-tuple-element.17.rest_0_.refs_1_), channel_id=1, source_target_pairs={{0,4},{4,8},{8,12},{12,14},{14,10},{10,6},{6,2},{2,0},{1,5},{5,9},... | collective-permute-start | bytes 589832 | tf_op jit(solution)/shard_map/ppermute | solution.py:497
  7.8 15.8 %collective-permute-start.3 = (bf16[64,1536]{1,0:T(8,128)(2,1)S(1)}, bf16[64,1536]{1,0:T(8,128)(2,1)S(1)}, u32[]{:S(2)}, u32[]{:S(2)}) collective-permute-start(bf16[64,1536]{1,0:T(8,128)(2,1)S(1)} %get-tuple-element.17.rest_0_.refs_1_), channel_id=1, source_target_pairs={{4,0},{8,4},{12,8},{14,12},{10,14},{6,10},{2,6},{0,2},{5,1},{9,5},... | collective-permute-start | bytes 589832 | tf_op jit(solution)/shard_map/ppermute | solution.py:498
  7.8 2.5 %copy-start.1 = (bf16[2560,4,256]{2,1,0:T(4,128)(2,1)S(1)}, bf16[2560,4,256]{2,1,0:T(4,128)(2,1)}, u32[]{:S(2)}) copy-start(bf16[2560,4,256]{2,1,0:T(4,128)(2,1)} %param.14) | copy-start | bytes 15728644
  12.3 2.7 %copy-start = (bf16[384,2560]{1,0:T(8,128)(2,1)S(1)}, bf16[384,2560]{1,0:T(8,128)(2,1)}, u32[]{:S(2)}) copy-start(bf16[384,2560]{1,0:T(8,128)(2,1)} %refs_6_.3) | copy-start | bytes 5898244
  15.0 3.7 %copy-start.13 = (f32[384,384]{1,0:T(8,128)}, f32[384,384]{1,0:T(8,128)S(1)}, u32[]{:S(2)}) copy-start(f32[384,384]{1,0:T(8,128)S(1)} %get-tuple-element.19.rest_0_.table_ref) | copy-start | bytes 1769476
  15.0 16.4 %copy-start.6 = (s32[8,8]{1,0:T(8,128)S(1)}, s32[8,8]{1,0:T(8,128)}, u32[]{:S(2)}) copy-start(s32[8,8]{1,0:T(8,128)} %constant.12.clone.owner_ref) | copy-start | bytes 772
  15.0 16.4 %copy-start.8 = (s32[8]{0:T(128)S(1)}, s32[8]{0:T(128)}, u32[]{:S(2)}) copy-start(s32[8]{0:T(128)} %adapter_ref.7) | copy-start | bytes 100
  19.6 8.1 %collective-permute-start.5 = (bf16[64,1536]{1,0:T(8,128)(2,1)}, bf16[64,1536]{1,0:T(8,128)(2,1)S(1)}, u32[]{:S(2)}, u32[]{:S(2)}) collective-permute-start(bf16[64,1536]{1,0:T(8,128)(2,1)} %get-tuple-element.22.refs_5_), channel_id=1, source_target_pairs={{0,4},{4,8},{8,12},{12,14},{14,10},{10,6},{6,2},{2,0},{1,5},{5,9},... | collective-permute-start | bytes 589832 | tf_op jit(solution)/shard_map/ppermute | solution.py:497
  21.6 7.7 %collective-permute-start.7 = (bf16[64,1536]{1,0:T(8,128)(2,1)}, bf16[64,1536]{1,0:T(8,128)(2,1)}, u32[]{:S(2)}, u32[]{:S(2)}) collective-permute-start(bf16[64,1536]{1,0:T(8,128)(2,1)} %get-tuple-element.23.refs_8_), channel_id=1, source_target_pairs={{4,0},{8,4},{12,8},{14,12},{10,14},{6,10},{2,6},{0,2},{5,1},{9,5},... | collective-permute-start | bytes 589832 | tf_op jit(solution)/shard_map/ppermute | solution.py:498
  21.6 8.3 %collective-permute-start.4 = (bf16[64,1536]{1,0:T(8,128)(2,1)S(1)}, bf16[64,1536]{1,0:T(8,128)(2,1)}, u32[]{:S(2)}, u32[]{:S(2)}) collective-permute-start(bf16[64,1536]{1,0:T(8,128)(2,1)S(1)} %collective-permute-done.2.refs_4_.rest_1_), channel_id=1, source_target_pairs={{0,4},{4,8},{8,12},{12,14},{14,10},{10,6},{6,2},{2,0},{1,5},{5,9},... | collective-permute-start | bytes 589832 | tf_op jit(solution)/shard_map/ppermute | solution.py:497
  23.7 7.7 %collective-permute-start.6 = (bf16[64,1536]{1,0:T(8,128)(2,1)S(1)}, bf16[64,1536]{1,0:T(8,128)(2,1)}, u32[]{:S(2)}, u32[]{:S(2)}) collective-permute-start(bf16[64,1536]{1,0:T(8,128)(2,1)S(1)} %collective-permute-done.3.refs_7_.rest_2_), channel_id=1, source_target_pairs={{4,0},{8,4},{12,8},{14,12},{10,14},{6,10},{2,6},{0,2},{5,1},{9,5},... | collective-permute-start | bytes 589832 | tf_op jit(solution)/shard_map/ppermute | solution.py:498
  31.4 0.9 %copy-start.4 = (bf16[64,1536]{1,0:T(8,128)(2,1)S(1)}, bf16[64,1536]{1,0:T(8,128)(2,1)}, u32[]{:S(2)}) copy-start(bf16[64,1536]{1,0:T(8,128)(2,1)} %copy-done.3) | copy-start | bytes 589828
  32.3 12.9 %copy-start.10 = (s32[8]{0:T(128)S(1)}, s32[8]{0:T(128)}, u32[]{:S(2)}) copy-start(s32[8]{0:T(128)} %length_ref.5) | copy-start | bytes 100
  32.3 12.9 %copy-start.12 = (bf16[384,16,128]{2,1,0:T(8,128)(2,1)S(1)}, bf16[384,16,128]{2,1,0:T(8,128)(2,1)}, u32[]{:S(2)}) copy-start(bf16[384,16,128]{2,1,0:T(8,128)(2,1)} %query_ref.3) | copy-start | bytes 4718596
  32.3 12.9 %copy-start.14 = (f32[384,384]{1,0:T(8,128)S(1)}, f32[384,384]{1,0:T(8,128)}, u32[]{:S(2)}) copy-start(f32[384,384]{1,0:T(8,128)} %copy-done.13) | copy-start | bytes 1769476
  32.3 12.9 %copy-start.15 = (bf16[8,128,2,128]{3,2,1,0:T(2,128)(2,1)S(1)}, bf16[8,128,2,128]{3,2,1,0:T(2,128)(2,1)}, u32[]{:S(2)}) copy-start(bf16[8,128,2,128]{3,2,1,0:T(2,128)(2,1)} %param.21) | copy-start | bytes 1572868
  32.3 12.9 %copy-start.16 = (bf16[8,128,2,128]{3,2,1,0:T(2,128)(2,1)S(1)}, bf16[8,128,2,128]{3,2,1,0:T(2,128)(2,1)}, u32[]{:S(2)}) copy-start(bf16[8,128,2,128]{3,2,1,0:T(2,128)(2,1)} %param.22) | copy-start | bytes 1572868
  32.3 12.9 %copy-start.17 = (f32[128]{0:T(128)S(1)}, f32[128]{0:T(128)}, u32[]{:S(2)}) copy-start(f32[128]{0:T(128)} %param.23) | copy-start | bytes 1540
  32.4 12.9 %copy-start.19 = (f32[384,512]{1,0:T(8,128)S(1)}, f32[384,512]{1,0:T(8,128)}, u32[]{:S(2)}) copy-start(f32[384,512]{1,0:T(8,128)} %copy-done.18) | copy-start | bytes 2359300
  35.1 10.1 %collective-permute-start.8 = (f32[384,512]{1,0:T(8,128)S(1)}, f32[384,512]{1,0:T(8,128)S(1)}, u32[]{:S(2)}, u32[]{:S(2)}) collective-permute-start(f32[384,512]{1,0:T(8,128)S(1)} %get-tuple-element.25), channel_id=1, source_target_pairs={{0,1},{1,0},{2,3},{3,2},{4,5},{5,4},{6,7},{7,6},{8,9},{9,8},{10,11... | collective-permute-start | bytes 2359304 | tf_op jit(solution)/shard_map/ppermute | solution.py:528
  35.2 8.0 %collective-permute-start.12 = (bf16[64,1536]{1,0:T(8,128)(2,1)}, bf16[64,1536]{1,0:T(8,128)(2,1)S(1)}, u32[]{:S(2)}, u32[]{:S(2)}) collective-permute-start(bf16[64,1536]{1,0:T(8,128)(2,1)} %collective-permute-done.7.refs_14_), channel_id=1, source_target_pairs={{4,0},{8,4},{12,8},{14,12},{10,14},{6,10},{2,6},{0,2},{5,1},{9,5},... | collective-permute-start | bytes 589832 | tf_op jit(solution)/shard_map/ppermute | solution.py:498
  35.5 8.0 %collective-permute-start.9 = (bf16[64,1536]{1,0:T(8,128)(2,1)}, bf16[64,1536]{1,0:T(8,128)(2,1)S(1)}, u32[]{:S(2)}, u32[]{:S(2)}) collective-permute-start(bf16[64,1536]{1,0:T(8,128)(2,1)} %collective-permute-done.4.refs_10_.rest_3_), channel_id=1, source_target_pairs={{0,4},{4,8},{8,12},{12,14},{14,10},{10,6},{6,2},{2,0},{1,5},{5,9},... | collective-permute-start | bytes 589832 | tf_op jit(solution)/shard_map/ppermute | solution.py:497
  37.2 1.6 %collective-permute-start.15 = (f32[5,48,64]{2,1,0:T(8,128)S(1)}, f32[5,48,64]{2,1,0:T(8,128)S(1)}, u32[]{:S(2)}, u32[]{:S(2)}) collective-permute-start(f32[5,48,64]{2,1,0:T(8,128)S(1)} %get-tuple-element.26.shrunk_here_ref), channel_id=1, source_target_pairs={{0,1},{1,0},{2,3},{3,2},{4,5},{5,4},{6,7},{7,6},{8,9},{9,8},{10,11... | collective-permute-start | bytes 184328 | tf_op jit(solution)/shard_map/ppermute | solution.py:529
  37.2 15.5 %collective-permute-start.10 = (bf16[64,1536]{1,0:T(8,128)(2,1)S(1)}, bf16[64,1536]{1,0:T(8,128)(2,1)S(1)}, u32[]{:S(2)}, u32[]{:S(2)}) collective-permute-start(bf16[64,1536]{1,0:T(8,128)(2,1)S(1)} %collective-permute-done.5.refs_11_), channel_id=1, source_target_pairs={{0,4},{4,8},{8,12},{12,14},{14,10},{10,6},{6,2},{2,0},{1,5},{5,9},... | collective-permute-start | bytes 589832 | tf_op jit(solution)/shard_map/ppermute | solution.py:497
  38.8 13.9 %collective-permute-start.11 = (bf16[64,1536]{1,0:T(8,128)(2,1)}, bf16[64,1536]{1,0:T(8,128)(2,1)S(1)}, u32[]{:S(2)}, u32[]{:S(2)}) collective-permute-start(bf16[64,1536]{1,0:T(8,128)(2,1)} %collective-permute-done.6.refs_13_.rest_4_), channel_id=1, source_target_pairs={{4,0},{8,4},{12,8},{14,12},{10,14},{6,10},{2,6},{0,2},{5,1},{9,5},... | collective-permute-start | bytes 589832 | tf_op jit(solution)/shard_map/ppermute | solution.py:498
  43.1 9.6 %collective-permute-start.14 = (bf16[64,1536]{1,0:T(8,128)(2,1)S(1)}, bf16[64,1536]{1,0:T(8,128)(2,1)S(1)}, u32[]{:S(2)}, u32[]{:S(2)}) collective-permute-start(bf16[64,1536]{1,0:T(8,128)(2,1)S(1)} %collective-permute-done.12.refs_5_), channel_id=1, source_target_pairs={{4,0},{8,4},{12,8},{14,12},{10,14},{6,10},{2,6},{0,2},{5,1},{9,5},... | collective-permute-start | bytes 589832 | tf_op jit(solution)/shard_map/ppermute | solution.py:507
  43.5 9.3 %collective-permute-start.13 = (bf16[64,1536]{1,0:T(8,128)(2,1)S(1)}, bf16[64,1536]{1,0:T(8,128)(2,1)S(1)}, u32[]{:S(2)}, u32[]{:S(2)}) collective-permute-start(bf16[64,1536]{1,0:T(8,128)(2,1)S(1)} %collective-permute-done.9.refs_1_.rest_0_), channel_id=1, source_target_pairs={{0,4},{4,8},{8,12},{12,14},{14,10},{10,6},{6,2},{2,0},{1,5},{5,9},... | collective-permute-start | bytes 589832 | tf_op jit(solution)/shard_map/ppermute | solution.py:507
  53.8 1.3 %collective-permute-start.16 = (f32[3,48,64]{2,1,0:T(8,128)S(1)}, f32[3,48,64]{2,1,0:T(8,128)S(1)}, u32[]{:S(2)}, u32[]{:S(2)}) collective-permute-start(f32[3,48,64]{2,1,0:T(8,128)S(1)} %shrink.3.shrunk_here_ref), channel_id=1, source_target_pairs={{0,1},{1,0},{2,3},{3,2},{4,5},{5,4},{6,7},{7,6},{8,9},{9,8},{10,11... | collective-permute-start | bytes 110600 | tf_op jit(solution)/shard_map/ppermute | solution.py:529
  (5 other events, 3.8 us)

commit v6 on v5

--- a/solution.py
+++ b/solution.py
@@ -234,17 +234,19 @@
     )(cache_lengths, tree_parents, frequency, weight_rows, *after)
 
 
-def shrink_kernel(me_ref, owner_ref, adapter_ref, *refs, columns, cut, held_count):
-    output_ref = refs[len(refs) - held_count - 1]
+def shrink_kernel(me_ref, owner_ref, adapter_ref, *refs, columns, cut):
+    output_ref = refs[-1]
     contract = (((1,), (1,)), ((), ()))
     for b in range(output_ref.shape[0]):
-        hidden_ref, one_ref, two_ref = refs[3 * b : 3 * b + 3]
-        output_ref[b] = lax.dot_general(
+        hidden_ref, away_ref, one_ref, two_ref = refs[4 * b : 4 * b + 4]
+        output_ref[b, :, :columns] = away_ref[...]
+        partial = lax.dot_general(
             hidden_ref[:, :cut], one_ref[:, columns:], contract, preferred_element_type=F32
         ) + lax.dot_general(hidden_ref[:, cut:], two_ref[...], contract, preferred_element_type=F32)
-
-
-def shrink_rows(where, slot, hidden_states, pieces, tree_size, columns, cut, after, held):
+        output_ref[b, :, columns:] = jnp.concatenate([partial, jnp.zeros_like(partial)], 1)
+
+
+def shrink_rows(where, slot, hidden_states, away, pieces, tree_size, columns, cut, after):
     rank_size = pieces[0][0].shape[0]
     in_specs, operands = [], []
     for b, (one, two) in enumerate(pieces):
@@ -253,28 +255,30 @@
                 (tree_size, hidden_states.shape[1]),
                 lambda i, *refs, b=b: (request_at(refs, slot + b), 0),
             ),
+            pl.BlockSpec(
+                (tree_size, columns), lambda i, *refs, b=b: (request_at(refs, slot + b), 0)
+            ),
             pl.BlockSpec(one.shape, lambda i, *refs: (0, 0)),
             pl.BlockSpec(two.shape, lambda i, *refs: (0, 0)),
         ]
-        operands += [hidden_states, one, two]
+        operands += [hidden_states, away, one, two]
     count = len(pieces)
+    width = columns + 2 * rank_size
     return pl.pallas_call(
-        functools.partial(shrink_kernel, columns=columns, cut=cut, held_count=len(held)),
+        functools.partial(shrink_kernel, columns=columns, cut=cut),
         grid_spec=pltpu.PrefetchScalarGridSpec(
             num_scalar_prefetch=3,
             grid=(1,),
-            in_specs=in_specs + [ANYWHERE] * (len(after) + len(held)),
-            out_specs=[pl.BlockSpec((count, tree_size, rank_size), lambda i, *refs: (0, 0, 0))]
-            + [ANYWHERE] * len(held),
-        ),
-        out_shape=[jax.ShapeDtypeStruct((count, tree_size, rank_size), F32)] + shapes_of(held),
-        input_output_aliases={3 + len(operands) + len(after) + k: 1 + k for k in range(len(held))},
+            in_specs=in_specs + [ANYWHERE] * len(after),
+            out_specs=pl.BlockSpec((count, tree_size, width), lambda i, *refs: (0, 0, 0)),
+        ),
+        out_shape=jax.ShapeDtypeStruct((count, tree_size, width), F32),
         cost_estimate=pl.CostEstimate(
-            flops=count * 300_000_000, bytes_accessed=count * 2_000_000, transcendentals=0
+            flops=count * 30000000, bytes_accessed=count * 200000, transcendentals=0
         ),
         compiler_params=pltpu.CompilerParams(vmem_limit_bytes=14 * 1024 * 1024),
         name="shrink",
-    )(*where, *operands, *after, *held)
+    )(*where, *operands, *after)
 
 
 def finish_kernel(
@@ -283,7 +287,6 @@
     adapter_ref,
     length_ref,
     here_ref,
-    there_ref,
     shrunk_here_ref,
     shrunk_there_ref,
     table_ref,
@@ -317,14 +320,15 @@
 
         expand = expand_ref[...]
     length = length_ref[request_at((me_ref, owner_ref, adapter_ref), slot + pl.program_id(0))]
-    shrunk = shrunk_here_ref[0] + shrunk_there_ref[0]
+    ranks = slice(columns, columns + expand.shape[0])
+    shrunk = shrunk_here_ref[0, :, ranks] + shrunk_there_ref[0, :, ranks]
     high = shrunk.astype(BF16)
     left = shrunk - high.astype(F32)
     middle = left.astype(BF16)
     low = (left - middle.astype(F32)).astype(BF16)
     terms = jnp.dot(jnp.concatenate([low, middle, high], 0), expand, preferred_element_type=F32)
     delta = terms[:tree_size] + terms[tree_size : 2 * tree_size] + terms[2 * tree_size :]
-    projected = (here_ref[...] + there_ref[...]) + delta
+    projected = (here_ref[...] + shrunk_there_ref[0, :, :columns]) + delta
     cosine = table_ref[:, :head_size]
     sine = table_ref[:, head_size : 2 * head_size]
     gain = gain_ref[...]
@@ -375,17 +379,18 @@
     ).astype(BF16)
 
 
-def finish(where, slot, batch, there, shared, previous):
+def finish(where, slot, batch, shared, previous):
     shrunk_here, shrunk_there, pieces = batch
     lengths, gain, here, table, queries, key_rows, value_rows = shared
     spot = lambda i, refs: request_at(refs[:3], slot + i)
-    count, tree_size, rank_size = shrunk_here.shape
+    count, tree_size, width = shrunk_here.shape
+    rank_size = pieces[0].shape[0]
     requests = lengths.shape[0]
     rows, heads, head_size = queries.shape
     columns = here.shape[1]
     kv_heads = columns // (2 * head_size)
     row_block = lambda width: pl.BlockSpec((tree_size, width), lambda i, *refs: (spot(i, refs), 0))
-    shrunk_block = pl.BlockSpec((1, tree_size, rank_size), lambda i, *refs: (i, 0, 0))
+    shrunk_block = pl.BlockSpec((1, tree_size, width), lambda i, *refs: (i, 0, 0))
     cached_block = pl.BlockSpec(
         (key_rows.shape[0] // requests, head_size), lambda i, *refs: (spot(i, refs), 0)
     )
@@ -393,7 +398,6 @@
         (tree_size, heads, head_size), lambda i, *refs: (spot(i, refs), 0, 0)
     )
     in_specs = [
-        row_block(columns),
         row_block(columns),
         shrunk_block,
         shrunk_block,
@@ -403,7 +407,7 @@
         cached_block,
         cached_block,
     ] + [pl.BlockSpec((rank_size, columns), lambda i, *refs: (0, 0))] * count
-    operands = [*where, lengths, here, there, shrunk_here, shrunk_there, table, gain, queries]
+    operands = [*where, lengths, here, shrunk_here, shrunk_there, table, gain, queries]
     operands += [key_rows, value_rows, *pieces]
     aliases = {}
     if previous is not None:
@@ -431,7 +435,7 @@
         ],
         input_output_aliases=aliases,
         cost_estimate=pl.CostEstimate(
-            flops=count * 900_000_000, bytes_accessed=count * 3_000_000, transcendentals=0
+            flops=count * 90000000, bytes_accessed=count * 300000, transcendentals=0
         ),
         compiler_params=pltpu.CompilerParams(vmem_limit_bytes=16 * 1024 * 1024),
         name="finish",
@@ -517,21 +521,25 @@
     )
     outputs = None
     if pool_count == requests:
+        near = 3
+        groups = [
+            (arrivals[:near], []),
+            (arrivals[near:-3], []),
+            (arrivals[-3:], []),
+        ]
         slot = 0
-        for group in (arrivals[:-3], arrivals[-3:]):
-            after = [] if outputs is None else [outputs[2]]
-            held = [away] if outputs is None else []
-            partial, *held = shrink_rows(
-                where, slot, hidden_states, group, tree_size, columns, cut, after, held
+        for group, after in groups:
+            if outputs is not None:
+                after = after + [outputs[2]]
+            partial = shrink_rows(
+                where, slot, hidden_states, away, group, tree_size, columns, cut, after
             )
-            if held:
-                there = lax.ppermute(held[0], "tp", swap)
             batch = (partial, lax.ppermute(partial, "tp", swap), [piece[0] for piece in group])
-            outputs = finish(where, slot, batch, there, shared, outputs)
+            outputs = finish(where, slot, batch, shared, outputs)
             slot += len(group)
     else:
         parts = [
-            shrink_rows(where, slot, hidden_states, [piece], tree_size, columns, cut, [], [])[0]
+            shrink_rows(where, slot, hidden_states, away, [piece], tree_size, columns, cut, [])
             for slot, piece in enumerate(arrivals)
         ]
         owners_here = lax.dynamic_index_in_dim(jnp.asarray(owners), me, 0, keepdims=False)
@@ -545,8 +553,7 @@
             lax.ppermute(partial, "tp", swap),
             [expands[r] for r in range(requests)],
         )
-        there = lax.ppermute(away, "tp", swap)
-        outputs = finish((every[:1], every[None, :], every), 0, batch, there, shared, None)
+        outputs = finish((every[:1], every[None, :], every), 0, batch, shared, None)
     attention, cache_rows, _ = outputs
     tree_cache = (
         cache_rows.reshape(row_count, 2, heads_here, head_size)

time: 59.9 us -> 55.9 us (0.933)
  waiting for transfers between devices: 12.9 us -> 11 us
  local copies, waits for them, and re-layouts: 8.21 us -> 6.4 us
    ppermute x6, waiting for transfers between devices: 4.68 us -> 0.25 us  [per_device(): front = tuple((lax.ppermute(piece, 'pool', onward) for piece in front))]
    ppermute x1, waiting for transfers between devices: 0.01 us -> 3.44 us  [per_device(): lax.ppermute(rear[1], 'pool', backward)]
    ppermute x6, starting transfers between devices: 0.81 us -> 4.07 us  [per_device(): rear = tuple((lax.ppermute(piece, 'pool', backward) for piece in rear))]
    ppermute x6, starting transfers between devices: 12.5 us -> 9.31 us  [per_device(): front = tuple((lax.ppermute(piece, 'pool', onward) for piece in front))]
    unnamed x40 -> x28, local copies, waits for them, and re-layouts: 8.21 us -> 6.4 us
    ppermute x1, starting transfers between devices: 0.29 us -> 1.9 us  [per_device(): lax.ppermute(rear[1], 'pool', backward)]
    ppermute x1, starting transfers between devices: 1.74 us -> 0.13 us  [per_device(): lax.ppermute(front[0], 'pool', onward)]
    ppermute x6, waiting for transfers between devices: 6.95 us -> 5.66 us  [per_device(): rear = tuple((lax.ppermute(piece, 'pool', backward) for piece in rear))]
  transfers between devices with their start and end apart: 17 -> 17, of which waited for: 6 -> 5; matrix products, arithmetic and copies ran while one was open for 0% -> 0% of each run, Pallas kernels for 23% -> 27%
where the time goes in v6:
time: 55.9 us; the launch traced here: 55.6 us
  Pallas kernels  21.8 us (39%)
  starting transfers between devices  15.5 us (28%)
  waiting for transfers between devices  11 us (20%)
  local copies, waits for them, and re-layouts  6.4 us (11%)
  between operations  0.86 us (2%)
    pallas_call x3, Pallas kernels, finish(): pl.pallas_call(functools.partial(finish_kernel, count=count, slot=slot, k...  12.4 us
    ppermute x6, starting transfers between devices, per_device(): front = tuple((lax.ppermute(piece, 'pool', onward) for piece in front))  9.31 us
    unnamed x28, local copies, waits for them, and re-layouts  6.4 us
    ppermute x6, waiting for transfers between devices, per_device(): rear = tuple((lax.ppermute(piece, 'pool', backward) for piece in rear))  5.66 us
    ppermute x6, starting transfers between devices, per_device(): rear = tuple((lax.ppermute(piece, 'pool', backward) for piece in rear))  4.07 us
    pallas_call x1, Pallas kernels, base_product(): pl.pallas_call(functools.partial(base_kernel, held_count=len(held)), grid...  3.68 us
    ppermute x1, waiting for transfers between devices, per_device(): lax.ppermute(rear[1], 'pool', backward)  3.44 us
    pallas_call x3, Pallas kernels, shrink_rows(): pl.pallas_call(functools.partial(shrink_kernel, columns=columns, cut=cut)...  2.91 us
  transfers between devices with their start and end apart: 17, of which 5 were waited for; matrix products, arithmetic and copies ran while one was open for 0% of the time, Pallas kernels for 27%

profile of v6, /device:TPU:0, one launch (start us, length us, event | category | flops | bytes accessed | tf_op | source)
XLA Modules:
  0.0 55.6 jit_solution(2203006113921333743)
XLA Ops:
  0.6 1.0 %copy-done.5 = bf16[1,2560,64]{1,2,0:T(8,128)(2,1)S(1)} copy-done((bf16[1,2560,64]{1,2,0:T(8,128)(2,1)S(1)}, bf16[1,2560,64]{1,2,0:T(8,128)(2,1)}, u32[]{:S(2)}) %copy-start.5) | copy-done | bytes 327704
  1.6 0.9 %copy-done.7 = bf16[1,64,4,256]{3,2,1,0:T(4,128)(2,1)S(1)} copy-done((bf16[1,64,4,256]{3,2,1,0:T(4,128)(2,1)S(1)}, bf16[1,64,4,256]{3,2,1,0:T(4,128)(2,1)}, u32[]{:S(2)}) %copy-start.7) | copy-done | bytes 131096
  2.5 0.2 pack.1
  2.7 3.1 %collective-permute-start = (bf16[64,1536]{1,0:T(8,128)(2,1)S(1)}, bf16[64,1536]{1,0:T(8,128)(2,1)S(1)}, u32[]{:S(2)}, u32[]{:S(2)}) collective-permute-start(bf16[64,1536]{1,0:T(8,128)(2,1)S(1)} %get-tuple-element.21.refs_3_), channel_id=1, source_target_pairs={{0,4},{4,8},{8,12},{12,14},{14,10},{10,6},{6,2},{2,0},{1,5},{5,9},... | collective-permute-start | bytes 589832 | tf_op jit(solution)/shard_map/ppermute | solution.py:501
  5.8 2.0 %collective-permute-start.2 = (bf16[64,1536]{1,0:T(8,128)(2,1)S(1)}, bf16[64,1536]{1,0:T(8,128)(2,1)S(1)}, u32[]{:S(2)}, u32[]{:S(2)}) collective-permute-start(bf16[64,1536]{1,0:T(8,128)(2,1)S(1)} %get-tuple-element.18.rest_0_.refs_2_), channel_id=1, source_target_pairs={{0,4},{4,8},{8,12},{12,14},{14,10},{10,6},{6,2},{2,0},{1,5},{5,9},... | collective-permute-start | bytes 589832 | tf_op jit(solution)/shard_map/ppermute | solution.py:501
  7.8 2.5 %copy-done.2 = bf16[2560,4,256]{2,1,0:T(4,128)(2,1)S(1)} copy-done((bf16[2560,4,256]{2,1,0:T(4,128)(2,1)S(1)}, bf16[2560,4,256]{2,1,0:T(4,128)(2,1)}, u32[]{:S(2)}) %copy-start.2) | copy-done | bytes 5242904
  10.3 0.7 %copy-done.9 = s32[8]{0:T(128)S(1)} copy-done((s32[8]{0:T(128)S(1)}, s32[8]{0:T(128)}, u32[]{:S(2)}) %copy-start.9) | copy-done | bytes 56
  10.9 0.7 %copy-done.12 = s32[8,48]{1,0:T(8,128)S(1)} copy-done((s32[8,48]{1,0:T(8,128)S(1)}, s32[8,48]{1,0:T(8,128)}, u32[]{:S(2)}) %copy-start.12) | copy-done | bytes 1560
  11.6 0.7 %copy-done.13 = f32[1,128]{1,0:T(1,128)S(1)} copy-done((f32[1,128]{1,0:T(1,128)S(1)}, f32[1,128]{1,0:T(1,128)}, u32[]{:S(2)}) %copy-start.13) | copy-done | bytes 536
  12.3 2.6 %tree.1 = (f32[384,384]{1,0:T(8,128)S(1)}, bf16[20480,128]{1,0:T(8,128)(2,1)S(1)}) custom-call(s32[8]{0:T(128)S(1)} %copy-done.9, s32[8,48]{1,0:T(8,128)S(1)} %copy-done.12, f32[1,128]{1,0:T(1,128)S(1)} %copy-done.13, bf16[20480,128]{1,0:T(8,128)(2,1)S(1)} %bitcast.23, bf16[64,1536]{1,0:T(8,128)(2,1)S(1)} %get-tuple-element.18.rest_0_.refs_2_), custom_call_target="tpu_custom_call" | custom-call | flops 1000000000 | bytes 8000000 | tf_op jit(solution)/shard_map/tree/pallas_call | solution.py:218
  15.0 3.7 %base.1 = (f32[384,512]{1,0:T(8,128)S(1)}, f32[384,512]{1,0:T(8,128)S(1)}, bf16[64,1536]{1,0:T(8,128)(2,1)S(1)}, bf16[64,1536]{1,0:T(8,128)(2,1)S(1)}) custom-call(s32[1]{0:T(128)} %bitcast.1.core_ref, bf16[384,2560]{1,0:T(8,128)(2,1)S(1)} %copy-done, ...), custom_call_target="tpu_custom_call", output_to_operand_aliasing={{2}: (4, {}), {3}: (5, {})} | custom-call | flops 4000000000 | bytes 9000000 | tf_op jit(solution)/shard_map/base/pallas_call | solution.py:142
  18.8 1.0 %shrink.3.shrunk_here_ref = f32[3,48,640]{2,1,0:T(8,128)S(1)} custom-call(s32[1]{0:T(128)} %bitcast.me_ref, s32[8,8]{1,0:T(8,128)S(1)} %copy-done.6, s32[8]{0:T(128)S(1)} %copy-done.8, bf16[384,2560]{1,0:T(8,128)(2,1)S(1)} %copy-done, f32[384,512]{1,0:T(8,128)S(1)} %get-tuple-element.23.refs_1_.refs_5_.refs_9_, ...), custom_call_target="tpu_custom_call" | custom-call | flops 90000000 | bytes 600000 | tf_op jit(solution)/shard_map/shrink/pallas_call | solution.py:267
  19.8 2.0 %collective-permute-start.10 = (bf16[64,1536]{1,0:T(8,128)(2,1)S(1)}, bf16[64,1536]{1,0:T(8,128)(2,1)S(1)}, u32[]{:S(2)}, u32[]{:S(2)}) collective-permute-start(bf16[64,1536]{1,0:T(8,128)(2,1)S(1)} %get-tuple-element.25.refs_11_), channel_id=1, source_target_pairs={{4,0},{8,4},{12,8},{14,12},{10,14},{6,10},{2,6},{0,2},{5,1},{9,5},... | collective-permute-start | bytes 589832 | tf_op jit(solution)/shard_map/ppermute | solution.py:502
  21.8 0.2 collective-permute-start.3
  22.0 1.9 %collective-permute-start.5 = (bf16[64,1536]{1,0:T(8,128)(2,1)S(1)}, bf16[64,1536]{1,0:T(8,128)(2,1)S(1)}, u32[]{:S(2)}, u32[]{:S(2)}) collective-permute-start(bf16[64,1536]{1,0:T(8,128)(2,1)S(1)} %get-tuple-element.24.refs_7_), channel_id=1, source_target_pairs={{0,4},{4,8},{8,12},{12,14},{14,10},{10,6},{6,2},{2,0},{1,5},{5,9},... | collective-permute-start | bytes 589832 | tf_op jit(solution)/shard_map/ppermute | solution.py:501
  23.9 0.1 collective-permute-start.8
  24.0 3.6 %collective-permute-done.10.refs_7_ = bf16[64,1536]{1,0:T(8,128)(2,1)S(1)} collective-permute-done((bf16[64,1536]{1,0:T(8,128)(2,1)S(1)}, bf16[64,1536]{1,0:T(8,128)(2,1)S(1)}, u32[]{:S(2)}, u32[]{:S(2)}) %collective-permute-start.10) | collective-permute-done | bytes 196640 | tf_op jit(solution)/shard_map/ppermute | solution.py:502
  27.6 1.9 %collective-permute-start.11 = (bf16[64,1536]{1,0:T(8,128)(2,1)S(1)}, bf16[64,1536]{1,0:T(8,128)(2,1)S(1)}, u32[]{:S(2)}, u32[]{:S(2)}) collective-permute-start(bf16[64,1536]{1,0:T(8,128)(2,1)S(1)} %collective-permute-done.10.refs_7_), channel_id=1, source_target_pairs={{4,0},{8,4},{12,8},{14,12},{10,14},{6,10},{2,6},{0,2},{5,1},{9,5},... | collective-permute-start | bytes 589832 | tf_op jit(solution)/shard_map/ppermute | solution.py:502
  29.6 0.1 collective-permute-start.4
  29.7 4.5 %finish.3 = (bf16[384,16,128]{2,1,0:T(8,128)(2,1)}, bf16[1536,128]{1,0:T(8,128)(2,1)}, f32[8,128]{1,0:T(8,128)S(1)}) custom-call(s32[1]{0:T(128)} %bitcast.me_ref, s32[8,8]{1,0:T(8,128)S(1)} %copy-done.6, s32[8]{0:T(128)S(1)} %copy-done.8, s32[8]{0:T(128)S(1)} %copy-done.10, f32[384,512]{1,0:T(8,128)S(1)} %get-tuple-element.22.here_ref, ...), custom_call_target="tpu_custom_call" | custom-call | flops 270000000 | bytes 900000 | tf_op jit(solution)/shard_map/finish/pallas_call | solution.py:418
  34.2 0.9 %shrink.4.shrunk_here_ref = f32[2,48,640]{2,1,0:T(8,128)S(1)} custom-call(s32[1]{0:T(128)} %bitcast.me_ref, s32[8,8]{1,0:T(8,128)S(1)} %copy-done.6, s32[8]{0:T(128)S(1)} %copy-done.8, bf16[384,2560]{1,0:T(8,128)(2,1)S(1)} %copy-done, f32[384,512]{1,0:T(8,128)S(1)} %get-tuple-element.23.refs_1_.refs_5_.refs_9_, ...), custom_call_target="tpu_custom_call" | custom-call | flops 60000000 | bytes 400000 | tf_op jit(solution)/shard_map/shrink/pallas_call | solution.py:267
  35.2 0.1 collective-permute-start.15
  35.2 2.0 %collective-permute-start.6 = (bf16[64,1536]{1,0:T(8,128)(2,1)S(1)}, bf16[64,1536]{1,0:T(8,128)(2,1)S(1)}, u32[]{:S(2)}, u32[]{:S(2)}) collective-permute-start(bf16[64,1536]{1,0:T(8,128)(2,1)S(1)} %collective-permute-done.5.refs_3_), channel_id=1, source_target_pairs={{0,4},{4,8},{8,12},{12,14},{14,10},{10,6},{6,2},{2,0},{1,5},{5,9},... | collective-permute-start | bytes 589832 | tf_op jit(solution)/shard_map/ppermute | solution.py:501
  37.3 1.9 %collective-permute-start.13 = (bf16[64,1536]{1,0:T(8,128)(2,1)S(1)}, bf16[64,1536]{1,0:T(8,128)(2,1)S(1)}, u32[]{:S(2)}, u32[]{:S(2)}) collective-permute-start(bf16[64,1536]{1,0:T(8,128)(2,1)S(1)} %collective-permute-done.11.refs_7_), channel_id=1, source_target_pairs={{4,0},{8,4},{12,8},{14,12},{10,14},{6,10},{2,6},{0,2},{5,1},{9,5},... | collective-permute-start | bytes 589832 | tf_op jit(solution)/shard_map/ppermute | solution.py:511
  39.2 0.1 collective-permute-start.12
  39.4 3.4 %finish.4 = (bf16[384,16,128]{2,1,0:T(8,128)(2,1)}, bf16[1536,128]{1,0:T(8,128)(2,1)}, f32[8,128]{1,0:T(8,128)S(1)}) custom-call(s32[1]{0:T(128)} %bitcast.me_ref, s32[8,8]{1,0:T(8,128)S(1)} %copy-done.6, s32[8]{0:T(128)S(1)} %copy-done.8, s32[8]{0:T(128)S(1)} %copy-done.10, ...), custom_call_target="tpu_custom_call", output_to_operand_aliasing={{0}: (14, {}), {1}: (15, {})} | custom-call | flops 180000000 | bytes 600000 | tf_op jit(solution)/shard_map/finish/pallas_call | solution.py:418
  42.8 0.2 collective-permute-done.6.refs_3_
  43.0 2.0 %collective-permute-done.9.refs_6_.rest_1_ = bf16[64,1536]{1,0:T(8,128)(2,1)S(1)} collective-permute-done((bf16[64,1536]{1,0:T(8,128)(2,1)S(1)}, bf16[64,1536]{1,0:T(8,128)(2,1)S(1)}, u32[]{:S(2)}, u32[]{:S(2)}) %collective-permute-start.9) | collective-permute-done | bytes 196640 | tf_op jit(solution)/shard_map/ppermute | solution.py:502
  45.0 3.4 %collective-permute-done.13.refs_11_ = bf16[64,1536]{1,0:T(8,128)(2,1)S(1)} collective-permute-done((bf16[64,1536]{1,0:T(8,128)(2,1)S(1)}, bf16[64,1536]{1,0:T(8,128)(2,1)S(1)}, u32[]{:S(2)}, u32[]{:S(2)}) %collective-permute-start.13) | collective-permute-done | bytes 196640 | tf_op jit(solution)/shard_map/ppermute | solution.py:511
  48.4 1.0 %shrink.5.shrunk_here_ref = f32[3,48,640]{2,1,0:T(8,128)S(1)} custom-call(s32[1]{0:T(128)} %bitcast.me_ref, s32[8,8]{1,0:T(8,128)S(1)} %copy-done.6, s32[8]{0:T(128)S(1)} %copy-done.8, bf16[384,2560]{1,0:T(8,128)(2,1)S(1)} %copy-done, f32[384,512]{1,0:T(8,128)S(1)} %get-tuple-element.23.refs_1_.refs_5_.refs_9_, ...), custom_call_target="tpu_custom_call" | custom-call | flops 90000000 | bytes 600000 | tf_op jit(solution)/shard_map/shrink/pallas_call | solution.py:267
  49.5 1.7 %collective-permute-done.16.shrunk_there_ref = f32[3,48,640]{2,1,0:T(8,128)S(1)} collective-permute-done((f32[3,48,640]{2,1,0:T(8,128)S(1)}, f32[3,48,640]{2,1,0:T(8,128)S(1)}, u32[]{:S(2)}, u32[]{:S(2)}) %collective-permute-start.16) | collective-permute-done | bytes 368672 | tf_op jit(solution)/shard_map/ppermute | solution.py:537
  51.1 4.5 %finish.5 = (bf16[384,16,128]{2,1,0:T(8,128)(2,1)}, bf16[1536,128]{1,0:T(8,128)(2,1)}, f32[8,128]{1,0:T(8,128)}) custom-call(s32[1]{0:T(128)} %bitcast.me_ref, s32[8,8]{1,0:T(8,128)S(1)} %copy-done.6, s32[8]{0:T(128)S(1)} %copy-done.8, s32[8]{0:T(128)S(1)} %copy-done.10, ...), custom_call_target="tpu_custom_call", output_to_operand_aliasing={{0}: (15, {}), {1}: (16, {})} | custom-call | flops 270000000 | bytes 900000 | tf_op jit(solution)/shard_map/finish/pallas_call | solution.py:418
  (39 shorter events, 0.3 us)
Async XLA Ops:
  0.6 1.0 %copy-start.5 = (bf16[1,2560,64]{1,2,0:T(8,128)(2,1)S(1)}, bf16[1,2560,64]{1,2,0:T(8,128)(2,1)}, u32[]{:S(2)}) copy-start(bf16[1,2560,64]{1,2,0:T(8,128)(2,1)} %param.15) | copy-start | bytes 983044
  1.6 0.9 %copy-start.7 = (bf16[1,64,4,256]{3,2,1,0:T(4,128)(2,1)S(1)}, bf16[1,64,4,256]{3,2,1,0:T(4,128)(2,1)}, u32[]{:S(2)}) copy-start(bf16[1,64,4,256]{3,2,1,0:T(4,128)(2,1)} %param.16) | copy-start | bytes 393220
  2.7 12.2 %collective-permute-start = (bf16[64,1536]{1,0:T(8,128)(2,1)S(1)}, bf16[64,1536]{1,0:T(8,128)(2,1)S(1)}, u32[]{:S(2)}, u32[]{:S(2)}) collective-permute-start(bf16[64,1536]{1,0:T(8,128)(2,1)S(1)} %get-tuple-element.21.refs_3_), channel_id=1, source_target_pairs={{0,4},{4,8},{8,12},{12,14},{14,10},{10,6},{6,2},{2,0},{1,5},{5,9},... | collective-permute-start | bytes 589832 | tf_op jit(solution)/shard_map/ppermute | solution.py:501
  5.8 9.2 %collective-permute-start.1 = (bf16[64,1536]{1,0:T(8,128)(2,1)S(1)}, bf16[64,1536]{1,0:T(8,128)(2,1)S(1)}, u32[]{:S(2)}, u32[]{:S(2)}) collective-permute-start(bf16[64,1536]{1,0:T(8,128)(2,1)S(1)} %get-tuple-element.21.refs_3_), channel_id=1, source_target_pairs={{4,0},{8,4},{12,8},{14,12},{10,14},{6,10},{2,6},{0,2},{5,1},{9,5},... | collective-permute-start | bytes 589832 | tf_op jit(solution)/shard_map/ppermute | solution.py:502
  5.8 12.9 %collective-permute-start.2 = (bf16[64,1536]{1,0:T(8,128)(2,1)S(1)}, bf16[64,1536]{1,0:T(8,128)(2,1)S(1)}, u32[]{:S(2)}, u32[]{:S(2)}) collective-permute-start(bf16[64,1536]{1,0:T(8,128)(2,1)S(1)} %get-tuple-element.18.rest_0_.refs_2_), channel_id=1, source_target_pairs={{0,4},{4,8},{8,12},{12,14},{14,10},{10,6},{6,2},{2,0},{1,5},{5,9},... | collective-permute-start | bytes 589832 | tf_op jit(solution)/shard_map/ppermute | solution.py:501
  7.8 10.9 %collective-permute-start.7 = (bf16[64,1536]{1,0:T(8,128)(2,1)S(1)}, bf16[64,1536]{1,0:T(8,128)(2,1)S(1)}, u32[]{:S(2)}, u32[]{:S(2)}) collective-permute-start(bf16[64,1536]{1,0:T(8,128)(2,1)S(1)} %get-tuple-element.18.rest_0_.refs_2_), channel_id=1, source_target_pairs={{4,0},{8,4},{12,8},{14,12},{10,14},{6,10},{2,6},{0,2},{5,1},{9,5},... | collective-permute-start | bytes 589832 | tf_op jit(solution)/shard_map/ppermute | solution.py:502
  7.8 2.5 %copy-start.2 = (bf16[2560,4,256]{2,1,0:T(4,128)(2,1)S(1)}, bf16[2560,4,256]{2,1,0:T(4,128)(2,1)}, u32[]{:S(2)}) copy-start(bf16[2560,4,256]{2,1,0:T(4,128)(2,1)} %param.14) | copy-start | bytes 15728644
  10.3 0.7 %copy-start.9 = (s32[8]{0:T(128)S(1)}, s32[8]{0:T(128)}, u32[]{:S(2)}) copy-start(s32[8]{0:T(128)} %length_ref.7) | copy-start | bytes 100
  10.9 0.7 %copy-start.12 = (s32[8,48]{1,0:T(8,128)S(1)}, s32[8,48]{1,0:T(8,128)}, u32[]{:S(2)}) copy-start(s32[8,48]{1,0:T(8,128)} %parent_ref.1) | copy-start | bytes 4612
  11.6 0.7 %copy-start.13 = (f32[1,128]{1,0:T(1,128)S(1)}, f32[1,128]{1,0:T(1,128)}, u32[]{:S(2)}) copy-start(f32[1,128]{1,0:T(1,128)} %constant.13.clone.frequency_ref) | copy-start | bytes 1540
  12.3 2.7 %copy-start = (bf16[384,2560]{1,0:T(8,128)(2,1)S(1)}, bf16[384,2560]{1,0:T(8,128)(2,1)}, u32[]{:S(2)}) copy-start(bf16[384,2560]{1,0:T(8,128)(2,1)} %refs_8_.3) | copy-start | bytes 5898244
  15.0 3.7 %copy-start.6 = (s32[8,8]{1,0:T(8,128)S(1)}, s32[8,8]{1,0:T(8,128)}, u32[]{:S(2)}) copy-start(s32[8,8]{1,0:T(8,128)} %constant.12.clone.owner_ref) | copy-start | bytes 772
  15.0 3.7 %copy-start.8 = (s32[8]{0:T(128)S(1)}, s32[8]{0:T(128)}, u32[]{:S(2)}) copy-start(s32[8]{0:T(128)} %adapter_ref.11) | copy-start | bytes 100
  18.7 11.0 %copy-start.1 = (bf16[384,16,128]{2,1,0:T(8,128)(2,1)S(1)}, bf16[384,16,128]{2,1,0:T(8,128)(2,1)}, u32[]{:S(2)}) copy-start(bf16[384,16,128]{2,1,0:T(8,128)(2,1)} %query_ref.5) | copy-start | bytes 4718596
  18.7 11.0 %copy-start.3 = (bf16[8,128,2,128]{3,2,1,0:T(2,128)(2,1)S(1)}, bf16[8,128,2,128]{3,2,1,0:T(2,128)(2,1)}, u32[]{:S(2)}) copy-start(bf16[8,128,2,128]{3,2,1,0:T(2,128)(2,1)} %param.21) | copy-start | bytes 1572868
  18.7 11.0 %copy-start.4 = (bf16[8,128,2,128]{3,2,1,0:T(2,128)(2,1)S(1)}, bf16[8,128,2,128]{3,2,1,0:T(2,128)(2,1)}, u32[]{:S(2)}) copy-start(bf16[8,128,2,128]{3,2,1,0:T(2,128)(2,1)} %param.22) | copy-start | bytes 1572868
  18.8 11.0 %copy-start.10 = (s32[8]{0:T(128)S(1)}, s32[8]{0:T(128)}, u32[]{:S(2)}) copy-start(s32[8]{0:T(128)} %length_ref.7) | copy-start | bytes 100
  18.8 11.0 %copy-start.11 = (f32[128]{0:T(128)S(1)}, f32[128]{0:T(128)}, u32[]{:S(2)}) copy-start(f32[128]{0:T(128)} %param.23) | copy-start | bytes 1540
  19.8 9.9 %collective-permute-start.14 = (f32[3,48,640]{2,1,0:T(8,128)S(1)}, f32[3,48,640]{2,1,0:T(8,128)S(1)}, u32[]{:S(2)}, u32[]{:S(2)}) collective-permute-start(f32[3,48,640]{2,1,0:T(8,128)S(1)} %shrink.3.shrunk_here_ref), channel_id=1, source_target_pairs={{0,1},{1,0},{2,3},{3,2},{4,5},{5,4},{6,7},{7,6},{8,9},{9,8},{10,11... | collective-permute-start | bytes 1105928 | tf_op jit(solution)/shard_map/ppermute | solution.py:537
  19.8 7.8 %collective-permute-start.10 = (bf16[64,1536]{1,0:T(8,128)(2,1)S(1)}, bf16[64,1536]{1,0:T(8,128)(2,1)S(1)}, u32[]{:S(2)}, u32[]{:S(2)}) collective-permute-start(bf16[64,1536]{1,0:T(8,128)(2,1)S(1)} %get-tuple-element.25.refs_11_), channel_id=1, source_target_pairs={{4,0},{8,4},{12,8},{14,12},{10,14},{6,10},{2,6},{0,2},{5,1},{9,5},... | collective-permute-start | bytes 589832 | tf_op jit(solution)/shard_map/ppermute | solution.py:502
  21.8 7.7 %collective-permute-start.3 = (bf16[64,1536]{1,0:T(8,128)(2,1)S(1)}, bf16[64,1536]{1,0:T(8,128)(2,1)S(1)}, u32[]{:S(2)}, u32[]{:S(2)}) collective-permute-start(bf16[64,1536]{1,0:T(8,128)(2,1)S(1)} %collective-permute-done.2.refs_6_.rest_1_), channel_id=1, source_target_pairs={{0,4},{4,8},{8,12},{12,14},{14,10},{10,6},{6,2},{2,0},{1,5},{5,9},... | collective-permute-start | bytes 589832 | tf_op jit(solution)/shard_map/ppermute | solution.py:501
  22.0 12.3 %collective-permute-start.5 = (bf16[64,1536]{1,0:T(8,128)(2,1)S(1)}, bf16[64,1536]{1,0:T(8,128)(2,1)S(1)}, u32[]{:S(2)}, u32[]{:S(2)}) collective-permute-start(bf16[64,1536]{1,0:T(8,128)(2,1)S(1)} %get-tuple-element.24.refs_7_), channel_id=1, source_target_pairs={{0,4},{4,8},{8,12},{12,14},{14,10},{10,6},{6,2},{2,0},{1,5},{5,9},... | collective-permute-start | bytes 589832 | tf_op jit(solution)/shard_map/ppermute | solution.py:501
  23.9 10.3 %collective-permute-start.8 = (bf16[64,1536]{1,0:T(8,128)(2,1)S(1)}, bf16[64,1536]{1,0:T(8,128)(2,1)S(1)}, u32[]{:S(2)}, u32[]{:S(2)}) collective-permute-start(bf16[64,1536]{1,0:T(8,128)(2,1)S(1)} %collective-permute-done.7.refs_10_.rest_2_), channel_id=1, source_target_pairs={{4,0},{8,4},{12,8},{14,12},{10,14},{6,10},{2,6},{0,2},{5,1},{9,5},... | collective-permute-start | bytes 589832 | tf_op jit(solution)/shard_map/ppermute | solution.py:502
  27.6 9.7 %collective-permute-start.11 = (bf16[64,1536]{1,0:T(8,128)(2,1)S(1)}, bf16[64,1536]{1,0:T(8,128)(2,1)S(1)}, u32[]{:S(2)}, u32[]{:S(2)}) collective-permute-start(bf16[64,1536]{1,0:T(8,128)(2,1)S(1)} %collective-permute-done.10.refs_7_), channel_id=1, source_target_pairs={{4,0},{8,4},{12,8},{14,12},{10,14},{6,10},{2,6},{0,2},{5,1},{9,5},... | collective-permute-start | bytes 589832 | tf_op jit(solution)/shard_map/ppermute | solution.py:502
  29.6 9.7 %collective-permute-start.4 = (bf16[64,1536]{1,0:T(8,128)(2,1)S(1)}, bf16[64,1536]{1,0:T(8,128)(2,1)S(1)}, u32[]{:S(2)}, u32[]{:S(2)}) collective-permute-start(bf16[64,1536]{1,0:T(8,128)(2,1)S(1)} %collective-permute-done.3.refs_2_.rest_0_), channel_id=1, source_target_pairs={{0,4},{4,8},{8,12},{12,14},{14,10},{10,6},{6,2},{2,0},{1,5},{5,9},... | collective-permute-start | bytes 589832 | tf_op jit(solution)/shard_map/ppermute | solution.py:501
  35.2 4.2 %collective-permute-start.15 = (f32[2,48,640]{2,1,0:T(8,128)S(1)}, f32[2,48,640]{2,1,0:T(8,128)S(1)}, u32[]{:S(2)}, u32[]{:S(2)}) collective-permute-start(f32[2,48,640]{2,1,0:T(8,128)S(1)} %shrink.4.shrunk_here_ref), channel_id=1, source_target_pairs={{0,1},{1,0},{2,3},{3,2},{4,5},{5,4},{6,7},{7,6},{8,9},{9,8},{10,11... | collective-permute-start | bytes 737288 | tf_op jit(solution)/shard_map/ppermute | solution.py:537
  35.2 7.7 %collective-permute-start.6 = (bf16[64,1536]{1,0:T(8,128)(2,1)S(1)}, bf16[64,1536]{1,0:T(8,128)(2,1)S(1)}, u32[]{:S(2)}, u32[]{:S(2)}) collective-permute-start(bf16[64,1536]{1,0:T(8,128)(2,1)S(1)} %collective-permute-done.5.refs_3_), channel_id=1, source_target_pairs={{0,4},{4,8},{8,12},{12,14},{14,10},{10,6},{6,2},{2,0},{1,5},{5,9},... | collective-permute-start | bytes 589832 | tf_op jit(solution)/shard_map/ppermute | solution.py:501
  37.3 7.7 %collective-permute-start.9 = (bf16[64,1536]{1,0:T(8,128)(2,1)S(1)}, bf16[64,1536]{1,0:T(8,128)(2,1)S(1)}, u32[]{:S(2)}, u32[]{:S(2)}) collective-permute-start(bf16[64,1536]{1,0:T(8,128)(2,1)S(1)} %collective-permute-done.8.refs_6_.rest_1_), channel_id=1, source_target_pairs={{4,0},{8,4},{12,8},{14,12},{10,14},{6,10},{2,6},{0,2},{5,1},{9,5},... | collective-permute-start | bytes 589832 | tf_op jit(solution)/shard_map/ppermute | solution.py:502
  37.3 11.1 %collective-permute-start.13 = (bf16[64,1536]{1,0:T(8,128)(2,1)S(1)}, bf16[64,1536]{1,0:T(8,128)(2,1)S(1)}, u32[]{:S(2)}, u32[]{:S(2)}) collective-permute-start(bf16[64,1536]{1,0:T(8,128)(2,1)S(1)} %collective-permute-done.11.refs_7_), channel_id=1, source_target_pairs={{4,0},{8,4},{12,8},{14,12},{10,14},{6,10},{2,6},{0,2},{5,1},{9,5},... | collective-permute-start | bytes 589832 | tf_op jit(solution)/shard_map/ppermute | solution.py:511
  39.2 9.2 %collective-permute-start.12 = (bf16[64,1536]{1,0:T(8,128)(2,1)S(1)}, bf16[64,1536]{1,0:T(8,128)(2,1)S(1)}, u32[]{:S(2)}, u32[]{:S(2)}) collective-permute-start(bf16[64,1536]{1,0:T(8,128)(2,1)S(1)} %collective-permute-done.4.refs_2_.rest_0_), channel_id=1, source_target_pairs={{0,4},{4,8},{8,12},{12,14},{14,10},{10,6},{6,2},{2,0},{1,5},{5,9},... | collective-permute-start | bytes 589832 | tf_op jit(solution)/shard_map/ppermute | solution.py:511
  49.4 1.7 %collective-permute-start.16 = (f32[3,48,640]{2,1,0:T(8,128)S(1)}, f32[3,48,640]{2,1,0:T(8,128)S(1)}, u32[]{:S(2)}, u32[]{:S(2)}) collective-permute-start(f32[3,48,640]{2,1,0:T(8,128)S(1)} %shrink.5.shrunk_here_ref), channel_id=1, source_target_pairs={{0,1},{1,0},{2,3},{3,2},{4,5},{5,4},{6,7},{7,6},{8,9},{9,8},{10,11... | collective-permute-start | bytes 1105928 | tf_op jit(solution)/shard_map/ppermute | solution.py:537

commit v7 on v6

--- a/solution.py
+++ b/solution.py
@@ -166,12 +166,11 @@
     )(core, hidden_states, weight_rows, *after, *held)
 
 
-def tree_kernel(length_ref, parent_ref, frequency_ref, weight_ref, *rest, kv_heads):
+def tree_kernel(length_ref, parent_ref, weight_ref, *rest, head_size, kv_heads):
     table_ref, moved_ref, semaphore = rest[-3:]
     move = pltpu.make_async_copy(weight_ref, moved_ref, semaphore)
     move.start()
     requests, nodes = parent_ref.shape
-    head_size = frequency_ref.shape[1]
     node = lax.broadcasted_iota(jnp.int32, (nodes, nodes), 0)
     same = node == lax.broadcasted_iota(jnp.int32, (nodes, nodes), 1)
     spare = table_ref.shape[1] - 2 * head_size
@@ -193,12 +192,14 @@
         reached = 2 * reached
     lane = lax.broadcasted_iota(jnp.int32, (nodes, head_size), 1)
     sign = jnp.where(lane < head_size // 2, -1.0, 1.0)
+    power = lax.broadcasted_iota(jnp.int32, (1, head_size), 1) % (head_size // 2)
+    frequency = jnp.exp(power.astype(F32) * (-2.0 * math.log(1000000.0) / head_size))
     ones = jnp.ones((nodes, head_size), BF16)
     for r in range(requests):
         b = below[r]
         depth = lax.dot_general(b, ones, (((0,), (0,)), ((), ())), preferred_element_type=F32)
         positions = length_ref[r].astype(F32) + depth - 1.0
-        angles = positions * frequency_ref[...]
+        angles = positions * frequency
         rows = slice(nodes * r, nodes * (r + 1))
         wide = lax.dot_general(b, spread, (((0,), (0,)), ((), ())), preferred_element_type=F32)
         table_ref[rows, :] = jnp.concatenate(
@@ -209,18 +210,15 @@
 
 def tree_tables(cache_lengths, tree_parents, head_size, kv_heads, weight_rows, after):
     requests, nodes = tree_parents.shape
-    half_size = head_size // 2
-    frequency = np.exp(np.arange(half_size) * (-2.0 * math.log(1000000.0) / head_size))
-    frequency = np.concatenate([frequency, frequency]).reshape(1, head_size).astype(np.float32)
     whole = lambda shape: pl.BlockSpec(shape, lambda i, n: (0,) * len(shape))
     rows = requests * nodes
     width = 2 * head_size + -(-kv_heads * nodes // 128) * 128
     return pl.pallas_call(
-        functools.partial(tree_kernel, kv_heads=kv_heads),
+        functools.partial(tree_kernel, head_size=head_size, kv_heads=kv_heads),
         grid_spec=pltpu.PrefetchScalarGridSpec(
             num_scalar_prefetch=1,
             grid=(1,),
-            in_specs=[whole(tree_parents.shape), whole((1, head_size)), pl.BlockSpec(memory_space=pltpu.HBM)]
+            in_specs=[whole(tree_parents.shape), ANYWHERE]
             + [ANYWHERE] * len(after),
             out_specs=[whole((rows, width)), ANYWHERE],
             scratch_shapes=[pltpu.SemaphoreType.DMA],
@@ -231,7 +229,7 @@
         ),
         compiler_params=pltpu.CompilerParams(vmem_limit_bytes=8 * 1024 * 1024),
         name="tree",
-    )(cache_lengths, tree_parents, frequency, weight_rows, *after)
+    )(cache_lengths, tree_parents, weight_rows, *after)
 
 
 def shrink_kernel(me_ref, owner_ref, adapter_ref, *refs, columns, cut):
@@ -435,7 +433,7 @@
         ],
         input_output_aliases=aliases,
         cost_estimate=pl.CostEstimate(
-            flops=count * 90000000, bytes_accessed=count * 300000, transcendentals=0
+            flops=count * 900000000, bytes_accessed=count * 3000000, transcendentals=0
         ),
         compiler_params=pltpu.CompilerParams(vmem_limit_bytes=16 * 1024 * 1024),
         name="finish",

time: 55.9 us -> 57.8 us (1.034)
  waiting for transfers between devices: 11 us -> 13.6 us
  local copies, waits for them, and re-layouts: 6.4 us -> 5.74 us
    ppermute x6, waiting for transfers between devices: 0.25 us -> 4.87 us  [per_device(): front = tuple((lax.ppermute(piece, 'pool', onward) for piece in front))]
    ppermute x6, waiting for transfers between devices: 5.66 us -> 3.66 us  [per_device(): rear = tuple((lax.ppermute(piece, 'pool', backward) for piece in rear))]
    ppermute x6, starting transfers between devices: 4.07 us -> 5.44 us  [per_device(): rear = tuple((lax.ppermute(piece, 'pool', backward) for piece in rear))]
    ppermute x6, starting transfers between devices: 9.31 us -> 7.97 us  [per_device(): front = tuple((lax.ppermute(piece, 'pool', onward) for piece in front))]
    ppermute x1, waiting for transfers between devices: 3.44 us -> 2.14 us  [per_device(): lax.ppermute(rear[1], 'pool', backward)]
    ppermute x1, waiting for transfers between devices: 0.01 us -> 1.3 us  [per_device(): lax.ppermute(front[0], 'pool', onward)]
    unnamed x28 -> x26, local copies, waits for them, and re-layouts: 6.4 us -> 5.74 us
  transfers between devices with their start and end apart: 17 -> 17, of which waited for: 5 -> 7; matrix products, arithmetic and copies ran while one was open for 0% -> 0% of each run, Pallas kernels for 27% -> 25%
where the time goes in v7:
time: 57.8 us; the launch traced here: 57.6 us
  Pallas kernels  21.8 us (38%)
  starting transfers between devices  15.5 us (27%)
  waiting for transfers between devices  13.6 us (24%)
  local copies, waits for them, and re-layouts  5.74 us (10%)
  between operations  0.86 us (1%)
    pallas_call x3, Pallas kernels, finish(): pl.pallas_call(functools.partial(finish_kernel, count=count, slot=slot, k...  12.4 us
    ppermute x6, starting transfers between devices, per_device(): front = tuple((lax.ppermute(piece, 'pool', onward) for piece in front))  7.97 us
    unnamed x26, local copies, waits for them, and re-layouts  5.74 us
    ppermute x6, starting transfers between devices, per_device(): rear = tuple((lax.ppermute(piece, 'pool', backward) for piece in rear))  5.44 us
    ppermute x6, waiting for transfers between devices, per_device(): front = tuple((lax.ppermute(piece, 'pool', onward) for piece in front))  4.87 us
    pallas_call x1, Pallas kernels, base_product(): pl.pallas_call(functools.partial(base_kernel, held_count=len(held)), grid...  3.67 us
    ppermute x6, waiting for transfers between devices, per_device(): rear = tuple((lax.ppermute(piece, 'pool', backward) for piece in rear))  3.66 us
    pallas_call x3, Pallas kernels, shrink_rows(): pl.pallas_call(functools.partial(shrink_kernel, columns=columns, cut=cut)...  2.9 us
  transfers between devices with their start and end apart: 17, of which 7 were waited for; matrix products, arithmetic and copies ran while one was open for 0% of the time, Pallas kernels for 25%

profile of v7, /device:TPU:0, one launch (start us, length us, event | category | flops | bytes accessed | tf_op | source)
XLA Modules:
  0.0 57.6 jit_solution(3948966621570614132)
XLA Ops:
  0.6 1.0 %copy-done.5 = bf16[1,2560,64]{1,2,0:T(8,128)(2,1)S(1)} copy-done((bf16[1,2560,64]{1,2,0:T(8,128)(2,1)S(1)}, bf16[1,2560,64]{1,2,0:T(8,128)(2,1)}, u32[]{:S(2)}) %copy-start.5) | copy-done | bytes 327704
  1.6 0.9 %copy-done.6 = bf16[1,64,4,256]{3,2,1,0:T(4,128)(2,1)S(1)} copy-done((bf16[1,64,4,256]{3,2,1,0:T(4,128)(2,1)S(1)}, bf16[1,64,4,256]{3,2,1,0:T(4,128)(2,1)}, u32[]{:S(2)}) %copy-start.6) | copy-done | bytes 131096
  2.5 0.2 pack.1
  2.7 3.1 %collective-permute-start = (bf16[64,1536]{1,0:T(8,128)(2,1)S(1)}, bf16[64,1536]{1,0:T(8,128)(2,1)S(1)}, u32[]{:S(2)}, u32[]{:S(2)}) collective-permute-start(bf16[64,1536]{1,0:T(8,128)(2,1)S(1)} %get-tuple-element.21.refs_3_), channel_id=1, source_target_pairs={{0,4},{4,8},{8,12},{12,14},{14,10},{10,6},{6,2},{2,0},{1,5},{5,9},... | collective-permute-start | bytes 589832 | tf_op jit(solution)/shard_map/ppermute | solution.py:499
  5.8 2.0 %collective-permute-start.2 = (bf16[64,1536]{1,0:T(8,128)(2,1)S(1)}, bf16[64,1536]{1,0:T(8,128)(2,1)S(1)}, u32[]{:S(2)}, u32[]{:S(2)}) collective-permute-start(bf16[64,1536]{1,0:T(8,128)(2,1)S(1)} %get-tuple-element.18.rest_0_.refs_2_), channel_id=1, source_target_pairs={{0,4},{4,8},{8,12},{12,14},{14,10},{10,6},{6,2},{2,0},{1,5},{5,9},... | collective-permute-start | bytes 589832 | tf_op jit(solution)/shard_map/ppermute | solution.py:499
  7.8 2.5 %copy-done.1 = bf16[2560,4,256]{2,1,0:T(4,128)(2,1)S(1)} copy-done((bf16[2560,4,256]{2,1,0:T(4,128)(2,1)S(1)}, bf16[2560,4,256]{2,1,0:T(4,128)(2,1)}, u32[]{:S(2)}) %copy-start.1) | copy-done | bytes 5242904
  10.3 0.7 %copy-done.9 = s32[8,48]{1,0:T(8,128)S(1)} copy-done((s32[8,48]{1,0:T(8,128)S(1)}, s32[8,48]{1,0:T(8,128)}, u32[]{:S(2)}) %copy-start.9) | copy-done | bytes 1560
  11.0 0.7 %copy-done.10 = s32[8]{0:T(128)S(1)} copy-done((s32[8]{0:T(128)S(1)}, s32[8]{0:T(128)}, u32[]{:S(2)}) %copy-start.10) | copy-done | bytes 56
  11.6 2.6 %tree.1 = (f32[384,384]{1,0:T(8,128)S(1)}, bf16[20480,128]{1,0:T(8,128)(2,1)S(1)}) custom-call(s32[8]{0:T(128)S(1)} %copy-done.10, s32[8,48]{1,0:T(8,128)S(1)} %copy-done.9, bf16[20480,128]{1,0:T(8,128)(2,1)S(1)} %bitcast.23, bf16[64,1536]{1,0:T(8,128)(2,1)S(1)} %get-tuple-element.18.rest_0_.refs_2_), custom_call_target="tpu_custom_call" | custom-call | flops 1000000000 | bytes 8000000 | tf_op jit(solution)/shard_map/tree/pallas_call | solution.py:216
  14.3 3.7 %base.1 = (f32[384,512]{1,0:T(8,128)S(1)}, f32[384,512]{1,0:T(8,128)S(1)}, bf16[64,1536]{1,0:T(8,128)(2,1)S(1)}, bf16[64,1536]{1,0:T(8,128)(2,1)S(1)}) custom-call(s32[1]{0:T(128)} %bitcast.1.core_ref, bf16[384,2560]{1,0:T(8,128)(2,1)S(1)} %copy-done, ...), custom_call_target="tpu_custom_call", output_to_operand_aliasing={{2}: (4, {}), {3}: (5, {})} | custom-call | flops 4000000000 | bytes 9000000 | tf_op jit(solution)/shard_map/base/pallas_call | solution.py:142
  18.1 1.0 %shrink.3.shrunk_here_ref = f32[3,48,640]{2,1,0:T(8,128)S(1)} custom-call(s32[1]{0:T(128)} %bitcast.me_ref, s32[8,8]{1,0:T(8,128)S(1)} %copy-done.7, s32[8]{0:T(128)S(1)} %copy-done.8, bf16[384,2560]{1,0:T(8,128)(2,1)S(1)} %copy-done, f32[384,512]{1,0:T(8,128)S(1)} %get-tuple-element.23.refs_1_.refs_5_.refs_9_, ...), custom_call_target="tpu_custom_call" | custom-call | flops 90000000 | bytes 600000 | tf_op jit(solution)/shard_map/shrink/pallas_call | solution.py:265
  19.1 2.0 %collective-permute-start.10 = (bf16[64,1536]{1,0:T(8,128)(2,1)S(1)}, bf16[64,1536]{1,0:T(8,128)(2,1)S(1)}, u32[]{:S(2)}, u32[]{:S(2)}) collective-permute-start(bf16[64,1536]{1,0:T(8,128)(2,1)S(1)} %get-tuple-element.25.refs_11_), channel_id=1, source_target_pairs={{4,0},{8,4},{12,8},{14,12},{10,14},{6,10},{2,6},{0,2},{5,1},{9,5},... | collective-permute-start | bytes 589832 | tf_op jit(solution)/shard_map/ppermute | solution.py:500
  21.2 0.2 collective-permute-start.5
  21.3 1.9 %collective-permute-start.3 = (bf16[64,1536]{1,0:T(8,128)(2,1)S(1)}, bf16[64,1536]{1,0:T(8,128)(2,1)S(1)}, u32[]{:S(2)}, u32[]{:S(2)}) collective-permute-start(bf16[64,1536]{1,0:T(8,128)(2,1)S(1)} %collective-permute-done.2.refs_6_.rest_1_), channel_id=1, source_target_pairs={{0,4},{4,8},{8,12},{12,14},{14,10},{10,6},{6,2},{2,0},{1,5},{5,9},... | collective-permute-start | bytes 589832 | tf_op jit(solution)/shard_map/ppermute | solution.py:499
  23.4 4.5 %finish.3 = (bf16[384,16,128]{2,1,0:T(8,128)(2,1)}, bf16[1536,128]{1,0:T(8,128)(2,1)}, f32[8,128]{1,0:T(8,128)S(1)}) custom-call(s32[1]{0:T(128)} %bitcast.me_ref, s32[8,8]{1,0:T(8,128)S(1)} %copy-done.7, s32[8]{0:T(128)S(1)} %copy-done.8, s32[8]{0:T(128)S(1)} %copy-done.11, f32[384,512]{1,0:T(8,128)S(1)} %get-tuple-element.22.here_ref, ...), custom_call_target="tpu_custom_call" | custom-call | flops 2700000000 | bytes 9000000 | tf_op jit(solution)/shard_map/finish/pallas_call | solution.py:416
  27.9 1.0 %collective-permute-done.5.refs_3_ = bf16[64,1536]{1,0:T(8,128)(2,1)S(1)} collective-permute-done((bf16[64,1536]{1,0:T(8,128)(2,1)S(1)}, bf16[64,1536]{1,0:T(8,128)(2,1)S(1)}, u32[]{:S(2)}, u32[]{:S(2)}) %collective-permute-start.5) | collective-permute-done | bytes 196640 | tf_op jit(solution)/shard_map/ppermute | solution.py:499
  28.9 3.5 %collective-permute-done.3.refs_2_.rest_0_ = bf16[64,1536]{1,0:T(8,128)(2,1)S(1)} collective-permute-done((bf16[64,1536]{1,0:T(8,128)(2,1)S(1)}, bf16[64,1536]{1,0:T(8,128)(2,1)S(1)}, u32[]{:S(2)}, u32[]{:S(2)}) %collective-permute-start.3) | collective-permute-done | bytes 196640 | tf_op jit(solution)/shard_map/ppermute | solution.py:499
  32.4 0.9 %shrink.4.shrunk_here_ref = f32[2,48,640]{2,1,0:T(8,128)S(1)} custom-call(s32[1]{0:T(128)} %bitcast.me_ref, s32[8,8]{1,0:T(8,128)S(1)} %copy-done.7, s32[8]{0:T(128)S(1)} %copy-done.8, bf16[384,2560]{1,0:T(8,128)(2,1)S(1)} %copy-done, f32[384,512]{1,0:T(8,128)S(1)} %get-tuple-element.23.refs_1_.refs_5_.refs_9_, ...), custom_call_target="tpu_custom_call" | custom-call | flops 60000000 | bytes 400000 | tf_op jit(solution)/shard_map/shrink/pallas_call | solution.py:265
  33.4 1.6 %collective-permute-start.11 = (bf16[64,1536]{1,0:T(8,128)(2,1)S(1)}, bf16[64,1536]{1,0:T(8,128)(2,1)S(1)}, u32[]{:S(2)}, u32[]{:S(2)}) collective-permute-start(bf16[64,1536]{1,0:T(8,128)(2,1)S(1)} %collective-permute-done.10.refs_7_), channel_id=1, source_target_pairs={{4,0},{8,4},{12,8},{14,12},{10,14},{6,10},{2,6},{0,2},{5,1},{9,5},... | collective-permute-start | bytes 589832 | tf_op jit(solution)/shard_map/ppermute | solution.py:500
  35.0 0.4 collective-permute-start.4
  35.4 0.3 collective-permute-start.6
  35.8 1.7 %collective-permute-start.9 = (bf16[64,1536]{1,0:T(8,128)(2,1)S(1)}, bf16[64,1536]{1,0:T(8,128)(2,1)S(1)}, u32[]{:S(2)}, u32[]{:S(2)}) collective-permute-start(bf16[64,1536]{1,0:T(8,128)(2,1)S(1)} %collective-permute-done.8.refs_6_.rest_1_), channel_id=1, source_target_pairs={{4,0},{8,4},{12,8},{14,12},{10,14},{6,10},{2,6},{0,2},{5,1},{9,5},... | collective-permute-start | bytes 589832 | tf_op jit(solution)/shard_map/ppermute | solution.py:500
  37.5 3.6 %collective-permute-done.11.refs_7_ = bf16[64,1536]{1,0:T(8,128)(2,1)S(1)} collective-permute-done((bf16[64,1536]{1,0:T(8,128)(2,1)S(1)}, bf16[64,1536]{1,0:T(8,128)(2,1)S(1)}, u32[]{:S(2)}, u32[]{:S(2)}) %collective-permute-start.11) | collective-permute-done | bytes 196640 | tf_op jit(solution)/shard_map/ppermute | solution.py:500
  41.1 1.6 %collective-permute-start.13 = (bf16[64,1536]{1,0:T(8,128)(2,1)S(1)}, bf16[64,1536]{1,0:T(8,128)(2,1)S(1)}, u32[]{:S(2)}, u32[]{:S(2)}) collective-permute-start(bf16[64,1536]{1,0:T(8,128)(2,1)S(1)} %collective-permute-done.11.refs_7_), channel_id=1, source_target_pairs={{4,0},{8,4},{12,8},{14,12},{10,14},{6,10},{2,6},{0,2},{5,1},{9,5},... | collective-permute-start | bytes 589832 | tf_op jit(solution)/shard_map/ppermute | solution.py:509
  42.7 0.4 collective-permute-start.12
  43.2 3.4 %finish.4 = (bf16[384,16,128]{2,1,0:T(8,128)(2,1)}, bf16[1536,128]{1,0:T(8,128)(2,1)}, f32[8,128]{1,0:T(8,128)S(1)}) custom-call(s32[1]{0:T(128)} %bitcast.me_ref, s32[8,8]{1,0:T(8,128)S(1)} %copy-done.7, s32[8]{0:T(128)S(1)} %copy-done.8, s32[8]{0:T(128)S(1)} %copy-done.11, ...), custom_call_target="tpu_custom_call", output_to_operand_aliasing={{0}: (14, {}), {1}: (15, {})} | custom-call | flops 1800000000 | bytes 6000000 | tf_op jit(solution)/shard_map/finish/pallas_call | solution.py:416
  46.6 0.3 collective-permute-done.6.refs_3_
  46.9 2.1 %collective-permute-done.13.refs_11_ = bf16[64,1536]{1,0:T(8,128)(2,1)S(1)} collective-permute-done((bf16[64,1536]{1,0:T(8,128)(2,1)S(1)}, bf16[64,1536]{1,0:T(8,128)(2,1)S(1)}, u32[]{:S(2)}, u32[]{:S(2)}) %collective-permute-start.13) | collective-permute-done | bytes 196640 | tf_op jit(solution)/shard_map/ppermute | solution.py:509
  49.1 1.3 %collective-permute-done.12.refs_10_.rest_2_ = bf16[64,1536]{1,0:T(8,128)(2,1)S(1)} collective-permute-done((bf16[64,1536]{1,0:T(8,128)(2,1)S(1)}, bf16[64,1536]{1,0:T(8,128)(2,1)S(1)}, u32[]{:S(2)}, u32[]{:S(2)}) %collective-permute-start.12) | collective-permute-done | bytes 196640 | tf_op jit(solution)/shard_map/ppermute | solution.py:509
  50.4 1.0 %shrink.5.shrunk_here_ref = f32[3,48,640]{2,1,0:T(8,128)S(1)} custom-call(s32[1]{0:T(128)} %bitcast.me_ref, s32[8,8]{1,0:T(8,128)S(1)} %copy-done.7, s32[8]{0:T(128)S(1)} %copy-done.8, bf16[384,2560]{1,0:T(8,128)(2,1)S(1)} %copy-done, f32[384,512]{1,0:T(8,128)S(1)} %get-tuple-element.23.refs_1_.refs_5_.refs_9_, ...), custom_call_target="tpu_custom_call" | custom-call | flops 90000000 | bytes 600000 | tf_op jit(solution)/shard_map/shrink/pallas_call | solution.py:265
  51.4 1.7 %collective-permute-done.16.shrunk_there_ref = f32[3,48,640]{2,1,0:T(8,128)S(1)} collective-permute-done((f32[3,48,640]{2,1,0:T(8,128)S(1)}, f32[3,48,640]{2,1,0:T(8,128)S(1)}, u32[]{:S(2)}, u32[]{:S(2)}) %collective-permute-start.16) | collective-permute-done | bytes 368672 | tf_op jit(solution)/shard_map/ppermute | solution.py:535
  53.1 4.5 %finish.5 = (bf16[384,16,128]{2,1,0:T(8,128)(2,1)}, bf16[1536,128]{1,0:T(8,128)(2,1)}, f32[8,128]{1,0:T(8,128)}) custom-call(s32[1]{0:T(128)} %bitcast.me_ref, s32[8,8]{1,0:T(8,128)S(1)} %copy-done.7, s32[8]{0:T(128)S(1)} %copy-done.8, s32[8]{0:T(128)S(1)} %copy-done.11, ...), custom_call_target="tpu_custom_call", output_to_operand_aliasing={{0}: (15, {}), {1}: (16, {})} | custom-call | flops 2700000000 | bytes 9000000 | tf_op jit(solution)/shard_map/finish/pallas_call | solution.py:416
  (37 shorter events, 0.3 us)
Async XLA Ops:
  0.6 1.0 %copy-start.5 = (bf16[1,2560,64]{1,2,0:T(8,128)(2,1)S(1)}, bf16[1,2560,64]{1,2,0:T(8,128)(2,1)}, u32[]{:S(2)}) copy-start(bf16[1,2560,64]{1,2,0:T(8,128)(2,1)} %param.14) | copy-start | bytes 983044
  1.6 0.9 %copy-start.6 = (bf16[1,64,4,256]{3,2,1,0:T(4,128)(2,1)S(1)}, bf16[1,64,4,256]{3,2,1,0:T(4,128)(2,1)}, u32[]{:S(2)}) copy-start(bf16[1,64,4,256]{3,2,1,0:T(4,128)(2,1)} %param.15) | copy-start | bytes 393220
  2.7 11.6 %collective-permute-start = (bf16[64,1536]{1,0:T(8,128)(2,1)S(1)}, bf16[64,1536]{1,0:T(8,128)(2,1)S(1)}, u32[]{:S(2)}, u32[]{:S(2)}) collective-permute-start(bf16[64,1536]{1,0:T(8,128)(2,1)S(1)} %get-tuple-element.21.refs_3_), channel_id=1, source_target_pairs={{0,4},{4,8},{8,12},{12,14},{14,10},{10,6},{6,2},{2,0},{1,5},{5,9},... | collective-permute-start | bytes 589832 | tf_op jit(solution)/shard_map/ppermute | solution.py:499
  5.8 8.5 %collective-permute-start.1 = (bf16[64,1536]{1,0:T(8,128)(2,1)S(1)}, bf16[64,1536]{1,0:T(8,128)(2,1)S(1)}, u32[]{:S(2)}, u32[]{:S(2)}) collective-permute-start(bf16[64,1536]{1,0:T(8,128)(2,1)S(1)} %get-tuple-element.21.refs_3_), channel_id=1, source_target_pairs={{4,0},{8,4},{12,8},{14,12},{10,14},{6,10},{2,6},{0,2},{5,1},{9,5},... | collective-permute-start | bytes 589832 | tf_op jit(solution)/shard_map/ppermute | solution.py:500
  5.8 12.2 %collective-permute-start.2 = (bf16[64,1536]{1,0:T(8,128)(2,1)S(1)}, bf16[64,1536]{1,0:T(8,128)(2,1)S(1)}, u32[]{:S(2)}, u32[]{:S(2)}) collective-permute-start(bf16[64,1536]{1,0:T(8,128)(2,1)S(1)} %get-tuple-element.18.rest_0_.refs_2_), channel_id=1, source_target_pairs={{0,4},{4,8},{8,12},{12,14},{14,10},{10,6},{6,2},{2,0},{1,5},{5,9},... | collective-permute-start | bytes 589832 | tf_op jit(solution)/shard_map/ppermute | solution.py:499
  7.8 10.2 %collective-permute-start.7 = (bf16[64,1536]{1,0:T(8,128)(2,1)S(1)}, bf16[64,1536]{1,0:T(8,128)(2,1)S(1)}, u32[]{:S(2)}, u32[]{:S(2)}) collective-permute-start(bf16[64,1536]{1,0:T(8,128)(2,1)S(1)} %get-tuple-element.18.rest_0_.refs_2_), channel_id=1, source_target_pairs={{4,0},{8,4},{12,8},{14,12},{10,14},{6,10},{2,6},{0,2},{5,1},{9,5},... | collective-permute-start | bytes 589832 | tf_op jit(solution)/shard_map/ppermute | solution.py:500
  7.8 2.5 %copy-start.1 = (bf16[2560,4,256]{2,1,0:T(4,128)(2,1)S(1)}, bf16[2560,4,256]{2,1,0:T(4,128)(2,1)}, u32[]{:S(2)}) copy-start(bf16[2560,4,256]{2,1,0:T(4,128)(2,1)} %param.13) | copy-start | bytes 15728644
  10.3 0.7 %copy-start.9 = (s32[8,48]{1,0:T(8,128)S(1)}, s32[8,48]{1,0:T(8,128)}, u32[]{:S(2)}) copy-start(s32[8,48]{1,0:T(8,128)} %parent_ref.1) | copy-start | bytes 4612
  11.0 0.7 %copy-start.10 = (s32[8]{0:T(128)S(1)}, s32[8]{0:T(128)}, u32[]{:S(2)}) copy-start(s32[8]{0:T(128)} %length_ref.7) | copy-start | bytes 100
  11.6 2.7 %copy-start = (bf16[384,2560]{1,0:T(8,128)(2,1)S(1)}, bf16[384,2560]{1,0:T(8,128)(2,1)}, u32[]{:S(2)}) copy-start(bf16[384,2560]{1,0:T(8,128)(2,1)} %refs_8_.3) | copy-start | bytes 5898244
  14.3 3.7 %copy-start.7 = (s32[8,8]{1,0:T(8,128)S(1)}, s32[8,8]{1,0:T(8,128)}, u32[]{:S(2)}) copy-start(s32[8,8]{1,0:T(8,128)} %constant.10.clone.owner_ref) | copy-start | bytes 772
  14.3 3.7 %copy-start.8 = (s32[8]{0:T(128)S(1)}, s32[8]{0:T(128)}, u32[]{:S(2)}) copy-start(s32[8]{0:T(128)} %adapter_ref.11) | copy-start | bytes 100
  18.1 5.3 %copy-start.2 = (bf16[384,16,128]{2,1,0:T(8,128)(2,1)S(1)}, bf16[384,16,128]{2,1,0:T(8,128)(2,1)}, u32[]{:S(2)}) copy-start(bf16[384,16,128]{2,1,0:T(8,128)(2,1)} %query_ref.5) | copy-start | bytes 4718596
  18.1 5.3 %copy-start.3 = (bf16[8,128,2,128]{3,2,1,0:T(2,128)(2,1)S(1)}, bf16[8,128,2,128]{3,2,1,0:T(2,128)(2,1)}, u32[]{:S(2)}) copy-start(bf16[8,128,2,128]{3,2,1,0:T(2,128)(2,1)} %param.20) | copy-start | bytes 1572868
  18.1 5.3 %copy-start.4 = (bf16[8,128,2,128]{3,2,1,0:T(2,128)(2,1)S(1)}, bf16[8,128,2,128]{3,2,1,0:T(2,128)(2,1)}, u32[]{:S(2)}) copy-start(bf16[8,128,2,128]{3,2,1,0:T(2,128)(2,1)} %param.21) | copy-start | bytes 1572868
  18.1 5.3 %copy-start.11 = (s32[8]{0:T(128)S(1)}, s32[8]{0:T(128)}, u32[]{:S(2)}) copy-start(s32[8]{0:T(128)} %length_ref.7) | copy-start | bytes 100
  18.1 5.3 %copy-start.12 = (f32[128]{0:T(128)S(1)}, f32[128]{0:T(128)}, u32[]{:S(2)}) copy-start(f32[128]{0:T(128)} %param.22) | copy-start | bytes 1540
  19.1 4.2 %collective-permute-start.14 = (f32[3,48,640]{2,1,0:T(8,128)S(1)}, f32[3,48,640]{2,1,0:T(8,128)S(1)}, u32[]{:S(2)}, u32[]{:S(2)}) collective-permute-start(f32[3,48,640]{2,1,0:T(8,128)S(1)} %shrink.3.shrunk_here_ref), channel_id=1, source_target_pairs={{0,1},{1,0},{2,3},{3,2},{4,5},{5,4},{6,7},{7,6},{8,9},{9,8},{10,11... | collective-permute-start | bytes 1105928 | tf_op jit(solution)/shard_map/ppermute | solution.py:535
  19.1 8.7 %collective-permute-start.10 = (bf16[64,1536]{1,0:T(8,128)(2,1)S(1)}, bf16[64,1536]{1,0:T(8,128)(2,1)S(1)}, u32[]{:S(2)}, u32[]{:S(2)}) collective-permute-start(bf16[64,1536]{1,0:T(8,128)(2,1)S(1)} %get-tuple-element.25.refs_11_), channel_id=1, source_target_pairs={{4,0},{8,4},{12,8},{14,12},{10,14},{6,10},{2,6},{0,2},{5,1},{9,5},... | collective-permute-start | bytes 589832 | tf_op jit(solution)/shard_map/ppermute | solution.py:500
  21.2 7.7 %collective-permute-start.5 = (bf16[64,1536]{1,0:T(8,128)(2,1)S(1)}, bf16[64,1536]{1,0:T(8,128)(2,1)S(1)}, u32[]{:S(2)}, u32[]{:S(2)}) collective-permute-start(bf16[64,1536]{1,0:T(8,128)(2,1)S(1)} %get-tuple-element.24.refs_7_), channel_id=1, source_target_pairs={{0,4},{4,8},{8,12},{12,14},{14,10},{10,6},{6,2},{2,0},{1,5},{5,9},... | collective-permute-start | bytes 589832 | tf_op jit(solution)/shard_map/ppermute | solution.py:499
  21.3 11.0 %collective-permute-start.3 = (bf16[64,1536]{1,0:T(8,128)(2,1)S(1)}, bf16[64,1536]{1,0:T(8,128)(2,1)S(1)}, u32[]{:S(2)}, u32[]{:S(2)}) collective-permute-start(bf16[64,1536]{1,0:T(8,128)(2,1)S(1)} %collective-permute-done.2.refs_6_.rest_1_), channel_id=1, source_target_pairs={{0,4},{4,8},{8,12},{12,14},{14,10},{10,6},{6,2},{2,0},{1,5},{5,9},... | collective-permute-start | bytes 589832 | tf_op jit(solution)/shard_map/ppermute | solution.py:499
  23.2 9.1 %collective-permute-start.8 = (bf16[64,1536]{1,0:T(8,128)(2,1)S(1)}, bf16[64,1536]{1,0:T(8,128)(2,1)S(1)}, u32[]{:S(2)}, u32[]{:S(2)}) collective-permute-start(bf16[64,1536]{1,0:T(8,128)(2,1)S(1)} %collective-permute-done.7.refs_10_.rest_2_), channel_id=1, source_target_pairs={{4,0},{8,4},{12,8},{14,12},{10,14},{6,10},{2,6},{0,2},{5,1},{9,5},... | collective-permute-start | bytes 589832 | tf_op jit(solution)/shard_map/ppermute | solution.py:500
  33.3 9.9 %collective-permute-start.15 = (f32[2,48,640]{2,1,0:T(8,128)S(1)}, f32[2,48,640]{2,1,0:T(8,128)S(1)}, u32[]{:S(2)}, u32[]{:S(2)}) collective-permute-start(f32[2,48,640]{2,1,0:T(8,128)S(1)} %shrink.4.shrunk_here_ref), channel_id=1, source_target_pairs={{0,1},{1,0},{2,3},{3,2},{4,5},{5,4},{6,7},{7,6},{8,9},{9,8},{10,11... | collective-permute-start | bytes 737288 | tf_op jit(solution)/shard_map/ppermute | solution.py:535
  33.4 7.8 %collective-permute-start.11 = (bf16[64,1536]{1,0:T(8,128)(2,1)S(1)}, bf16[64,1536]{1,0:T(8,128)(2,1)S(1)}, u32[]{:S(2)}, u32[]{:S(2)}) collective-permute-start(bf16[64,1536]{1,0:T(8,128)(2,1)S(1)} %collective-permute-done.10.refs_7_), channel_id=1, source_target_pairs={{4,0},{8,4},{12,8},{14,12},{10,14},{6,10},{2,6},{0,2},{5,1},{9,5},... | collective-permute-start | bytes 589832 | tf_op jit(solution)/shard_map/ppermute | solution.py:500
  35.0 7.7 %collective-permute-start.4 = (bf16[64,1536]{1,0:T(8,128)(2,1)S(1)}, bf16[64,1536]{1,0:T(8,128)(2,1)S(1)}, u32[]{:S(2)}, u32[]{:S(2)}) collective-permute-start(bf16[64,1536]{1,0:T(8,128)(2,1)S(1)} %collective-permute-done.3.refs_2_.rest_0_), channel_id=1, source_target_pairs={{0,4},{4,8},{8,12},{12,14},{14,10},{10,6},{6,2},{2,0},{1,5},{5,9},... | collective-permute-start | bytes 589832 | tf_op jit(solution)/shard_map/ppermute | solution.py:499
  35.4 11.5 %collective-permute-start.6 = (bf16[64,1536]{1,0:T(8,128)(2,1)S(1)}, bf16[64,1536]{1,0:T(8,128)(2,1)S(1)}, u32[]{:S(2)}, u32[]{:S(2)}) collective-permute-start(bf16[64,1536]{1,0:T(8,128)(2,1)S(1)} %collective-permute-done.5.refs_3_), channel_id=1, source_target_pairs={{0,4},{4,8},{8,12},{12,14},{14,10},{10,6},{6,2},{2,0},{1,5},{5,9},... | collective-permute-start | bytes 589832 | tf_op jit(solution)/shard_map/ppermute | solution.py:499
  35.8 11.2 %collective-permute-start.9 = (bf16[64,1536]{1,0:T(8,128)(2,1)S(1)}, bf16[64,1536]{1,0:T(8,128)(2,1)S(1)}, u32[]{:S(2)}, u32[]{:S(2)}) collective-permute-start(bf16[64,1536]{1,0:T(8,128)(2,1)S(1)} %collective-permute-done.8.refs_6_.rest_1_), channel_id=1, source_target_pairs={{4,0},{8,4},{12,8},{14,12},{10,14},{6,10},{2,6},{0,2},{5,1},{9,5},... | collective-permute-start | bytes 589832 | tf_op jit(solution)/shard_map/ppermute | solution.py:500
  41.1 8.0 %collective-permute-start.13 = (bf16[64,1536]{1,0:T(8,128)(2,1)S(1)}, bf16[64,1536]{1,0:T(8,128)(2,1)S(1)}, u32[]{:S(2)}, u32[]{:S(2)}) collective-permute-start(bf16[64,1536]{1,0:T(8,128)(2,1)S(1)} %collective-permute-done.11.refs_7_), channel_id=1, source_target_pairs={{4,0},{8,4},{12,8},{14,12},{10,14},{6,10},{2,6},{0,2},{5,1},{9,5},... | collective-permute-start | bytes 589832 | tf_op jit(solution)/shard_map/ppermute | solution.py:509
  42.7 7.7 %collective-permute-start.12 = (bf16[64,1536]{1,0:T(8,128)(2,1)S(1)}, bf16[64,1536]{1,0:T(8,128)(2,1)S(1)}, u32[]{:S(2)}, u32[]{:S(2)}) collective-permute-start(bf16[64,1536]{1,0:T(8,128)(2,1)S(1)} %collective-permute-done.4.refs_2_.rest_0_), channel_id=1, source_target_pairs={{0,4},{4,8},{8,12},{12,14},{14,10},{10,6},{6,2},{2,0},{1,5},{5,9},... | collective-permute-start | bytes 589832 | tf_op jit(solution)/shard_map/ppermute | solution.py:509
  51.4 1.7 %collective-permute-start.16 = (f32[3,48,640]{2,1,0:T(8,128)S(1)}, f32[3,48,640]{2,1,0:T(8,128)S(1)}, u32[]{:S(2)}, u32[]{:S(2)}) collective-permute-start(f32[3,48,640]{2,1,0:T(8,128)S(1)} %shrink.5.shrunk_here_ref), channel_id=1, source_target_pairs={{0,1},{1,0},{2,3},{3,2},{4,5},{5,4},{6,7},{7,6},{8,9},{9,8},{10,11... | collective-permute-start | bytes 1105928 | tf_op jit(solution)/shard_map/ppermute | solution.py:535

commit v8 on v7

--- a/solution.py
+++ b/solution.py
@@ -47,6 +47,18 @@
     for r in range(1, adapter_ref.shape[0]):
         request = jnp.where(adapter_ref[r] == owner, jnp.int32(r), request)
     return request
+
+
+def hold(array, token):
+    return pl.pallas_call(
+        lambda array_ref, token_ref, output_ref: None,
+        in_specs=[ANYWHERE, ANYWHERE],
+        out_specs=ANYWHERE,
+        out_shape=jax.ShapeDtypeStruct(array.shape, array.dtype),
+        input_output_aliases={0: 0},
+        compiler_params=pltpu.CompilerParams(vmem_limit_bytes=4 * 1024 * 1024),
+        name="hold",
+    )(array, token)
 
 
 def pack_kernel(core_ref, shrink_ref, expand_ref, first_ref, second_ref, *, cut, heads_here):
@@ -433,7 +445,7 @@
         ],
         input_output_aliases=aliases,
         cost_estimate=pl.CostEstimate(
-            flops=count * 900000000, bytes_accessed=count * 3000000, transcendentals=0
+            flops=count * 90000000, bytes_accessed=count * 300000, transcendentals=0
         ),
         compiler_params=pltpu.CompilerParams(vmem_limit_bytes=16 * 1024 * 1024),
         name="finish",
@@ -495,6 +507,20 @@
     table, weight_rows = tree_tables(
         cache_lengths, tree_parents, head_size, heads_here, weight_rows, [first]
     )
+    split_batches = pool_count == requests
+    near = 3
+    done = [(None, 0)]
+    shared = None
+
+    def finish_batch(group):
+        outputs, slot = done[-1]
+        after = [] if outputs is None else [outputs[2]]
+        partial = shrink_rows(
+            where, slot, hidden_states, away, group, tree_size, columns, cut, after
+        )
+        batch = (partial, lax.ppermute(partial, "tp", swap), [piece[0] for piece in group])
+        done.append((finish(where, slot, batch, shared, outputs), slot + len(group)))
+
     for step in range(1, half):
         front = tuple(lax.ppermute(piece, "pool", onward) for piece in front)
         rear = tuple(lax.ppermute(piece, "pool", backward) for piece in rear)
@@ -503,38 +529,29 @@
             here, away, *held = base_product(
                 core, hidden_states, weight_rows, kv_heads * kv_width, [table], held
             )
-        front, rear = (front[0], held[0]), (rear[0], held[1])
+            shared = (
+                cache_lengths,
+                key_gain.reshape(1, head_size),
+                here,
+                table,
+                queries,
+                key_rows,
+                value_rows,
+            )
+        first_front = front[0]
+        if step == 2 and split_batches:
+            finish_batch(arrivals[:near])
+            token = done[-1][0][2]
+            first_front, held[1] = hold(first_front, token), hold(held[1], token)
+        front, rear = (first_front, held[0]), (rear[0], held[1])
         arrivals += [front, rear]
     arrivals.append(
         (lax.ppermute(front[0], "pool", onward), lax.ppermute(rear[1], "pool", backward))
     )
-    shared = (
-        cache_lengths,
-        key_gain.reshape(1, head_size),
-        here,
-        table,
-        queries,
-        key_rows,
-        value_rows,
-    )
-    outputs = None
-    if pool_count == requests:
-        near = 3
-        groups = [
-            (arrivals[:near], []),
-            (arrivals[near:-3], []),
-            (arrivals[-3:], []),
-        ]
-        slot = 0
-        for group, after in groups:
-            if outputs is not None:
-                after = after + [outputs[2]]
-            partial = shrink_rows(
-                where, slot, hidden_states, away, group, tree_size, columns, cut, after
-            )
-            batch = (partial, lax.ppermute(partial, "tp", swap), [piece[0] for piece in group])
-            outputs = finish(where, slot, batch, shared, outputs)
-            slot += len(group)
+    if split_batches:
+        finish_batch(arrivals[near:-3])
+        finish_batch(arrivals[-3:])
+        outputs = done[-1][0]
     else:
         parts = [
             shrink_rows(where, slot, hidden_states, away, [piece], tree_size, columns, cut, [])

time: 57.8 us -> 53.1 us (0.919)
  waiting for transfers between devices: 13.6 us -> 8.97 us
    ppermute x6, waiting for transfers between devices: 3.66 us -> 0.15 us  [per_device(): rear = tuple((lax.ppermute(piece, 'pool', backward) for piece in rear))]
    ppermute x1, waiting for transfers between devices: 2.14 us -> 3.69 us  [per_device(): lax.ppermute(rear[1], 'pool', backward)]
    ppermute x6, waiting for transfers between devices: 4.87 us -> 3.44 us  [per_device(): front = tuple((lax.ppermute(piece, 'pool', onward) for piece in front))]
    ppermute x1, waiting for transfers between devices: 1.3 us -> 0.01 us  [per_device(): lax.ppermute(front[0], 'pool', onward)]
  transfers between devices with their start and end apart: 17 -> 17, of which waited for: 7 -> 5; matrix products, arithmetic and copies ran while one was open for 0% -> 0% of each run, Pallas kernels for 25% -> 29%
where the time goes in v8:
time: 53.1 us; the launch traced here: 52.9 us
  Pallas kernels  21.8 us (41%)
  starting transfers between devices  15.5 us (29%)
  waiting for transfers between devices  8.97 us (17%)
  local copies, waits for them, and re-layouts  5.74 us (11%)
  between operations  0.86 us (2%)
    pallas_call x3, Pallas kernels, finish(): pl.pallas_call(functools.partial(finish_kernel, count=count, slot=slot, k...  12.4 us
    ppermute x6, starting transfers between devices, per_device(): front = tuple((lax.ppermute(piece, 'pool', onward) for piece in front))  7.52 us
    ppermute x6, starting transfers between devices, per_device(): rear = tuple((lax.ppermute(piece, 'pool', backward) for piece in rear))  5.89 us
    unnamed x26, local copies, waits for them, and re-layouts  5.74 us
    ppermute x1, waiting for transfers between devices, per_device(): lax.ppermute(rear[1], 'pool', backward)  3.69 us
    pallas_call x1, Pallas kernels, base_product(): pl.pallas_call(functools.partial(base_kernel, held_count=len(held)), grid...  3.68 us
    ppermute x6, waiting for transfers between devices, per_device(): front = tuple((lax.ppermute(piece, 'pool', onward) for piece in front))  3.44 us
    pallas_call x3, Pallas kernels, shrink_rows(): pl.pallas_call(functools.partial(shrink_kernel, columns=columns, cut=cut)...  2.91 us
  transfers between devices with their start and end apart: 17, of which 5 were waited for; matrix products, arithmetic and copies ran while one was open for 0% of the time, Pallas kernels for 29%

profile of v8, /device:TPU:0, one launch (start us, length us, event | category | flops | bytes accessed | tf_op | source)
XLA Modules:
  0.0 52.9 jit_solution(6024109728567259489)
XLA Ops:
  0.6 1.0 %copy-done.5 = bf16[1,2560,64]{1,2,0:T(8,128)(2,1)S(1)} copy-done((bf16[1,2560,64]{1,2,0:T(8,128)(2,1)S(1)}, bf16[1,2560,64]{1,2,0:T(8,128)(2,1)}, u32[]{:S(2)}) %copy-start.5) | copy-done | bytes 327704
  1.6 0.9 %copy-done.7 = bf16[1,64,4,256]{3,2,1,0:T(4,128)(2,1)S(1)} copy-done((bf16[1,64,4,256]{3,2,1,0:T(4,128)(2,1)S(1)}, bf16[1,64,4,256]{3,2,1,0:T(4,128)(2,1)}, u32[]{:S(2)}) %copy-start.7) | copy-done | bytes 131096
  2.5 0.2 pack.1
  2.7 3.1 %collective-permute-start = (bf16[64,1536]{1,0:T(8,128)(2,1)S(1)}, bf16[64,1536]{1,0:T(8,128)(2,1)S(1)}, u32[]{:S(2)}, u32[]{:S(2)}) collective-permute-start(bf16[64,1536]{1,0:T(8,128)(2,1)S(1)} %get-tuple-element.21.refs_3_), channel_id=1, source_target_pairs={{0,4},{4,8},{8,12},{12,14},{14,10},{10,6},{6,2},{2,0},{1,5},{5,9},... | collective-permute-start | bytes 589832 | tf_op jit(solution)/shard_map/ppermute | solution.py:525
  5.8 2.0 %collective-permute-start.2 = (bf16[64,1536]{1,0:T(8,128)(2,1)S(1)}, bf16[64,1536]{1,0:T(8,128)(2,1)S(1)}, u32[]{:S(2)}, u32[]{:S(2)}) collective-permute-start(bf16[64,1536]{1,0:T(8,128)(2,1)S(1)} %get-tuple-element.18.rest_0_.refs_2_), channel_id=1, source_target_pairs={{0,4},{4,8},{8,12},{12,14},{14,10},{10,6},{6,2},{2,0},{1,5},{5,9},... | collective-permute-start | bytes 589832 | tf_op jit(solution)/shard_map/ppermute | solution.py:525
  7.8 2.5 %copy-done.2 = bf16[2560,4,256]{2,1,0:T(4,128)(2,1)S(1)} copy-done((bf16[2560,4,256]{2,1,0:T(4,128)(2,1)S(1)}, bf16[2560,4,256]{2,1,0:T(4,128)(2,1)}, u32[]{:S(2)}) %copy-start.2) | copy-done | bytes 5242904
  10.3 0.7 %copy-done.9 = s32[8]{0:T(128)S(1)} copy-done((s32[8]{0:T(128)S(1)}, s32[8]{0:T(128)}, u32[]{:S(2)}) %copy-start.9) | copy-done | bytes 56
  10.9 0.7 %copy-done.12 = s32[8,48]{1,0:T(8,128)S(1)} copy-done((s32[8,48]{1,0:T(8,128)S(1)}, s32[8,48]{1,0:T(8,128)}, u32[]{:S(2)}) %copy-start.12) | copy-done | bytes 1560
  11.6 2.6 %tree.1 = (f32[384,384]{1,0:T(8,128)S(1)}, bf16[20480,128]{1,0:T(8,128)(2,1)S(1)}) custom-call(s32[8]{0:T(128)S(1)} %copy-done.9, s32[8,48]{1,0:T(8,128)S(1)} %copy-done.12, bf16[20480,128]{1,0:T(8,128)(2,1)S(1)} %bitcast.23, bf16[64,1536]{1,0:T(8,128)(2,1)S(1)} %get-tuple-element.18.rest_0_.refs_2_), custom_call_target="tpu_custom_call" | custom-call | flops 1000000000 | bytes 8000000 | tf_op jit(solution)/shard_map/tree/pallas_call | solution.py:228
  14.3 3.7 %base.1 = (f32[384,512]{1,0:T(8,128)S(1)}, f32[384,512]{1,0:T(8,128)S(1)}, bf16[64,1536]{1,0:T(8,128)(2,1)S(1)}, bf16[64,1536]{1,0:T(8,128)(2,1)S(1)}) custom-call(s32[1]{0:T(128)} %bitcast.1.core_ref, bf16[384,2560]{1,0:T(8,128)(2,1)S(1)} %copy-done, ...), custom_call_target="tpu_custom_call", output_to_operand_aliasing={{2}: (4, {}), {3}: (5, {})} | custom-call | flops 4000000000 | bytes 9000000 | tf_op jit(solution)/shard_map/base/pallas_call | solution.py:154
  18.1 1.0 %shrink.3.shrunk_here_ref = f32[3,48,640]{2,1,0:T(8,128)S(1)} custom-call(s32[1]{0:T(128)} %bitcast.me_ref, s32[8,8]{1,0:T(8,128)S(1)} %copy-done.6, s32[8]{0:T(128)S(1)} %copy-done.8, bf16[384,2560]{1,0:T(8,128)(2,1)S(1)} %copy-done, f32[384,512]{1,0:T(8,128)S(1)} %get-tuple-element.23.refs_1_.refs_5_.refs_9_, ...), custom_call_target="tpu_custom_call" | custom-call | flops 90000000 | bytes 600000 | tf_op jit(solution)/shard_map/shrink/pallas_call | solution.py:277
  19.1 2.0 %collective-permute-start.11 = (bf16[64,1536]{1,0:T(8,128)(2,1)S(1)}, bf16[64,1536]{1,0:T(8,128)(2,1)S(1)}, u32[]{:S(2)}, u32[]{:S(2)}) collective-permute-start(bf16[64,1536]{1,0:T(8,128)(2,1)S(1)} %get-tuple-element.25.refs_11_), channel_id=1, source_target_pairs={{4,0},{8,4},{12,8},{14,12},{10,14},{6,10},{2,6},{0,2},{5,1},{9,5},... | collective-permute-start | bytes 589832 | tf_op jit(solution)/shard_map/ppermute | solution.py:526
  21.2 0.2 collective-permute-start.3
  21.3 1.9 %collective-permute-start.7 = (bf16[64,1536]{1,0:T(8,128)(2,1)S(1)}, bf16[64,1536]{1,0:T(8,128)(2,1)S(1)}, u32[]{:S(2)}, u32[]{:S(2)}) collective-permute-start(bf16[64,1536]{1,0:T(8,128)(2,1)S(1)} %get-tuple-element.24.refs_7_), channel_id=1, source_target_pairs={{0,4},{4,8},{8,12},{12,14},{14,10},{10,6},{6,2},{2,0},{1,5},{5,9},... | collective-permute-start | bytes 589832 | tf_op jit(solution)/shard_map/ppermute | solution.py:525
  23.3 0.1 collective-permute-start.9
  23.4 4.5 %finish.3 = (bf16[384,16,128]{2,1,0:T(8,128)(2,1)}, bf16[1536,128]{1,0:T(8,128)(2,1)}, f32[8,128]{1,0:T(8,128)S(1)}) custom-call(s32[1]{0:T(128)} %bitcast.me_ref, s32[8,8]{1,0:T(8,128)S(1)} %copy-done.6, s32[8]{0:T(128)S(1)} %copy-done.8, s32[8]{0:T(128)S(1)} %copy-done.10, f32[384,512]{1,0:T(8,128)S(1)} %get-tuple-element.22.here_ref, ...), custom_call_target="tpu_custom_call" | custom-call | flops 270000000 | bytes 900000 | tf_op jit(solution)/shard_map/finish/pallas_call | solution.py:428
  27.9 1.9 %collective-permute-start.12 = (bf16[64,1536]{1,0:T(8,128)(2,1)S(1)}, bf16[64,1536]{1,0:T(8,128)(2,1)S(1)}, u32[]{:S(2)}, u32[]{:S(2)}) collective-permute-start(bf16[64,1536]{1,0:T(8,128)(2,1)S(1)} %hold.3.refs_7_), channel_id=1, source_target_pairs={{4,0},{8,4},{12,8},{14,12},{10,14},{6,10},{2,6},{0,2},{5,1},{9,5},... | collective-permute-start | bytes 589832 | tf_op jit(solution)/shard_map/ppermute | solution.py:526
  29.8 0.2 collective-permute-start.6
  29.9 3.2 %collective-permute-done.7.refs_3_ = bf16[64,1536]{1,0:T(8,128)(2,1)S(1)} collective-permute-done((bf16[64,1536]{1,0:T(8,128)(2,1)S(1)}, bf16[64,1536]{1,0:T(8,128)(2,1)S(1)}, u32[]{:S(2)}, u32[]{:S(2)}) %collective-permute-start.7) | collective-permute-done | bytes 196640 | tf_op jit(solution)/shard_map/ppermute | solution.py:525
  33.1 0.9 %shrink.4.shrunk_here_ref = f32[2,48,640]{2,1,0:T(8,128)S(1)} custom-call(s32[1]{0:T(128)} %bitcast.me_ref, s32[8,8]{1,0:T(8,128)S(1)} %copy-done.6, s32[8]{0:T(128)S(1)} %copy-done.8, bf16[384,2560]{1,0:T(8,128)(2,1)S(1)} %copy-done, f32[384,512]{1,0:T(8,128)S(1)} %get-tuple-element.23.refs_1_.refs_5_.refs_9_, bf16[64,1536]{1,0:T(8,128)(2,1)S(1)} %hold.2.refs_2_.rest_0_, ...), custom_call_target="tpu_custom_call" | custom-call | flops 60000000 | bytes 400000 | tf_op jit(solution)/shard_map/shrink/pallas_call | solution.py:277
  34.0 0.1 collective-permute-start.15
  34.1 0.2 collective-permute-start.8
  34.3 1.9 %collective-permute-start.10 = (bf16[64,1536]{1,0:T(8,128)(2,1)S(1)}, bf16[64,1536]{1,0:T(8,128)(2,1)S(1)}, u32[]{:S(2)}, u32[]{:S(2)}) collective-permute-start(bf16[64,1536]{1,0:T(8,128)(2,1)S(1)} %collective-permute-done.9.refs_6_.rest_1_), channel_id=1, source_target_pairs={{4,0},{8,4},{12,8},{14,12},{10,14},{6,10},{2,6},{0,2},{5,1},{9,5},... | collective-permute-start | bytes 589832 | tf_op jit(solution)/shard_map/ppermute | solution.py:526
  36.2 1.6 %collective-permute-start.14 = (bf16[64,1536]{1,0:T(8,128)(2,1)S(1)}, bf16[64,1536]{1,0:T(8,128)(2,1)S(1)}, u32[]{:S(2)}, u32[]{:S(2)}) collective-permute-start(bf16[64,1536]{1,0:T(8,128)(2,1)S(1)} %collective-permute-done.12.refs_7_), channel_id=1, source_target_pairs={{4,0},{8,4},{12,8},{14,12},{10,14},{6,10},{2,6},{0,2},{5,1},{9,5},... | collective-permute-start | bytes 589832 | tf_op jit(solution)/shard_map/ppermute | solution.py:549
  37.8 0.4 collective-permute-start.13
  38.2 3.4 %finish.4 = (bf16[384,16,128]{2,1,0:T(8,128)(2,1)}, bf16[1536,128]{1,0:T(8,128)(2,1)}, f32[8,128]{1,0:T(8,128)S(1)}) custom-call(s32[1]{0:T(128)} %bitcast.me_ref, s32[8,8]{1,0:T(8,128)S(1)} %copy-done.6, s32[8]{0:T(128)S(1)} %copy-done.8, s32[8]{0:T(128)S(1)} %copy-done.10, ...), custom_call_target="tpu_custom_call", output_to_operand_aliasing={{0}: (14, {}), {1}: (15, {})} | custom-call | flops 180000000 | bytes 600000 | tf_op jit(solution)/shard_map/finish/pallas_call | solution.py:428
  41.7 0.2 collective-permute-done.8.refs_3_
  41.9 0.1 collective-permute-done.10.refs_6_.rest_1_
  42.0 3.7 %collective-permute-done.14.refs_11_ = bf16[64,1536]{1,0:T(8,128)(2,1)S(1)} collective-permute-done((bf16[64,1536]{1,0:T(8,128)(2,1)S(1)}, bf16[64,1536]{1,0:T(8,128)(2,1)S(1)}, u32[]{:S(2)}, u32[]{:S(2)}) %collective-permute-start.14) | collective-permute-done | bytes 196640 | tf_op jit(solution)/shard_map/ppermute | solution.py:549
  45.7 1.0 %shrink.5.shrunk_here_ref = f32[3,48,640]{2,1,0:T(8,128)S(1)} custom-call(s32[1]{0:T(128)} %bitcast.me_ref, s32[8,8]{1,0:T(8,128)S(1)} %copy-done.6, s32[8]{0:T(128)S(1)} %copy-done.8, bf16[384,2560]{1,0:T(8,128)(2,1)S(1)} %copy-done, f32[384,512]{1,0:T(8,128)S(1)} %get-tuple-element.23.refs_1_.refs_5_.refs_9_, ...), custom_call_target="tpu_custom_call" | custom-call | flops 90000000 | bytes 600000 | tf_op jit(solution)/shard_map/shrink/pallas_call | solution.py:277
  46.7 1.7 %collective-permute-done.16.shrunk_there_ref = f32[3,48,640]{2,1,0:T(8,128)S(1)} collective-permute-done((f32[3,48,640]{2,1,0:T(8,128)S(1)}, f32[3,48,640]{2,1,0:T(8,128)S(1)}, u32[]{:S(2)}, u32[]{:S(2)}) %collective-permute-start.16) | collective-permute-done | bytes 368672 | tf_op jit(solution)/shard_map/ppermute | solution.py:521
  48.4 4.5 %finish.5 = (bf16[384,16,128]{2,1,0:T(8,128)(2,1)}, bf16[1536,128]{1,0:T(8,128)(2,1)}, f32[8,128]{1,0:T(8,128)}) custom-call(s32[1]{0:T(128)} %bitcast.me_ref, s32[8,8]{1,0:T(8,128)S(1)} %copy-done.6, s32[8]{0:T(128)S(1)} %copy-done.8, s32[8]{0:T(128)S(1)} %copy-done.10, ...), custom_call_target="tpu_custom_call", output_to_operand_aliasing={{0}: (15, {}), {1}: (16, {})} | custom-call | flops 270000000 | bytes 900000 | tf_op jit(solution)/shard_map/finish/pallas_call | solution.py:428
  (39 shorter events, 0.1 us)
Async XLA Ops:
  0.6 1.0 %copy-start.5 = (bf16[1,2560,64]{1,2,0:T(8,128)(2,1)S(1)}, bf16[1,2560,64]{1,2,0:T(8,128)(2,1)}, u32[]{:S(2)}) copy-start(bf16[1,2560,64]{1,2,0:T(8,128)(2,1)} %param.14) | copy-start | bytes 983044
  1.6 0.9 %copy-start.7 = (bf16[1,64,4,256]{3,2,1,0:T(4,128)(2,1)S(1)}, bf16[1,64,4,256]{3,2,1,0:T(4,128)(2,1)}, u32[]{:S(2)}) copy-start(bf16[1,64,4,256]{3,2,1,0:T(4,128)(2,1)} %param.15) | copy-start | bytes 393220
  2.7 11.6 %collective-permute-start = (bf16[64,1536]{1,0:T(8,128)(2,1)S(1)}, bf16[64,1536]{1,0:T(8,128)(2,1)S(1)}, u32[]{:S(2)}, u32[]{:S(2)}) collective-permute-start(bf16[64,1536]{1,0:T(8,128)(2,1)S(1)} %get-tuple-element.21.refs_3_), channel_id=1, source_target_pairs={{0,4},{4,8},{8,12},{12,14},{14,10},{10,6},{6,2},{2,0},{1,5},{5,9},... | collective-permute-start | bytes 589832 | tf_op jit(solution)/shard_map/ppermute | solution.py:525
  5.8 8.5 %collective-permute-start.1 = (bf16[64,1536]{1,0:T(8,128)(2,1)S(1)}, bf16[64,1536]{1,0:T(8,128)(2,1)S(1)}, u32[]{:S(2)}, u32[]{:S(2)}) collective-permute-start(bf16[64,1536]{1,0:T(8,128)(2,1)S(1)} %get-tuple-element.21.refs_3_), channel_id=1, source_target_pairs={{4,0},{8,4},{12,8},{14,12},{10,14},{6,10},{2,6},{0,2},{5,1},{9,5},... | collective-permute-start | bytes 589832 | tf_op jit(solution)/shard_map/ppermute | solution.py:526
  5.8 12.2 %collective-permute-start.2 = (bf16[64,1536]{1,0:T(8,128)(2,1)S(1)}, bf16[64,1536]{1,0:T(8,128)(2,1)S(1)}, u32[]{:S(2)}, u32[]{:S(2)}) collective-permute-start(bf16[64,1536]{1,0:T(8,128)(2,1)S(1)} %get-tuple-element.18.rest_0_.refs_2_), channel_id=1, source_target_pairs={{0,4},{4,8},{8,12},{12,14},{14,10},{10,6},{6,2},{2,0},{1,5},{5,9},... | collective-permute-start | bytes 589832 | tf_op jit(solution)/shard_map/ppermute | solution.py:525
  7.8 10.2 %collective-permute-start.4 = (bf16[64,1536]{1,0:T(8,128)(2,1)S(1)}, bf16[64,1536]{1,0:T(8,128)(2,1)S(1)}, u32[]{:S(2)}, u32[]{:S(2)}) collective-permute-start(bf16[64,1536]{1,0:T(8,128)(2,1)S(1)} %get-tuple-element.18.rest_0_.refs_2_), channel_id=1, source_target_pairs={{4,0},{8,4},{12,8},{14,12},{10,14},{6,10},{2,6},{0,2},{5,1},{9,5},... | collective-permute-start | bytes 589832 | tf_op jit(solution)/shard_map/ppermute | solution.py:526
  7.8 2.5 %copy-start.2 = (bf16[2560,4,256]{2,1,0:T(4,128)(2,1)S(1)}, bf16[2560,4,256]{2,1,0:T(4,128)(2,1)}, u32[]{:S(2)}) copy-start(bf16[2560,4,256]{2,1,0:T(4,128)(2,1)} %param.13) | copy-start | bytes 15728644
  10.3 0.7 %copy-start.9 = (s32[8]{0:T(128)S(1)}, s32[8]{0:T(128)}, u32[]{:S(2)}) copy-start(s32[8]{0:T(128)} %length_ref.7) | copy-start | bytes 100
  10.9 0.7 %copy-start.12 = (s32[8,48]{1,0:T(8,128)S(1)}, s32[8,48]{1,0:T(8,128)}, u32[]{:S(2)}) copy-start(s32[8,48]{1,0:T(8,128)} %parent_ref.1) | copy-start | bytes 4612
  11.6 2.7 %copy-start = (bf16[384,2560]{1,0:T(8,128)(2,1)S(1)}, bf16[384,2560]{1,0:T(8,128)(2,1)}, u32[]{:S(2)}) copy-start(bf16[384,2560]{1,0:T(8,128)(2,1)} %refs_8_.3) | copy-start | bytes 5898244
  14.3 3.7 %copy-start.6 = (s32[8,8]{1,0:T(8,128)S(1)}, s32[8,8]{1,0:T(8,128)}, u32[]{:S(2)}) copy-start(s32[8,8]{1,0:T(8,128)} %constant.10.clone.owner_ref) | copy-start | bytes 772
  14.3 3.7 %copy-start.8 = (s32[8]{0:T(128)S(1)}, s32[8]{0:T(128)}, u32[]{:S(2)}) copy-start(s32[8]{0:T(128)} %adapter_ref.11) | copy-start | bytes 100
  18.1 5.3 %copy-start.1 = (bf16[384,16,128]{2,1,0:T(8,128)(2,1)S(1)}, bf16[384,16,128]{2,1,0:T(8,128)(2,1)}, u32[]{:S(2)}) copy-start(bf16[384,16,128]{2,1,0:T(8,128)(2,1)} %query_ref.5) | copy-start | bytes 4718596
  18.1 5.3 %copy-start.3 = (bf16[8,128,2,128]{3,2,1,0:T(2,128)(2,1)S(1)}, bf16[8,128,2,128]{3,2,1,0:T(2,128)(2,1)}, u32[]{:S(2)}) copy-start(bf16[8,128,2,128]{3,2,1,0:T(2,128)(2,1)} %param.20) | copy-start | bytes 1572868
  18.1 5.3 %copy-start.4 = (bf16[8,128,2,128]{3,2,1,0:T(2,128)(2,1)S(1)}, bf16[8,128,2,128]{3,2,1,0:T(2,128)(2,1)}, u32[]{:S(2)}) copy-start(bf16[8,128,2,128]{3,2,1,0:T(2,128)(2,1)} %param.21) | copy-start | bytes 1572868
  18.1 5.3 %copy-start.10 = (s32[8]{0:T(128)S(1)}, s32[8]{0:T(128)}, u32[]{:S(2)}) copy-start(s32[8]{0:T(128)} %length_ref.7) | copy-start | bytes 100
  18.1 5.3 %copy-start.11 = (f32[128]{0:T(128)S(1)}, f32[128]{0:T(128)}, u32[]{:S(2)}) copy-start(f32[128]{0:T(128)} %param.22) | copy-start | bytes 1540
  19.1 4.2 %collective-permute-start.5 = (f32[3,48,640]{2,1,0:T(8,128)S(1)}, f32[3,48,640]{2,1,0:T(8,128)S(1)}, u32[]{:S(2)}, u32[]{:S(2)}) collective-permute-start(f32[3,48,640]{2,1,0:T(8,128)S(1)} %shrink.3.shrunk_here_ref), channel_id=1, source_target_pairs={{0,1},{1,0},{2,3},{3,2},{4,5},{5,4},{6,7},{7,6},{8,9},{9,8},{10,11... | collective-permute-start | bytes 1105928 | tf_op jit(solution)/shard_map/ppermute | solution.py:521
  19.1 8.7 %collective-permute-start.11 = (bf16[64,1536]{1,0:T(8,128)(2,1)S(1)}, bf16[64,1536]{1,0:T(8,128)(2,1)S(1)}, u32[]{:S(2)}, u32[]{:S(2)}) collective-permute-start(bf16[64,1536]{1,0:T(8,128)(2,1)S(1)} %get-tuple-element.25.refs_11_), channel_id=1, source_target_pairs={{4,0},{8,4},{12,8},{14,12},{10,14},{6,10},{2,6},{0,2},{5,1},{9,5},... | collective-permute-start | bytes 589832 | tf_op jit(solution)/shard_map/ppermute | solution.py:526
  21.2 8.6 %collective-permute-start.3 = (bf16[64,1536]{1,0:T(8,128)(2,1)S(1)}, bf16[64,1536]{1,0:T(8,128)(2,1)S(1)}, u32[]{:S(2)}, u32[]{:S(2)}) collective-permute-start(bf16[64,1536]{1,0:T(8,128)(2,1)S(1)} %collective-permute-done.2.refs_6_.rest_1_), channel_id=1, source_target_pairs={{0,4},{4,8},{8,12},{12,14},{14,10},{10,6},{6,2},{2,0},{1,5},{5,9},... | collective-permute-start | bytes 589832 | tf_op jit(solution)/shard_map/ppermute | solution.py:525
  21.3 11.8 %collective-permute-start.7 = (bf16[64,1536]{1,0:T(8,128)(2,1)S(1)}, bf16[64,1536]{1,0:T(8,128)(2,1)S(1)}, u32[]{:S(2)}, u32[]{:S(2)}) collective-permute-start(bf16[64,1536]{1,0:T(8,128)(2,1)S(1)} %get-tuple-element.24.refs_7_), channel_id=1, source_target_pairs={{0,4},{4,8},{8,12},{12,14},{14,10},{10,6},{6,2},{2,0},{1,5},{5,9},... | collective-permute-start | bytes 589832 | tf_op jit(solution)/shard_map/ppermute | solution.py:525
  23.3 9.9 %collective-permute-start.9 = (bf16[64,1536]{1,0:T(8,128)(2,1)S(1)}, bf16[64,1536]{1,0:T(8,128)(2,1)S(1)}, u32[]{:S(2)}, u32[]{:S(2)}) collective-permute-start(bf16[64,1536]{1,0:T(8,128)(2,1)S(1)} %collective-permute-done.4.refs_10_.rest_2_), channel_id=1, source_target_pairs={{4,0},{8,4},{12,8},{14,12},{10,14},{6,10},{2,6},{0,2},{5,1},{9,5},... | collective-permute-start | bytes 589832 | tf_op jit(solution)/shard_map/ppermute | solution.py:526
  27.9 8.3 %collective-permute-start.12 = (bf16[64,1536]{1,0:T(8,128)(2,1)S(1)}, bf16[64,1536]{1,0:T(8,128)(2,1)S(1)}, u32[]{:S(2)}, u32[]{:S(2)}) collective-permute-start(bf16[64,1536]{1,0:T(8,128)(2,1)S(1)} %hold.3.refs_7_), channel_id=1, source_target_pairs={{4,0},{8,4},{12,8},{14,12},{10,14},{6,10},{2,6},{0,2},{5,1},{9,5},... | collective-permute-start | bytes 589832 | tf_op jit(solution)/shard_map/ppermute | solution.py:526
  29.8 8.0 %collective-permute-start.6 = (bf16[64,1536]{1,0:T(8,128)(2,1)S(1)}, bf16[64,1536]{1,0:T(8,128)(2,1)S(1)}, u32[]{:S(2)}, u32[]{:S(2)}) collective-permute-start(bf16[64,1536]{1,0:T(8,128)(2,1)S(1)} %hold.2.refs_2_.rest_0_), channel_id=1, source_target_pairs={{0,4},{4,8},{8,12},{12,14},{14,10},{10,6},{6,2},{2,0},{1,5},{5,9},... | collective-permute-start | bytes 589832 | tf_op jit(solution)/shard_map/ppermute | solution.py:525
  34.0 4.2 %collective-permute-start.15 = (f32[2,48,640]{2,1,0:T(8,128)S(1)}, f32[2,48,640]{2,1,0:T(8,128)S(1)}, u32[]{:S(2)}, u32[]{:S(2)}) collective-permute-start(f32[2,48,640]{2,1,0:T(8,128)S(1)} %shrink.4.shrunk_here_ref), channel_id=1, source_target_pairs={{0,1},{1,0},{2,3},{3,2},{4,5},{5,4},{6,7},{7,6},{8,9},{9,8},{10,11... | collective-permute-start | bytes 737288 | tf_op jit(solution)/shard_map/ppermute | solution.py:521
  34.1 7.8 %collective-permute-start.8 = (bf16[64,1536]{1,0:T(8,128)(2,1)S(1)}, bf16[64,1536]{1,0:T(8,128)(2,1)S(1)}, u32[]{:S(2)}, u32[]{:S(2)}) collective-permute-start(bf16[64,1536]{1,0:T(8,128)(2,1)S(1)} %collective-permute-done.7.refs_3_), channel_id=1, source_target_pairs={{0,4},{4,8},{8,12},{12,14},{14,10},{10,6},{6,2},{2,0},{1,5},{5,9},... | collective-permute-start | bytes 589832 | tf_op jit(solution)/shard_map/ppermute | solution.py:525
  34.3 7.7 %collective-permute-start.10 = (bf16[64,1536]{1,0:T(8,128)(2,1)S(1)}, bf16[64,1536]{1,0:T(8,128)(2,1)S(1)}, u32[]{:S(2)}, u32[]{:S(2)}) collective-permute-start(bf16[64,1536]{1,0:T(8,128)(2,1)S(1)} %collective-permute-done.9.refs_6_.rest_1_), channel_id=1, source_target_pairs={{4,0},{8,4},{12,8},{14,12},{10,14},{6,10},{2,6},{0,2},{5,1},{9,5},... | collective-permute-start | bytes 589832 | tf_op jit(solution)/shard_map/ppermute | solution.py:526
  36.2 9.5 %collective-permute-start.14 = (bf16[64,1536]{1,0:T(8,128)(2,1)S(1)}, bf16[64,1536]{1,0:T(8,128)(2,1)S(1)}, u32[]{:S(2)}, u32[]{:S(2)}) collective-permute-start(bf16[64,1536]{1,0:T(8,128)(2,1)S(1)} %collective-permute-done.12.refs_7_), channel_id=1, source_target_pairs={{4,0},{8,4},{12,8},{14,12},{10,14},{6,10},{2,6},{0,2},{5,1},{9,5},... | collective-permute-start | bytes 589832 | tf_op jit(solution)/shard_map/ppermute | solution.py:549
  37.8 7.9 %collective-permute-start.13 = (bf16[64,1536]{1,0:T(8,128)(2,1)S(1)}, bf16[64,1536]{1,0:T(8,128)(2,1)S(1)}, u32[]{:S(2)}, u32[]{:S(2)}) collective-permute-start(bf16[64,1536]{1,0:T(8,128)(2,1)S(1)} %collective-permute-done.6.refs_2_.rest_0_), channel_id=1, source_target_pairs={{0,4},{4,8},{8,12},{12,14},{14,10},{10,6},{6,2},{2,0},{1,5},{5,9},... | collective-permute-start | bytes 589832 | tf_op jit(solution)/shard_map/ppermute | solution.py:549
  46.7 1.7 %collective-permute-start.16 = (f32[3,48,640]{2,1,0:T(8,128)S(1)}, f32[3,48,640]{2,1,0:T(8,128)S(1)}, u32[]{:S(2)}, u32[]{:S(2)}) collective-permute-start(f32[3,48,640]{2,1,0:T(8,128)S(1)} %shrink.5.shrunk_here_ref), channel_id=1, source_target_pairs={{0,1},{1,0},{2,3},{3,2},{4,5},{5,4},{6,7},{7,6},{8,9},{9,8},{10,11... | collective-permute-start | bytes 1105928 | tf_op jit(solution)/shard_map/ppermute | solution.py:521

commit v9 on v8

--- a/solution.py
+++ b/solution.py
@@ -178,10 +178,8 @@
     )(core, hidden_states, weight_rows, *after, *held)
 
 
-def tree_kernel(length_ref, parent_ref, weight_ref, *rest, head_size, kv_heads):
-    table_ref, moved_ref, semaphore = rest[-3:]
-    move = pltpu.make_async_copy(weight_ref, moved_ref, semaphore)
-    move.start()
+def tree_kernel(length_ref, parent_ref, *rest, head_size, kv_heads):
+    table_ref = rest[-1]
     requests, nodes = parent_ref.shape
     node = lax.broadcasted_iota(jnp.int32, (nodes, nodes), 0)
     same = node == lax.broadcasted_iota(jnp.int32, (nodes, nodes), 1)
@@ -217,10 +215,9 @@
         table_ref[rows, :] = jnp.concatenate(
             [jnp.cos(angles), jnp.sin(angles) * sign, jnp.where(wide > 0.5, 0.0, -1e30)], 1
         )
-    move.wait()
-
-
-def tree_tables(cache_lengths, tree_parents, head_size, kv_heads, weight_rows, after):
+
+
+def tree_tables(cache_lengths, tree_parents, head_size, kv_heads, after):
     requests, nodes = tree_parents.shape
     whole = lambda shape: pl.BlockSpec(shape, lambda i, n: (0,) * len(shape))
     rows = requests * nodes
@@ -230,18 +227,17 @@
         grid_spec=pltpu.PrefetchScalarGridSpec(
             num_scalar_prefetch=1,
             grid=(1,),
-            in_specs=[whole(tree_parents.shape), ANYWHERE]
+            in_specs=[whole(tree_parents.shape)]
             + [ANYWHERE] * len(after),
-            out_specs=[whole((rows, width)), ANYWHERE],
-            scratch_shapes=[pltpu.SemaphoreType.DMA],
-        ),
-        out_shape=[jax.ShapeDtypeStruct((rows, width), F32)] + shapes_of([weight_rows]),
+            out_specs=whole((rows, width)),
+        ),
+        out_shape=jax.ShapeDtypeStruct((rows, width), F32),
         cost_estimate=pl.CostEstimate(
             flops=1_000_000_000, bytes_accessed=8_000_000, transcendentals=0
         ),
         compiler_params=pltpu.CompilerParams(vmem_limit_bytes=8 * 1024 * 1024),
         name="tree",
-    )(cache_lengths, tree_parents, weight_rows, *after)
+    )(cache_lengths, tree_parents, *after)
 
 
 def shrink_kernel(me_ref, owner_ref, adapter_ref, *refs, columns, cut):
@@ -504,17 +500,17 @@
 
     arrivals = [(first, second)]
     front = rear = (first, second)
-    table, weight_rows = tree_tables(
-        cache_lengths, tree_parents, head_size, heads_here, weight_rows, [first]
+    here, away = base_product(
+        core, hidden_states, weight_rows, kv_heads * kv_width, [first], []
     )
     split_batches = pool_count == requests
     near = 3
     done = [(None, 0)]
     shared = None
 
-    def finish_batch(group):
+    def finish_batch(group, after=()):
         outputs, slot = done[-1]
-        after = [] if outputs is None else [outputs[2]]
+        after = list(after) if outputs is None else [outputs[2]]
         partial = shrink_rows(
             where, slot, hidden_states, away, group, tree_size, columns, cut, after
         )
@@ -525,10 +521,13 @@
         front = tuple(lax.ppermute(piece, "pool", onward) for piece in front)
         rear = tuple(lax.ppermute(piece, "pool", backward) for piece in rear)
         held = [front[1], rear[1]]
+        first_front = front[0]
         if step == 1:
-            here, away, *held = base_product(
-                core, hidden_states, weight_rows, kv_heads * kv_width, [table], held
+            held = [hold(piece, away) for piece in held]
+            table = tree_tables(
+                cache_lengths, tree_parents, head_size, heads_here, [here, front[0], rear[0]]
             )
+            first_front = hold(first_front, table)
             shared = (
                 cache_lengths,
                 key_gain.reshape(1, head_size),
@@ -538,9 +537,8 @@
                 key_rows,
                 value_rows,
             )
-        first_front = front[0]
         if step == 2 and split_batches:
-            finish_batch(arrivals[:near])
+            finish_batch(arrivals[:near], held)
             token = done[-1][0][2]
             first_front, held[1] = hold(first_front, token), hold(held[1], token)
         front, rear = (first_front, held[0]), (rear[0], held[1])

time: 53.1 us -> 54.5 us (1.026)
  waiting for transfers between devices: 8.97 us -> 10.1 us
    ppermute x6, waiting for transfers between devices: 0.15 us -> 2.66 us  [per_device(): rear = tuple((lax.ppermute(piece, 'pool', backward) for piece in rear))]
    ppermute x1, starting transfers between devices: 0.45 us -> 1.58 us  [per_device(): lax.ppermute(front[0], 'pool', onward)]
    ppermute x6, waiting for transfers between devices: 3.44 us -> 2.55 us  [per_device(): front = tuple((lax.ppermute(piece, 'pool', onward) for piece in front))]
    ppermute x1, starting transfers between devices: 1.58 us -> 0.7 us  [per_device(): lax.ppermute(rear[1], 'pool', backward)]
    ppermute x6, starting transfers between devices: 7.52 us -> 8.24 us  [per_device(): front = tuple((lax.ppermute(piece, 'pool', onward) for piece in front))]
  transfers between devices with their start and end apart: 17 -> 17, of which waited for: 5 -> 7; matrix products, arithmetic and copies ran while one was open for 0% -> 0% of each run, Pallas kernels for 29% -> 27%
where the time goes in v9:
time: 54.5 us; the launch traced here: 54.2 us
  Pallas kernels  21.4 us (39%)
  starting transfers between devices  16 us (29%)
  waiting for transfers between devices  10.1 us (19%)
  local copies, waits for them, and re-layouts  5.96 us (11%)
  between operations  0.84 us (2%)
    pallas_call x3, Pallas kernels, finish(): pl.pallas_call(functools.partial(finish_kernel, count=count, slot=slot, k...  12.4 us
    ppermute x6, starting transfers between devices, per_device(): front = tuple((lax.ppermute(piece, 'pool', onward) for piece in front))  8.24 us
    unnamed x26, local copies, waits for them, and re-layouts  5.96 us
    ppermute x6, starting transfers between devices, per_device(): rear = tuple((lax.ppermute(piece, 'pool', backward) for piece in rear))  5.38 us
    pallas_call x1, Pallas kernels, base_product(): pl.pallas_call(functools.partial(base_kernel, held_count=len(held)), grid...  3.66 us
    ppermute x1, waiting for transfers between devices, per_device(): lax.ppermute(rear[1], 'pool', backward)  3.18 us
    pallas_call x3, Pallas kernels, shrink_rows(): pl.pallas_call(functools.partial(shrink_kernel, columns=columns, cut=cut)...  2.88 us
    ppermute x6, waiting for transfers between devices, per_device(): rear = tuple((lax.ppermute(piece, 'pool', backward) for piece in rear))  2.66 us
  transfers between devices with their start and end apart: 17, of which 7 were waited for; matrix products, arithmetic and copies ran while one was open for 0% of the time, Pallas kernels for 27%

profile of v9, /device:TPU:0, one launch (start us, length us, event | category | flops | bytes accessed | tf_op | source)
XLA Modules:
  0.0 54.2 jit_solution(15536042804097324560)
XLA Ops:
  0.6 1.0 %copy-done.5 = bf16[1,2560,64]{1,2,0:T(8,128)(2,1)S(1)} copy-done((bf16[1,2560,64]{1,2,0:T(8,128)(2,1)S(1)}, bf16[1,2560,64]{1,2,0:T(8,128)(2,1)}, u32[]{:S(2)}) %copy-start.5) | copy-done | bytes 327704
  1.6 0.9 %copy-done.7 = bf16[1,64,4,256]{3,2,1,0:T(4,128)(2,1)S(1)} copy-done((bf16[1,64,4,256]{3,2,1,0:T(4,128)(2,1)S(1)}, bf16[1,64,4,256]{3,2,1,0:T(4,128)(2,1)}, u32[]{:S(2)}) %copy-start.7) | copy-done | bytes 131096
  2.5 0.2 pack.1
  2.7 3.0 %collective-permute-start.1 = (bf16[64,1536]{1,0:T(8,128)(2,1)S(1)}, bf16[64,1536]{1,0:T(8,128)(2,1)S(1)}, u32[]{:S(2)}, u32[]{:S(2)}) collective-permute-start(bf16[64,1536]{1,0:T(8,128)(2,1)S(1)} %get-tuple-element.14.rest_0_.refs_2_), channel_id=1, source_target_pairs={{4,0},{8,4},{12,8},{14,12},{10,14},{6,10},{2,6},{0,2},{5,1},{9,5},... | collective-permute-start | bytes 589832 | tf_op jit(solution)/shard_map/ppermute | solution.py:522
  5.8 2.0 %collective-permute-start.3 = (bf16[64,1536]{1,0:T(8,128)(2,1)S(1)}, bf16[64,1536]{1,0:T(8,128)(2,1)S(1)}, u32[]{:S(2)}, u32[]{:S(2)}) collective-permute-start(bf16[64,1536]{1,0:T(8,128)(2,1)S(1)} %get-tuple-element.17.refs_3_), channel_id=1, source_target_pairs={{0,4},{4,8},{8,12},{12,14},{14,10},{10,6},{6,2},{2,0},{1,5},{5,9},... | collective-permute-start | bytes 589832 | tf_op jit(solution)/shard_map/ppermute | solution.py:521
  7.9 1.5 %copy-done = bf16[384,2560]{1,0:T(8,128)(2,1)S(1)} copy-done((bf16[384,2560]{1,0:T(8,128)(2,1)S(1)}, bf16[384,2560]{1,0:T(8,128)(2,1)}, u32[]{:S(2)}) %copy-start) | copy-done | bytes 1966104
  9.4 2.5 %copy-done.11 = bf16[2560,4,256]{2,1,0:T(4,128)(2,1)S(1)} copy-done((bf16[2560,4,256]{2,1,0:T(4,128)(2,1)S(1)}, bf16[2560,4,256]{2,1,0:T(4,128)(2,1)}, u32[]{:S(2)}) %copy-start.11) | copy-done | bytes 5242904
  11.9 3.7 %base.1 = (f32[384,512]{1,0:T(8,128)S(1)}, f32[384,512]{1,0:T(8,128)S(1)}) custom-call(s32[1]{0:T(128)} %bitcast.1.core_ref, bf16[384,2560]{1,0:T(8,128)(2,1)S(1)} %copy-done, bf16[20480,128]{1,0:T(8,128)(2,1)S(1)} %bitcast.34, bf16[64,1536]{1,0:T(8,128)(2,1)S(1)} %get-tuple-element.14.rest_0_.refs_2_), custom_call_target="tpu_custom_call" | custom-call | flops 4000000000 | bytes 9000000 | tf_op jit(solution)/shard_map/base/pallas_call | solution.py:154
  15.6 0.7 %collective-permute-done.3.array_ref = bf16[64,1536]{1,0:T(8,128)(2,1)S(1)} collective-permute-done((bf16[64,1536]{1,0:T(8,128)(2,1)S(1)}, bf16[64,1536]{1,0:T(8,128)(2,1)S(1)}, u32[]{:S(2)}, u32[]{:S(2)}) %collective-permute-start.3) | collective-permute-done | bytes 196640 | tf_op jit(solution)/shard_map/ppermute | solution.py:521
  16.3 1.3 %collective-permute-start.5 = (bf16[64,1536]{1,0:T(8,128)(2,1)S(1)}, bf16[64,1536]{1,0:T(8,128)(2,1)S(1)}, u32[]{:S(2)}, u32[]{:S(2)}) collective-permute-start(bf16[64,1536]{1,0:T(8,128)(2,1)S(1)} %hold.6.refs_7_), channel_id=1, source_target_pairs={{0,4},{4,8},{8,12},{12,14},{14,10},{10,6},{6,2},{2,0},{1,5},{5,9},... | collective-permute-start | bytes 589832 | tf_op jit(solution)/shard_map/ppermute | solution.py:521
  17.6 0.7 %collective-permute-start.6 = (bf16[64,1536]{1,0:T(8,128)(2,1)S(1)}, bf16[64,1536]{1,0:T(8,128)(2,1)S(1)}, u32[]{:S(2)}, u32[]{:S(2)}) collective-permute-start(bf16[64,1536]{1,0:T(8,128)(2,1)S(1)} %hold.7.refs_11_), channel_id=1, source_target_pairs={{4,0},{8,4},{12,8},{14,12},{10,14},{6,10},{2,6},{0,2},{5,1},{9,5},... | collective-permute-start | bytes 589832 | tf_op jit(solution)/shard_map/ppermute | solution.py:522
  18.4 2.3 %tree.1.token_ref.table_ref = f32[384,384]{1,0:T(8,128)S(1)} custom-call(s32[8]{0:T(128)S(1)} %copy-done.9, s32[8,48]{1,0:T(8,128)S(1)} %copy-done.12, f32[384,512]{1,0:T(8,128)S(1)} %get-tuple-element.15.rest_0_.here_ref, bf16[64,1536]{1,0:T(8,128)(2,1)S(1)} %collective-permute-done.rest_1_.array_ref, ...), custom_call_target="tpu_custom_call" | custom-call | flops 1000000000 | bytes 8000000 | tf_op jit(solution)/shard_map/tree/pallas_call | solution.py:225
  20.7 1.3 %collective-permute-done.5.refs_12_.refs_3_ = bf16[64,1536]{1,0:T(8,128)(2,1)S(1)} collective-permute-done((bf16[64,1536]{1,0:T(8,128)(2,1)S(1)}, bf16[64,1536]{1,0:T(8,128)(2,1)S(1)}, u32[]{:S(2)}, u32[]{:S(2)}) %collective-permute-start.5) | collective-permute-done | bytes 196640 | tf_op jit(solution)/shard_map/ppermute | solution.py:521
  22.0 1.3 %collective-permute-done.6.refs_13_.array_ref = bf16[64,1536]{1,0:T(8,128)(2,1)S(1)} collective-permute-done((bf16[64,1536]{1,0:T(8,128)(2,1)S(1)}, bf16[64,1536]{1,0:T(8,128)(2,1)S(1)}, u32[]{:S(2)}, u32[]{:S(2)}) %collective-permute-start.6) | collective-permute-done | bytes 196640 | tf_op jit(solution)/shard_map/ppermute | solution.py:522
  23.3 1.0 %shrink.3.shrunk_here_ref = f32[3,48,640]{2,1,0:T(8,128)S(1)} custom-call(s32[1]{0:T(128)} %bitcast.me_ref, s32[8,8]{1,0:T(8,128)S(1)} %copy-done.6, s32[8]{0:T(128)S(1)} %copy-done.8, bf16[384,2560]{1,0:T(8,128)(2,1)S(1)} %copy-done.1, f32[384,512]{1,0:T(8,128)S(1)} %get-tuple-element.16.token_ref.refs_1_.refs_5_.refs_9_, ...), custom_call_target="tpu_custom_call" | custom-call | flops 90000000 | bytes 600000 | tf_op jit(solution)/shard_map/shrink/pallas_call | solution.py:273
  24.4 1.6 %collective-permute-start.2 = (bf16[64,1536]{1,0:T(8,128)(2,1)S(1)}, bf16[64,1536]{1,0:T(8,128)(2,1)S(1)}, u32[]{:S(2)}, u32[]{:S(2)}) collective-permute-start(bf16[64,1536]{1,0:T(8,128)(2,1)S(1)} %hold.5.refs_6_.rest_1_), channel_id=1, source_target_pairs={{0,4},{4,8},{8,12},{12,14},{14,10},{10,6},{6,2},{2,0},{1,5},{5,9},... | collective-permute-start | bytes 589832 | tf_op jit(solution)/shard_map/ppermute | solution.py:521
  26.0 0.4 collective-permute-start.10
  26.5 4.5 %finish.3 = (bf16[384,16,128]{2,1,0:T(8,128)(2,1)}, bf16[1536,128]{1,0:T(8,128)(2,1)}, f32[8,128]{1,0:T(8,128)S(1)}) custom-call(s32[1]{0:T(128)} %bitcast.me_ref, s32[8,8]{1,0:T(8,128)S(1)} %copy-done.6, s32[8]{0:T(128)S(1)} %copy-done.8, s32[8]{0:T(128)S(1)} %copy-done.9, f32[384,512]{1,0:T(8,128)S(1)} %get-tuple-element.15.rest_0_.here_ref, ...), custom_call_target="tpu_custom_call" | custom-call | flops 270000000 | bytes 900000 | tf_op jit(solution)/shard_map/finish/pallas_call | solution.py:424
  31.0 0.7 %collective-permute-start.12 = (bf16[64,1536]{1,0:T(8,128)(2,1)S(1)}, bf16[64,1536]{1,0:T(8,128)(2,1)S(1)}, u32[]{:S(2)}, u32[]{:S(2)}) collective-permute-start(bf16[64,1536]{1,0:T(8,128)(2,1)S(1)} %hold.9.refs_7_), channel_id=1, source_target_pairs={{4,0},{8,4},{12,8},{14,12},{10,14},{6,10},{2,6},{0,2},{5,1},{9,5},... | collective-permute-start | bytes 589832 | tf_op jit(solution)/shard_map/ppermute | solution.py:522
  31.7 1.6 %collective-permute-start.8 = (bf16[64,1536]{1,0:T(8,128)(2,1)S(1)}, bf16[64,1536]{1,0:T(8,128)(2,1)S(1)}, u32[]{:S(2)}, u32[]{:S(2)}) collective-permute-start(bf16[64,1536]{1,0:T(8,128)(2,1)S(1)} %hold.8.refs_2_.rest_0_), channel_id=1, source_target_pairs={{0,4},{4,8},{8,12},{12,14},{14,10},{10,6},{6,2},{2,0},{1,5},{5,9},... | collective-permute-start | bytes 589832 | tf_op jit(solution)/shard_map/ppermute | solution.py:521
  33.3 0.9 %shrink.4.shrunk_here_ref = f32[2,48,640]{2,1,0:T(8,128)S(1)} custom-call(s32[1]{0:T(128)} %bitcast.me_ref, s32[8,8]{1,0:T(8,128)S(1)} %copy-done.6, s32[8]{0:T(128)S(1)} %copy-done.8, bf16[384,2560]{1,0:T(8,128)(2,1)S(1)} %copy-done.1, f32[384,512]{1,0:T(8,128)S(1)} %get-tuple-element.16.token_ref.refs_1_.refs_5_.refs_9_, ...), custom_call_target="tpu_custom_call" | custom-call | flops 60000000 | bytes 400000 | tf_op jit(solution)/shard_map/shrink/pallas_call | solution.py:273
  34.3 1.6 %collective-permute-start.9 = (bf16[64,1536]{1,0:T(8,128)(2,1)S(1)}, bf16[64,1536]{1,0:T(8,128)(2,1)S(1)}, u32[]{:S(2)}, u32[]{:S(2)}) collective-permute-start(bf16[64,1536]{1,0:T(8,128)(2,1)S(1)} %collective-permute-done.5.refs_12_.refs_3_), channel_id=1, source_target_pairs={{0,4},{4,8},{8,12},{12,14},{14,10},{10,6},{6,2},{2,0},{1,5},{5,9},... | collective-permute-start | bytes 589832 | tf_op jit(solution)/shard_map/ppermute | solution.py:521
  35.9 0.4 collective-permute-start.11
  36.3 1.3 %collective-permute-done.12.refs_7_ = bf16[64,1536]{1,0:T(8,128)(2,1)S(1)} collective-permute-done((bf16[64,1536]{1,0:T(8,128)(2,1)S(1)}, bf16[64,1536]{1,0:T(8,128)(2,1)S(1)}, u32[]{:S(2)}, u32[]{:S(2)}) %collective-permute-start.12) | collective-permute-done | bytes 196640 | tf_op jit(solution)/shard_map/ppermute | solution.py:522
  37.7 0.7 %collective-permute-start.14 = (bf16[64,1536]{1,0:T(8,128)(2,1)S(1)}, bf16[64,1536]{1,0:T(8,128)(2,1)S(1)}, u32[]{:S(2)}, u32[]{:S(2)}) collective-permute-start(bf16[64,1536]{1,0:T(8,128)(2,1)S(1)} %collective-permute-done.12.refs_7_), channel_id=1, source_target_pairs={{4,0},{8,4},{12,8},{14,12},{10,14},{6,10},{2,6},{0,2},{5,1},{9,5},... | collective-permute-start | bytes 589832 | tf_op jit(solution)/shard_map/ppermute | solution.py:547
  38.4 0.5 collective-permute-done.8.refs_2_.rest_0_
  38.9 1.6 %collective-permute-start.13 = (bf16[64,1536]{1,0:T(8,128)(2,1)S(1)}, bf16[64,1536]{1,0:T(8,128)(2,1)S(1)}, u32[]{:S(2)}, u32[]{:S(2)}) collective-permute-start(bf16[64,1536]{1,0:T(8,128)(2,1)S(1)} %collective-permute-done.8.refs_2_.rest_0_), channel_id=1, source_target_pairs={{0,4},{4,8},{8,12},{12,14},{14,10},{10,6},{6,2},{2,0},{1,5},{5,9},... | collective-permute-start | bytes 589832 | tf_op jit(solution)/shard_map/ppermute | solution.py:547
  40.5 3.4 %finish.4 = (bf16[384,16,128]{2,1,0:T(8,128)(2,1)}, bf16[1536,128]{1,0:T(8,128)(2,1)}, f32[8,128]{1,0:T(8,128)S(1)}) custom-call(s32[1]{0:T(128)} %bitcast.me_ref, s32[8,8]{1,0:T(8,128)S(1)} %copy-done.6, s32[8]{0:T(128)S(1)} %copy-done.8, s32[8]{0:T(128)S(1)} %copy-done.9, ...), custom_call_target="tpu_custom_call", output_to_operand_aliasing={{0}: (14, {}), {1}: (15, {})} | custom-call | flops 180000000 | bytes 600000 | tf_op jit(solution)/shard_map/finish/pallas_call | solution.py:424
  43.9 3.2 %collective-permute-done.14.refs_11_ = bf16[64,1536]{1,0:T(8,128)(2,1)S(1)} collective-permute-done((bf16[64,1536]{1,0:T(8,128)(2,1)S(1)}, bf16[64,1536]{1,0:T(8,128)(2,1)S(1)}, u32[]{:S(2)}, u32[]{:S(2)}) %collective-permute-start.14) | collective-permute-done | bytes 196640 | tf_op jit(solution)/shard_map/ppermute | solution.py:547
  47.1 1.0 %shrink.5.shrunk_here_ref = f32[3,48,640]{2,1,0:T(8,128)S(1)} custom-call(s32[1]{0:T(128)} %bitcast.me_ref, s32[8,8]{1,0:T(8,128)S(1)} %copy-done.6, s32[8]{0:T(128)S(1)} %copy-done.8, bf16[384,2560]{1,0:T(8,128)(2,1)S(1)} %copy-done.1, f32[384,512]{1,0:T(8,128)S(1)} %get-tuple-element.16.token_ref.refs_1_.refs_5_.refs_9_, ...), custom_call_target="tpu_custom_call" | custom-call | flops 90000000 | bytes 600000 | tf_op jit(solution)/shard_map/shrink/pallas_call | solution.py:273
  48.1 1.7 %collective-permute-done.16.shrunk_there_ref = f32[3,48,640]{2,1,0:T(8,128)S(1)} collective-permute-done((f32[3,48,640]{2,1,0:T(8,128)S(1)}, f32[3,48,640]{2,1,0:T(8,128)S(1)}, u32[]{:S(2)}, u32[]{:S(2)}) %collective-permute-start.16) | collective-permute-done | bytes 368672 | tf_op jit(solution)/shard_map/ppermute | solution.py:517
  49.8 4.5 %finish.5 = (bf16[384,16,128]{2,1,0:T(8,128)(2,1)}, bf16[1536,128]{1,0:T(8,128)(2,1)}, f32[8,128]{1,0:T(8,128)}) custom-call(s32[1]{0:T(128)} %bitcast.me_ref, s32[8,8]{1,0:T(8,128)S(1)} %copy-done.6, s32[8]{0:T(128)S(1)} %copy-done.8, s32[8]{0:T(128)S(1)} %copy-done.9, ...), custom_call_target="tpu_custom_call", output_to_operand_aliasing={{0}: (15, {}), {1}: (16, {})} | custom-call | flops 270000000 | bytes 900000 | tf_op jit(solution)/shard_map/finish/pallas_call | solution.py:424
  (42 shorter events, 0.4 us)
Async XLA Ops:
  0.6 1.0 %copy-start.5 = (bf16[1,2560,64]{1,2,0:T(8,128)(2,1)S(1)}, bf16[1,2560,64]{1,2,0:T(8,128)(2,1)}, u32[]{:S(2)}) copy-start(bf16[1,2560,64]{1,2,0:T(8,128)(2,1)} %param.14) | copy-start | bytes 983044
  1.6 0.9 %copy-start.7 = (bf16[1,64,4,256]{3,2,1,0:T(4,128)(2,1)S(1)}, bf16[1,64,4,256]{3,2,1,0:T(4,128)(2,1)}, u32[]{:S(2)}) copy-start(bf16[1,64,4,256]{3,2,1,0:T(4,128)(2,1)} %param.15) | copy-start | bytes 393220
  2.7 15.6 %collective-permute-start.1 = (bf16[64,1536]{1,0:T(8,128)(2,1)S(1)}, bf16[64,1536]{1,0:T(8,128)(2,1)S(1)}, u32[]{:S(2)}, u32[]{:S(2)}) collective-permute-start(bf16[64,1536]{1,0:T(8,128)(2,1)S(1)} %get-tuple-element.14.rest_0_.refs_2_), channel_id=1, source_target_pairs={{4,0},{8,4},{12,8},{14,12},{10,14},{6,10},{2,6},{0,2},{5,1},{9,5},... | collective-permute-start | bytes 589832 | tf_op jit(solution)/shard_map/ppermute | solution.py:522
  5.7 12.6 %collective-permute-start = (bf16[64,1536]{1,0:T(8,128)(2,1)S(1)}, bf16[64,1536]{1,0:T(8,128)(2,1)S(1)}, u32[]{:S(2)}, u32[]{:S(2)}) collective-permute-start(bf16[64,1536]{1,0:T(8,128)(2,1)S(1)} %get-tuple-element.14.rest_0_.refs_2_), channel_id=1, source_target_pairs={{0,4},{4,8},{8,12},{12,14},{14,10},{10,6},{6,2},{2,0},{1,5},{5,9},... | collective-permute-start | bytes 589832 | tf_op jit(solution)/shard_map/ppermute | solution.py:521
  5.8 10.5 %collective-permute-start.3 = (bf16[64,1536]{1,0:T(8,128)(2,1)S(1)}, bf16[64,1536]{1,0:T(8,128)(2,1)S(1)}, u32[]{:S(2)}, u32[]{:S(2)}) collective-permute-start(bf16[64,1536]{1,0:T(8,128)(2,1)S(1)} %get-tuple-element.17.refs_3_), channel_id=1, source_target_pairs={{0,4},{4,8},{8,12},{12,14},{14,10},{10,6},{6,2},{2,0},{1,5},{5,9},... | collective-permute-start | bytes 589832 | tf_op jit(solution)/shard_map/ppermute | solution.py:521
  7.8 9.8 %collective-permute-start.4 = (bf16[64,1536]{1,0:T(8,128)(2,1)S(1)}, bf16[64,1536]{1,0:T(8,128)(2,1)S(1)}, u32[]{:S(2)}, u32[]{:S(2)}) collective-permute-start(bf16[64,1536]{1,0:T(8,128)(2,1)S(1)} %get-tuple-element.17.refs_3_), channel_id=1, source_target_pairs={{4,0},{8,4},{12,8},{14,12},{10,14},{6,10},{2,6},{0,2},{5,1},{9,5},... | collective-permute-start | bytes 589832 | tf_op jit(solution)/shard_map/ppermute | solution.py:522
  7.9 1.5 %copy-start = (bf16[384,2560]{1,0:T(8,128)(2,1)S(1)}, bf16[384,2560]{1,0:T(8,128)(2,1)}, u32[]{:S(2)}) copy-start(bf16[384,2560]{1,0:T(8,128)(2,1)} %refs_8_.3) | copy-start | bytes 5898244
  9.4 2.5 %copy-start.11 = (bf16[2560,4,256]{2,1,0:T(4,128)(2,1)S(1)}, bf16[2560,4,256]{2,1,0:T(4,128)(2,1)}, u32[]{:S(2)}) copy-start(bf16[2560,4,256]{2,1,0:T(4,128)(2,1)} %param.13) | copy-start | bytes 15728644
  15.6 2.8 %copy-start.9 = (s32[8]{0:T(128)S(1)}, s32[8]{0:T(128)}, u32[]{:S(2)}) copy-start(s32[8]{0:T(128)} %length_ref.7) | copy-start | bytes 100
  15.6 2.8 %copy-start.12 = (s32[8,48]{1,0:T(8,128)S(1)}, s32[8,48]{1,0:T(8,128)}, u32[]{:S(2)}) copy-start(s32[8,48]{1,0:T(8,128)} %parent_ref.1) | copy-start | bytes 4612
  16.3 5.7 %collective-permute-start.5 = (bf16[64,1536]{1,0:T(8,128)(2,1)S(1)}, bf16[64,1536]{1,0:T(8,128)(2,1)S(1)}, u32[]{:S(2)}, u32[]{:S(2)}) collective-permute-start(bf16[64,1536]{1,0:T(8,128)(2,1)S(1)} %hold.6.refs_7_), channel_id=1, source_target_pairs={{0,4},{4,8},{8,12},{12,14},{14,10},{10,6},{6,2},{2,0},{1,5},{5,9},... | collective-permute-start | bytes 589832 | tf_op jit(solution)/shard_map/ppermute | solution.py:521
  17.6 5.7 %collective-permute-start.6 = (bf16[64,1536]{1,0:T(8,128)(2,1)S(1)}, bf16[64,1536]{1,0:T(8,128)(2,1)S(1)}, u32[]{:S(2)}, u32[]{:S(2)}) collective-permute-start(bf16[64,1536]{1,0:T(8,128)(2,1)S(1)} %hold.7.refs_11_), channel_id=1, source_target_pairs={{4,0},{8,4},{12,8},{14,12},{10,14},{6,10},{2,6},{0,2},{5,1},{9,5},... | collective-permute-start | bytes 589832 | tf_op jit(solution)/shard_map/ppermute | solution.py:522
  18.3 4.9 %copy-start.1 = (bf16[384,2560]{1,0:T(8,128)(2,1)S(1)}, bf16[384,2560]{1,0:T(8,128)(2,1)}, u32[]{:S(2)}) copy-start(bf16[384,2560]{1,0:T(8,128)(2,1)} %refs_8_.3) | copy-start | bytes 5898244
  18.4 4.9 %copy-start.6 = (s32[8,8]{1,0:T(8,128)S(1)}, s32[8,8]{1,0:T(8,128)}, u32[]{:S(2)}) copy-start(s32[8,8]{1,0:T(8,128)} %constant.10.clone.owner_ref) | copy-start | bytes 772
  18.4 4.9 %copy-start.8 = (s32[8]{0:T(128)S(1)}, s32[8]{0:T(128)}, u32[]{:S(2)}) copy-start(s32[8]{0:T(128)} %adapter_ref.11) | copy-start | bytes 100
  23.3 3.2 %copy-start.2 = (bf16[384,16,128]{2,1,0:T(8,128)(2,1)S(1)}, bf16[384,16,128]{2,1,0:T(8,128)(2,1)}, u32[]{:S(2)}) copy-start(bf16[384,16,128]{2,1,0:T(8,128)(2,1)} %query_ref.5) | copy-start | bytes 4718596
  23.3 3.1 %copy-start.3 = (bf16[8,128,2,128]{3,2,1,0:T(2,128)(2,1)S(1)}, bf16[8,128,2,128]{3,2,1,0:T(2,128)(2,1)}, u32[]{:S(2)}) copy-start(bf16[8,128,2,128]{3,2,1,0:T(2,128)(2,1)} %param.20) | copy-start | bytes 1572868
  23.3 3.1 %copy-start.4 = (bf16[8,128,2,128]{3,2,1,0:T(2,128)(2,1)S(1)}, bf16[8,128,2,128]{3,2,1,0:T(2,128)(2,1)}, u32[]{:S(2)}) copy-start(bf16[8,128,2,128]{3,2,1,0:T(2,128)(2,1)} %param.21) | copy-start | bytes 1572868
  23.3 3.1 %copy-start.10 = (f32[128]{0:T(128)S(1)}, f32[128]{0:T(128)}, u32[]{:S(2)}) copy-start(f32[128]{0:T(128)} %param.22) | copy-start | bytes 1540
  24.3 2.1 %collective-permute-start.7 = (f32[3,48,640]{2,1,0:T(8,128)S(1)}, f32[3,48,640]{2,1,0:T(8,128)S(1)}, u32[]{:S(2)}, u32[]{:S(2)}) collective-permute-start(f32[3,48,640]{2,1,0:T(8,128)S(1)} %shrink.3.shrunk_here_ref), channel_id=1, source_target_pairs={{0,1},{1,0},{2,3},{3,2},{4,5},{5,4},{6,7},{7,6},{8,9},{9,8},{10,11... | collective-permute-start | bytes 1105928 | tf_op jit(solution)/shard_map/ppermute | solution.py:517
  24.4 7.3 %collective-permute-start.2 = (bf16[64,1536]{1,0:T(8,128)(2,1)S(1)}, bf16[64,1536]{1,0:T(8,128)(2,1)S(1)}, u32[]{:S(2)}, u32[]{:S(2)}) collective-permute-start(bf16[64,1536]{1,0:T(8,128)(2,1)S(1)} %hold.5.refs_6_.rest_1_), channel_id=1, source_target_pairs={{0,4},{4,8},{8,12},{12,14},{14,10},{10,6},{6,2},{2,0},{1,5},{5,9},... | collective-permute-start | bytes 589832 | tf_op jit(solution)/shard_map/ppermute | solution.py:521
  26.0 7.3 %collective-permute-start.10 = (bf16[64,1536]{1,0:T(8,128)(2,1)S(1)}, bf16[64,1536]{1,0:T(8,128)(2,1)S(1)}, u32[]{:S(2)}, u32[]{:S(2)}) collective-permute-start(bf16[64,1536]{1,0:T(8,128)(2,1)S(1)} %collective-permute-done.1.rest_2_.refs_10_), channel_id=1, source_target_pairs={{4,0},{8,4},{12,8},{14,12},{10,14},{6,10},{2,6},{0,2},{5,1},{9,5},... | collective-permute-start | bytes 589832 | tf_op jit(solution)/shard_map/ppermute | solution.py:522
  31.0 6.7 %collective-permute-start.12 = (bf16[64,1536]{1,0:T(8,128)(2,1)S(1)}, bf16[64,1536]{1,0:T(8,128)(2,1)S(1)}, u32[]{:S(2)}, u32[]{:S(2)}) collective-permute-start(bf16[64,1536]{1,0:T(8,128)(2,1)S(1)} %hold.9.refs_7_), channel_id=1, source_target_pairs={{4,0},{8,4},{12,8},{14,12},{10,14},{6,10},{2,6},{0,2},{5,1},{9,5},... | collective-permute-start | bytes 589832 | tf_op jit(solution)/shard_map/ppermute | solution.py:522
  31.7 7.2 %collective-permute-start.8 = (bf16[64,1536]{1,0:T(8,128)(2,1)S(1)}, bf16[64,1536]{1,0:T(8,128)(2,1)S(1)}, u32[]{:S(2)}, u32[]{:S(2)}) collective-permute-start(bf16[64,1536]{1,0:T(8,128)(2,1)S(1)} %hold.8.refs_2_.rest_0_), channel_id=1, source_target_pairs={{0,4},{4,8},{8,12},{12,14},{14,10},{10,6},{6,2},{2,0},{1,5},{5,9},... | collective-permute-start | bytes 589832 | tf_op jit(solution)/shard_map/ppermute | solution.py:521
  34.2 6.3 %collective-permute-start.15 = (f32[2,48,640]{2,1,0:T(8,128)S(1)}, f32[2,48,640]{2,1,0:T(8,128)S(1)}, u32[]{:S(2)}, u32[]{:S(2)}) collective-permute-start(f32[2,48,640]{2,1,0:T(8,128)S(1)} %shrink.4.shrunk_here_ref), channel_id=1, source_target_pairs={{0,1},{1,0},{2,3},{3,2},{4,5},{5,4},{6,7},{7,6},{8,9},{9,8},{10,11... | collective-permute-start | bytes 737288 | tf_op jit(solution)/shard_map/ppermute | solution.py:517
  34.3 9.6 %collective-permute-start.9 = (bf16[64,1536]{1,0:T(8,128)(2,1)S(1)}, bf16[64,1536]{1,0:T(8,128)(2,1)S(1)}, u32[]{:S(2)}, u32[]{:S(2)}) collective-permute-start(bf16[64,1536]{1,0:T(8,128)(2,1)S(1)} %collective-permute-done.5.refs_12_.refs_3_), channel_id=1, source_target_pairs={{0,4},{4,8},{8,12},{12,14},{14,10},{10,6},{6,2},{2,0},{1,5},{5,9},... | collective-permute-start | bytes 589832 | tf_op jit(solution)/shard_map/ppermute | solution.py:521
  35.9 8.0 %collective-permute-start.11 = (bf16[64,1536]{1,0:T(8,128)(2,1)S(1)}, bf16[64,1536]{1,0:T(8,128)(2,1)S(1)}, u32[]{:S(2)}, u32[]{:S(2)}) collective-permute-start(bf16[64,1536]{1,0:T(8,128)(2,1)S(1)} %collective-permute-done.10.refs_6_.rest_1_), channel_id=1, source_target_pairs={{4,0},{8,4},{12,8},{14,12},{10,14},{6,10},{2,6},{0,2},{5,1},{9,5},... | collective-permute-start | bytes 589832 | tf_op jit(solution)/shard_map/ppermute | solution.py:522
  37.7 9.4 %collective-permute-start.14 = (bf16[64,1536]{1,0:T(8,128)(2,1)S(1)}, bf16[64,1536]{1,0:T(8,128)(2,1)S(1)}, u32[]{:S(2)}, u32[]{:S(2)}) collective-permute-start(bf16[64,1536]{1,0:T(8,128)(2,1)S(1)} %collective-permute-done.12.refs_7_), channel_id=1, source_target_pairs={{4,0},{8,4},{12,8},{14,12},{10,14},{6,10},{2,6},{0,2},{5,1},{9,5},... | collective-permute-start | bytes 589832 | tf_op jit(solution)/shard_map/ppermute | solution.py:547
  38.9 8.2 %collective-permute-start.13 = (bf16[64,1536]{1,0:T(8,128)(2,1)S(1)}, bf16[64,1536]{1,0:T(8,128)(2,1)S(1)}, u32[]{:S(2)}, u32[]{:S(2)}) collective-permute-start(bf16[64,1536]{1,0:T(8,128)(2,1)S(1)} %collective-permute-done.8.refs_2_.rest_0_), channel_id=1, source_target_pairs={{0,4},{4,8},{8,12},{12,14},{14,10},{10,6},{6,2},{2,0},{1,5},{5,9},... | collective-permute-start | bytes 589832 | tf_op jit(solution)/shard_map/ppermute | solution.py:547
  48.1 1.7 %collective-permute-start.16 = (f32[3,48,640]{2,1,0:T(8,128)S(1)}, f32[3,48,640]{2,1,0:T(8,128)S(1)}, u32[]{:S(2)}, u32[]{:S(2)}) collective-permute-start(f32[3,48,640]{2,1,0:T(8,128)S(1)} %shrink.5.shrunk_here_ref), channel_id=1, source_target_pairs={{0,1},{1,0},{2,3},{3,2},{4,5},{5,4},{6,7},{7,6},{8,9},{9,8},{10,11... | collective-permute-start | bytes 1105928 | tf_op jit(solution)/shard_map/ppermute | solution.py:517

commit v10 on v9

--- a/solution.py
+++ b/solution.py
@@ -525,9 +525,8 @@
         if step == 1:
             held = [hold(piece, away) for piece in held]
             table = tree_tables(
-                cache_lengths, tree_parents, head_size, heads_here, [here, front[0], rear[0]]
+                cache_lengths, tree_parents, head_size, heads_here, [here]
             )
-            first_front = hold(first_front, table)
             shared = (
                 cache_lengths,
                 key_gain.reshape(1, head_size),
@@ -538,9 +537,8 @@
                 value_rows,
             )
         if step == 2 and split_batches:
-            finish_batch(arrivals[:near], held)
-            token = done[-1][0][2]
-            first_front, held[1] = hold(first_front, token), hold(held[1], token)
+            finish_batch(arrivals[:near])
+            first_front, held[1] = hold(first_front, table), hold(held[1], table)
         front, rear = (first_front, held[0]), (rear[0], held[1])
         arrivals += [front, rear]
     arrivals.append(

time: 54.5 us -> 53.3 us (0.978)
  waiting for transfers between devices: 10.1 us -> 9.41 us
    ppermute x6, waiting for transfers between devices: 2.55 us -> 0.27 us  [per_device(): front = tuple((lax.ppermute(piece, 'pool', onward) for piece in front))]
    ppermute x6, starting transfers between devices: 5.38 us -> 4.01 us  [per_device(): rear = tuple((lax.ppermute(piece, 'pool', backward) for piece in rear))]
    ppermute x1, starting transfers between devices: 1.58 us -> 0.22 us  [per_device(): lax.ppermute(front[0], 'pool', onward)]
    ppermute x6, waiting for transfers between devices: 2.66 us -> 4.01 us  [per_device(): rear = tuple((lax.ppermute(piece, 'pool', backward) for piece in rear))]
    ppermute x1, starting transfers between devices: 0.7 us -> 1.8 us  [per_device(): lax.ppermute(rear[1], 'pool', backward)]
    ppermute x6, starting transfers between devices: 8.24 us -> 9.31 us  [per_device(): front = tuple((lax.ppermute(piece, 'pool', onward) for piece in front))]
    unnamed x26 -> x24, local copies, waits for them, and re-layouts: 5.96 us -> 5.94 us
  transfers between devices with their start and end apart: 17 -> 17, of which waited for: 7 -> 6; matrix products, arithmetic and copies ran while one was open for 0% -> 0% of each run, Pallas kernels for 27% -> 28%
where the time goes in v10:
time: 53.3 us; the launch traced here: 53 us
  Pallas kernels  21.4 us (40%)
  starting transfers between devices  15.5 us (29%)
  waiting for transfers between devices  9.41 us (18%)
  local copies, waits for them, and re-layouts  5.94 us (11%)
  between operations  0.82 us (2%)
    pallas_call x3, Pallas kernels, finish(): pl.pallas_call(functools.partial(finish_kernel, count=count, slot=slot, k...  12.4 us
    ppermute x6, starting transfers between devices, per_device(): front = tuple((lax.ppermute(piece, 'pool', onward) for piece in front))  9.31 us
    unnamed x24, local copies, waits for them, and re-layouts  5.94 us
    ppermute x6, waiting for transfers between devices, per_device(): rear = tuple((lax.ppermute(piece, 'pool', backward) for piece in rear))  4.01 us
    ppermute x6, starting transfers between devices, per_device(): rear = tuple((lax.ppermute(piece, 'pool', backward) for piece in rear))  4.01 us
    pallas_call x1, Pallas kernels, base_product(): pl.pallas_call(functools.partial(base_kernel, held_count=len(held)), grid...  3.66 us
    ppermute x1, waiting for transfers between devices, per_device(): lax.ppermute(rear[1], 'pool', backward)  3.44 us
    pallas_call x3, Pallas kernels, shrink_rows(): pl.pallas_call(functools.partial(shrink_kernel, columns=columns, cut=cut)...  2.91 us
  transfers between devices with their start and end apart: 17, of which 6 were waited for; matrix products, arithmetic and copies ran while one was open for 0% of the time, Pallas kernels for 28%

profile of v10, /device:TPU:0, one launch (start us, length us, event | category | flops | bytes accessed | tf_op | source)
XLA Modules:
  0.0 53.0 jit_solution(5359309645189559385)
XLA Ops:
  0.6 1.0 %copy-done.4 = bf16[1,2560,64]{1,2,0:T(8,128)(2,1)S(1)} copy-done((bf16[1,2560,64]{1,2,0:T(8,128)(2,1)S(1)}, bf16[1,2560,64]{1,2,0:T(8,128)(2,1)}, u32[]{:S(2)}) %copy-start.4) | copy-done | bytes 327704
  1.6 0.9 %copy-done.6 = bf16[1,64,4,256]{3,2,1,0:T(4,128)(2,1)S(1)} copy-done((bf16[1,64,4,256]{3,2,1,0:T(4,128)(2,1)S(1)}, bf16[1,64,4,256]{3,2,1,0:T(4,128)(2,1)}, u32[]{:S(2)}) %copy-start.6) | copy-done | bytes 131096
  2.5 0.2 pack.1
  2.7 3.1 %collective-permute-start.3 = (bf16[64,1536]{1,0:T(8,128)(2,1)S(1)}, bf16[64,1536]{1,0:T(8,128)(2,1)S(1)}, u32[]{:S(2)}, u32[]{:S(2)}) collective-permute-start(bf16[64,1536]{1,0:T(8,128)(2,1)S(1)} %get-tuple-element.17.refs_3_), channel_id=1, source_target_pairs={{0,4},{4,8},{8,12},{12,14},{14,10},{10,6},{6,2},{2,0},{1,5},{5,9},... | collective-permute-start | bytes 589832 | tf_op jit(solution)/shard_map/ppermute | solution.py:521
  5.8 2.0 %collective-permute-start = (bf16[64,1536]{1,0:T(8,128)(2,1)S(1)}, bf16[64,1536]{1,0:T(8,128)(2,1)S(1)}, u32[]{:S(2)}, u32[]{:S(2)}) collective-permute-start(bf16[64,1536]{1,0:T(8,128)(2,1)S(1)} %get-tuple-element.14.rest_0_.refs_2_), channel_id=1, source_target_pairs={{0,4},{4,8},{8,12},{12,14},{14,10},{10,6},{6,2},{2,0},{1,5},{5,9},... | collective-permute-start | bytes 589832 | tf_op jit(solution)/shard_map/ppermute | solution.py:521
  7.8 1.5 %copy-done = bf16[384,2560]{1,0:T(8,128)(2,1)S(1)} copy-done((bf16[384,2560]{1,0:T(8,128)(2,1)S(1)}, bf16[384,2560]{1,0:T(8,128)(2,1)}, u32[]{:S(2)}) %copy-start) | copy-done | bytes 1966104
  9.4 2.5 %copy-done.10 = bf16[2560,4,256]{2,1,0:T(4,128)(2,1)S(1)} copy-done((bf16[2560,4,256]{2,1,0:T(4,128)(2,1)S(1)}, bf16[2560,4,256]{2,1,0:T(4,128)(2,1)}, u32[]{:S(2)}) %copy-start.10) | copy-done | bytes 5242904
  11.8 3.7 %base.1 = (f32[384,512]{1,0:T(8,128)S(1)}, f32[384,512]{1,0:T(8,128)S(1)}) custom-call(s32[1]{0:T(128)} %bitcast.1.core_ref, bf16[384,2560]{1,0:T(8,128)(2,1)S(1)} %copy-done, bf16[20480,128]{1,0:T(8,128)(2,1)S(1)} %bitcast.34, bf16[64,1536]{1,0:T(8,128)(2,1)S(1)} %get-tuple-element.14.rest_0_.refs_2_), custom_call_target="tpu_custom_call" | custom-call | flops 4000000000 | bytes 9000000 | tf_op jit(solution)/shard_map/base/pallas_call | solution.py:154
  15.6 0.8 %collective-permute-done.6.refs_10_.rest_2_ = bf16[64,1536]{1,0:T(8,128)(2,1)S(1)} collective-permute-done((bf16[64,1536]{1,0:T(8,128)(2,1)S(1)}, bf16[64,1536]{1,0:T(8,128)(2,1)S(1)}, u32[]{:S(2)}, u32[]{:S(2)}) %collective-permute-start.6) | collective-permute-done | bytes 196640 | tf_op jit(solution)/shard_map/ppermute | solution.py:522
  16.4 1.0 %shrink.3.shrunk_here_ref = f32[3,48,640]{2,1,0:T(8,128)S(1)} custom-call(s32[1]{0:T(128)} %bitcast.me_ref, s32[8,8]{1,0:T(8,128)S(1)} %copy-done.5, s32[8]{0:T(128)S(1)} %copy-done.7, bf16[384,2560]{1,0:T(8,128)(2,1)S(1)} %copy-done, f32[384,512]{1,0:T(8,128)S(1)} %get-tuple-element.16.token_ref.refs_1_.refs_5_.refs_9_, ...), custom_call_target="tpu_custom_call" | custom-call | flops 90000000 | bytes 600000 | tf_op jit(solution)/shard_map/shrink/pallas_call | solution.py:273
  17.4 1.8 %collective-permute-start.10 = (bf16[64,1536]{1,0:T(8,128)(2,1)S(1)}, bf16[64,1536]{1,0:T(8,128)(2,1)S(1)}, u32[]{:S(2)}, u32[]{:S(2)}) collective-permute-start(bf16[64,1536]{1,0:T(8,128)(2,1)S(1)} %hold.6.refs_11_), channel_id=1, source_target_pairs={{4,0},{8,4},{12,8},{14,12},{10,14},{6,10},{2,6},{0,2},{5,1},{9,5},... | collective-permute-start | bytes 589832 | tf_op jit(solution)/shard_map/ppermute | solution.py:522
  19.2 0.2 collective-permute-start.1
  19.5 1.9 %collective-permute-start.4 = (bf16[64,1536]{1,0:T(8,128)(2,1)S(1)}, bf16[64,1536]{1,0:T(8,128)(2,1)S(1)}, u32[]{:S(2)}, u32[]{:S(2)}) collective-permute-start(bf16[64,1536]{1,0:T(8,128)(2,1)S(1)} %hold.5.refs_7_), channel_id=1, source_target_pairs={{0,4},{4,8},{8,12},{12,14},{14,10},{10,6},{6,2},{2,0},{1,5},{5,9},... | collective-permute-start | bytes 589832 | tf_op jit(solution)/shard_map/ppermute | solution.py:521
  21.3 0.2 collective-permute-start.7
  21.5 2.3 %tree.1.token_ref.table_ref = f32[384,384]{1,0:T(8,128)S(1)} custom-call(s32[8]{0:T(128)S(1)} %copy-done.8, s32[8,48]{1,0:T(8,128)S(1)} %copy-done.11, f32[384,512]{1,0:T(8,128)S(1)} %get-tuple-element.15.rest_0_.here_ref), custom_call_target="tpu_custom_call" | custom-call | flops 1000000000 | bytes 8000000 | tf_op jit(solution)/shard_map/tree/pallas_call | solution.py:225
  23.8 1.3 %collective-permute-done.10.array_ref = bf16[64,1536]{1,0:T(8,128)(2,1)S(1)} collective-permute-done((bf16[64,1536]{1,0:T(8,128)(2,1)S(1)}, bf16[64,1536]{1,0:T(8,128)(2,1)S(1)}, u32[]{:S(2)}, u32[]{:S(2)}) %collective-permute-start.10) | collective-permute-done | bytes 196640 | tf_op jit(solution)/shard_map/ppermute | solution.py:522
  25.1 1.8 %collective-permute-start.11 = (bf16[64,1536]{1,0:T(8,128)(2,1)S(1)}, bf16[64,1536]{1,0:T(8,128)(2,1)S(1)}, u32[]{:S(2)}, u32[]{:S(2)}) collective-permute-start(bf16[64,1536]{1,0:T(8,128)(2,1)S(1)} %hold.7.refs_7_), channel_id=1, source_target_pairs={{4,0},{8,4},{12,8},{14,12},{10,14},{6,10},{2,6},{0,2},{5,1},{9,5},... | collective-permute-start | bytes 589832 | tf_op jit(solution)/shard_map/ppermute | solution.py:522
  27.0 0.2 collective-permute-start.2
  27.2 4.5 %finish.3 = (bf16[384,16,128]{2,1,0:T(8,128)(2,1)}, bf16[1536,128]{1,0:T(8,128)(2,1)}, f32[8,128]{1,0:T(8,128)S(1)}) custom-call(s32[1]{0:T(128)} %bitcast.me_ref, s32[8,8]{1,0:T(8,128)S(1)} %copy-done.5, s32[8]{0:T(128)S(1)} %copy-done.7, s32[8]{0:T(128)S(1)} %copy-done.8, f32[384,512]{1,0:T(8,128)S(1)} %get-tuple-element.15.rest_0_.here_ref, ...), custom_call_target="tpu_custom_call" | custom-call | flops 270000000 | bytes 900000 | tf_op jit(solution)/shard_map/finish/pallas_call | solution.py:424
  31.7 0.9 %shrink.4.shrunk_here_ref = f32[2,48,640]{2,1,0:T(8,128)S(1)} custom-call(s32[1]{0:T(128)} %bitcast.me_ref, s32[8,8]{1,0:T(8,128)S(1)} %copy-done.5, s32[8]{0:T(128)S(1)} %copy-done.7, bf16[384,2560]{1,0:T(8,128)(2,1)S(1)} %copy-done, f32[384,512]{1,0:T(8,128)S(1)} %get-tuple-element.16.token_ref.refs_1_.refs_5_.refs_9_, ...), custom_call_target="tpu_custom_call" | custom-call | flops 60000000 | bytes 400000 | tf_op jit(solution)/shard_map/shrink/pallas_call | solution.py:273
  32.7 0.1 collective-permute-start.15
  32.7 1.9 %collective-permute-start.5 = (bf16[64,1536]{1,0:T(8,128)(2,1)S(1)}, bf16[64,1536]{1,0:T(8,128)(2,1)S(1)}, u32[]{:S(2)}, u32[]{:S(2)}) collective-permute-start(bf16[64,1536]{1,0:T(8,128)(2,1)S(1)} %collective-permute-done.4.refs_3_), channel_id=1, source_target_pairs={{0,4},{4,8},{8,12},{12,14},{14,10},{10,6},{6,2},{2,0},{1,5},{5,9},... | collective-permute-start | bytes 589832 | tf_op jit(solution)/shard_map/ppermute | solution.py:521
  34.6 0.2 collective-permute-start.8
  34.8 1.8 %collective-permute-start.13 = (bf16[64,1536]{1,0:T(8,128)(2,1)S(1)}, bf16[64,1536]{1,0:T(8,128)(2,1)S(1)}, u32[]{:S(2)}, u32[]{:S(2)}) collective-permute-start(bf16[64,1536]{1,0:T(8,128)(2,1)S(1)} %collective-permute-done.11.refs_7_), channel_id=1, source_target_pairs={{4,0},{8,4},{12,8},{14,12},{10,14},{6,10},{2,6},{0,2},{5,1},{9,5},... | collective-permute-start | bytes 589832 | tf_op jit(solution)/shard_map/ppermute | solution.py:545
  36.6 0.2 collective-permute-start.12
  36.8 3.4 %finish.4 = (bf16[384,16,128]{2,1,0:T(8,128)(2,1)}, bf16[1536,128]{1,0:T(8,128)(2,1)}, f32[8,128]{1,0:T(8,128)S(1)}) custom-call(s32[1]{0:T(128)} %bitcast.me_ref, s32[8,8]{1,0:T(8,128)S(1)} %copy-done.5, s32[8]{0:T(128)S(1)} %copy-done.7, s32[8]{0:T(128)S(1)} %copy-done.8, ...), custom_call_target="tpu_custom_call", output_to_operand_aliasing={{0}: (14, {}), {1}: (15, {})} | custom-call | flops 180000000 | bytes 600000 | tf_op jit(solution)/shard_map/finish/pallas_call | solution.py:424
  40.3 0.2 collective-permute-done.5.refs_3_
  40.5 1.9 %collective-permute-done.8.refs_6_.rest_1_ = bf16[64,1536]{1,0:T(8,128)(2,1)S(1)} collective-permute-done((bf16[64,1536]{1,0:T(8,128)(2,1)S(1)}, bf16[64,1536]{1,0:T(8,128)(2,1)S(1)}, u32[]{:S(2)}, u32[]{:S(2)}) %collective-permute-start.8) | collective-permute-done | bytes 196640 | tf_op jit(solution)/shard_map/ppermute | solution.py:522
  42.4 3.4 %collective-permute-done.13.refs_11_ = bf16[64,1536]{1,0:T(8,128)(2,1)S(1)} collective-permute-done((bf16[64,1536]{1,0:T(8,128)(2,1)S(1)}, bf16[64,1536]{1,0:T(8,128)(2,1)S(1)}, u32[]{:S(2)}, u32[]{:S(2)}) %collective-permute-start.13) | collective-permute-done | bytes 196640 | tf_op jit(solution)/shard_map/ppermute | solution.py:545
  45.8 1.0 %shrink.5.shrunk_here_ref = f32[3,48,640]{2,1,0:T(8,128)S(1)} custom-call(s32[1]{0:T(128)} %bitcast.me_ref, s32[8,8]{1,0:T(8,128)S(1)} %copy-done.5, s32[8]{0:T(128)S(1)} %copy-done.7, bf16[384,2560]{1,0:T(8,128)(2,1)S(1)} %copy-done, f32[384,512]{1,0:T(8,128)S(1)} %get-tuple-element.16.token_ref.refs_1_.refs_5_.refs_9_, ...), custom_call_target="tpu_custom_call" | custom-call | flops 90000000 | bytes 600000 | tf_op jit(solution)/shard_map/shrink/pallas_call | solution.py:273
  46.9 1.7 %collective-permute-done.16.shrunk_there_ref = f32[3,48,640]{2,1,0:T(8,128)S(1)} collective-permute-done((f32[3,48,640]{2,1,0:T(8,128)S(1)}, f32[3,48,640]{2,1,0:T(8,128)S(1)}, u32[]{:S(2)}, u32[]{:S(2)}) %collective-permute-start.16) | collective-permute-done | bytes 368672 | tf_op jit(solution)/shard_map/ppermute | solution.py:517
  48.5 4.5 %finish.5 = (bf16[384,16,128]{2,1,0:T(8,128)(2,1)}, bf16[1536,128]{1,0:T(8,128)(2,1)}, f32[8,128]{1,0:T(8,128)}) custom-call(s32[1]{0:T(128)} %bitcast.me_ref, s32[8,8]{1,0:T(8,128)S(1)} %copy-done.5, s32[8]{0:T(128)S(1)} %copy-done.7, s32[8]{0:T(128)S(1)} %copy-done.8, ...), custom_call_target="tpu_custom_call", output_to_operand_aliasing={{0}: (15, {}), {1}: (16, {})} | custom-call | flops 270000000 | bytes 900000 | tf_op jit(solution)/shard_map/finish/pallas_call | solution.py:424
  (39 shorter events, 0.2 us)
Async XLA Ops:
  0.6 1.0 %copy-start.4 = (bf16[1,2560,64]{1,2,0:T(8,128)(2,1)S(1)}, bf16[1,2560,64]{1,2,0:T(8,128)(2,1)}, u32[]{:S(2)}) copy-start(bf16[1,2560,64]{1,2,0:T(8,128)(2,1)} %param.14) | copy-start | bytes 983044
  1.6 0.9 %copy-start.6 = (bf16[1,64,4,256]{3,2,1,0:T(4,128)(2,1)S(1)}, bf16[1,64,4,256]{3,2,1,0:T(4,128)(2,1)}, u32[]{:S(2)}) copy-start(bf16[1,64,4,256]{3,2,1,0:T(4,128)(2,1)} %param.15) | copy-start | bytes 393220
  2.7 12.8 %collective-permute-start.3 = (bf16[64,1536]{1,0:T(8,128)(2,1)S(1)}, bf16[64,1536]{1,0:T(8,128)(2,1)S(1)}, u32[]{:S(2)}, u32[]{:S(2)}) collective-permute-start(bf16[64,1536]{1,0:T(8,128)(2,1)S(1)} %get-tuple-element.17.refs_3_), channel_id=1, source_target_pairs={{0,4},{4,8},{8,12},{12,14},{14,10},{10,6},{6,2},{2,0},{1,5},{5,9},... | collective-permute-start | bytes 589832 | tf_op jit(solution)/shard_map/ppermute | solution.py:521
  5.8 9.8 %collective-permute-start.9 = (bf16[64,1536]{1,0:T(8,128)(2,1)S(1)}, bf16[64,1536]{1,0:T(8,128)(2,1)S(1)}, u32[]{:S(2)}, u32[]{:S(2)}) collective-permute-start(bf16[64,1536]{1,0:T(8,128)(2,1)S(1)} %get-tuple-element.17.refs_3_), channel_id=1, source_target_pairs={{4,0},{8,4},{12,8},{14,12},{10,14},{6,10},{2,6},{0,2},{5,1},{9,5},... | collective-permute-start | bytes 589832 | tf_op jit(solution)/shard_map/ppermute | solution.py:522
  5.8 9.8 %collective-permute-start = (bf16[64,1536]{1,0:T(8,128)(2,1)S(1)}, bf16[64,1536]{1,0:T(8,128)(2,1)S(1)}, u32[]{:S(2)}, u32[]{:S(2)}) collective-permute-start(bf16[64,1536]{1,0:T(8,128)(2,1)S(1)} %get-tuple-element.14.rest_0_.refs_2_), channel_id=1, source_target_pairs={{0,4},{4,8},{8,12},{12,14},{14,10},{10,6},{6,2},{2,0},{1,5},{5,9},... | collective-permute-start | bytes 589832 | tf_op jit(solution)/shard_map/ppermute | solution.py:521
  7.8 8.5 %collective-permute-start.6 = (bf16[64,1536]{1,0:T(8,128)(2,1)S(1)}, bf16[64,1536]{1,0:T(8,128)(2,1)S(1)}, u32[]{:S(2)}, u32[]{:S(2)}) collective-permute-start(bf16[64,1536]{1,0:T(8,128)(2,1)S(1)} %get-tuple-element.14.rest_0_.refs_2_), channel_id=1, source_target_pairs={{4,0},{8,4},{12,8},{14,12},{10,14},{6,10},{2,6},{0,2},{5,1},{9,5},... | collective-permute-start | bytes 589832 | tf_op jit(solution)/shard_map/ppermute | solution.py:522
  7.8 1.5 %copy-start = (bf16[384,2560]{1,0:T(8,128)(2,1)S(1)}, bf16[384,2560]{1,0:T(8,128)(2,1)}, u32[]{:S(2)}) copy-start(bf16[384,2560]{1,0:T(8,128)(2,1)} %refs_8_.3) | copy-start | bytes 5898244
  9.4 2.5 %copy-start.10 = (bf16[2560,4,256]{2,1,0:T(4,128)(2,1)S(1)}, bf16[2560,4,256]{2,1,0:T(4,128)(2,1)}, u32[]{:S(2)}) copy-start(bf16[2560,4,256]{2,1,0:T(4,128)(2,1)} %param.13) | copy-start | bytes 15728644
  15.5 0.8 %copy-start.5 = (s32[8,8]{1,0:T(8,128)S(1)}, s32[8,8]{1,0:T(8,128)}, u32[]{:S(2)}) copy-start(s32[8,8]{1,0:T(8,128)} %constant.10.clone.owner_ref) | copy-start | bytes 772
  15.5 0.8 %copy-start.7 = (s32[8]{0:T(128)S(1)}, s32[8]{0:T(128)}, u32[]{:S(2)}) copy-start(s32[8]{0:T(128)} %adapter_ref.11) | copy-start | bytes 100
  16.4 5.1 %copy-start.8 = (s32[8]{0:T(128)S(1)}, s32[8]{0:T(128)}, u32[]{:S(2)}) copy-start(s32[8]{0:T(128)} %length_ref.7) | copy-start | bytes 100
  16.4 5.1 %copy-start.11 = (s32[8,48]{1,0:T(8,128)S(1)}, s32[8,48]{1,0:T(8,128)}, u32[]{:S(2)}) copy-start(s32[8,48]{1,0:T(8,128)} %parent_ref.1) | copy-start | bytes 4612
  17.4 9.8 %collective-permute-start.14 = (f32[3,48,640]{2,1,0:T(8,128)S(1)}, f32[3,48,640]{2,1,0:T(8,128)S(1)}, u32[]{:S(2)}, u32[]{:S(2)}) collective-permute-start(f32[3,48,640]{2,1,0:T(8,128)S(1)} %shrink.3.shrunk_here_ref), channel_id=1, source_target_pairs={{0,1},{1,0},{2,3},{3,2},{4,5},{5,4},{6,7},{7,6},{8,9},{9,8},{10,11... | collective-permute-start | bytes 1105928 | tf_op jit(solution)/shard_map/ppermute | solution.py:517
  17.4 7.7 %collective-permute-start.10 = (bf16[64,1536]{1,0:T(8,128)(2,1)S(1)}, bf16[64,1536]{1,0:T(8,128)(2,1)S(1)}, u32[]{:S(2)}, u32[]{:S(2)}) collective-permute-start(bf16[64,1536]{1,0:T(8,128)(2,1)S(1)} %hold.6.refs_11_), channel_id=1, source_target_pairs={{4,0},{8,4},{12,8},{14,12},{10,14},{6,10},{2,6},{0,2},{5,1},{9,5},... | collective-permute-start | bytes 589832 | tf_op jit(solution)/shard_map/ppermute | solution.py:522
  19.2 7.7 %collective-permute-start.1 = (bf16[64,1536]{1,0:T(8,128)(2,1)S(1)}, bf16[64,1536]{1,0:T(8,128)(2,1)S(1)}, u32[]{:S(2)}, u32[]{:S(2)}) collective-permute-start(bf16[64,1536]{1,0:T(8,128)(2,1)S(1)} %collective-permute-done.refs_6_.rest_1_), channel_id=1, source_target_pairs={{0,4},{4,8},{8,12},{12,14},{14,10},{10,6},{6,2},{2,0},{1,5},{5,9},... | collective-permute-start | bytes 589832 | tf_op jit(solution)/shard_map/ppermute | solution.py:521
  19.5 12.3 %collective-permute-start.4 = (bf16[64,1536]{1,0:T(8,128)(2,1)S(1)}, bf16[64,1536]{1,0:T(8,128)(2,1)S(1)}, u32[]{:S(2)}, u32[]{:S(2)}) collective-permute-start(bf16[64,1536]{1,0:T(8,128)(2,1)S(1)} %hold.5.refs_7_), channel_id=1, source_target_pairs={{0,4},{4,8},{8,12},{12,14},{14,10},{10,6},{6,2},{2,0},{1,5},{5,9},... | collective-permute-start | bytes 589832 | tf_op jit(solution)/shard_map/ppermute | solution.py:521
  21.3 10.4 %collective-permute-start.7 = (bf16[64,1536]{1,0:T(8,128)(2,1)S(1)}, bf16[64,1536]{1,0:T(8,128)(2,1)S(1)}, u32[]{:S(2)}, u32[]{:S(2)}) collective-permute-start(bf16[64,1536]{1,0:T(8,128)(2,1)S(1)} %collective-permute-done.6.refs_10_.rest_2_), channel_id=1, source_target_pairs={{4,0},{8,4},{12,8},{14,12},{10,14},{6,10},{2,6},{0,2},{5,1},{9,5},... | collective-permute-start | bytes 589832 | tf_op jit(solution)/shard_map/ppermute | solution.py:522
  21.5 5.7 %copy-start.2 = (bf16[8,128,2,128]{3,2,1,0:T(2,128)(2,1)S(1)}, bf16[8,128,2,128]{3,2,1,0:T(2,128)(2,1)}, u32[]{:S(2)}) copy-start(bf16[8,128,2,128]{3,2,1,0:T(2,128)(2,1)} %param.20) | copy-start | bytes 1572868
  21.5 5.7 %copy-start.3 = (bf16[8,128,2,128]{3,2,1,0:T(2,128)(2,1)S(1)}, bf16[8,128,2,128]{3,2,1,0:T(2,128)(2,1)}, u32[]{:S(2)}) copy-start(bf16[8,128,2,128]{3,2,1,0:T(2,128)(2,1)} %param.21) | copy-start | bytes 1572868
  23.8 3.4 %copy-start.1 = (bf16[384,16,128]{2,1,0:T(8,128)(2,1)S(1)}, bf16[384,16,128]{2,1,0:T(8,128)(2,1)}, u32[]{:S(2)}) copy-start(bf16[384,16,128]{2,1,0:T(8,128)(2,1)} %query_ref.5) | copy-start | bytes 4718596
  23.8 3.4 %copy-start.9 = (f32[128]{0:T(128)S(1)}, f32[128]{0:T(128)}, u32[]{:S(2)}) copy-start(f32[128]{0:T(128)} %param.22) | copy-start | bytes 1540
  25.1 9.7 %collective-permute-start.11 = (bf16[64,1536]{1,0:T(8,128)(2,1)S(1)}, bf16[64,1536]{1,0:T(8,128)(2,1)S(1)}, u32[]{:S(2)}, u32[]{:S(2)}) collective-permute-start(bf16[64,1536]{1,0:T(8,128)(2,1)S(1)} %hold.7.refs_7_), channel_id=1, source_target_pairs={{4,0},{8,4},{12,8},{14,12},{10,14},{6,10},{2,6},{0,2},{5,1},{9,5},... | collective-permute-start | bytes 589832 | tf_op jit(solution)/shard_map/ppermute | solution.py:522
  27.0 9.6 %collective-permute-start.2 = (bf16[64,1536]{1,0:T(8,128)(2,1)S(1)}, bf16[64,1536]{1,0:T(8,128)(2,1)S(1)}, u32[]{:S(2)}, u32[]{:S(2)}) collective-permute-start(bf16[64,1536]{1,0:T(8,128)(2,1)S(1)} %hold.4.refs_2_.rest_0_), channel_id=1, source_target_pairs={{0,4},{4,8},{8,12},{12,14},{14,10},{10,6},{6,2},{2,0},{1,5},{5,9},... | collective-permute-start | bytes 589832 | tf_op jit(solution)/shard_map/ppermute | solution.py:521
  32.7 4.2 %collective-permute-start.15 = (f32[2,48,640]{2,1,0:T(8,128)S(1)}, f32[2,48,640]{2,1,0:T(8,128)S(1)}, u32[]{:S(2)}, u32[]{:S(2)}) collective-permute-start(f32[2,48,640]{2,1,0:T(8,128)S(1)} %shrink.4.shrunk_here_ref), channel_id=1, source_target_pairs={{0,1},{1,0},{2,3},{3,2},{4,5},{5,4},{6,7},{7,6},{8,9},{9,8},{10,11... | collective-permute-start | bytes 737288 | tf_op jit(solution)/shard_map/ppermute | solution.py:517
  32.7 7.7 %collective-permute-start.5 = (bf16[64,1536]{1,0:T(8,128)(2,1)S(1)}, bf16[64,1536]{1,0:T(8,128)(2,1)S(1)}, u32[]{:S(2)}, u32[]{:S(2)}) collective-permute-start(bf16[64,1536]{1,0:T(8,128)(2,1)S(1)} %collective-permute-done.4.refs_3_), channel_id=1, source_target_pairs={{0,4},{4,8},{8,12},{12,14},{14,10},{10,6},{6,2},{2,0},{1,5},{5,9},... | collective-permute-start | bytes 589832 | tf_op jit(solution)/shard_map/ppermute | solution.py:521
  34.6 7.7 %collective-permute-start.8 = (bf16[64,1536]{1,0:T(8,128)(2,1)S(1)}, bf16[64,1536]{1,0:T(8,128)(2,1)S(1)}, u32[]{:S(2)}, u32[]{:S(2)}) collective-permute-start(bf16[64,1536]{1,0:T(8,128)(2,1)S(1)} %collective-permute-done.7.refs_6_.rest_1_), channel_id=1, source_target_pairs={{4,0},{8,4},{12,8},{14,12},{10,14},{6,10},{2,6},{0,2},{5,1},{9,5},... | collective-permute-start | bytes 589832 | tf_op jit(solution)/shard_map/ppermute | solution.py:522
  34.8 11.0 %collective-permute-start.13 = (bf16[64,1536]{1,0:T(8,128)(2,1)S(1)}, bf16[64,1536]{1,0:T(8,128)(2,1)S(1)}, u32[]{:S(2)}, u32[]{:S(2)}) collective-permute-start(bf16[64,1536]{1,0:T(8,128)(2,1)S(1)} %collective-permute-done.11.refs_7_), channel_id=1, source_target_pairs={{4,0},{8,4},{12,8},{14,12},{10,14},{6,10},{2,6},{0,2},{5,1},{9,5},... | collective-permute-start | bytes 589832 | tf_op jit(solution)/shard_map/ppermute | solution.py:545
  36.6 9.2 %collective-permute-start.12 = (bf16[64,1536]{1,0:T(8,128)(2,1)S(1)}, bf16[64,1536]{1,0:T(8,128)(2,1)S(1)}, u32[]{:S(2)}, u32[]{:S(2)}) collective-permute-start(bf16[64,1536]{1,0:T(8,128)(2,1)S(1)} %collective-permute-done.2.refs_2_.rest_0_), channel_id=1, source_target_pairs={{0,4},{4,8},{8,12},{12,14},{14,10},{10,6},{6,2},{2,0},{1,5},{5,9},... | collective-permute-start | bytes 589832 | tf_op jit(solution)/shard_map/ppermute | solution.py:545
  46.8 1.7 %collective-permute-start.16 = (f32[3,48,640]{2,1,0:T(8,128)S(1)}, f32[3,48,640]{2,1,0:T(8,128)S(1)}, u32[]{:S(2)}, u32[]{:S(2)}) collective-permute-start(f32[3,48,640]{2,1,0:T(8,128)S(1)} %shrink.5.shrunk_here_ref), channel_id=1, source_target_pairs={{0,1},{1,0},{2,3},{3,2},{4,5},{5,4},{6,7},{7,6},{8,9},{9,8},{10,11... | collective-permute-start | bytes 1105928 | tf_op jit(solution)/shard_map/ppermute | solution.py:517

commit v11 on v10

--- a/solution.py
+++ b/solution.py
@@ -508,9 +508,9 @@
     done = [(None, 0)]
     shared = None
 
-    def finish_batch(group, after=()):
+    def finish_batch(group):
         outputs, slot = done[-1]
-        after = list(after) if outputs is None else [outputs[2]]
+        after = [] if len(done) < 3 else [outputs[2]]
         partial = shrink_rows(
             where, slot, hidden_states, away, group, tree_size, columns, cut, after
         )

time: 53.3 us -> 54.1 us (1.015)
  Pallas kernels: 21.4 us -> 26.1 us
  waiting for transfers between devices: 9.41 us -> 5.14 us
    ppermute x1, waiting for transfers between devices: 3.44 us -> 0.01 us  [per_device(): lax.ppermute(rear[1], 'pool', backward)]
    pallas_call x3, Pallas kernels: 2.91 us -> 5.26 us  [shrink_rows(): pl.pallas_call(functools.partial(shrink_kernel, columns=columns, cut=cut)...]
    ppermute x1, starting transfers between devices: 0.22 us -> 1.97 us  [per_device(): lax.ppermute(front[0], 'pool', onward)]
    ppermute x1, starting transfers between devices: 1.8 us -> 0.06 us  [per_device(): lax.ppermute(rear[1], 'pool', backward)]
    ppermute x6, waiting for transfers between devices: 4.01 us -> 2.31 us  [per_device(): rear = tuple((lax.ppermute(piece, 'pool', backward) for piece in rear))]
    pallas_call x3, Pallas kernels: 12.4 us -> 14 us  [finish(): pl.pallas_call(functools.partial(finish_kernel, count=count, slot=slot, k...]
    ppermute x6, waiting for transfers between devices: 0.27 us -> 1.14 us  [per_device(): front = tuple((lax.ppermute(piece, 'pool', onward) for piece in front))]
    pallas_call x1, Pallas kernels: 0.17 us -> 0.86 us  [pack(): pl.pallas_call(functools.partial(pack_kernel, cut=cut, heads_here=heads_h...]
  transfers between devices with their start and end apart: 17 -> 17, of which waited for: 6 -> 3; matrix products, arithmetic and copies ran while one was open for 0% -> 0% of each run, Pallas kernels for 28% -> 37%
where the time goes in v11:
time: 54.1 us; the launch traced here: 53.7 us
  Pallas kernels  26.1 us (48%)
  starting transfers between devices  15.7 us (29%)
  local copies, waits for them, and re-layouts  5.95 us (11%)
  waiting for transfers between devices  5.14 us (10%)
  between operations  0.85 us (2%)
    pallas_call x3, Pallas kernels, finish(): pl.pallas_call(functools.partial(finish_kernel, count=count, slot=slot, k...  14 us
    ppermute x6, starting transfers between devices, per_device(): front = tuple((lax.ppermute(piece, 'pool', onward) for piece in front))  9 us
    unnamed x26, local copies, waits for them, and re-layouts  5.95 us
    pallas_call x3, Pallas kernels, shrink_rows(): pl.pallas_call(functools.partial(shrink_kernel, columns=columns, cut=cut)...  5.26 us
    ppermute x6, starting transfers between devices, per_device(): rear = tuple((lax.ppermute(piece, 'pool', backward) for piece in rear))  4.49 us
    pallas_call x1, Pallas kernels, base_product(): pl.pallas_call(functools.partial(base_kernel, held_count=len(held)), grid...  3.66 us
    ppermute x6, waiting for transfers between devices, per_device(): rear = tuple((lax.ppermute(piece, 'pool', backward) for piece in rear))  2.31 us
    pallas_call x1, Pallas kernels, tree_tables(): pl.pallas_call(functools.partial(tree_kernel, head_size=head_size, kv_hea...  2.27 us
  transfers between devices with their start and end apart: 17, of which 3 were waited for; matrix products, arithmetic and copies ran while one was open for 0% of the time, Pallas kernels for 37%

profile of v11, /device:TPU:0, one launch (start us, length us, event | category | flops | bytes accessed | tf_op | source)
XLA Modules:
  0.0 53.7 jit_solution(3108308275244653451)
XLA Ops:
  0.6 1.0 %copy-done.5 = bf16[1,2560,64]{1,2,0:T(8,128)(2,1)S(1)} copy-done((bf16[1,2560,64]{1,2,0:T(8,128)(2,1)S(1)}, bf16[1,2560,64]{1,2,0:T(8,128)(2,1)}, u32[]{:S(2)}) %copy-start.5) | copy-done | bytes 327704
  1.6 0.9 %copy-done.7 = bf16[1,64,4,256]{3,2,1,0:T(4,128)(2,1)S(1)} copy-done((bf16[1,64,4,256]{3,2,1,0:T(4,128)(2,1)S(1)}, bf16[1,64,4,256]{3,2,1,0:T(4,128)(2,1)}, u32[]{:S(2)}) %copy-start.7) | copy-done | bytes 131096
  2.5 0.9 %pack.1 = (bf16[64,1536]{1,0:T(8,128)(2,1)}, bf16[64,1536]{1,0:T(8,128)(2,1)}) custom-call(s32[1]{0:T(128)} %bitcast.1.core_ref, bf16[64,2560]{1,0:T(8,128)(2,1)S(1)} %bitcast.29, bf16[512,128]{1,0:T(8,128)(2,1)S(1)} %bitcast.30), custom_call_target="tpu_custom_call" | custom-call | tf_op jit(solution)/shard_map/pack/pallas_call | solution.py:85
  3.4 3.0 %collective-permute-start.3 = (bf16[64,1536]{1,0:T(8,128)(2,1)}, bf16[64,1536]{1,0:T(8,128)(2,1)}, u32[]{:S(2)}, u32[]{:S(2)}) collective-permute-start(bf16[64,1536]{1,0:T(8,128)(2,1)} %get-tuple-element.16.refs_3_), channel_id=1, source_target_pairs={{0,4},{4,8},{8,12},{12,14},{14,10},{10,6},{6,2},{2,0},{1,5},{5,9},... | collective-permute-start | bytes 589832 | tf_op jit(solution)/shard_map/ppermute | solution.py:521
  6.4 2.0 %collective-permute-start = (bf16[64,1536]{1,0:T(8,128)(2,1)}, bf16[64,1536]{1,0:T(8,128)(2,1)}, u32[]{:S(2)}, u32[]{:S(2)}) collective-permute-start(bf16[64,1536]{1,0:T(8,128)(2,1)} %get-tuple-element.13.rest_0_.refs_2_), channel_id=1, source_target_pairs={{0,4},{4,8},{8,12},{12,14},{14,10},{10,6},{6,2},{2,0},{1,5},{5,9},... | collective-permute-start | bytes 589832 | tf_op jit(solution)/shard_map/ppermute | solution.py:521
  8.4 1.5 %copy-done = bf16[384,2560]{1,0:T(8,128)(2,1)S(1)} copy-done((bf16[384,2560]{1,0:T(8,128)(2,1)S(1)}, bf16[384,2560]{1,0:T(8,128)(2,1)}, u32[]{:S(2)}) %copy-start) | copy-done | bytes 1966104
  10.0 2.5 %copy-done.11 = bf16[2560,4,256]{2,1,0:T(4,128)(2,1)S(1)} copy-done((bf16[2560,4,256]{2,1,0:T(4,128)(2,1)S(1)}, bf16[2560,4,256]{2,1,0:T(4,128)(2,1)}, u32[]{:S(2)}) %copy-start.11) | copy-done | bytes 5242904
  12.5 3.7 %base.1 = (f32[384,512]{1,0:T(8,128)S(1)}, f32[384,512]{1,0:T(8,128)S(1)}) custom-call(s32[1]{0:T(128)} %bitcast.1.core_ref, bf16[384,2560]{1,0:T(8,128)(2,1)S(1)} %copy-done, bf16[20480,128]{1,0:T(8,128)(2,1)S(1)} %bitcast.34, bf16[64,1536]{1,0:T(8,128)(2,1)} %get-tuple-element.13.rest_0_.refs_2_), custom_call_target="tpu_custom_call" | custom-call | flops 4000000000 | bytes 9000000 | tf_op jit(solution)/shard_map/base/pallas_call | solution.py:154
  16.1 0.0 copy-start.6
  16.2 2.0 %collective-permute-start.10 = (bf16[64,1536]{1,0:T(8,128)(2,1)}, bf16[64,1536]{1,0:T(8,128)(2,1)}, u32[]{:S(2)}, u32[]{:S(2)}) collective-permute-start(bf16[64,1536]{1,0:T(8,128)(2,1)} %hold.6.refs_11_), channel_id=1, source_target_pairs={{4,0},{8,4},{12,8},{14,12},{10,14},{6,10},{2,6},{0,2},{5,1},{9,5},... | collective-permute-start | bytes 589832 | tf_op jit(solution)/shard_map/ppermute | solution.py:522
  18.2 0.1 collective-permute-start.1
  18.4 2.3 %shrink.4.shrunk_here_ref = f32[3,48,640]{2,1,0:T(8,128)S(1)} custom-call(s32[1]{0:T(128)} %bitcast.me_ref, s32[8,8]{1,0:T(8,128)S(1)} %copy-done.6, s32[8]{0:T(128)S(1)} %copy-done.8, bf16[384,2560]{1,0:T(8,128)(2,1)S(1)} %copy-done.1, f32[384,512]{1,0:T(8,128)S(1)} %get-tuple-element.15.token_ref.refs_1_.refs_5_.refs_9_, ...), custom_call_target="tpu_custom_call" | custom-call | flops 90000000 | bytes 600000 | tf_op jit(solution)/shard_map/shrink/pallas_call | solution.py:273
  20.7 0.1 collective-permute-start.15
  20.8 2.0 %collective-permute-start.4 = (bf16[64,1536]{1,0:T(8,128)(2,1)}, bf16[64,1536]{1,0:T(8,128)(2,1)S(1)}, u32[]{:S(2)}, u32[]{:S(2)}) collective-permute-start(bf16[64,1536]{1,0:T(8,128)(2,1)} %hold.5.refs_7_), channel_id=1, source_target_pairs={{0,4},{4,8},{8,12},{12,14},{14,10},{10,6},{6,2},{2,0},{1,5},{5,9},... | collective-permute-start | bytes 589832 | tf_op jit(solution)/shard_map/ppermute | solution.py:521
  22.8 0.1 collective-permute-start.7
  22.9 2.3 %tree.1.token_ref.table_ref = f32[384,384]{1,0:T(8,128)S(1)} custom-call(s32[8]{0:T(128)S(1)} %copy-done.9, s32[8,48]{1,0:T(8,128)S(1)} %copy-done.12, f32[384,512]{1,0:T(8,128)S(1)} %get-tuple-element.14.rest_0_.here_ref), custom_call_target="tpu_custom_call" | custom-call | flops 1000000000 | bytes 8000000 | tf_op jit(solution)/shard_map/tree/pallas_call | solution.py:225
  25.2 1.9 %collective-permute-start.11 = (bf16[64,1536]{1,0:T(8,128)(2,1)}, bf16[64,1536]{1,0:T(8,128)(2,1)S(1)}, u32[]{:S(2)}, u32[]{:S(2)}) collective-permute-start(bf16[64,1536]{1,0:T(8,128)(2,1)} %hold.7.refs_7_), channel_id=1, source_target_pairs={{4,0},{8,4},{12,8},{14,12},{10,14},{6,10},{2,6},{0,2},{5,1},{9,5},... | collective-permute-start | bytes 589832 | tf_op jit(solution)/shard_map/ppermute | solution.py:522
  27.2 0.2 collective-permute-start.2
  27.4 1.1 %collective-permute-done.4.refs_3_ = bf16[64,1536]{1,0:T(8,128)(2,1)S(1)} collective-permute-done((bf16[64,1536]{1,0:T(8,128)(2,1)}, bf16[64,1536]{1,0:T(8,128)(2,1)S(1)}, u32[]{:S(2)}, u32[]{:S(2)}) %collective-permute-start.4) | collective-permute-done | bytes 196640 | tf_op jit(solution)/shard_map/ppermute | solution.py:521
  28.5 2.3 %collective-permute-done.7.refs_6_.rest_1_ = bf16[64,1536]{1,0:T(8,128)(2,1)S(1)} collective-permute-done((bf16[64,1536]{1,0:T(8,128)(2,1)}, bf16[64,1536]{1,0:T(8,128)(2,1)S(1)}, u32[]{:S(2)}, u32[]{:S(2)}) %collective-permute-start.7) | collective-permute-done | bytes 196640 | tf_op jit(solution)/shard_map/ppermute | solution.py:522
  30.8 1.9 %shrink.3.shrunk_here_ref = f32[2,48,640]{2,1,0:T(8,128)S(1)} custom-call(s32[1]{0:T(128)} %bitcast.me_ref, s32[8,8]{1,0:T(8,128)S(1)} %copy-done.6, s32[8]{0:T(128)S(1)} %copy-done.8, bf16[384,2560]{1,0:T(8,128)(2,1)S(1)} %copy-done.1, f32[384,512]{1,0:T(8,128)S(1)} %get-tuple-element.15.token_ref.refs_1_.refs_5_.refs_9_, ...), custom_call_target="tpu_custom_call" | custom-call | flops 60000000 | bytes 400000 | tf_op jit(solution)/shard_map/shrink/pallas_call | solution.py:273
  32.7 0.1 collective-permute-start.14
  32.8 1.6 %collective-permute-start.5 = (bf16[64,1536]{1,0:T(8,128)(2,1)S(1)}, bf16[64,1536]{1,0:T(8,128)(2,1)S(1)}, u32[]{:S(2)}, u32[]{:S(2)}) collective-permute-start(bf16[64,1536]{1,0:T(8,128)(2,1)S(1)} %collective-permute-done.4.refs_3_), channel_id=1, source_target_pairs={{0,4},{4,8},{8,12},{12,14},{14,10},{10,6},{6,2},{2,0},{1,5},{5,9},... | collective-permute-start | bytes 589832 | tf_op jit(solution)/shard_map/ppermute | solution.py:521
  34.4 0.4 collective-permute-start.8
  34.9 0.1 collective-permute-start.13
  34.9 2.0 %collective-permute-start.12 = (bf16[64,1536]{1,0:T(8,128)(2,1)S(1)}, bf16[64,1536]{1,0:T(8,128)(2,1)S(1)}, u32[]{:S(2)}, u32[]{:S(2)}) collective-permute-start(bf16[64,1536]{1,0:T(8,128)(2,1)S(1)} %collective-permute-done.2.refs_2_.rest_0_), channel_id=1, source_target_pairs={{0,4},{4,8},{8,12},{12,14},{14,10},{10,6},{6,2},{2,0},{1,5},{5,9},... | collective-permute-start | bytes 589832 | tf_op jit(solution)/shard_map/ppermute | solution.py:545
  36.9 5.3 %finish.3 = (bf16[384,16,128]{2,1,0:T(8,128)(2,1)}, bf16[1536,128]{1,0:T(8,128)(2,1)}, f32[8,128]{1,0:T(8,128)}) custom-call(s32[1]{0:T(128)} %bitcast.me_ref, s32[8,8]{1,0:T(8,128)S(1)} %copy-done.6, s32[8]{0:T(128)S(1)} %copy-done.8, s32[8]{0:T(128)S(1)} %copy-done.9, f32[384,512]{1,0:T(8,128)S(1)} %get-tuple-element.14.rest_0_.here_ref, ...), custom_call_target="tpu_custom_call" | custom-call | flops 270000000 | bytes 900000 | tf_op jit(solution)/shard_map/finish/pallas_call | solution.py:424
  42.3 4.2 %finish.4 = (bf16[384,16,128]{2,1,0:T(8,128)(2,1)}, bf16[1536,128]{1,0:T(8,128)(2,1)}, f32[8,128]{1,0:T(8,128)S(1)}) custom-call(s32[1]{0:T(128)} %bitcast.me_ref, s32[8,8]{1,0:T(8,128)S(1)} %copy-done.6, s32[8]{0:T(128)S(1)} %copy-done.8, s32[8]{0:T(128)S(1)} %copy-done.9, ...), custom_call_target="tpu_custom_call", output_to_operand_aliasing={{0}: (14, {}), {1}: (15, {})} | custom-call | flops 180000000 | bytes 600000 | tf_op jit(solution)/shard_map/finish/pallas_call | solution.py:424
  46.5 1.0 %shrink.5.shrunk_here_ref = f32[3,48,640]{2,1,0:T(8,128)S(1)} custom-call(s32[1]{0:T(128)} %bitcast.me_ref, s32[8,8]{1,0:T(8,128)S(1)} %copy-done.6, s32[8]{0:T(128)S(1)} %copy-done.8, bf16[384,2560]{1,0:T(8,128)(2,1)S(1)} %copy-done.1, f32[384,512]{1,0:T(8,128)S(1)} %get-tuple-element.15.token_ref.refs_1_.refs_5_.refs_9_, ...), custom_call_target="tpu_custom_call" | custom-call | flops 90000000 | bytes 600000 | tf_op jit(solution)/shard_map/shrink/pallas_call | solution.py:273
  47.5 0.0 collective-permute-start.16
  47.5 1.7 %collective-permute-done.16.shrunk_there_ref = f32[3,48,640]{2,1,0:T(8,128)S(1)} collective-permute-done((f32[3,48,640]{2,1,0:T(8,128)S(1)}, f32[3,48,640]{2,1,0:T(8,128)S(1)}, u32[]{:S(2)}, u32[]{:S(2)}) %collective-permute-start.16) | collective-permute-done | bytes 368672 | tf_op jit(solution)/shard_map/ppermute | solution.py:517
  49.2 4.5 %finish.5 = (bf16[384,16,128]{2,1,0:T(8,128)(2,1)}, bf16[1536,128]{1,0:T(8,128)(2,1)}, f32[8,128]{1,0:T(8,128)}) custom-call(s32[1]{0:T(128)} %bitcast.me_ref, s32[8,8]{1,0:T(8,128)S(1)} %copy-done.6, s32[8]{0:T(128)S(1)} %copy-done.8, s32[8]{0:T(128)S(1)} %copy-done.9, ...), custom_call_target="tpu_custom_call", output_to_operand_aliasing={{0}: (15, {}), {1}: (16, {})} | custom-call | flops 270000000 | bytes 900000 | tf_op jit(solution)/shard_map/finish/pallas_call | solution.py:424
  (41 shorter events, 0.1 us)
Async XLA Ops:
  0.6 1.0 %copy-start.5 = (bf16[1,2560,64]{1,2,0:T(8,128)(2,1)S(1)}, bf16[1,2560,64]{1,2,0:T(8,128)(2,1)}, u32[]{:S(2)}) copy-start(bf16[1,2560,64]{1,2,0:T(8,128)(2,1)} %param.14) | copy-start | bytes 983044
  1.6 0.9 %copy-start.7 = (bf16[1,64,4,256]{3,2,1,0:T(4,128)(2,1)S(1)}, bf16[1,64,4,256]{3,2,1,0:T(4,128)(2,1)}, u32[]{:S(2)}) copy-start(bf16[1,64,4,256]{3,2,1,0:T(4,128)(2,1)} %param.15) | copy-start | bytes 393220
  3.4 15.0 %collective-permute-start.3 = (bf16[64,1536]{1,0:T(8,128)(2,1)}, bf16[64,1536]{1,0:T(8,128)(2,1)}, u32[]{:S(2)}, u32[]{:S(2)}) collective-permute-start(bf16[64,1536]{1,0:T(8,128)(2,1)} %get-tuple-element.16.refs_3_), channel_id=1, source_target_pairs={{0,4},{4,8},{8,12},{12,14},{14,10},{10,6},{6,2},{2,0},{1,5},{5,9},... | collective-permute-start | bytes 589832 | tf_op jit(solution)/shard_map/ppermute | solution.py:521
  6.4 9.8 %collective-permute-start.9 = (bf16[64,1536]{1,0:T(8,128)(2,1)}, bf16[64,1536]{1,0:T(8,128)(2,1)}, u32[]{:S(2)}, u32[]{:S(2)}) collective-permute-start(bf16[64,1536]{1,0:T(8,128)(2,1)} %get-tuple-element.16.refs_3_), channel_id=1, source_target_pairs={{4,0},{8,4},{12,8},{14,12},{10,14},{6,10},{2,6},{0,2},{5,1},{9,5},... | collective-permute-start | bytes 589832 | tf_op jit(solution)/shard_map/ppermute | solution.py:522
  6.4 11.8 %collective-permute-start = (bf16[64,1536]{1,0:T(8,128)(2,1)}, bf16[64,1536]{1,0:T(8,128)(2,1)}, u32[]{:S(2)}, u32[]{:S(2)}) collective-permute-start(bf16[64,1536]{1,0:T(8,128)(2,1)} %get-tuple-element.13.rest_0_.refs_2_), channel_id=1, source_target_pairs={{0,4},{4,8},{8,12},{12,14},{14,10},{10,6},{6,2},{2,0},{1,5},{5,9},... | collective-permute-start | bytes 589832 | tf_op jit(solution)/shard_map/ppermute | solution.py:521
  8.4 9.9 %collective-permute-start.6 = (bf16[64,1536]{1,0:T(8,128)(2,1)}, bf16[64,1536]{1,0:T(8,128)(2,1)}, u32[]{:S(2)}, u32[]{:S(2)}) collective-permute-start(bf16[64,1536]{1,0:T(8,128)(2,1)} %get-tuple-element.13.rest_0_.refs_2_), channel_id=1, source_target_pairs={{4,0},{8,4},{12,8},{14,12},{10,14},{6,10},{2,6},{0,2},{5,1},{9,5},... | collective-permute-start | bytes 589832 | tf_op jit(solution)/shard_map/ppermute | solution.py:522
  8.4 1.5 %copy-start = (bf16[384,2560]{1,0:T(8,128)(2,1)S(1)}, bf16[384,2560]{1,0:T(8,128)(2,1)}, u32[]{:S(2)}) copy-start(bf16[384,2560]{1,0:T(8,128)(2,1)} %refs_8_.3) | copy-start | bytes 5898244
  10.0 2.5 %copy-start.11 = (bf16[2560,4,256]{2,1,0:T(4,128)(2,1)S(1)}, bf16[2560,4,256]{2,1,0:T(4,128)(2,1)}, u32[]{:S(2)}) copy-start(bf16[2560,4,256]{2,1,0:T(4,128)(2,1)} %param.13) | copy-start | bytes 15728644
  16.1 2.2 %copy-start.1 = (bf16[384,2560]{1,0:T(8,128)(2,1)S(1)}, bf16[384,2560]{1,0:T(8,128)(2,1)}, u32[]{:S(2)}) copy-start(bf16[384,2560]{1,0:T(8,128)(2,1)} %refs_8_.3) | copy-start | bytes 5898244
  16.1 2.2 %copy-start.6 = (s32[8,8]{1,0:T(8,128)S(1)}, s32[8,8]{1,0:T(8,128)}, u32[]{:S(2)}) copy-start(s32[8,8]{1,0:T(8,128)} %constant.10.clone.owner_ref) | copy-start | bytes 772
  16.1 2.2 %copy-start.8 = (s32[8]{0:T(128)S(1)}, s32[8]{0:T(128)}, u32[]{:S(2)}) copy-start(s32[8]{0:T(128)} %adapter_ref.11) | copy-start | bytes 100
  16.2 9.0 %collective-permute-start.10 = (bf16[64,1536]{1,0:T(8,128)(2,1)}, bf16[64,1536]{1,0:T(8,128)(2,1)}, u32[]{:S(2)}, u32[]{:S(2)}) collective-permute-start(bf16[64,1536]{1,0:T(8,128)(2,1)} %hold.6.refs_11_), channel_id=1, source_target_pairs={{4,0},{8,4},{12,8},{14,12},{10,14},{6,10},{2,6},{0,2},{5,1},{9,5},... | collective-permute-start | bytes 589832 | tf_op jit(solution)/shard_map/ppermute | solution.py:522
  18.2 8.9 %collective-permute-start.1 = (bf16[64,1536]{1,0:T(8,128)(2,1)}, bf16[64,1536]{1,0:T(8,128)(2,1)}, u32[]{:S(2)}, u32[]{:S(2)}) collective-permute-start(bf16[64,1536]{1,0:T(8,128)(2,1)} %collective-permute-done.refs_6_.rest_1_), channel_id=1, source_target_pairs={{0,4},{4,8},{8,12},{12,14},{14,10},{10,6},{6,2},{2,0},{1,5},{5,9},... | collective-permute-start | bytes 589832 | tf_op jit(solution)/shard_map/ppermute | solution.py:521
  18.4 4.5 %copy-start.9 = (s32[8]{0:T(128)S(1)}, s32[8]{0:T(128)}, u32[]{:S(2)}) copy-start(s32[8]{0:T(128)} %length_ref.7) | copy-start | bytes 100
  18.4 4.5 %copy-start.12 = (s32[8,48]{1,0:T(8,128)S(1)}, s32[8,48]{1,0:T(8,128)}, u32[]{:S(2)}) copy-start(s32[8,48]{1,0:T(8,128)} %parent_ref.1) | copy-start | bytes 4612
  20.7 13.7 %collective-permute-start.15 = (f32[3,48,640]{2,1,0:T(8,128)S(1)}, f32[3,48,640]{2,1,0:T(8,128)S(1)}, u32[]{:S(2)}, u32[]{:S(2)}) collective-permute-start(f32[3,48,640]{2,1,0:T(8,128)S(1)} %shrink.4.shrunk_here_ref), channel_id=1, source_target_pairs={{0,1},{1,0},{2,3},{3,2},{4,5},{5,4},{6,7},{7,6},{8,9},{9,8},{10,11... | collective-permute-start | bytes 1105928 | tf_op jit(solution)/shard_map/ppermute | solution.py:517
  20.8 7.7 %collective-permute-start.4 = (bf16[64,1536]{1,0:T(8,128)(2,1)}, bf16[64,1536]{1,0:T(8,128)(2,1)S(1)}, u32[]{:S(2)}, u32[]{:S(2)}) collective-permute-start(bf16[64,1536]{1,0:T(8,128)(2,1)} %hold.5.refs_7_), channel_id=1, source_target_pairs={{0,4},{4,8},{8,12},{12,14},{14,10},{10,6},{6,2},{2,0},{1,5},{5,9},... | collective-permute-start | bytes 589832 | tf_op jit(solution)/shard_map/ppermute | solution.py:521
  22.8 8.0 %collective-permute-start.7 = (bf16[64,1536]{1,0:T(8,128)(2,1)}, bf16[64,1536]{1,0:T(8,128)(2,1)S(1)}, u32[]{:S(2)}, u32[]{:S(2)}) collective-permute-start(bf16[64,1536]{1,0:T(8,128)(2,1)} %collective-permute-done.6.refs_10_.rest_2_), channel_id=1, source_target_pairs={{4,0},{8,4},{12,8},{14,12},{10,14},{6,10},{2,6},{0,2},{5,1},{9,5},... | collective-permute-start | bytes 589832 | tf_op jit(solution)/shard_map/ppermute | solution.py:522
  25.2 9.7 %collective-permute-start.11 = (bf16[64,1536]{1,0:T(8,128)(2,1)}, bf16[64,1536]{1,0:T(8,128)(2,1)S(1)}, u32[]{:S(2)}, u32[]{:S(2)}) collective-permute-start(bf16[64,1536]{1,0:T(8,128)(2,1)} %hold.7.refs_7_), channel_id=1, source_target_pairs={{4,0},{8,4},{12,8},{14,12},{10,14},{6,10},{2,6},{0,2},{5,1},{9,5},... | collective-permute-start | bytes 589832 | tf_op jit(solution)/shard_map/ppermute | solution.py:522
  27.1 9.8 %copy-start.2 = (bf16[384,16,128]{2,1,0:T(8,128)(2,1)S(1)}, bf16[384,16,128]{2,1,0:T(8,128)(2,1)}, u32[]{:S(2)}) copy-start(bf16[384,16,128]{2,1,0:T(8,128)(2,1)} %query_ref.5) | copy-start | bytes 4718596
  27.1 9.8 %copy-start.3 = (bf16[8,128,2,128]{3,2,1,0:T(2,128)(2,1)S(1)}, bf16[8,128,2,128]{3,2,1,0:T(2,128)(2,1)}, u32[]{:S(2)}) copy-start(bf16[8,128,2,128]{3,2,1,0:T(2,128)(2,1)} %param.20) | copy-start | bytes 1572868
  27.2 9.8 %copy-start.4 = (bf16[8,128,2,128]{3,2,1,0:T(2,128)(2,1)S(1)}, bf16[8,128,2,128]{3,2,1,0:T(2,128)(2,1)}, u32[]{:S(2)}) copy-start(bf16[8,128,2,128]{3,2,1,0:T(2,128)(2,1)} %param.21) | copy-start | bytes 1572868
  27.2 9.8 %copy-start.10 = (f32[128]{0:T(128)S(1)}, f32[128]{0:T(128)}, u32[]{:S(2)}) copy-start(f32[128]{0:T(128)} %param.22) | copy-start | bytes 1540
  27.2 7.8 %collective-permute-start.2 = (bf16[64,1536]{1,0:T(8,128)(2,1)}, bf16[64,1536]{1,0:T(8,128)(2,1)S(1)}, u32[]{:S(2)}, u32[]{:S(2)}) collective-permute-start(bf16[64,1536]{1,0:T(8,128)(2,1)} %hold.4.refs_2_.rest_0_), channel_id=1, source_target_pairs={{0,4},{4,8},{8,12},{12,14},{14,10},{10,6},{6,2},{2,0},{1,5},{5,9},... | collective-permute-start | bytes 589832 | tf_op jit(solution)/shard_map/ppermute | solution.py:521
  32.7 9.5 %collective-permute-start.14 = (f32[2,48,640]{2,1,0:T(8,128)S(1)}, f32[2,48,640]{2,1,0:T(8,128)S(1)}, u32[]{:S(2)}, u32[]{:S(2)}) collective-permute-start(f32[2,48,640]{2,1,0:T(8,128)S(1)} %shrink.3.shrunk_here_ref), channel_id=1, source_target_pairs={{0,1},{1,0},{2,3},{3,2},{4,5},{5,4},{6,7},{7,6},{8,9},{9,8},{10,11... | collective-permute-start | bytes 737288 | tf_op jit(solution)/shard_map/ppermute | solution.py:517
  32.8 13.7 %collective-permute-start.5 = (bf16[64,1536]{1,0:T(8,128)(2,1)S(1)}, bf16[64,1536]{1,0:T(8,128)(2,1)S(1)}, u32[]{:S(2)}, u32[]{:S(2)}) collective-permute-start(bf16[64,1536]{1,0:T(8,128)(2,1)S(1)} %collective-permute-done.4.refs_3_), channel_id=1, source_target_pairs={{0,4},{4,8},{8,12},{12,14},{14,10},{10,6},{6,2},{2,0},{1,5},{5,9},... | collective-permute-start | bytes 589832 | tf_op jit(solution)/shard_map/ppermute | solution.py:521
  34.4 12.0 %collective-permute-start.8 = (bf16[64,1536]{1,0:T(8,128)(2,1)S(1)}, bf16[64,1536]{1,0:T(8,128)(2,1)S(1)}, u32[]{:S(2)}, u32[]{:S(2)}) collective-permute-start(bf16[64,1536]{1,0:T(8,128)(2,1)S(1)} %collective-permute-done.7.refs_6_.rest_1_), channel_id=1, source_target_pairs={{4,0},{8,4},{12,8},{14,12},{10,14},{6,10},{2,6},{0,2},{5,1},{9,5},... | collective-permute-start | bytes 589832 | tf_op jit(solution)/shard_map/ppermute | solution.py:522
  34.9 11.6 %collective-permute-start.13 = (bf16[64,1536]{1,0:T(8,128)(2,1)S(1)}, bf16[64,1536]{1,0:T(8,128)(2,1)S(1)}, u32[]{:S(2)}, u32[]{:S(2)}) collective-permute-start(bf16[64,1536]{1,0:T(8,128)(2,1)S(1)} %collective-permute-done.11.refs_7_), channel_id=1, source_target_pairs={{4,0},{8,4},{12,8},{14,12},{10,14},{6,10},{2,6},{0,2},{5,1},{9,5},... | collective-permute-start | bytes 589832 | tf_op jit(solution)/shard_map/ppermute | solution.py:545
  34.9 11.5 %collective-permute-start.12 = (bf16[64,1536]{1,0:T(8,128)(2,1)S(1)}, bf16[64,1536]{1,0:T(8,128)(2,1)S(1)}, u32[]{:S(2)}, u32[]{:S(2)}) collective-permute-start(bf16[64,1536]{1,0:T(8,128)(2,1)S(1)} %collective-permute-done.2.refs_2_.rest_0_), channel_id=1, source_target_pairs={{0,4},{4,8},{8,12},{12,14},{14,10},{10,6},{6,2},{2,0},{1,5},{5,9},... | collective-permute-start | bytes 589832 | tf_op jit(solution)/shard_map/ppermute | solution.py:545
  47.5 1.7 %collective-permute-start.16 = (f32[3,48,640]{2,1,0:T(8,128)S(1)}, f32[3,48,640]{2,1,0:T(8,128)S(1)}, u32[]{:S(2)}, u32[]{:S(2)}) collective-permute-start(f32[3,48,640]{2,1,0:T(8,128)S(1)} %shrink.5.shrunk_here_ref), channel_id=1, source_target_pairs={{0,1},{1,0},{2,3},{3,2},{4,5},{5,4},{6,7},{7,6},{8,9},{9,8},{10,11... | collective-permute-start | bytes 1105928 | tf_op jit(solution)/shard_map/ppermute | solution.py:517

commit v12 on v11

--- a/solution.py
+++ b/solution.py
@@ -508,12 +508,13 @@
     done = [(None, 0)]
     shared = None
 
-    def finish_batch(group):
+    def finish_batch(group, partial=None):
         outputs, slot = done[-1]
         after = [] if len(done) < 3 else [outputs[2]]
-        partial = shrink_rows(
-            where, slot, hidden_states, away, group, tree_size, columns, cut, after
-        )
+        if partial is None:
+            partial = shrink_rows(
+                where, slot, hidden_states, away, group, tree_size, columns, cut, after
+            )
         batch = (partial, lax.ppermute(partial, "tp", swap), [piece[0] for piece in group])
         done.append((finish(where, slot, batch, shared, outputs), slot + len(group)))
 
@@ -523,7 +524,20 @@
         held = [front[1], rear[1]]
         first_front = front[0]
         if step == 1:
-            held = [hold(piece, away) for piece in held]
+            token = away
+            if split_batches:
+                token = near_partial = shrink_rows(
+                    where,
+                    0,
+                    hidden_states,
+                    away,
+                    arrivals + [front, rear],
+                    tree_size,
+                    columns,
+                    cut,
+                    [],
+                )
+            held = [hold(piece, token) for piece in held]
             table = tree_tables(
                 cache_lengths, tree_parents, head_size, heads_here, [here]
             )
@@ -537,7 +551,7 @@
                 value_rows,
             )
         if step == 2 and split_batches:
-            finish_batch(arrivals[:near])
+            finish_batch(arrivals[:near], near_partial)
             first_front, held[1] = hold(first_front, table), hold(held[1], table)
         front, rear = (first_front, held[0]), (rear[0], held[1])
         arrivals += [front, rear]

time: 54.1 us -> 50 us (0.924)
  Pallas kernels: 26.1 us -> 21.4 us
  waiting for transfers between devices: 5.14 us -> 6.98 us
  starting transfers between devices: 15.7 us -> 14.7 us
    ppermute x6, waiting for transfers between devices: 1.14 us -> 4.46 us  [per_device(): front = tuple((lax.ppermute(piece, 'pool', onward) for piece in front))]
    pallas_call x3, Pallas kernels: 5.26 us -> 2.9 us  [shrink_rows(): pl.pallas_call(functools.partial(shrink_kernel, columns=columns, cut=cut)...]
    pallas_call x3, Pallas kernels: 14 us -> 12.4 us  [finish(): pl.pallas_call(functools.partial(finish_kernel, count=count, slot=slot, k...]
    ppermute x1, starting transfers between devices: 1.97 us -> 0.47 us  [per_device(): lax.ppermute(front[0], 'pool', onward)]
    ppermute x1, starting transfers between devices: 0.06 us -> 1.56 us  [per_device(): lax.ppermute(rear[1], 'pool', backward)]
    ppermute x6, waiting for transfers between devices: 2.31 us -> 0.82 us  [per_device(): rear = tuple((lax.ppermute(piece, 'pool', backward) for piece in rear))]
    pallas_call x1, Pallas kernels: 0.86 us -> 0.17 us  [pack(): pl.pallas_call(functools.partial(pack_kernel, cut=cut, heads_here=heads_h...]
    ppermute x6, starting transfers between devices: 9 us -> 8.39 us  [per_device(): front = tuple((lax.ppermute(piece, 'pool', onward) for piece in front))]
  transfers between devices with their start and end apart: 17 -> 17, of which waited for: 3 -> 4; matrix products, arithmetic and copies ran while one was open for 0% -> 0% of each run, Pallas kernels for 37% -> 30%
where the time goes in v12:
time: 50 us; the launch traced here: 49.8 us
  Pallas kernels  21.4 us (43%)
  starting transfers between devices  14.7 us (29%)
  waiting for transfers between devices  6.98 us (14%)
  local copies, waits for them, and re-layouts  5.93 us (12%)
  between operations  0.8 us (2%)
    pallas_call x3, Pallas kernels, finish(): pl.pallas_call(functools.partial(finish_kernel, count=count, slot=slot, k...  12.4 us
    ppermute x6, starting transfers between devices, per_device(): front = tuple((lax.ppermute(piece, 'pool', onward) for piece in front))  8.39 us
    unnamed x24, local copies, waits for them, and re-layouts  5.93 us
    ppermute x6, waiting for transfers between devices, per_device(): front = tuple((lax.ppermute(piece, 'pool', onward) for piece in front))  4.46 us
    ppermute x6, starting transfers between devices, per_device(): rear = tuple((lax.ppermute(piece, 'pool', backward) for piece in rear))  4.2 us
    pallas_call x1, Pallas kernels, base_product(): pl.pallas_call(functools.partial(base_kernel, held_count=len(held)), grid...  3.65 us
    pallas_call x3, Pallas kernels, shrink_rows(): pl.pallas_call(functools.partial(shrink_kernel, columns=columns, cut=cut)...  2.9 us
    pallas_call x1, Pallas kernels, tree_tables(): pl.pallas_call(functools.partial(tree_kernel, head_size=head_size, kv_hea...  2.27 us
  transfers between devices with their start and end apart: 17, of which 4 were waited for; matrix products, arithmetic and copies ran while one was open for 0% of the time, Pallas kernels for 30%

profile of v12, /device:TPU:0, one launch (start us, length us, event | category | flops | bytes accessed | tf_op | source)
XLA Modules:
  0.0 49.8 jit_solution(7824347840920195598)
XLA Ops:
  0.6 1.0 %copy-done.4 = bf16[1,2560,64]{1,2,0:T(8,128)(2,1)S(1)} copy-done((bf16[1,2560,64]{1,2,0:T(8,128)(2,1)S(1)}, bf16[1,2560,64]{1,2,0:T(8,128)(2,1)}, u32[]{:S(2)}) %copy-start.4) | copy-done | bytes 327704
  1.6 0.9 %copy-done.6 = bf16[1,64,4,256]{3,2,1,0:T(4,128)(2,1)S(1)} copy-done((bf16[1,64,4,256]{3,2,1,0:T(4,128)(2,1)S(1)}, bf16[1,64,4,256]{3,2,1,0:T(4,128)(2,1)}, u32[]{:S(2)}) %copy-start.6) | copy-done | bytes 131096
  2.5 0.2 pack.1
  2.7 3.1 %collective-permute-start = (bf16[64,1536]{1,0:T(8,128)(2,1)S(1)}, bf16[64,1536]{1,0:T(8,128)(2,1)S(1)}, u32[]{:S(2)}, u32[]{:S(2)}) collective-permute-start(bf16[64,1536]{1,0:T(8,128)(2,1)S(1)} %get-tuple-element.13.rest_0_.refs_2_), channel_id=1, source_target_pairs={{0,4},{4,8},{8,12},{12,14},{14,10},{10,6},{6,2},{2,0},{1,5},{5,9},... | collective-permute-start | bytes 589832 | tf_op jit(solution)/shard_map/ppermute | solution.py:522
  5.8 0.0 collective-permute-start.4
  5.8 2.0 %collective-permute-start.3 = (bf16[64,1536]{1,0:T(8,128)(2,1)S(1)}, bf16[64,1536]{1,0:T(8,128)(2,1)S(1)}, u32[]{:S(2)}, u32[]{:S(2)}) collective-permute-start(bf16[64,1536]{1,0:T(8,128)(2,1)S(1)} %get-tuple-element.16.refs_3_), channel_id=1, source_target_pairs={{0,4},{4,8},{8,12},{12,14},{14,10},{10,6},{6,2},{2,0},{1,5},{5,9},... | collective-permute-start | bytes 589832 | tf_op jit(solution)/shard_map/ppermute | solution.py:522
  7.8 1.5 %copy-done = bf16[384,2560]{1,0:T(8,128)(2,1)S(1)} copy-done((bf16[384,2560]{1,0:T(8,128)(2,1)S(1)}, bf16[384,2560]{1,0:T(8,128)(2,1)}, u32[]{:S(2)}) %copy-start) | copy-done | bytes 1966104
  9.4 2.5 %copy-done.10 = bf16[2560,4,256]{2,1,0:T(4,128)(2,1)S(1)} copy-done((bf16[2560,4,256]{2,1,0:T(4,128)(2,1)S(1)}, bf16[2560,4,256]{2,1,0:T(4,128)(2,1)}, u32[]{:S(2)}) %copy-start.10) | copy-done | bytes 5242904
  11.8 3.7 %base.1 = (f32[384,512]{1,0:T(8,128)S(1)}, f32[384,512]{1,0:T(8,128)S(1)}) custom-call(s32[1]{0:T(128)} %bitcast.1.core_ref, bf16[384,2560]{1,0:T(8,128)(2,1)S(1)} %copy-done, bf16[20480,128]{1,0:T(8,128)(2,1)S(1)} %bitcast.34, bf16[64,1536]{1,0:T(8,128)(2,1)S(1)} %get-tuple-element.13.rest_0_.refs_2_), custom_call_target="tpu_custom_call" | custom-call | flops 4000000000 | bytes 9000000 | tf_op jit(solution)/shard_map/base/pallas_call | solution.py:154
  15.5 0.8 %collective-permute-done.5.refs_11_.array_ref = bf16[64,1536]{1,0:T(8,128)(2,1)S(1)} collective-permute-done((bf16[64,1536]{1,0:T(8,128)(2,1)S(1)}, bf16[64,1536]{1,0:T(8,128)(2,1)S(1)}, u32[]{:S(2)}, u32[]{:S(2)}) %collective-permute-start.5) | collective-permute-done | bytes 196640 | tf_op jit(solution)/shard_map/ppermute | solution.py:523
  16.4 1.0 %shrink.3.token_ref.shrunk_here_ref = f32[3,48,640]{2,1,0:T(8,128)S(1)} custom-call(s32[1]{0:T(128)} %bitcast.me_ref, s32[8,8]{1,0:T(8,128)S(1)} %copy-done.5, s32[8]{0:T(128)S(1)} %copy-done.7, bf16[384,2560]{1,0:T(8,128)(2,1)S(1)} %copy-done, f32[384,512]{1,0:T(8,128)S(1)} %get-tuple-element.15.refs_1_.refs_5_.refs_9_, ...), custom_call_target="tpu_custom_call" | custom-call | flops 90000000 | bytes 600000 | tf_op jit(solution)/shard_map/shrink/pallas_call | solution.py:273
  17.4 1.2 %collective-permute-start.10 = (bf16[64,1536]{1,0:T(8,128)(2,1)S(1)}, bf16[64,1536]{1,0:T(8,128)(2,1)S(1)}, u32[]{:S(2)}, u32[]{:S(2)}) collective-permute-start(bf16[64,1536]{1,0:T(8,128)(2,1)S(1)} %hold.6), channel_id=1, source_target_pairs={{4,0},{8,4},{12,8},{14,12},{10,14},{6,10},{2,6},{0,2},{5,1},{9,5},... | collective-permute-start | bytes 589832 | tf_op jit(solution)/shard_map/ppermute | solution.py:523
  18.6 0.8 %collective-permute-start.1 = (bf16[64,1536]{1,0:T(8,128)(2,1)S(1)}, bf16[64,1536]{1,0:T(8,128)(2,1)S(1)}, u32[]{:S(2)}, u32[]{:S(2)}) collective-permute-start(bf16[64,1536]{1,0:T(8,128)(2,1)S(1)} %collective-permute-done.refs_6_.rest_1_), channel_id=1, source_target_pairs={{0,4},{4,8},{8,12},{12,14},{14,10},{10,6},{6,2},{2,0},{1,5},{5,9},... | collective-permute-start | bytes 589832 | tf_op jit(solution)/shard_map/ppermute | solution.py:522
  19.4 1.6 %collective-permute-start.6 = (bf16[64,1536]{1,0:T(8,128)(2,1)S(1)}, bf16[64,1536]{1,0:T(8,128)(2,1)S(1)}, u32[]{:S(2)}, u32[]{:S(2)}) collective-permute-start(bf16[64,1536]{1,0:T(8,128)(2,1)S(1)} %hold.5), channel_id=1, source_target_pairs={{0,4},{4,8},{8,12},{12,14},{14,10},{10,6},{6,2},{2,0},{1,5},{5,9},... | collective-permute-start | bytes 589832 | tf_op jit(solution)/shard_map/ppermute | solution.py:522
  21.0 0.4 collective-permute-start.8
  21.5 2.3 %tree.1.token_ref.table_ref = f32[384,384]{1,0:T(8,128)S(1)} custom-call(s32[8]{0:T(128)S(1)} %copy-done.8, s32[8,48]{1,0:T(8,128)S(1)} %copy-done.11, f32[384,512]{1,0:T(8,128)S(1)} %get-tuple-element.14.rest_0_.here_ref), custom_call_target="tpu_custom_call" | custom-call | flops 1000000000 | bytes 8000000 | tf_op jit(solution)/shard_map/tree/pallas_call | solution.py:225
  23.8 1.2 %collective-permute-start.11 = (bf16[64,1536]{1,0:T(8,128)(2,1)S(1)}, bf16[64,1536]{1,0:T(8,128)(2,1)S(1)}, u32[]{:S(2)}, u32[]{:S(2)}) collective-permute-start(bf16[64,1536]{1,0:T(8,128)(2,1)S(1)} %hold.7.refs_7_), channel_id=1, source_target_pairs={{4,0},{8,4},{12,8},{14,12},{10,14},{6,10},{2,6},{0,2},{5,1},{9,5},... | collective-permute-start | bytes 589832 | tf_op jit(solution)/shard_map/ppermute | solution.py:523
  25.0 1.1 %collective-permute-done.1.array_ref = bf16[64,1536]{1,0:T(8,128)(2,1)S(1)} collective-permute-done((bf16[64,1536]{1,0:T(8,128)(2,1)S(1)}, bf16[64,1536]{1,0:T(8,128)(2,1)S(1)}, u32[]{:S(2)}, u32[]{:S(2)}) %collective-permute-start.1) | collective-permute-done | bytes 196640 | tf_op jit(solution)/shard_map/ppermute | solution.py:522
  26.1 0.1 collective-permute-start.2
  26.2 3.4 %collective-permute-done.6.refs_3_ = bf16[64,1536]{1,0:T(8,128)(2,1)S(1)} collective-permute-done((bf16[64,1536]{1,0:T(8,128)(2,1)S(1)}, bf16[64,1536]{1,0:T(8,128)(2,1)S(1)}, u32[]{:S(2)}, u32[]{:S(2)}) %collective-permute-start.6) | collective-permute-done | bytes 196640 | tf_op jit(solution)/shard_map/ppermute | solution.py:522
  29.5 0.9 %shrink.4.shrunk_here_ref = f32[2,48,640]{2,1,0:T(8,128)S(1)} custom-call(s32[1]{0:T(128)} %bitcast.me_ref, s32[8,8]{1,0:T(8,128)S(1)} %copy-done.5, s32[8]{0:T(128)S(1)} %copy-done.7, bf16[384,2560]{1,0:T(8,128)(2,1)S(1)} %copy-done, f32[384,512]{1,0:T(8,128)S(1)} %get-tuple-element.15.refs_1_.refs_5_.refs_9_, bf16[64,1536]{1,0:T(8,128)(2,1)S(1)} %hold.4.refs_2_.rest_0_, ...), custom_call_target="tpu_custom_call" | custom-call | flops 60000000 | bytes 400000 | tf_op jit(solution)/shard_map/shrink/pallas_call | solution.py:273
  30.5 0.1 collective-permute-start.14
  30.5 0.8 %collective-permute-start.7 = (bf16[64,1536]{1,0:T(8,128)(2,1)S(1)}, bf16[64,1536]{1,0:T(8,128)(2,1)S(1)}, u32[]{:S(2)}, u32[]{:S(2)}) collective-permute-start(bf16[64,1536]{1,0:T(8,128)(2,1)S(1)} %collective-permute-done.6.refs_3_), channel_id=1, source_target_pairs={{0,4},{4,8},{8,12},{12,14},{14,10},{10,6},{6,2},{2,0},{1,5},{5,9},... | collective-permute-start | bytes 589832 | tf_op jit(solution)/shard_map/ppermute | solution.py:522
  31.4 1.2 %collective-permute-start.9 = (bf16[64,1536]{1,0:T(8,128)(2,1)S(1)}, bf16[64,1536]{1,0:T(8,128)(2,1)S(1)}, u32[]{:S(2)}, u32[]{:S(2)}) collective-permute-start(bf16[64,1536]{1,0:T(8,128)(2,1)S(1)} %collective-permute-done.8.refs_6_.rest_1_), channel_id=1, source_target_pairs={{4,0},{8,4},{12,8},{14,12},{10,14},{6,10},{2,6},{0,2},{5,1},{9,5},... | collective-permute-start | bytes 589832 | tf_op jit(solution)/shard_map/ppermute | solution.py:523
  32.6 1.6 %collective-permute-start.13 = (bf16[64,1536]{1,0:T(8,128)(2,1)S(1)}, bf16[64,1536]{1,0:T(8,128)(2,1)S(1)}, u32[]{:S(2)}, u32[]{:S(2)}) collective-permute-start(bf16[64,1536]{1,0:T(8,128)(2,1)S(1)} %collective-permute-done.11.refs_7_), channel_id=1, source_target_pairs={{4,0},{8,4},{12,8},{14,12},{10,14},{6,10},{2,6},{0,2},{5,1},{9,5},... | collective-permute-start | bytes 589832 | tf_op jit(solution)/shard_map/ppermute | solution.py:559
  34.2 0.5 collective-permute-start.12
  34.7 4.5 %finish.3 = (bf16[384,16,128]{2,1,0:T(8,128)(2,1)}, bf16[1536,128]{1,0:T(8,128)(2,1)}, f32[8,128]{1,0:T(8,128)}) custom-call(s32[1]{0:T(128)} %bitcast.me_ref, s32[8,8]{1,0:T(8,128)S(1)} %copy-done.5, s32[8]{0:T(128)S(1)} %copy-done.7, s32[8]{0:T(128)S(1)} %copy-done.8, f32[384,512]{1,0:T(8,128)S(1)} %get-tuple-element.14.rest_0_.here_ref, ...), custom_call_target="tpu_custom_call" | custom-call | flops 270000000 | bytes 900000 | tf_op jit(solution)/shard_map/finish/pallas_call | solution.py:424
  39.2 3.4 %finish.4 = (bf16[384,16,128]{2,1,0:T(8,128)(2,1)}, bf16[1536,128]{1,0:T(8,128)(2,1)}, f32[8,128]{1,0:T(8,128)S(1)}) custom-call(s32[1]{0:T(128)} %bitcast.me_ref, s32[8,8]{1,0:T(8,128)S(1)} %copy-done.5, s32[8]{0:T(128)S(1)} %copy-done.7, s32[8]{0:T(128)S(1)} %copy-done.8, ...), custom_call_target="tpu_custom_call", output_to_operand_aliasing={{0}: (14, {}), {1}: (15, {})} | custom-call | flops 180000000 | bytes 600000 | tf_op jit(solution)/shard_map/finish/pallas_call | solution.py:424
  42.6 1.0 %shrink.5.shrunk_here_ref = f32[3,48,640]{2,1,0:T(8,128)S(1)} custom-call(s32[1]{0:T(128)} %bitcast.me_ref, s32[8,8]{1,0:T(8,128)S(1)} %copy-done.5, s32[8]{0:T(128)S(1)} %copy-done.7, bf16[384,2560]{1,0:T(8,128)(2,1)S(1)} %copy-done, f32[384,512]{1,0:T(8,128)S(1)} %get-tuple-element.15.refs_1_.refs_5_.refs_9_, ...), custom_call_target="tpu_custom_call" | custom-call | flops 90000000 | bytes 600000 | tf_op jit(solution)/shard_map/shrink/pallas_call | solution.py:273
  43.6 0.0 collective-permute-start.16
  43.6 1.7 %collective-permute-done.16.shrunk_there_ref = f32[3,48,640]{2,1,0:T(8,128)S(1)} collective-permute-done((f32[3,48,640]{2,1,0:T(8,128)S(1)}, f32[3,48,640]{2,1,0:T(8,128)S(1)}, u32[]{:S(2)}, u32[]{:S(2)}) %collective-permute-start.16) | collective-permute-done | bytes 368672 | tf_op jit(solution)/shard_map/ppermute | solution.py:518
  45.3 4.5 %finish.5 = (bf16[384,16,128]{2,1,0:T(8,128)(2,1)}, bf16[1536,128]{1,0:T(8,128)(2,1)}, f32[8,128]{1,0:T(8,128)}) custom-call(s32[1]{0:T(128)} %bitcast.me_ref, s32[8,8]{1,0:T(8,128)S(1)} %copy-done.5, s32[8]{0:T(128)S(1)} %copy-done.7, s32[8]{0:T(128)S(1)} %copy-done.8, ...), custom_call_target="tpu_custom_call", output_to_operand_aliasing={{0}: (15, {}), {1}: (16, {})} | custom-call | flops 270000000 | bytes 900000 | tf_op jit(solution)/shard_map/finish/pallas_call | solution.py:424
  (39 shorter events, 0.1 us)
Async XLA Ops:
  0.6 1.0 %copy-start.4 = (bf16[1,2560,64]{1,2,0:T(8,128)(2,1)S(1)}, bf16[1,2560,64]{1,2,0:T(8,128)(2,1)}, u32[]{:S(2)}) copy-start(bf16[1,2560,64]{1,2,0:T(8,128)(2,1)} %param.14) | copy-start | bytes 983044
  1.6 0.9 %copy-start.6 = (bf16[1,64,4,256]{3,2,1,0:T(4,128)(2,1)S(1)}, bf16[1,64,4,256]{3,2,1,0:T(4,128)(2,1)}, u32[]{:S(2)}) copy-start(bf16[1,64,4,256]{3,2,1,0:T(4,128)(2,1)} %param.15) | copy-start | bytes 393220
  2.7 12.8 %collective-permute-start = (bf16[64,1536]{1,0:T(8,128)(2,1)S(1)}, bf16[64,1536]{1,0:T(8,128)(2,1)S(1)}, u32[]{:S(2)}, u32[]{:S(2)}) collective-permute-start(bf16[64,1536]{1,0:T(8,128)(2,1)S(1)} %get-tuple-element.13.rest_0_.refs_2_), channel_id=1, source_target_pairs={{0,4},{4,8},{8,12},{12,14},{14,10},{10,6},{6,2},{2,0},{1,5},{5,9},... | collective-permute-start | bytes 589832 | tf_op jit(solution)/shard_map/ppermute | solution.py:522
  5.8 9.7 %collective-permute-start.4 = (bf16[64,1536]{1,0:T(8,128)(2,1)S(1)}, bf16[64,1536]{1,0:T(8,128)(2,1)S(1)}, u32[]{:S(2)}, u32[]{:S(2)}) collective-permute-start(bf16[64,1536]{1,0:T(8,128)(2,1)S(1)} %get-tuple-element.13.rest_0_.refs_2_), channel_id=1, source_target_pairs={{4,0},{8,4},{12,8},{14,12},{10,14},{6,10},{2,6},{0,2},{5,1},{9,5},... | collective-permute-start | bytes 589832 | tf_op jit(solution)/shard_map/ppermute | solution.py:523
  5.8 9.7 %collective-permute-start.3 = (bf16[64,1536]{1,0:T(8,128)(2,1)S(1)}, bf16[64,1536]{1,0:T(8,128)(2,1)S(1)}, u32[]{:S(2)}, u32[]{:S(2)}) collective-permute-start(bf16[64,1536]{1,0:T(8,128)(2,1)S(1)} %get-tuple-element.16.refs_3_), channel_id=1, source_target_pairs={{0,4},{4,8},{8,12},{12,14},{14,10},{10,6},{6,2},{2,0},{1,5},{5,9},... | collective-permute-start | bytes 589832 | tf_op jit(solution)/shard_map/ppermute | solution.py:522
  7.8 8.5 %collective-permute-start.5 = (bf16[64,1536]{1,0:T(8,128)(2,1)S(1)}, bf16[64,1536]{1,0:T(8,128)(2,1)S(1)}, u32[]{:S(2)}, u32[]{:S(2)}) collective-permute-start(bf16[64,1536]{1,0:T(8,128)(2,1)S(1)} %get-tuple-element.16.refs_3_), channel_id=1, source_target_pairs={{4,0},{8,4},{12,8},{14,12},{10,14},{6,10},{2,6},{0,2},{5,1},{9,5},... | collective-permute-start | bytes 589832 | tf_op jit(solution)/shard_map/ppermute | solution.py:523
  7.8 1.5 %copy-start = (bf16[384,2560]{1,0:T(8,128)(2,1)S(1)}, bf16[384,2560]{1,0:T(8,128)(2,1)}, u32[]{:S(2)}) copy-start(bf16[384,2560]{1,0:T(8,128)(2,1)} %refs_8_.3) | copy-start | bytes 5898244
  9.4 2.5 %copy-start.10 = (bf16[2560,4,256]{2,1,0:T(4,128)(2,1)S(1)}, bf16[2560,4,256]{2,1,0:T(4,128)(2,1)}, u32[]{:S(2)}) copy-start(bf16[2560,4,256]{2,1,0:T(4,128)(2,1)} %param.13) | copy-start | bytes 15728644
  11.8 4.5 %copy-start.5 = (s32[8,8]{1,0:T(8,128)S(1)}, s32[8,8]{1,0:T(8,128)}, u32[]{:S(2)}) copy-start(s32[8,8]{1,0:T(8,128)} %constant.10.clone.owner_ref) | copy-start | bytes 772
  11.8 4.5 %copy-start.7 = (s32[8]{0:T(128)S(1)}, s32[8]{0:T(128)}, u32[]{:S(2)}) copy-start(s32[8]{0:T(128)} %adapter_ref.11) | copy-start | bytes 100
  16.4 5.1 %copy-start.8 = (s32[8]{0:T(128)S(1)}, s32[8]{0:T(128)}, u32[]{:S(2)}) copy-start(s32[8]{0:T(128)} %length_ref.7) | copy-start | bytes 100
  16.4 5.1 %copy-start.11 = (s32[8,48]{1,0:T(8,128)S(1)}, s32[8,48]{1,0:T(8,128)}, u32[]{:S(2)}) copy-start(s32[8,48]{1,0:T(8,128)} %parent_ref.1) | copy-start | bytes 4612
  17.4 6.4 %collective-permute-start.10 = (bf16[64,1536]{1,0:T(8,128)(2,1)S(1)}, bf16[64,1536]{1,0:T(8,128)(2,1)S(1)}, u32[]{:S(2)}, u32[]{:S(2)}) collective-permute-start(bf16[64,1536]{1,0:T(8,128)(2,1)S(1)} %hold.6), channel_id=1, source_target_pairs={{4,0},{8,4},{12,8},{14,12},{10,14},{6,10},{2,6},{0,2},{5,1},{9,5},... | collective-permute-start | bytes 589832 | tf_op jit(solution)/shard_map/ppermute | solution.py:523
  18.6 7.5 %collective-permute-start.1 = (bf16[64,1536]{1,0:T(8,128)(2,1)S(1)}, bf16[64,1536]{1,0:T(8,128)(2,1)S(1)}, u32[]{:S(2)}, u32[]{:S(2)}) collective-permute-start(bf16[64,1536]{1,0:T(8,128)(2,1)S(1)} %collective-permute-done.refs_6_.rest_1_), channel_id=1, source_target_pairs={{0,4},{4,8},{8,12},{12,14},{14,10},{10,6},{6,2},{2,0},{1,5},{5,9},... | collective-permute-start | bytes 589832 | tf_op jit(solution)/shard_map/ppermute | solution.py:522
  19.4 11.9 %collective-permute-start.15 = (f32[3,48,640]{2,1,0:T(8,128)S(1)}, f32[3,48,640]{2,1,0:T(8,128)S(1)}, u32[]{:S(2)}, u32[]{:S(2)}) collective-permute-start(f32[3,48,640]{2,1,0:T(8,128)S(1)} %shrink.3.token_ref.shrunk_here_ref), channel_id=1, source_target_pairs={{0,1},{1,0},{2,3},{3,2},{4,5},{5,4},{6,7},{7,6},{8,9},{9,8},{10,11... | collective-permute-start | bytes 1105928 | tf_op jit(solution)/shard_map/ppermute | solution.py:518
  19.4 10.1 %collective-permute-start.6 = (bf16[64,1536]{1,0:T(8,128)(2,1)S(1)}, bf16[64,1536]{1,0:T(8,128)(2,1)S(1)}, u32[]{:S(2)}, u32[]{:S(2)}) collective-permute-start(bf16[64,1536]{1,0:T(8,128)(2,1)S(1)} %hold.5), channel_id=1, source_target_pairs={{0,4},{4,8},{8,12},{12,14},{14,10},{10,6},{6,2},{2,0},{1,5},{5,9},... | collective-permute-start | bytes 589832 | tf_op jit(solution)/shard_map/ppermute | solution.py:522
  21.0 8.5 %collective-permute-start.8 = (bf16[64,1536]{1,0:T(8,128)(2,1)S(1)}, bf16[64,1536]{1,0:T(8,128)(2,1)S(1)}, u32[]{:S(2)}, u32[]{:S(2)}) collective-permute-start(bf16[64,1536]{1,0:T(8,128)(2,1)S(1)} %collective-permute-done.4.refs_10_.rest_2_), channel_id=1, source_target_pairs={{4,0},{8,4},{12,8},{14,12},{10,14},{6,10},{2,6},{0,2},{5,1},{9,5},... | collective-permute-start | bytes 589832 | tf_op jit(solution)/shard_map/ppermute | solution.py:523
  23.8 8.9 %collective-permute-start.11 = (bf16[64,1536]{1,0:T(8,128)(2,1)S(1)}, bf16[64,1536]{1,0:T(8,128)(2,1)S(1)}, u32[]{:S(2)}, u32[]{:S(2)}) collective-permute-start(bf16[64,1536]{1,0:T(8,128)(2,1)S(1)} %hold.7.refs_7_), channel_id=1, source_target_pairs={{4,0},{8,4},{12,8},{14,12},{10,14},{6,10},{2,6},{0,2},{5,1},{9,5},... | collective-permute-start | bytes 589832 | tf_op jit(solution)/shard_map/ppermute | solution.py:523
  26.1 8.6 %copy-start.1 = (bf16[384,16,128]{2,1,0:T(8,128)(2,1)S(1)}, bf16[384,16,128]{2,1,0:T(8,128)(2,1)}, u32[]{:S(2)}) copy-start(bf16[384,16,128]{2,1,0:T(8,128)(2,1)} %query_ref.5) | copy-start | bytes 4718596
  26.1 8.6 %copy-start.2 = (bf16[8,128,2,128]{3,2,1,0:T(2,128)(2,1)S(1)}, bf16[8,128,2,128]{3,2,1,0:T(2,128)(2,1)}, u32[]{:S(2)}) copy-start(bf16[8,128,2,128]{3,2,1,0:T(2,128)(2,1)} %param.20) | copy-start | bytes 1572868
  26.1 8.6 %copy-start.3 = (bf16[8,128,2,128]{3,2,1,0:T(2,128)(2,1)S(1)}, bf16[8,128,2,128]{3,2,1,0:T(2,128)(2,1)}, u32[]{:S(2)}) copy-start(bf16[8,128,2,128]{3,2,1,0:T(2,128)(2,1)} %param.21) | copy-start | bytes 1572868
  26.1 8.6 %copy-start.9 = (f32[128]{0:T(128)S(1)}, f32[128]{0:T(128)}, u32[]{:S(2)}) copy-start(f32[128]{0:T(128)} %param.22) | copy-start | bytes 1540
  26.1 8.1 %collective-permute-start.2 = (bf16[64,1536]{1,0:T(8,128)(2,1)S(1)}, bf16[64,1536]{1,0:T(8,128)(2,1)S(1)}, u32[]{:S(2)}, u32[]{:S(2)}) collective-permute-start(bf16[64,1536]{1,0:T(8,128)(2,1)S(1)} %hold.4.refs_2_.rest_0_), channel_id=1, source_target_pairs={{0,4},{4,8},{8,12},{12,14},{14,10},{10,6},{6,2},{2,0},{1,5},{5,9},... | collective-permute-start | bytes 589832 | tf_op jit(solution)/shard_map/ppermute | solution.py:522
  30.5 8.7 %collective-permute-start.14 = (f32[2,48,640]{2,1,0:T(8,128)S(1)}, f32[2,48,640]{2,1,0:T(8,128)S(1)}, u32[]{:S(2)}, u32[]{:S(2)}) collective-permute-start(f32[2,48,640]{2,1,0:T(8,128)S(1)} %shrink.4.shrunk_here_ref), channel_id=1, source_target_pairs={{0,1},{1,0},{2,3},{3,2},{4,5},{5,4},{6,7},{7,6},{8,9},{9,8},{10,11... | collective-permute-start | bytes 737288 | tf_op jit(solution)/shard_map/ppermute | solution.py:518
  30.5 12.0 %collective-permute-start.7 = (bf16[64,1536]{1,0:T(8,128)(2,1)S(1)}, bf16[64,1536]{1,0:T(8,128)(2,1)S(1)}, u32[]{:S(2)}, u32[]{:S(2)}) collective-permute-start(bf16[64,1536]{1,0:T(8,128)(2,1)S(1)} %collective-permute-done.6.refs_3_), channel_id=1, source_target_pairs={{0,4},{4,8},{8,12},{12,14},{14,10},{10,6},{6,2},{2,0},{1,5},{5,9},... | collective-permute-start | bytes 589832 | tf_op jit(solution)/shard_map/ppermute | solution.py:522
  31.4 11.2 %collective-permute-start.9 = (bf16[64,1536]{1,0:T(8,128)(2,1)S(1)}, bf16[64,1536]{1,0:T(8,128)(2,1)S(1)}, u32[]{:S(2)}, u32[]{:S(2)}) collective-permute-start(bf16[64,1536]{1,0:T(8,128)(2,1)S(1)} %collective-permute-done.8.refs_6_.rest_1_), channel_id=1, source_target_pairs={{4,0},{8,4},{12,8},{14,12},{10,14},{6,10},{2,6},{0,2},{5,1},{9,5},... | collective-permute-start | bytes 589832 | tf_op jit(solution)/shard_map/ppermute | solution.py:523
  32.6 10.0 %collective-permute-start.13 = (bf16[64,1536]{1,0:T(8,128)(2,1)S(1)}, bf16[64,1536]{1,0:T(8,128)(2,1)S(1)}, u32[]{:S(2)}, u32[]{:S(2)}) collective-permute-start(bf16[64,1536]{1,0:T(8,128)(2,1)S(1)} %collective-permute-done.11.refs_7_), channel_id=1, source_target_pairs={{4,0},{8,4},{12,8},{14,12},{10,14},{6,10},{2,6},{0,2},{5,1},{9,5},... | collective-permute-start | bytes 589832 | tf_op jit(solution)/shard_map/ppermute | solution.py:559
  34.2 8.4 %collective-permute-start.12 = (bf16[64,1536]{1,0:T(8,128)(2,1)S(1)}, bf16[64,1536]{1,0:T(8,128)(2,1)S(1)}, u32[]{:S(2)}, u32[]{:S(2)}) collective-permute-start(bf16[64,1536]{1,0:T(8,128)(2,1)S(1)} %collective-permute-done.2.refs_2_.rest_0_), channel_id=1, source_target_pairs={{0,4},{4,8},{8,12},{12,14},{14,10},{10,6},{6,2},{2,0},{1,5},{5,9},... | collective-permute-start | bytes 589832 | tf_op jit(solution)/shard_map/ppermute | solution.py:559
  43.6 1.7 %collective-permute-start.16 = (f32[3,48,640]{2,1,0:T(8,128)S(1)}, f32[3,48,640]{2,1,0:T(8,128)S(1)}, u32[]{:S(2)}, u32[]{:S(2)}) collective-permute-start(f32[3,48,640]{2,1,0:T(8,128)S(1)} %shrink.5.shrunk_here_ref), channel_id=1, source_target_pairs={{0,1},{1,0},{2,3},{3,2},{4,5},{5,4},{6,7},{7,6},{8,9},{9,8},{10,11... | collective-permute-start | bytes 1105928 | tf_op jit(solution)/shard_map/ppermute | solution.py:518

commit v13 on v12

--- a/solution.py
+++ b/solution.py
@@ -173,7 +173,7 @@
         cost_estimate=pl.CostEstimate(
             flops=4_000_000_000, bytes_accessed=9_000_000, transcendentals=0
         ),
-        compiler_params=pltpu.CompilerParams(vmem_limit_bytes=24 * 1024 * 1024),
+        compiler_params=pltpu.CompilerParams(vmem_limit_bytes=52 * 1024 * 1024),
         name="base",
     )(core, hidden_states, weight_rows, *after, *held)
 

time: 50 us -> 49.9 us (level)
  local copies, waits for them, and re-layouts: 5.93 us -> 1.91 us
  Pallas kernels: 21.4 us -> 23.4 us
  waiting for transfers between devices: 6.98 us -> 8 us
  starting transfers between devices: 14.7 us -> 15.7 us
    unnamed x24 -> x22, local copies, waits for them, and re-layouts: 5.93 us -> 1.91 us
    ppermute x6, starting transfers between devices: 8.39 us -> 12 us  [per_device(): front = tuple((lax.ppermute(piece, 'pool', onward) for piece in front))]
    ppermute x6, starting transfers between devices: 4.2 us -> 1.59 us  [per_device(): rear = tuple((lax.ppermute(piece, 'pool', backward) for piece in rear))]
    pallas_call x1, Pallas kernels: 3.65 us -> 5.65 us  [base_product(): pl.pallas_call(functools.partial(base_kernel, held_count=len(held)), grid...]
    ppermute x6, waiting for transfers between devices: 0.82 us -> 2.46 us  [per_device(): rear = tuple((lax.ppermute(piece, 'pool', backward) for piece in rear))]
    ppermute x6, waiting for transfers between devices: 4.46 us -> 3.51 us  [per_device(): front = tuple((lax.ppermute(piece, 'pool', onward) for piece in front))]
    ppermute x1, starting transfers between devices: 1.56 us -> 0.91 us  [per_device(): lax.ppermute(rear[1], 'pool', backward)]
    ppermute x1, starting transfers between devices: 0.47 us -> 1.11 us  [per_device(): lax.ppermute(front[0], 'pool', onward)]
  transfers between devices with their start and end apart: 17 -> 17, of which waited for: 4 -> 8; matrix products, arithmetic and copies ran while one was open for 0% -> 0% of each run, Pallas kernels for 30% -> 34%
where the time goes in v13:
time: 49.9 us; the launch traced here: 49.8 us
  Pallas kernels  23.4 us (47%)
  starting transfers between devices  15.7 us (31%)
  waiting for transfers between devices  8 us (16%)
  local copies, waits for them, and re-layouts  1.91 us (4%)
  between operations  0.77 us (2%)
    pallas_call x3, Pallas kernels, finish(): pl.pallas_call(functools.partial(finish_kernel, count=count, slot=slot, k...  12.4 us
    ppermute x6, starting transfers between devices, per_device(): front = tuple((lax.ppermute(piece, 'pool', onward) for piece in front))  12 us
    pallas_call x1, Pallas kernels, base_product(): pl.pallas_call(functools.partial(base_kernel, held_count=len(held)), grid...  5.65 us
    ppermute x6, waiting for transfers between devices, per_device(): front = tuple((lax.ppermute(piece, 'pool', onward) for piece in front))  3.51 us
    pallas_call x3, Pallas kernels, shrink_rows(): pl.pallas_call(functools.partial(shrink_kernel, columns=columns, cut=cut)...  2.9 us
    ppermute x6, waiting for transfers between devices, per_device(): rear = tuple((lax.ppermute(piece, 'pool', backward) for piece in rear))  2.46 us
    pallas_call x1, Pallas kernels, tree_tables(): pl.pallas_call(functools.partial(tree_kernel, head_size=head_size, kv_hea...  2.27 us
    unnamed x22, local copies, waits for them, and re-layouts  1.91 us
  transfers between devices with their start and end apart: 17, of which 8 were waited for; matrix products, arithmetic and copies ran while one was open for 0% of the time, Pallas kernels for 34%

profile of v13, /device:TPU:0, one launch (start us, length us, event | category | flops | bytes accessed | tf_op | source)
XLA Modules:
  0.0 49.8 jit_solution(15721123882434790373)
XLA Ops:
  0.6 1.0 %copy-done.4 = bf16[1,2560,64]{1,2,0:T(8,128)(2,1)S(1)} copy-done((bf16[1,2560,64]{1,2,0:T(8,128)(2,1)S(1)}, bf16[1,2560,64]{1,2,0:T(8,128)(2,1)}, u32[]{:S(2)}) %copy-start.4) | copy-done | bytes 327704
  1.6 0.9 %copy-done.6 = bf16[1,64,4,256]{3,2,1,0:T(4,128)(2,1)S(1)} copy-done((bf16[1,64,4,256]{3,2,1,0:T(4,128)(2,1)S(1)}, bf16[1,64,4,256]{3,2,1,0:T(4,128)(2,1)}, u32[]{:S(2)}) %copy-start.6) | copy-done | bytes 131096
  2.5 0.2 pack.1
  2.7 3.1 %collective-permute-start = (bf16[64,1536]{1,0:T(8,128)(2,1)S(1)}, bf16[64,1536]{1,0:T(8,128)(2,1)S(1)}, u32[]{:S(2)}, u32[]{:S(2)}) collective-permute-start(bf16[64,1536]{1,0:T(8,128)(2,1)S(1)} %get-tuple-element.13.rest_0_.refs_2_), channel_id=1, source_target_pairs={{0,4},{4,8},{8,12},{12,14},{14,10},{10,6},{6,2},{2,0},{1,5},{5,9},... | collective-permute-start | bytes 589832 | tf_op jit(solution)/shard_map/ppermute | solution.py:522
  5.8 2.0 %collective-permute-start.3 = (bf16[64,1536]{1,0:T(8,128)(2,1)S(1)}, bf16[64,1536]{1,0:T(8,128)(2,1)S(1)}, u32[]{:S(2)}, u32[]{:S(2)}) collective-permute-start(bf16[64,1536]{1,0:T(8,128)(2,1)S(1)} %get-tuple-element.16.refs_3_), channel_id=1, source_target_pairs={{0,4},{4,8},{8,12},{12,14},{14,10},{10,6},{6,2},{2,0},{1,5},{5,9},... | collective-permute-start | bytes 589832 | tf_op jit(solution)/shard_map/ppermute | solution.py:522
  7.8 5.7 %base.1 = (f32[384,512]{1,0:T(8,128)S(1)}, f32[384,512]{1,0:T(8,128)S(1)}) custom-call(s32[1]{0:T(128)} %bitcast.1.core_ref, bf16[384,2560]{1,0:T(8,128)(2,1)} %refs_8_.3, bf16[20480,128]{1,0:T(8,128)(2,1)} %bitcast.35, bf16[64,1536]{1,0:T(8,128)(2,1)S(1)} %get-tuple-element.13.rest_0_.refs_2_), custom_call_target="tpu_custom_call" | custom-call | flops 4000000000 | bytes 9000000 | tf_op jit(solution)/shard_map/base/pallas_call | solution.py:154
  13.5 0.1 collective-permute-done.4.refs_10_.rest_2_
  13.6 1.2 %collective-permute-done.3.refs_7_.array_ref = bf16[64,1536]{1,0:T(8,128)(2,1)S(1)} collective-permute-done((bf16[64,1536]{1,0:T(8,128)(2,1)S(1)}, bf16[64,1536]{1,0:T(8,128)(2,1)S(1)}, u32[]{:S(2)}, u32[]{:S(2)}) %collective-permute-start.3) | collective-permute-done | bytes 196640 | tf_op jit(solution)/shard_map/ppermute | solution.py:522
  14.8 1.5 %collective-permute-done.5.refs_11_.array_ref = bf16[64,1536]{1,0:T(8,128)(2,1)S(1)} collective-permute-done((bf16[64,1536]{1,0:T(8,128)(2,1)S(1)}, bf16[64,1536]{1,0:T(8,128)(2,1)S(1)}, u32[]{:S(2)}, u32[]{:S(2)}) %collective-permute-start.5) | collective-permute-done | bytes 196640 | tf_op jit(solution)/shard_map/ppermute | solution.py:523
  16.4 1.0 %shrink.3.token_ref.shrunk_here_ref = f32[3,48,640]{2,1,0:T(8,128)S(1)} custom-call(s32[1]{0:T(128)} %bitcast.me_ref, s32[8,8]{1,0:T(8,128)S(1)} %copy-done.5, s32[8]{0:T(128)S(1)} %copy-done.7, bf16[384,2560]{1,0:T(8,128)(2,1)S(1)} %copy-done, f32[384,512]{1,0:T(8,128)S(1)} %get-tuple-element.15.refs_1_.refs_5_.refs_9_, ...), custom_call_target="tpu_custom_call" | custom-call | flops 90000000 | bytes 600000 | tf_op jit(solution)/shard_map/shrink/pallas_call | solution.py:273
  17.4 0.3 collective-permute-start.10
  17.7 1.7 %collective-permute-start.1 = (bf16[64,1536]{1,0:T(8,128)(2,1)S(1)}, bf16[64,1536]{1,0:T(8,128)(2,1)S(1)}, u32[]{:S(2)}, u32[]{:S(2)}) collective-permute-start(bf16[64,1536]{1,0:T(8,128)(2,1)S(1)} %collective-permute-done.refs_6_.rest_1_), channel_id=1, source_target_pairs={{0,4},{4,8},{8,12},{12,14},{14,10},{10,6},{6,2},{2,0},{1,5},{5,9},... | collective-permute-start | bytes 589832 | tf_op jit(solution)/shard_map/ppermute | solution.py:522
  19.5 1.6 %collective-permute-start.6 = (bf16[64,1536]{1,0:T(8,128)(2,1)S(1)}, bf16[64,1536]{1,0:T(8,128)(2,1)S(1)}, u32[]{:S(2)}, u32[]{:S(2)}) collective-permute-start(bf16[64,1536]{1,0:T(8,128)(2,1)S(1)} %hold.5), channel_id=1, source_target_pairs={{0,4},{4,8},{8,12},{12,14},{14,10},{10,6},{6,2},{2,0},{1,5},{5,9},... | collective-permute-start | bytes 589832 | tf_op jit(solution)/shard_map/ppermute | solution.py:522
  21.0 0.4 collective-permute-start.8
  21.5 2.3 %tree.1.token_ref.table_ref = f32[384,384]{1,0:T(8,128)S(1)} custom-call(s32[8]{0:T(128)S(1)} %copy-done.8, s32[8,48]{1,0:T(8,128)S(1)} %copy-done.10, f32[384,512]{1,0:T(8,128)S(1)} %get-tuple-element.14.rest_0_.here_ref), custom_call_target="tpu_custom_call" | custom-call | flops 1000000000 | bytes 8000000 | tf_op jit(solution)/shard_map/tree/pallas_call | solution.py:225
  23.8 0.3 collective-permute-start.11
  24.2 2.0 %collective-permute-start.2 = (bf16[64,1536]{1,0:T(8,128)(2,1)S(1)}, bf16[64,1536]{1,0:T(8,128)(2,1)S(1)}, u32[]{:S(2)}, u32[]{:S(2)}) collective-permute-start(bf16[64,1536]{1,0:T(8,128)(2,1)S(1)} %hold.4.refs_2_.rest_0_), channel_id=1, source_target_pairs={{0,4},{4,8},{8,12},{12,14},{14,10},{10,6},{6,2},{2,0},{1,5},{5,9},... | collective-permute-start | bytes 589832 | tf_op jit(solution)/shard_map/ppermute | solution.py:522
  26.2 2.2 %collective-permute-done.6.refs_3_ = bf16[64,1536]{1,0:T(8,128)(2,1)S(1)} collective-permute-done((bf16[64,1536]{1,0:T(8,128)(2,1)S(1)}, bf16[64,1536]{1,0:T(8,128)(2,1)S(1)}, u32[]{:S(2)}, u32[]{:S(2)}) %collective-permute-start.6) | collective-permute-done | bytes 196640 | tf_op jit(solution)/shard_map/ppermute | solution.py:522
  28.4 0.4 collective-permute-done.8.refs_6_.rest_1_
  28.8 0.9 %shrink.4.shrunk_here_ref = f32[2,48,640]{2,1,0:T(8,128)S(1)} custom-call(s32[1]{0:T(128)} %bitcast.me_ref, s32[8,8]{1,0:T(8,128)S(1)} %copy-done.5, s32[8]{0:T(128)S(1)} %copy-done.7, bf16[384,2560]{1,0:T(8,128)(2,1)S(1)} %copy-done, f32[384,512]{1,0:T(8,128)S(1)} %get-tuple-element.15.refs_1_.refs_5_.refs_9_, bf16[64,1536]{1,0:T(8,128)(2,1)S(1)} %hold.4.refs_2_.rest_0_, ...), custom_call_target="tpu_custom_call" | custom-call | flops 60000000 | bytes 400000 | tf_op jit(solution)/shard_map/shrink/pallas_call | solution.py:273
  29.7 0.1 collective-permute-start.14
  29.8 1.6 %collective-permute-start.7 = (bf16[64,1536]{1,0:T(8,128)(2,1)S(1)}, bf16[64,1536]{1,0:T(8,128)(2,1)S(1)}, u32[]{:S(2)}, u32[]{:S(2)}) collective-permute-start(bf16[64,1536]{1,0:T(8,128)(2,1)S(1)} %collective-permute-done.6.refs_3_), channel_id=1, source_target_pairs={{0,4},{4,8},{8,12},{12,14},{14,10},{10,6},{6,2},{2,0},{1,5},{5,9},... | collective-permute-start | bytes 589832 | tf_op jit(solution)/shard_map/ppermute | solution.py:522
  31.4 0.5 collective-permute-start.9
  31.9 0.4 collective-permute-done.11.refs_7_
  32.3 0.9 %collective-permute-start.13 = (bf16[64,1536]{1,0:T(8,128)(2,1)S(1)}, bf16[64,1536]{1,0:T(8,128)(2,1)S(1)}, u32[]{:S(2)}, u32[]{:S(2)}) collective-permute-start(bf16[64,1536]{1,0:T(8,128)(2,1)S(1)} %collective-permute-done.11.refs_7_), channel_id=1, source_target_pairs={{4,0},{8,4},{12,8},{14,12},{10,14},{6,10},{2,6},{0,2},{5,1},{9,5},... | collective-permute-start | bytes 589832 | tf_op jit(solution)/shard_map/ppermute | solution.py:559
  33.2 1.1 %collective-permute-start.12 = (bf16[64,1536]{1,0:T(8,128)(2,1)S(1)}, bf16[64,1536]{1,0:T(8,128)(2,1)S(1)}, u32[]{:S(2)}, u32[]{:S(2)}) collective-permute-start(bf16[64,1536]{1,0:T(8,128)(2,1)S(1)} %collective-permute-done.2.refs_2_.rest_0_), channel_id=1, source_target_pairs={{0,4},{4,8},{8,12},{12,14},{14,10},{10,6},{6,2},{2,0},{1,5},{5,9},... | collective-permute-start | bytes 589832 | tf_op jit(solution)/shard_map/ppermute | solution.py:559
  34.3 4.5 %finish.3 = (bf16[384,16,128]{2,1,0:T(8,128)(2,1)}, bf16[1536,128]{1,0:T(8,128)(2,1)}, f32[8,128]{1,0:T(8,128)}) custom-call(s32[1]{0:T(128)} %bitcast.me_ref, s32[8,8]{1,0:T(8,128)S(1)} %copy-done.5, s32[8]{0:T(128)S(1)} %copy-done.7, s32[8]{0:T(128)S(1)} %copy-done.8, f32[384,512]{1,0:T(8,128)S(1)} %get-tuple-element.14.rest_0_.here_ref, ...), custom_call_target="tpu_custom_call" | custom-call | flops 270000000 | bytes 900000 | tf_op jit(solution)/shard_map/finish/pallas_call | solution.py:424
  38.8 3.4 %finish.4 = (bf16[384,16,128]{2,1,0:T(8,128)(2,1)}, bf16[1536,128]{1,0:T(8,128)(2,1)}, f32[8,128]{1,0:T(8,128)S(1)}) custom-call(s32[1]{0:T(128)} %bitcast.me_ref, s32[8,8]{1,0:T(8,128)S(1)} %copy-done.5, s32[8]{0:T(128)S(1)} %copy-done.7, s32[8]{0:T(128)S(1)} %copy-done.8, ...), custom_call_target="tpu_custom_call", output_to_operand_aliasing={{0}: (14, {}), {1}: (15, {})} | custom-call | flops 180000000 | bytes 600000 | tf_op jit(solution)/shard_map/finish/pallas_call | solution.py:424
  42.2 0.3 collective-permute-done.13.refs_11_
  42.6 1.0 %shrink.5.shrunk_here_ref = f32[3,48,640]{2,1,0:T(8,128)S(1)} custom-call(s32[1]{0:T(128)} %bitcast.me_ref, s32[8,8]{1,0:T(8,128)S(1)} %copy-done.5, s32[8]{0:T(128)S(1)} %copy-done.7, bf16[384,2560]{1,0:T(8,128)(2,1)S(1)} %copy-done, f32[384,512]{1,0:T(8,128)S(1)} %get-tuple-element.15.refs_1_.refs_5_.refs_9_, ...), custom_call_target="tpu_custom_call" | custom-call | flops 90000000 | bytes 600000 | tf_op jit(solution)/shard_map/shrink/pallas_call | solution.py:273
  43.6 1.7 %collective-permute-done.16.shrunk_there_ref = f32[3,48,640]{2,1,0:T(8,128)S(1)} collective-permute-done((f32[3,48,640]{2,1,0:T(8,128)S(1)}, f32[3,48,640]{2,1,0:T(8,128)S(1)}, u32[]{:S(2)}, u32[]{:S(2)}) %collective-permute-start.16) | collective-permute-done | bytes 368672 | tf_op jit(solution)/shard_map/ppermute | solution.py:518
  45.3 4.5 %finish.5 = (bf16[384,16,128]{2,1,0:T(8,128)(2,1)}, bf16[1536,128]{1,0:T(8,128)(2,1)}, f32[8,128]{1,0:T(8,128)}) custom-call(s32[1]{0:T(128)} %bitcast.me_ref, s32[8,8]{1,0:T(8,128)S(1)} %copy-done.5, s32[8]{0:T(128)S(1)} %copy-done.7, s32[8]{0:T(128)S(1)} %copy-done.8, ...), custom_call_target="tpu_custom_call", output_to_operand_aliasing={{0}: (15, {}), {1}: (16, {})} | custom-call | flops 270000000 | bytes 900000 | tf_op jit(solution)/shard_map/finish/pallas_call | solution.py:424
  (37 shorter events, 0.2 us)
Async XLA Ops:
  0.6 1.0 %copy-start.4 = (bf16[1,2560,64]{1,2,0:T(8,128)(2,1)S(1)}, bf16[1,2560,64]{1,2,0:T(8,128)(2,1)}, u32[]{:S(2)}) copy-start(bf16[1,2560,64]{1,2,0:T(8,128)(2,1)} %param.14) | copy-start | bytes 983044
  1.6 0.9 %copy-start.6 = (bf16[1,64,4,256]{3,2,1,0:T(4,128)(2,1)S(1)}, bf16[1,64,4,256]{3,2,1,0:T(4,128)(2,1)}, u32[]{:S(2)}) copy-start(bf16[1,64,4,256]{3,2,1,0:T(4,128)(2,1)} %param.15) | copy-start | bytes 393220
  2.7 10.8 %collective-permute-start = (bf16[64,1536]{1,0:T(8,128)(2,1)S(1)}, bf16[64,1536]{1,0:T(8,128)(2,1)S(1)}, u32[]{:S(2)}, u32[]{:S(2)}) collective-permute-start(bf16[64,1536]{1,0:T(8,128)(2,1)S(1)} %get-tuple-element.13.rest_0_.refs_2_), channel_id=1, source_target_pairs={{0,4},{4,8},{8,12},{12,14},{14,10},{10,6},{6,2},{2,0},{1,5},{5,9},... | collective-permute-start | bytes 589832 | tf_op jit(solution)/shard_map/ppermute | solution.py:522
  5.8 7.8 %collective-permute-start.4 = (bf16[64,1536]{1,0:T(8,128)(2,1)S(1)}, bf16[64,1536]{1,0:T(8,128)(2,1)S(1)}, u32[]{:S(2)}, u32[]{:S(2)}) collective-permute-start(bf16[64,1536]{1,0:T(8,128)(2,1)S(1)} %get-tuple-element.13.rest_0_.refs_2_), channel_id=1, source_target_pairs={{4,0},{8,4},{12,8},{14,12},{10,14},{6,10},{2,6},{0,2},{5,1},{9,5},... | collective-permute-start | bytes 589832 | tf_op jit(solution)/shard_map/ppermute | solution.py:523
  5.8 9.0 %collective-permute-start.3 = (bf16[64,1536]{1,0:T(8,128)(2,1)S(1)}, bf16[64,1536]{1,0:T(8,128)(2,1)S(1)}, u32[]{:S(2)}, u32[]{:S(2)}) collective-permute-start(bf16[64,1536]{1,0:T(8,128)(2,1)S(1)} %get-tuple-element.16.refs_3_), channel_id=1, source_target_pairs={{0,4},{4,8},{8,12},{12,14},{14,10},{10,6},{6,2},{2,0},{1,5},{5,9},... | collective-permute-start | bytes 589832 | tf_op jit(solution)/shard_map/ppermute | solution.py:522
  7.8 8.5 %collective-permute-start.5 = (bf16[64,1536]{1,0:T(8,128)(2,1)S(1)}, bf16[64,1536]{1,0:T(8,128)(2,1)S(1)}, u32[]{:S(2)}, u32[]{:S(2)}) collective-permute-start(bf16[64,1536]{1,0:T(8,128)(2,1)S(1)} %get-tuple-element.16.refs_3_), channel_id=1, source_target_pairs={{4,0},{8,4},{12,8},{14,12},{10,14},{6,10},{2,6},{0,2},{5,1},{9,5},... | collective-permute-start | bytes 589832 | tf_op jit(solution)/shard_map/ppermute | solution.py:523
  7.8 8.5 %copy-start = (bf16[384,2560]{1,0:T(8,128)(2,1)S(1)}, bf16[384,2560]{1,0:T(8,128)(2,1)}, u32[]{:S(2)}) copy-start(bf16[384,2560]{1,0:T(8,128)(2,1)} %refs_8_.3) | copy-start | bytes 5898244
  7.8 8.5 %copy-start.5 = (s32[8,8]{1,0:T(8,128)S(1)}, s32[8,8]{1,0:T(8,128)}, u32[]{:S(2)}) copy-start(s32[8,8]{1,0:T(8,128)} %constant.10.clone.owner_ref) | copy-start | bytes 772
  7.8 8.5 %copy-start.7 = (s32[8]{0:T(128)S(1)}, s32[8]{0:T(128)}, u32[]{:S(2)}) copy-start(s32[8]{0:T(128)} %adapter_ref.11) | copy-start | bytes 100
  16.4 5.1 %copy-start.8 = (s32[8]{0:T(128)S(1)}, s32[8]{0:T(128)}, u32[]{:S(2)}) copy-start(s32[8]{0:T(128)} %length_ref.7) | copy-start | bytes 100
  16.4 5.1 %copy-start.10 = (s32[8,48]{1,0:T(8,128)S(1)}, s32[8,48]{1,0:T(8,128)}, u32[]{:S(2)}) copy-start(s32[8,48]{1,0:T(8,128)} %parent_ref.1) | copy-start | bytes 4612
  17.4 6.4 %collective-permute-start.10 = (bf16[64,1536]{1,0:T(8,128)(2,1)S(1)}, bf16[64,1536]{1,0:T(8,128)(2,1)S(1)}, u32[]{:S(2)}, u32[]{:S(2)}) collective-permute-start(bf16[64,1536]{1,0:T(8,128)(2,1)S(1)} %hold.6), channel_id=1, source_target_pairs={{4,0},{8,4},{12,8},{14,12},{10,14},{6,10},{2,6},{0,2},{5,1},{9,5},... | collective-permute-start | bytes 589832 | tf_op jit(solution)/shard_map/ppermute | solution.py:523
  17.7 6.5 %collective-permute-start.1 = (bf16[64,1536]{1,0:T(8,128)(2,1)S(1)}, bf16[64,1536]{1,0:T(8,128)(2,1)S(1)}, u32[]{:S(2)}, u32[]{:S(2)}) collective-permute-start(bf16[64,1536]{1,0:T(8,128)(2,1)S(1)} %collective-permute-done.refs_6_.rest_1_), channel_id=1, source_target_pairs={{0,4},{4,8},{8,12},{12,14},{14,10},{10,6},{6,2},{2,0},{1,5},{5,9},... | collective-permute-start | bytes 589832 | tf_op jit(solution)/shard_map/ppermute | solution.py:522
  19.5 11.9 %collective-permute-start.15 = (f32[3,48,640]{2,1,0:T(8,128)S(1)}, f32[3,48,640]{2,1,0:T(8,128)S(1)}, u32[]{:S(2)}, u32[]{:S(2)}) collective-permute-start(f32[3,48,640]{2,1,0:T(8,128)S(1)} %shrink.3.token_ref.shrunk_here_ref), channel_id=1, source_target_pairs={{0,1},{1,0},{2,3},{3,2},{4,5},{5,4},{6,7},{7,6},{8,9},{9,8},{10,11... | collective-permute-start | bytes 1105928 | tf_op jit(solution)/shard_map/ppermute | solution.py:518
  19.5 8.9 %collective-permute-start.6 = (bf16[64,1536]{1,0:T(8,128)(2,1)S(1)}, bf16[64,1536]{1,0:T(8,128)(2,1)S(1)}, u32[]{:S(2)}, u32[]{:S(2)}) collective-permute-start(bf16[64,1536]{1,0:T(8,128)(2,1)S(1)} %hold.5), channel_id=1, source_target_pairs={{0,4},{4,8},{8,12},{12,14},{14,10},{10,6},{6,2},{2,0},{1,5},{5,9},... | collective-permute-start | bytes 589832 | tf_op jit(solution)/shard_map/ppermute | solution.py:522
  21.0 7.7 %collective-permute-start.8 = (bf16[64,1536]{1,0:T(8,128)(2,1)S(1)}, bf16[64,1536]{1,0:T(8,128)(2,1)S(1)}, u32[]{:S(2)}, u32[]{:S(2)}) collective-permute-start(bf16[64,1536]{1,0:T(8,128)(2,1)S(1)} %collective-permute-done.4.refs_10_.rest_2_), channel_id=1, source_target_pairs={{4,0},{8,4},{12,8},{14,12},{10,14},{6,10},{2,6},{0,2},{5,1},{9,5},... | collective-permute-start | bytes 589832 | tf_op jit(solution)/shard_map/ppermute | solution.py:523
  23.8 8.5 %collective-permute-start.11 = (bf16[64,1536]{1,0:T(8,128)(2,1)S(1)}, bf16[64,1536]{1,0:T(8,128)(2,1)S(1)}, u32[]{:S(2)}, u32[]{:S(2)}) collective-permute-start(bf16[64,1536]{1,0:T(8,128)(2,1)S(1)} %hold.7.refs_7_), channel_id=1, source_target_pairs={{4,0},{8,4},{12,8},{14,12},{10,14},{6,10},{2,6},{0,2},{5,1},{9,5},... | collective-permute-start | bytes 589832 | tf_op jit(solution)/shard_map/ppermute | solution.py:523
  24.2 10.1 %copy-start.1 = (bf16[384,16,128]{2,1,0:T(8,128)(2,1)S(1)}, bf16[384,16,128]{2,1,0:T(8,128)(2,1)}, u32[]{:S(2)}) copy-start(bf16[384,16,128]{2,1,0:T(8,128)(2,1)} %query_ref.5) | copy-start | bytes 4718596
  24.2 10.1 %copy-start.2 = (bf16[8,128,2,128]{3,2,1,0:T(2,128)(2,1)S(1)}, bf16[8,128,2,128]{3,2,1,0:T(2,128)(2,1)}, u32[]{:S(2)}) copy-start(bf16[8,128,2,128]{3,2,1,0:T(2,128)(2,1)} %param.20) | copy-start | bytes 1572868
  24.2 10.1 %copy-start.3 = (bf16[8,128,2,128]{3,2,1,0:T(2,128)(2,1)S(1)}, bf16[8,128,2,128]{3,2,1,0:T(2,128)(2,1)}, u32[]{:S(2)}) copy-start(bf16[8,128,2,128]{3,2,1,0:T(2,128)(2,1)} %param.21) | copy-start | bytes 1572868
  24.2 10.1 %copy-start.9 = (f32[128]{0:T(128)S(1)}, f32[128]{0:T(128)}, u32[]{:S(2)}) copy-start(f32[128]{0:T(128)} %param.22) | copy-start | bytes 1540
  24.2 9.0 %collective-permute-start.2 = (bf16[64,1536]{1,0:T(8,128)(2,1)S(1)}, bf16[64,1536]{1,0:T(8,128)(2,1)S(1)}, u32[]{:S(2)}, u32[]{:S(2)}) collective-permute-start(bf16[64,1536]{1,0:T(8,128)(2,1)S(1)} %hold.4.refs_2_.rest_0_), channel_id=1, source_target_pairs={{0,4},{4,8},{8,12},{12,14},{14,10},{10,6},{6,2},{2,0},{1,5},{5,9},... | collective-permute-start | bytes 589832 | tf_op jit(solution)/shard_map/ppermute | solution.py:522
  29.7 9.1 %collective-permute-start.14 = (f32[2,48,640]{2,1,0:T(8,128)S(1)}, f32[2,48,640]{2,1,0:T(8,128)S(1)}, u32[]{:S(2)}, u32[]{:S(2)}) collective-permute-start(f32[2,48,640]{2,1,0:T(8,128)S(1)} %shrink.4.shrunk_here_ref), channel_id=1, source_target_pairs={{0,1},{1,0},{2,3},{3,2},{4,5},{5,4},{6,7},{7,6},{8,9},{9,8},{10,11... | collective-permute-start | bytes 737288 | tf_op jit(solution)/shard_map/ppermute | solution.py:518
  29.8 12.5 %collective-permute-start.7 = (bf16[64,1536]{1,0:T(8,128)(2,1)S(1)}, bf16[64,1536]{1,0:T(8,128)(2,1)S(1)}, u32[]{:S(2)}, u32[]{:S(2)}) collective-permute-start(bf16[64,1536]{1,0:T(8,128)(2,1)S(1)} %collective-permute-done.6.refs_3_), channel_id=1, source_target_pairs={{0,4},{4,8},{8,12},{12,14},{14,10},{10,6},{6,2},{2,0},{1,5},{5,9},... | collective-permute-start | bytes 589832 | tf_op jit(solution)/shard_map/ppermute | solution.py:522
  31.4 10.8 %collective-permute-start.9 = (bf16[64,1536]{1,0:T(8,128)(2,1)S(1)}, bf16[64,1536]{1,0:T(8,128)(2,1)S(1)}, u32[]{:S(2)}, u32[]{:S(2)}) collective-permute-start(bf16[64,1536]{1,0:T(8,128)(2,1)S(1)} %collective-permute-done.8.refs_6_.rest_1_), channel_id=1, source_target_pairs={{4,0},{8,4},{12,8},{14,12},{10,14},{6,10},{2,6},{0,2},{5,1},{9,5},... | collective-permute-start | bytes 589832 | tf_op jit(solution)/shard_map/ppermute | solution.py:523
  32.3 10.3 %collective-permute-start.13 = (bf16[64,1536]{1,0:T(8,128)(2,1)S(1)}, bf16[64,1536]{1,0:T(8,128)(2,1)S(1)}, u32[]{:S(2)}, u32[]{:S(2)}) collective-permute-start(bf16[64,1536]{1,0:T(8,128)(2,1)S(1)} %collective-permute-done.11.refs_7_), channel_id=1, source_target_pairs={{4,0},{8,4},{12,8},{14,12},{10,14},{6,10},{2,6},{0,2},{5,1},{9,5},... | collective-permute-start | bytes 589832 | tf_op jit(solution)/shard_map/ppermute | solution.py:559
  33.2 9.4 %collective-permute-start.12 = (bf16[64,1536]{1,0:T(8,128)(2,1)S(1)}, bf16[64,1536]{1,0:T(8,128)(2,1)S(1)}, u32[]{:S(2)}, u32[]{:S(2)}) collective-permute-start(bf16[64,1536]{1,0:T(8,128)(2,1)S(1)} %collective-permute-done.2.refs_2_.rest_0_), channel_id=1, source_target_pairs={{0,4},{4,8},{8,12},{12,14},{14,10},{10,6},{6,2},{2,0},{1,5},{5,9},... | collective-permute-start | bytes 589832 | tf_op jit(solution)/shard_map/ppermute | solution.py:559
  43.6 1.7 %collective-permute-start.16 = (f32[3,48,640]{2,1,0:T(8,128)S(1)}, f32[3,48,640]{2,1,0:T(8,128)S(1)}, u32[]{:S(2)}, u32[]{:S(2)}) collective-permute-start(f32[3,48,640]{2,1,0:T(8,128)S(1)} %shrink.5.shrunk_here_ref), channel_id=1, source_target_pairs={{0,1},{1,0},{2,3},{3,2},{4,5},{5,4},{6,7},{7,6},{8,9},{9,8},{10,11... | collective-permute-start | bytes 1105928 | tf_op jit(solution)/shard_map/ppermute | solution.py:518
